TPU v7x, 32 devices: a whole 2x2x4 slice. The times are simulated.
32 devices in a mesh: ctx: 8 (over z, y), tp: 4 (over x, core).
Axes of the slice: x: 2, y: 2, z: 4, core: 2. Of those that a mesh axis runs over, the one named last changes fastest.
Arguments:
- key_act: bfloat16 [2048, 2048], P('ctx', 'tp'), may hold values from -6 to 6
- value_act: bfloat16 [2048, 2048], P('ctx', 'tp'), may hold values from -6 to 6
- query_act: bfloat16 [2048, 2048], P('ctx', 'tp'), may hold values from -6 to 6
- grad_out: bfloat16 [2048, 2048], P('ctx', 'tp'), may hold values from -6 to 6
- long_filter: bfloat16 [2048, 2048], P('ctx', 'tp'), may hold values from -6 to 6
- w_key: bfloat16 [2048, 2048], P(None, 'tp'), may hold values from -0.125 to 0.125
- w_query: bfloat16 [2048, 2048], P(None, 'tp'), may hold values from -0.125 to 0.125
- w_value: bfloat16 [2048, 2048], P(None, 'tp'), may hold values from -0.125 to 0.125
Outputs:
- grad_input: bfloat16 [2048, 2048], P('ctx', 'tp')
- grad_filter: bfloat16 [2048, 2048], P('ctx', 'tp')
All inputs are finite; a program needn't handle non-finite values.
Results may differ from a plain program's by a relative error of at most 0.025.
Values may be sent and summed in bfloat16 or wider, within the bound.
No kernel may reach another device: no remote copies, remote signals or barrier semaphores. Data moves between devices by JAX's collectives and lax.ppermute only.
A program may use at most 128 MiB of HBM per device.

v0:
```python
import math

import jax
import jax.numpy as jnp
import numpy as np
from jax import lax
from jax.experimental import pallas as pl
from jax.experimental.pallas import tpu as pltpu
from jax.sharding import PartitionSpec as P

VMEM_LIMIT = 48 * 1024 * 1024


def compiler_params():
    return pltpu.CompilerParams(vmem_limit_bytes=VMEM_LIMIT)


def dft_tables(blocks, block_len, scale):
    index = np.arange(block_len)
    angle = 2.0 * np.pi * (np.outer(index, index) % block_len) / block_len
    cos, sin = np.cos(angle), np.sin(angle)
    forward = np.block([[cos, -sin], [sin, cos]])
    inverse = forward.T
    rows = np.arange(blocks + 1)
    phase = 2.0 * np.pi * np.outer(rows, index) / (2 * blocks * block_len)
    weight = np.where((rows == 0) | (rows == blocks), 1.0, 2.0)[:, None] * scale
    twiddle = np.stack(
        [np.cos(phase), np.sin(phase), weight * np.cos(phase), weight * np.sin(phase)]
    )
    return (
        jnp.asarray(forward, jnp.bfloat16),
        jnp.asarray(inverse, jnp.bfloat16),
        jnp.asarray(twiddle, jnp.float32),
    )


def half_spectrum(values):
    size = len(values)
    if size == 1:
        return [(values[0], None), (values[0], None)]
    even, odd = half_spectrum(values[0::2]), half_spectrum(values[1::2])
    half = size // 2
    bins = [None] * (size + 1)
    bins[0] = (even[0][0] + odd[0][0], None)
    bins[size] = (even[0][0] - odd[0][0], None)
    bins[half] = (even[half][0], -odd[half][0])
    for k in range(1, half):
        angle = math.pi * k / size
        cos, sin = math.cos(angle), math.sin(angle)
        even_re, even_im = even[k]
        odd_re, odd_im = odd[k]
        if 2 * k == half:
            turn_re = cos * (odd_re + odd_im)
            turn_im = cos * (odd_im - odd_re)
        else:
            turn_re = cos * odd_re + sin * odd_im
            turn_im = cos * odd_im - sin * odd_re
        bins[k] = (even_re + turn_re, even_im + turn_im)
        bins[size - k] = (even_re - turn_re, turn_im - even_im)
    return bins


def half_spectrum_adjoint(bins):
    size = len(bins) - 1
    if size == 1:
        return [bins[0][0] + bins[1][0]]
    half = size // 2
    even, odd = [None] * (half + 1), [None] * (half + 1)
    even[0] = (bins[0][0] + bins[size][0], None)
    odd[0] = (bins[0][0] - bins[size][0], None)
    even[half] = (bins[half][0], None)
    odd[half] = (-bins[half][1], None)
    for k in range(1, half):
        angle = math.pi * k / size
        cos, sin = math.cos(angle), math.sin(angle)
        low_re, low_im = bins[k]
        high_re, high_im = bins[size - k]
        even[k] = (low_re + high_re, low_im - high_im)
        turn_re, turn_im = low_re - high_re, low_im + high_im
        if 2 * k == half:
            odd[k] = (cos * (turn_re - turn_im), cos * (turn_re + turn_im))
        else:
            odd[k] = (cos * turn_re - sin * turn_im, cos * turn_im + sin * turn_re)
    values = [None] * size
    values[0::2] = half_spectrum_adjoint(even)
    values[1::2] = half_spectrum_adjoint(odd)
    return values


def gate_kernel(key_ref, value_ref, query_ref, grad_ref, filter_ref, out_ref):
    blocks, _, channels, block_len = out_ref.shape

    def put(slot, wide):
        turned = wide.T.astype(jnp.bfloat16)
        out_ref[:, slot] = turned.reshape(blocks, channels, block_len)

    put(0, key_ref[...].astype(jnp.float32) * value_ref[...].astype(jnp.float32))
    put(1, filter_ref[...].astype(jnp.float32))
    put(2, query_ref[...].astype(jnp.float32) * grad_ref[...].astype(jnp.float32))


def conv_kernel(in_ref, fwd_ref, inv_ref, twid_ref, out_ref, rows_ref, spec_ref):
    blocks, signals, channels, block_len = in_ref.shape
    chunk = min(channels, 16)
    steps = channels // chunk

    def analyse(step, carry):
        signal = step // steps
        start = pl.multiple_of((step % steps) * chunk, chunk)
        values = [
            in_ref[p, signal, pl.ds(start, chunk), :].astype(jnp.float32) for p in range(blocks)
        ]
        bins = half_spectrum(values)
        for k in range(blocks + 1):
            re, im = bins[k]
            if k == 0:
                im = jnp.zeros_like(re)
            else:
                cos, sin = twid_ref[0, k : k + 1, :], twid_ref[1, k : k + 1, :]
                if im is None:
                    re, im = re * cos, -(re * sin)
                else:
                    re, im = re * cos + im * sin, im * cos - re * sin
            rows_ref[k, signal, pl.ds(start, chunk), :block_len] = re.astype(jnp.bfloat16)
            rows_ref[k, signal, pl.ds(start, chunk), block_len:] = im.astype(jnp.bfloat16)
        return carry

    lax.fori_loop(0, signals * steps, analyse, 0)

    total = (blocks + 1) * signals * channels
    spec_ref[...] = jnp.dot(
        rows_ref[...].reshape(total, 2 * block_len),
        fwd_ref[...],
        preferred_element_type=jnp.float32,
    ).reshape(spec_ref.shape)

    def combine(step, carry):
        k = step // steps
        start = pl.multiple_of((step % steps) * chunk, chunk)
        rows = pl.ds(start, chunk)
        prod_re, prod_im = spec_ref[k, 0, rows, :block_len], spec_ref[k, 0, rows, block_len:]
        kern_re, kern_im = spec_ref[k, 1, rows, :block_len], spec_ref[k, 1, rows, block_len:]
        grad_re, grad_im = spec_ref[k, 2, rows, :block_len], spec_ref[k, 2, rows, block_len:]

        def put(slot, re, im):
            rows_ref[k, slot, rows, :block_len] = re.astype(jnp.bfloat16)
            rows_ref[k, slot, rows, block_len:] = im.astype(jnp.bfloat16)

        put(0, prod_re * kern_re - prod_im * kern_im, prod_re * kern_im + prod_im * kern_re)
        put(1, grad_re * kern_re + grad_im * kern_im, grad_im * kern_re - grad_re * kern_im)
        put(2, grad_re * prod_re + grad_im * prod_im, grad_im * prod_re - grad_re * prod_im)
        return carry

    lax.fori_loop(0, (blocks + 1) * steps, combine, 0)

    spec_ref[...] = jnp.dot(
        rows_ref[...].reshape(total, 2 * block_len),
        inv_ref[...],
        preferred_element_type=jnp.float32,
    ).reshape(spec_ref.shape)

    def synthesise(step, carry):
        signal = step // steps
        start = pl.multiple_of((step % steps) * chunk, chunk)
        rows = pl.ds(start, chunk)
        bins = []
        for k in range(blocks + 1):
            re, im = spec_ref[k, signal, rows, :block_len], spec_ref[k, signal, rows, block_len:]
            cos, sin = twid_ref[2, k : k + 1, :], twid_ref[3, k : k + 1, :]
            if k == 0:
                bins.append((re * cos, None))
            elif k == blocks:
                bins.append((re * cos - im * sin, None))
            else:
                bins.append((re * cos - im * sin, im * cos + re * sin))
        values = half_spectrum_adjoint(bins)
        for p in range(blocks):
            out_ref[p, signal, rows, :] = values[p].astype(jnp.bfloat16)
        return carry

    lax.fori_loop(0, signals * steps, synthesise, 0)


def project_kernel(
    back_ref, key_ref, value_ref, grad_ref, wk_ref, wq_ref, wv_ref, out_ref, filt_ref, lhs_ref
):
    blocks, _, channels, block_len = back_ref.shape
    width = blocks * channels

    @pl.when(pl.program_id(0) == 0)
    def _():
        def natural(slot):
            return back_ref[:, slot].reshape(width, block_len).astype(jnp.float32).T

        conv_out, grad_product = natural(0), natural(1)
        lhs_ref[0] = (grad_product * value_ref[...].astype(jnp.float32)).astype(jnp.bfloat16)
        lhs_ref[1] = (conv_out * grad_ref[...].astype(jnp.float32)).astype(jnp.bfloat16)
        lhs_ref[2] = (grad_product * key_ref[...].astype(jnp.float32)).astype(jnp.bfloat16)
        filt_ref[...] = natural(2).astype(jnp.bfloat16)

    dims = (((1,), (1,)), ((), ()))
    total = lax.dot_general(lhs_ref[0], wk_ref[...], dims, preferred_element_type=jnp.float32)
    total += lax.dot_general(lhs_ref[1], wq_ref[...], dims, preferred_element_type=jnp.float32)
    total += lax.dot_general(lhs_ref[2], wv_ref[...], dims, preferred_element_type=jnp.float32)
    out_ref[...] = total.astype(jnp.bfloat16)


def per_device(key_act, value_act, query_act, grad_out, long_filter, w_key, w_query, w_value):
    blocks = lax.axis_size("ctx")
    groups = lax.axis_size("tp")
    block_len, width = key_act.shape
    channels = width // blocks
    seq_len = blocks * block_len
    out_width = w_key.shape[0]
    part = out_width // groups

    sent = pl.pallas_call(
        gate_kernel,
        out_shape=jax.ShapeDtypeStruct((blocks, 3, channels, block_len), jnp.bfloat16),
        compiler_params=compiler_params(),
        name="gate",
    )(key_act, value_act, query_act, grad_out, long_filter)
    moved = lax.all_to_all(sent, "ctx", split_axis=0, concat_axis=0, tiled=True)

    forward, inverse, twiddle = dft_tables(
        blocks, block_len, 1.0 / (math.sqrt(seq_len) * 2 * seq_len)
    )
    results = pl.pallas_call(
        conv_kernel,
        out_shape=jax.ShapeDtypeStruct((blocks, 3, channels, block_len), jnp.bfloat16),
        scratch_shapes=[
            pltpu.VMEM((blocks + 1, 3, channels, 2 * block_len), jnp.bfloat16),
            pltpu.VMEM((blocks + 1, 3, channels, 2 * block_len), jnp.float32),
        ],
        compiler_params=compiler_params(),
        name="conv",
    )(moved, forward, inverse, twiddle)
    back = lax.all_to_all(results, "ctx", split_axis=0, concat_axis=0, tiled=True)

    whole = lambda shape: pl.BlockSpec(shape, lambda i: (0,) * len(shape))
    weight = pl.BlockSpec((part, width), lambda i: (i, 0))
    partial_sum, grad_filter = pl.pallas_call(
        project_kernel,
        grid=(groups,),
        in_specs=[
            whole((blocks, 3, channels, block_len)),
            whole((block_len, width)),
            whole((block_len, width)),
            whole((block_len, width)),
            weight,
            weight,
            weight,
        ],
        out_specs=[
            pl.BlockSpec((block_len, part), lambda i: (0, i)),
            whole((block_len, width)),
        ],
        out_shape=[
            jax.ShapeDtypeStruct((block_len, out_width), jnp.bfloat16),
            jax.ShapeDtypeStruct((block_len, width), jnp.bfloat16),
        ],
        scratch_shapes=[pltpu.VMEM((3, block_len, width), jnp.bfloat16)],
        compiler_params=compiler_params(),
        name="project",
    )(back, key_act, value_act, grad_out, w_key, w_query, w_value)
    grad_input = lax.psum_scatter(partial_sum, "tp", scatter_dimension=1, tiled=True)
    return (grad_input, grad_filter)


def solution(mesh):
    placed = (P("ctx", "tp"),) * 5 + (P(None, "tp"),) * 3
    return jax.shard_map(
        per_device,
        mesh=mesh,
        in_specs=placed,
        out_specs=(P("ctx", "tp"), P("ctx", "tp")),
        check_vma=False,
    )
```

profile of v0, /device:TPU:0, one launch (start us, length us, event | category | flops | bytes accessed | tf_op | source)
XLA Modules:
  0.0 104.3 jit_solution(87794860693934067)
XLA Ops:
  7.2 0.0 reduce-scatter.2.cloned.1.call-start
  7.2 0.0 copy-start.1
  7.2 0.9 copy-done.1
  8.2 0.0 copy-start.3
  8.2 0.9 copy-done.3
  9.1 0.0 copy-start.5
  9.1 0.9 copy-done.5
  10.1 0.0 copy-start.9
  10.1 0.9 copy-done.9
  11.0 0.0 copy-start.10
  11.0 0.9 copy-done.10
  12.0 0.0 copy-start.7
  12.0 0.0 copy-start.8
  12.0 0.0 copy-start.11
  12.0 0.3 gate.1
  12.3 27.4 %all_to_all.10.in_ref = bf16[8,3,64,256]{3,2,1,0:T(8,128)(2,1)S(1)} all-to-all(bf16[8,3,64,256]{3,2,1,0:T(8,128)(2,1)S(1)} %gate.1), channel_id=1, replica_groups=mesh['ctx'=8,'tp'=4] {'ctx'}, dimensions={0} | all-to-all | bytes 1572864 | tf_op jit(solution)/shard_map/all_to_all | solution.py:223
  39.6 0.0 copy-done.7
  39.6 0.0 copy-done.8
  39.6 0.0 copy-done.11
  39.6 0.0 copy-start
  39.7 0.0 copy-start.2
  39.7 0.0 copy-start.4
  39.7 0.0 copy-start.6
  39.7 5.0 %conv.1 = bf16[8,3,64,256]{3,2,1,0:T(8,128)(2,1)S(1)} custom-call(bf16[8,3,64,256]{3,2,1,0:T(8,128)(2,1)S(1)} %all_to_all.10.in_ref, bf16[512,512]{1,0:T(8,128)(2,1)S(1)} %copy-done.8, bf16[512,512]{1,0:T(8,128)(2,1)S(1)} %copy-done.7, f32[4,9,256]{2,1,0:T(8,128)S(1)} %copy-done.11), custom_call_target="tpu_custom_call" | custom-call | tf_op jit(solution)/shard_map/conv/pallas_call | solution.py:228
  44.7 23.2 %all_to_all.11.back_ref = bf16[8,3,64,256]{3,2,1,0:T(8,128)(2,1)S(1)} all-to-all(bf16[8,3,64,256]{3,2,1,0:T(8,128)(2,1)S(1)} %conv.1), channel_id=1, replica_groups=mesh['ctx'=8,'tp'=4] {'ctx'}, dimensions={0} | all-to-all | bytes 1572864 | tf_op jit(solution)/shard_map/all_to_all | solution.py:238
  67.9 0.0 copy-done
  67.9 0.0 copy-done.2
  67.9 0.0 copy-done.4
  67.9 0.0 copy-done.6
  67.9 5.5 %project.1 = (bf16[256,2048]{1,0:T(8,128)(2,1)}, bf16[256,512]{1,0:T(8,128)(2,1)}) custom-call(bf16[8,3,64,256]{3,2,1,0:T(8,128)(2,1)S(1)} %all_to_all.11.back_ref, bf16[256,512]{1,0:T(8,128)(2,1)S(1)} %copy-done.2, bf16[256,512]{1,0:T(8,128)(2,1)S(1)} %copy-done.4, bf16[256,512]{1,0:T(8,128)(2,1)S(1)} %copy-done.6, bf16[2048,512]{1,0:T(8,128)(2,1)S(1)} %copy-done, ...), custom_call_target="tpu_custom_call" | custom-call | tf_op jit(solution)/shard_map/project/pallas_call | solution.py:242
  73.4 0.0 reduce-scatter.2.cloned.1.call-update
  73.4 24.0 %reduce-scatter.2.cloned.1.call-done = bf16[256,512]{1,0:T(8,128)(2,1)} async-done(((bf16[256,2048]{1,0:T(8,128)(2,1)}), bf16[256,512]{1,0:T(8,128)(2,1)}) %reduce-scatter.2.cloned.1.call-update) | async-done | bytes 262160 | tf_op jit(solution)/shard_map/reduce_scatter | solution.py:266
Async XLA Ops:
  7.2 90.3 %reduce-scatter.2.cloned.1.call-start = ((), (), s32[]{:S(2)}) async-start(), calls=%async_computation.3 | async-start | bytes 1310720 | tf_op jit(solution)/shard_map/reduce_scatter | solution.py:266
  7.2 1.0 copy-start.1
  8.2 0.9 copy-start.3
  9.1 0.9 copy-start.5
  10.1 0.9 copy-start.9
  11.0 0.9 copy-start.10
  12.0 27.7 %copy-start.7 = (bf16[512,512]{1,0:T(8,128)(2,1)S(1)}, bf16[512,512]{1,0:T(8,128)(2,1)}, u32[]{:S(2)}) copy-start(bf16[512,512]{1,0:T(8,128)(2,1)} %constant.7.clone.inv_ref) | copy-start | bytes 1572868
  12.0 27.7 %copy-start.8 = (bf16[512,512]{1,0:T(8,128)(2,1)S(1)}, bf16[512,512]{1,0:T(8,128)(2,1)}, u32[]{:S(2)}) copy-start(bf16[512,512]{1,0:T(8,128)(2,1)} %constant.6.clone.fwd_ref) | copy-start | bytes 1572868
  12.0 27.7 %copy-start.11 = (f32[4,9,256]{2,1,0:T(8,128)S(1)}, f32[4,9,256]{2,1,0:T(8,128)}, u32[]{:S(2)}) copy-start(f32[4,9,256]{2,1,0:T(8,128)} %constant.8.clone.twid_ref) | copy-start | bytes 110596
  39.6 28.3 %copy-start = (bf16[2048,512]{1,0:T(8,128)(2,1)S(1)}, bf16[2048,512]{1,0:T(8,128)(2,1)}, u32[]{:S(2)}) copy-start(bf16[2048,512]{1,0:T(8,128)(2,1)} %wk_ref.1) | copy-start | bytes 6291460
  39.7 28.3 %copy-start.2 = (bf16[256,512]{1,0:T(8,128)(2,1)S(1)}, bf16[256,512]{1,0:T(8,128)(2,1)}, u32[]{:S(2)}) copy-start(bf16[256,512]{1,0:T(8,128)(2,1)} %key_ref.3) | copy-start | bytes 786436
  39.7 28.3 %copy-start.4 = (bf16[256,512]{1,0:T(8,128)(2,1)S(1)}, bf16[256,512]{1,0:T(8,128)(2,1)}, u32[]{:S(2)}) copy-start(bf16[256,512]{1,0:T(8,128)(2,1)} %value_ref.3) | copy-start | bytes 786436
  39.7 28.3 %copy-start.6 = (bf16[256,512]{1,0:T(8,128)(2,1)S(1)}, bf16[256,512]{1,0:T(8,128)(2,1)}, u32[]{:S(2)}) copy-start(bf16[256,512]{1,0:T(8,128)(2,1)} %grad_ref.3) | copy-start | bytes 786436
Sparse Core Ops, SparseCore 0:
  73.6 23.8 reduce-scatter.1
where the time goes:
time: 105 us; the launch traced here: 104 us
  blocking collectives  50.6 us (48%)
  waiting for transfers between devices  24.1 us (23%)
  between operations  14.1 us (13%)
  Pallas kernels  10.8 us (10%)
  local copies, waits for them, and re-layouts  4.78 us (5%)
    all_to_all x1, blocking collectives, per_device(): moved = lax.all_to_all(sent, 'ctx', split_axis=0, concat_axis=0, tiled=True)  27.4 us
    reduce_scatter x1, waiting for transfers between devices, per_device(): lax.psum_scatter(partial_sum, 'tp', scatter_dimension=1, tiled=True)  24 us
    all_to_all x1, blocking collectives, per_device(): lax.all_to_all(results, 'ctx', split_axis=0, concat_axis=0, tiled=True)  23.2 us
    pallas_call x1, Pallas kernels, per_device(): pl.pallas_call(project_kernel, grid=(groups,), in_specs=[whole((blocks, 3...  5.48 us
    pallas_call x1, Pallas kernels, per_device(): pl.pallas_call(conv_kernel, out_shape=jax.ShapeDtypeStruct((blocks, 3, ch...  5.02 us
    unnamed x24, local copies, waits for them, and re-layouts  4.78 us
  transfers between devices with their start and end apart: 1, of which 1 were waited for; matrix products, arithmetic and copies ran while one was open for 0% of the time, Pallas kernels for 0%

commit v1 on v0

--- a/solution.py
+++ b/solution.py
@@ -8,11 +8,9 @@
 from jax.experimental.pallas import tpu as pltpu
 from jax.sharding import PartitionSpec as P
 
-VMEM_LIMIT = 48 * 1024 * 1024
-
-
-def compiler_params():
-    return pltpu.CompilerParams(vmem_limit_bytes=VMEM_LIMIT)
+
+def compiler_params(mib):
+    return pltpu.CompilerParams(vmem_limit_bytes=mib * 1024 * 1024)
 
 
 def dft_tables(blocks, block_len, scale):
@@ -99,7 +97,7 @@
     put(2, query_ref[...].astype(jnp.float32) * grad_ref[...].astype(jnp.float32))
 
 
-def conv_kernel(in_ref, fwd_ref, inv_ref, twid_ref, out_ref, rows_ref, spec_ref):
+def conv_kernel(in_ref, fwd_ref, inv_ref, twid_ref, gates_ref, filt_ref, rows_ref, spec_ref):
     blocks, signals, channels, block_len = in_ref.shape
     chunk = min(channels, 16)
     steps = channels // chunk
@@ -159,9 +157,8 @@
         preferred_element_type=jnp.float32,
     ).reshape(spec_ref.shape)
 
-    def synthesise(step, carry):
-        signal = step // steps
-        start = pl.multiple_of((step % steps) * chunk, chunk)
+    def synthesise(step, out_ref, signal, slot):
+        start = pl.multiple_of(step * chunk, chunk)
         rows = pl.ds(start, chunk)
         bins = []
         for k in range(blocks + 1):
@@ -175,34 +172,58 @@
                 bins.append((re * cos - im * sin, im * cos + re * sin))
         values = half_spectrum_adjoint(bins)
         for p in range(blocks):
-            out_ref[p, signal, rows, :] = values[p].astype(jnp.bfloat16)
-        return carry
-
-    lax.fori_loop(0, signals * steps, synthesise, 0)
-
-
-def project_kernel(
-    back_ref, key_ref, value_ref, grad_ref, wk_ref, wq_ref, wv_ref, out_ref, filt_ref, lhs_ref
-):
+            out_ref[p, slot, rows, :] = values[p].astype(jnp.bfloat16)
+
+    @pl.loop(0, 2 * steps)
+    def _(step):
+        synthesise(step % steps, gates_ref, step // steps, step // steps)
+
+    @pl.loop(0, steps)
+    def _(step):
+        synthesise(step, filt_ref, 2, 0)
+
+
+def natural(back_ref, slot):
     blocks, _, channels, block_len = back_ref.shape
-    width = blocks * channels
-
-    @pl.when(pl.program_id(0) == 0)
-    def _():
-        def natural(slot):
-            return back_ref[:, slot].reshape(width, block_len).astype(jnp.float32).T
-
-        conv_out, grad_product = natural(0), natural(1)
-        lhs_ref[0] = (grad_product * value_ref[...].astype(jnp.float32)).astype(jnp.bfloat16)
-        lhs_ref[1] = (conv_out * grad_ref[...].astype(jnp.float32)).astype(jnp.bfloat16)
-        lhs_ref[2] = (grad_product * key_ref[...].astype(jnp.float32)).astype(jnp.bfloat16)
-        filt_ref[...] = natural(2).astype(jnp.bfloat16)
-
+    return back_ref[:, slot].reshape(blocks * channels, block_len).astype(jnp.float32).T
+
+
+def term(lhs_ref, weight_refs, group):
+    part = weight_refs[0].shape[0] // lax.axis_size("tp")
+    rows = pl.ds(pl.multiple_of(group * part, part), part)
     dims = (((1,), (1,)), ((), ()))
-    total = lax.dot_general(lhs_ref[0], wk_ref[...], dims, preferred_element_type=jnp.float32)
-    total += lax.dot_general(lhs_ref[1], wq_ref[...], dims, preferred_element_type=jnp.float32)
-    total += lax.dot_general(lhs_ref[2], wv_ref[...], dims, preferred_element_type=jnp.float32)
-    out_ref[...] = total.astype(jnp.bfloat16)
+    total = None
+    for slot, weight_ref in enumerate(weight_refs):
+        piece = lax.dot_general(
+            lhs_ref[slot], weight_ref[rows, :], dims, preferred_element_type=jnp.float32
+        )
+        total = piece if total is None else total + piece
+    return total
+
+
+def mate_kernel(back_ref, key_ref, value_ref, grad_ref, wk_ref, wq_ref, wv_ref, lhs_ref, out_ref):
+    conv_out, grad_product = natural(back_ref, 0), natural(back_ref, 1)
+    lhs_ref[0] = (grad_product * value_ref[...].astype(jnp.float32)).astype(jnp.bfloat16)
+    lhs_ref[1] = (conv_out * grad_ref[...].astype(jnp.float32)).astype(jnp.bfloat16)
+    lhs_ref[2] = (grad_product * key_ref[...].astype(jnp.float32)).astype(jnp.bfloat16)
+    me = lax.axis_index("tp")
+    for slot, distance in enumerate((3, 1)):
+        out_ref[slot] = term(lhs_ref, (wk_ref, wq_ref, wv_ref), me ^ distance).astype(jnp.bfloat16)
+
+
+def own_kernel(lhs_ref, wk_ref, wq_ref, wv_ref, far_ref, own_ref):
+    me = lax.axis_index("tp")
+    far_ref[...] = term(lhs_ref, (wk_ref, wq_ref, wv_ref), me ^ 2)
+    own_ref[...] = term(lhs_ref, (wk_ref, wq_ref, wv_ref), me)
+
+
+def turn_kernel(back_ref, out_ref):
+    out_ref[...] = natural(back_ref, 0).astype(jnp.bfloat16)
+
+
+def exchange(block, distance):
+    pairs = [(i, i ^ distance) for i in range(lax.axis_size("tp"))]
+    return lax.ppermute(block, "tp", pairs)
 
 
 def per_device(key_act, value_act, query_act, grad_out, long_filter, w_key, w_query, w_value):
@@ -211,13 +232,13 @@
     block_len, width = key_act.shape
     channels = width // blocks
     seq_len = blocks * block_len
-    out_width = w_key.shape[0]
-    part = out_width // groups
+    part = w_key.shape[0] // groups
+    flops = 2 * block_len * part * 3 * width
 
     sent = pl.pallas_call(
         gate_kernel,
         out_shape=jax.ShapeDtypeStruct((blocks, 3, channels, block_len), jnp.bfloat16),
-        compiler_params=compiler_params(),
+        compiler_params=compiler_params(60),
         name="gate",
     )(key_act, value_act, query_act, grad_out, long_filter)
     moved = lax.all_to_all(sent, "ctx", split_axis=0, concat_axis=0, tiled=True)
@@ -225,45 +246,51 @@
     forward, inverse, twiddle = dft_tables(
         blocks, block_len, 1.0 / (math.sqrt(seq_len) * 2 * seq_len)
     )
-    results = pl.pallas_call(
+    gates, filt = pl.pallas_call(
         conv_kernel,
-        out_shape=jax.ShapeDtypeStruct((blocks, 3, channels, block_len), jnp.bfloat16),
+        out_shape=[
+            jax.ShapeDtypeStruct((blocks, 2, channels, block_len), jnp.bfloat16),
+            jax.ShapeDtypeStruct((blocks, 1, channels, block_len), jnp.bfloat16),
+        ],
         scratch_shapes=[
             pltpu.VMEM((blocks + 1, 3, channels, 2 * block_len), jnp.bfloat16),
             pltpu.VMEM((blocks + 1, 3, channels, 2 * block_len), jnp.float32),
         ],
-        compiler_params=compiler_params(),
+        compiler_params=compiler_params(24),
         name="conv",
     )(moved, forward, inverse, twiddle)
-    back = lax.all_to_all(results, "ctx", split_axis=0, concat_axis=0, tiled=True)
-
-    whole = lambda shape: pl.BlockSpec(shape, lambda i: (0,) * len(shape))
-    weight = pl.BlockSpec((part, width), lambda i: (i, 0))
-    partial_sum, grad_filter = pl.pallas_call(
-        project_kernel,
-        grid=(groups,),
-        in_specs=[
-            whole((blocks, 3, channels, block_len)),
-            whole((block_len, width)),
-            whole((block_len, width)),
-            whole((block_len, width)),
-            weight,
-            weight,
-            weight,
+    back = lax.all_to_all(gates, "ctx", split_axis=0, concat_axis=0, tiled=True)
+    filt, back = lax.optimization_barrier((filt, back))
+    back_filt = lax.all_to_all(filt, "ctx", split_axis=0, concat_axis=0, tiled=True)
+
+    weights = (w_key, w_query, w_value)
+    lhs, to_mate = pl.pallas_call(
+        mate_kernel,
+        out_shape=[
+            jax.ShapeDtypeStruct((3, block_len, width), jnp.bfloat16),
+            jax.ShapeDtypeStruct((2, block_len, part), jnp.bfloat16),
         ],
-        out_specs=[
-            pl.BlockSpec((block_len, part), lambda i: (0, i)),
-            whole((block_len, width)),
-        ],
-        out_shape=[
-            jax.ShapeDtypeStruct((block_len, out_width), jnp.bfloat16),
-            jax.ShapeDtypeStruct((block_len, width), jnp.bfloat16),
-        ],
-        scratch_shapes=[pltpu.VMEM((3, block_len, width), jnp.bfloat16)],
-        compiler_params=compiler_params(),
-        name="project",
-    )(back, key_act, value_act, grad_out, w_key, w_query, w_value)
-    grad_input = lax.psum_scatter(partial_sum, "tp", scatter_dimension=1, tiled=True)
+        compiler_params=compiler_params(24),
+        cost_estimate=pl.CostEstimate(flops=2 * flops, bytes_accessed=1 << 23, transcendentals=0),
+        name="mate",
+    )(back, key_act, value_act, grad_out, *weights)
+    from_mate = exchange(to_mate, 1)
+    far, own = pl.pallas_call(
+        own_kernel,
+        out_shape=[jax.ShapeDtypeStruct((block_len, part), jnp.float32)] * 2,
+        compiler_params=compiler_params(24),
+        cost_estimate=pl.CostEstimate(flops=2 * flops, bytes_accessed=1 << 23, transcendentals=0),
+        name="own",
+    )(lhs, *weights)
+    from_far = exchange((far + from_mate[0].astype(jnp.float32)).astype(jnp.bfloat16), 2)
+    near = own + from_mate[1].astype(jnp.float32)
+    grad_input = (near + from_far.astype(jnp.float32)).astype(jnp.bfloat16)
+    grad_filter = pl.pallas_call(
+        turn_kernel,
+        out_shape=jax.ShapeDtypeStruct((block_len, width), jnp.bfloat16),
+        compiler_params=compiler_params(24),
+        name="turn",
+    )(back_filt)
     return (grad_input, grad_filter)
 
 

time: 105 us -> 77.7 us (0.74)
  waiting for transfers between devices: 24.1 us -> 6.17 us
  between operations: 14.1 us -> 0.75 us
  blocking collectives: 50.6 us -> 45.2 us
  starting transfers between devices: 0.04 us -> 5.2 us
  other arithmetic: 0 us -> 3.12 us
  Pallas kernels: 10.8 us -> 11.9 us
    reduce_scatter x1 -> x0, waiting for transfers between devices: 24 us -> none  [per_device(): lax.psum_scatter(partial_sum, 'tp', scatter_dimension=1, tiled=True)]
    all_to_all x1, blocking collectives: 23.2 us -> 17.5 us  [per_device(): back = lax.all_to_all(gates, 'ctx', split_axis=0, concat_axis=0, tiled=True)]
    all_to_all x0 -> x1, starting transfers between devices: none -> 3.64 us  [per_device(): lax.all_to_all(filt, 'ctx', split_axis=0, concat_axis=0, tiled=True)]
    ppermute x0 -> x2, waiting for transfers between devices: none -> 3.57 us  [exchange(): return lax.ppermute(block, 'tp', pairs)]
    convert_element_type x0 -> x2, other arithmetic: none -> 3.12 us  [the longest x1 1.91 us: per_device(): grad_input = (near + from_far.astype(jnp.float32)).astype(jnp.bfloat16)]
    all_to_all x0 -> x1, waiting for transfers between devices: none -> 2.6 us  [per_device(): lax.all_to_all(filt, 'ctx', split_axis=0, concat_axis=0, tiled=True)]
    pallas_call x1, Pallas kernels: 0.29 us -> 2.57 us  [per_device(): pl.pallas_call(gate_kernel, out_shape=jax.ShapeDtypeStruct((blocks, 3, ch...]
    ppermute x0 -> x2, starting transfers between devices: none -> 1.56 us  [exchange(): return lax.ppermute(block, 'tp', pairs)]
  transfers between devices with their start and end apart: 1 -> 3, of which waited for: 1 -> 2; matrix products, arithmetic and copies ran while one was open for 0% -> 2% of each run, Pallas kernels for 0% -> 2%
where the time goes in v1:
time: 77.7 us; the launch traced here: 77.2 us
  blocking collectives  45.2 us (58%)
  Pallas kernels  11.9 us (15%)
  waiting for transfers between devices  6.17 us (8%)
  starting transfers between devices  5.2 us (7%)
  local copies, waits for them, and re-layouts  4.81 us (6%)
  other arithmetic  3.12 us (4%)
    all_to_all x1, blocking collectives, per_device(): moved = lax.all_to_all(sent, 'ctx', split_axis=0, concat_axis=0, tiled=True)  27.7 us
    all_to_all x1, blocking collectives, per_device(): back = lax.all_to_all(gates, 'ctx', split_axis=0, concat_axis=0, tiled=True)  17.5 us
    pallas_call x1, Pallas kernels, per_device(): pl.pallas_call(conv_kernel, out_shape=[jax.ShapeDtypeStruct((blocks, 2, c...  5.7 us
    unnamed x24, local copies, waits for them, and re-layouts  4.81 us
    all_to_all x1, starting transfers between devices, per_device(): lax.all_to_all(filt, 'ctx', split_axis=0, concat_axis=0, tiled=True)  3.64 us
    ppermute x2, waiting for transfers between devices, exchange(): return lax.ppermute(block, 'tp', pairs)  3.57 us
    all_to_all x1, waiting for transfers between devices, per_device(): lax.all_to_all(filt, 'ctx', split_axis=0, concat_axis=0, tiled=True)  2.6 us
    pallas_call x1, Pallas kernels, per_device(): pl.pallas_call(gate_kernel, out_shape=jax.ShapeDtypeStruct((blocks, 3, ch...  2.57 us
  transfers between devices with their start and end apart: 3, of which 2 were waited for; matrix products, arithmetic and copies ran while one was open for 2% of the time, Pallas kernels for 2%

profile of v1, /device:TPU:0, one launch (start us, length us, event | category | flops | bytes accessed | tf_op | source)
XLA Modules:
  0.0 77.2 jit_solution(15480708393688861681)
XLA Ops:
  0.6 0.0 copy-start.11
  0.6 0.0 copy-start.9
  0.7 0.0 copy-start.10
  0.7 0.0 copy-start.6
  0.7 0.0 copy-start.7
  0.7 2.6 %gate.1 = bf16[8,3,64,256]{3,2,1,0:T(8,128)(2,1)} custom-call(bf16[256,512]{1,0:T(8,128)(2,1)} %key_ref.3, bf16[256,512]{1,0:T(8,128)(2,1)} %value_ref.3, bf16[256,512]{1,0:T(8,128)(2,1)} %query_ref.1, bf16[256,512]{1,0:T(8,128)(2,1)} %grad_ref.3, bf16[256,512]{1,0:T(8,128)(2,1)} %filter_ref.1), custom_call_target="tpu_custom_call" | custom-call | tf_op jit(solution)/shard_map/gate/pallas_call | solution.py:238
  3.3 0.0 copy-start
  3.3 0.0 copy-start.1
  3.3 0.0 copy-start.5
  3.3 27.7 %all_to_all.15.in_ref = bf16[8,3,64,256]{3,2,1,0:T(8,128)(2,1)S(1)} all-to-all(bf16[8,3,64,256]{3,2,1,0:T(8,128)(2,1)} %gate.1), channel_id=1, replica_groups=mesh['ctx'=8,'tp'=4] {'ctx'}, dimensions={0} | all-to-all | bytes 1572864 | tf_op jit(solution)/shard_map/all_to_all | solution.py:244
  31.0 0.0 copy-done.11
  31.0 0.0 copy-done.9
  31.0 0.0 copy-done.10
  31.0 5.7 %conv.1 = (bf16[8,2,64,256]{3,2,1,0:T(8,128)(2,1)S(1)}, bf16[8,1,64,256]{3,2,1,0:T(8,128)(2,1)}) custom-call(bf16[8,3,64,256]{3,2,1,0:T(8,128)(2,1)S(1)} %all_to_all.15.in_ref, bf16[512,512]{1,0:T(8,128)(2,1)S(1)} %copy-done.10, bf16[512,512]{1,0:T(8,128)(2,1)S(1)} %copy-done.9, f32[4,9,256]{2,1,0:T(8,128)S(1)} %copy-done.11), custom_call_target="tpu_custom_call" | custom-call | tf_op jit(solution)/shard_map/conv/pallas_call | solution.py:249
  36.7 17.5 %all_to_all.16.back_ref = bf16[8,2,64,256]{3,2,1,0:T(8,128)(2,1)S(1)} all-to-all(bf16[8,2,64,256]{3,2,1,0:T(8,128)(2,1)S(1)} %get-tuple-element.11), channel_id=1, replica_groups=mesh['ctx'=8,'tp'=4] {'ctx'}, dimensions={0} | all-to-all | bytes 1048576 | tf_op jit(solution)/shard_map/all_to_all | solution.py:262
  54.2 0.0 copy-done.6
  54.2 0.0 copy-done.7
  54.2 0.0 copy-done
  54.2 0.0 copy-done.1
  54.2 0.0 copy-done.5
  54.2 0.0 copy-start.3
  54.2 1.6 %copy-done.3 = bf16[2048,512]{1,0:T(8,128)(2,1)S(1)} copy-done((bf16[2048,512]{1,0:T(8,128)(2,1)S(1)}, bf16[2048,512]{1,0:T(8,128)(2,1)}, u32[]{:S(2)}) %copy-start.3) | copy-done | bytes 2097176
  55.8 1.8 %mate.1 = (bf16[3,256,512]{2,1,0:T(8,128)(2,1)S(1)}, bf16[2,256,512]{2,1,0:T(8,128)(2,1)}) custom-call(bf16[8,2,64,256]{3,2,1,0:T(8,128)(2,1)S(1)} %all_to_all.16.back_ref, bf16[256,512]{1,0:T(8,128)(2,1)S(1)} %copy-done.5, bf16[256,512]{1,0:T(8,128)(2,1)S(1)} %copy-done.6, bf16[256,512]{1,0:T(8,128)(2,1)S(1)} %copy-done.7, bf16[2048,512]{1,0:T(8,128)(2,1)S(1)} %copy-done, ...), custom_call_target="tpu_custom_call" | custom-call | flops 805306368 | bytes 8388608 | tf_op jit(solution)/shard_map/mate/pallas_call | solution.py:267
  57.7 0.0 collective-permute-start
  57.7 3.6 %all-to-all-start.2 = ((bf16[8,1,64,256]{3,2,1,0:T(8,128)(2,1)}), bf16[8,1,64,256]{3,2,1,0:T(8,128)(2,1)S(1)}, u32[]{:S(2)}, u32[]{:S(2)}) async-start(bf16[8,1,64,256]{3,2,1,0:T(8,128)(2,1)} %get-tuple-element.17), calls=%async_computation.2 | async-start | bytes 524288 | tf_op jit(solution)/shard_map/all_to_all | solution.py:264
  61.3 0.0 copy-start.2
  61.3 1.6 %copy-done.2 = bf16[2048,512]{1,0:T(8,128)(2,1)S(1)} copy-done((bf16[2048,512]{1,0:T(8,128)(2,1)S(1)}, bf16[2048,512]{1,0:T(8,128)(2,1)}, u32[]{:S(2)}) %copy-start.2) | copy-done | bytes 2097176
  62.9 0.0 copy-start.4
  62.9 1.6 %copy-done.4 = bf16[2048,512]{1,0:T(8,128)(2,1)S(1)} copy-done((bf16[2048,512]{1,0:T(8,128)(2,1)S(1)}, bf16[2048,512]{1,0:T(8,128)(2,1)}, u32[]{:S(2)}) %copy-start.4) | copy-done | bytes 2097176
  64.5 1.0 %own.1 = (f32[256,512]{1,0:T(8,128)S(1)}, f32[256,512]{1,0:T(8,128)S(1)}) custom-call(bf16[3,256,512]{2,1,0:T(8,128)(2,1)S(1)} %get-tuple-element.13.lhs_ref, bf16[2048,512]{1,0:T(8,128)(2,1)S(1)} %copy-done, bf16[2048,512]{1,0:T(8,128)(2,1)S(1)} %copy-done.2, bf16[2048,512]{1,0:T(8,128)(2,1)S(1)} %copy-done.4), custom_call_target="tpu_custom_call" | custom-call | flops 805306368 | bytes 8388608 | tf_op jit(solution)/shard_map/own/pallas_call | solution.py:278
  65.5 0.0 copy-start.8
  65.5 0.0 collective-permute-done
  65.5 1.2 %fusion = bf16[256,512]{1,0:T(8,128)(2,1)S(1)} fusion(f32[256,512]{1,0:T(8,128)S(1)} %get-tuple-element.16, bf16[2,256,512]{2,1,0:T(8,128)(2,1)} %collective-permute-done), kind=kLoop, calls=%fused_computation.1 | loop fusion | flops 393216 | bytes 1048576 | tf_op jit(solution)/shard_map/convert_element_type | solution.py:285
  66.7 0.0 copy-done.8
  66.7 1.6 %collective-permute-start.1 = (bf16[256,512]{1,0:T(8,128)(2,1)S(1)}, bf16[256,512]{1,0:T(8,128)(2,1)S(1)}, u32[]{:S(2)}, u32[]{:S(2)}) collective-permute-start(bf16[256,512]{1,0:T(8,128)(2,1)S(1)} %fusion), channel_id=1, source_target_pairs={{0,2},{1,3},{2,0},{3,1},{4,6},{5,7},{6,4},{7,5},{8,10},{9,11},{10,... | collective-permute-start | bytes 786440 | tf_op jit(solution)/shard_map/ppermute | solution.py:226
  68.3 2.6 %all-to-all-done.2.back_ref = bf16[8,1,64,256]{3,2,1,0:T(8,128)(2,1)S(1)} async-done(((bf16[8,1,64,256]{3,2,1,0:T(8,128)(2,1)}), bf16[8,1,64,256]{3,2,1,0:T(8,128)(2,1)S(1)}, u32[]{:S(2)}, u32[]{:S(2)}) %all-to-all-start.2) | async-done | bytes 262176 | tf_op jit(solution)/shard_map/all_to_all | solution.py:264
  70.9 0.8 %turn.1 = bf16[256,512]{1,0:T(8,128)(2,1)} custom-call(bf16[8,1,64,256]{3,2,1,0:T(8,128)(2,1)S(1)} %all-to-all-done.2.back_ref), custom_call_target="tpu_custom_call" | custom-call | tf_op jit(solution)/shard_map/turn/pallas_call | solution.py:288
  71.7 3.6 %collective-permute-done.1 = bf16[256,512]{1,0:T(8,128)(2,1)S(1)} collective-permute-done((bf16[256,512]{1,0:T(8,128)(2,1)S(1)}, bf16[256,512]{1,0:T(8,128)(2,1)S(1)}, u32[]{:S(2)}, u32[]{:S(2)}) %collective-permute-start.1) | collective-permute-done | bytes 262176 | tf_op jit(solution)/shard_map/ppermute | solution.py:226
  75.3 1.9 %fusion.2 = bf16[256,512]{1,0:T(8,128)(2,1)} fusion(f32[256,512]{1,0:T(8,128)} %copy-done.8, bf16[256,512]{1,0:T(8,128)(2,1)S(1)} %collective-permute-done.1, bf16[2,256,512]{2,1,0:T(8,128)(2,1)} %collective-permute-done), kind=kLoop, calls=%fused_computation.4 | loop fusion | flops 655360 | bytes 1310720 | tf_op jit(solution)/shard_map/convert_element_type | solution.py:287
Async XLA Ops:
  0.6 30.3 %copy-start.11 = (f32[4,9,256]{2,1,0:T(8,128)S(1)}, f32[4,9,256]{2,1,0:T(8,128)}, u32[]{:S(2)}) copy-start(f32[4,9,256]{2,1,0:T(8,128)} %constant.8.clone.twid_ref) | copy-start | bytes 110596
  0.6 30.3 %copy-start.9 = (bf16[512,512]{1,0:T(8,128)(2,1)S(1)}, bf16[512,512]{1,0:T(8,128)(2,1)}, u32[]{:S(2)}) copy-start(bf16[512,512]{1,0:T(8,128)(2,1)} %constant.7.clone.inv_ref) | copy-start | bytes 1572868
  0.7 30.3 %copy-start.10 = (bf16[512,512]{1,0:T(8,128)(2,1)S(1)}, bf16[512,512]{1,0:T(8,128)(2,1)}, u32[]{:S(2)}) copy-start(bf16[512,512]{1,0:T(8,128)(2,1)} %constant.6.clone.fwd_ref) | copy-start | bytes 1572868
  0.7 53.5 %copy-start.6 = (bf16[256,512]{1,0:T(8,128)(2,1)S(1)}, bf16[256,512]{1,0:T(8,128)(2,1)}, u32[]{:S(2)}) copy-start(bf16[256,512]{1,0:T(8,128)(2,1)} %value_ref.3) | copy-start | bytes 786436
  0.7 53.5 %copy-start.7 = (bf16[256,512]{1,0:T(8,128)(2,1)S(1)}, bf16[256,512]{1,0:T(8,128)(2,1)}, u32[]{:S(2)}) copy-start(bf16[256,512]{1,0:T(8,128)(2,1)} %grad_ref.3) | copy-start | bytes 786436
  3.3 50.9 %copy-start = (bf16[2048,512]{1,0:T(8,128)(2,1)S(1)}, bf16[2048,512]{1,0:T(8,128)(2,1)}, u32[]{:S(2)}) copy-start(bf16[2048,512]{1,0:T(8,128)(2,1)} %wk_ref.3) | copy-start | bytes 6291460
  3.3 50.9 %copy-start.1 = (bf16[2048,512]{1,0:T(8,128)(2,1)S(1)}, bf16[2048,512]{1,0:T(8,128)(2,1)}, u32[]{:S(2)}) copy-start(bf16[2048,512]{1,0:T(8,128)(2,1)} %wq_ref.3) | copy-start | bytes 6291460
  3.3 51.0 %copy-start.5 = (bf16[256,512]{1,0:T(8,128)(2,1)S(1)}, bf16[256,512]{1,0:T(8,128)(2,1)}, u32[]{:S(2)}) copy-start(bf16[256,512]{1,0:T(8,128)(2,1)} %key_ref.3) | copy-start | bytes 786436
  54.2 1.6 %copy-start.3 = (bf16[2048,512]{1,0:T(8,128)(2,1)S(1)}, bf16[2048,512]{1,0:T(8,128)(2,1)}, u32[]{:S(2)}) copy-start(bf16[2048,512]{1,0:T(8,128)(2,1)} %wv_ref.3) | copy-start | bytes 6291460
  57.7 7.8 %collective-permute-start = (bf16[2,256,512]{2,1,0:T(8,128)(2,1)}, bf16[2,256,512]{2,1,0:T(8,128)(2,1)}, u32[]{:S(2)}, u32[]{:S(2)}) collective-permute-start(bf16[2,256,512]{2,1,0:T(8,128)(2,1)} %get-tuple-element.15), channel_id=1, source_target_pairs={{0,1},{1,0},{2,3},{3,2},{4,5},{5,4},{6,7},{7,6},{8,9},{9,8},{10,11... | collective-permute-start | bytes 1572872 | tf_op jit(solution)/shard_map/ppermute | solution.py:226
  57.7 13.2 %all-to-all-start.2 = ((bf16[8,1,64,256]{3,2,1,0:T(8,128)(2,1)}), bf16[8,1,64,256]{3,2,1,0:T(8,128)(2,1)S(1)}, u32[]{:S(2)}, u32[]{:S(2)}) async-start(bf16[8,1,64,256]{3,2,1,0:T(8,128)(2,1)} %get-tuple-element.17), calls=%async_computation.2 | async-start | bytes 524288 | tf_op jit(solution)/shard_map/all_to_all | solution.py:264
  61.3 1.6 %copy-start.2 = (bf16[2048,512]{1,0:T(8,128)(2,1)S(1)}, bf16[2048,512]{1,0:T(8,128)(2,1)}, u32[]{:S(2)}) copy-start(bf16[2048,512]{1,0:T(8,128)(2,1)} %wq_ref.3) | copy-start | bytes 6291460
  62.9 1.6 %copy-start.4 = (bf16[2048,512]{1,0:T(8,128)(2,1)S(1)}, bf16[2048,512]{1,0:T(8,128)(2,1)}, u32[]{:S(2)}) copy-start(bf16[2048,512]{1,0:T(8,128)(2,1)} %wv_ref.3) | copy-start | bytes 6291460
  65.5 1.2 %copy-start.8 = (f32[256,512]{1,0:T(8,128)}, f32[256,512]{1,0:T(8,128)S(1)}, u32[]{:S(2)}) copy-start(f32[256,512]{1,0:T(8,128)S(1)} %get-tuple-element.14) | copy-start | bytes 1572868
  66.7 8.6 %collective-permute-start.1 = (bf16[256,512]{1,0:T(8,128)(2,1)S(1)}, bf16[256,512]{1,0:T(8,128)(2,1)S(1)}, u32[]{:S(2)}, u32[]{:S(2)}) collective-permute-start(bf16[256,512]{1,0:T(8,128)(2,1)S(1)} %fusion), channel_id=1, source_target_pairs={{0,2},{1,3},{2,0},{3,1},{4,6},{5,7},{6,4},{7,5},{8,10},{9,11},{10,... | collective-permute-start | bytes 786440 | tf_op jit(solution)/shard_map/ppermute | solution.py:226

commit v2 on v1

--- a/solution.py
+++ b/solution.py
@@ -85,20 +85,31 @@
     return values
 
 
-def gate_kernel(key_ref, value_ref, query_ref, grad_ref, filter_ref, out_ref):
-    blocks, _, channels, block_len = out_ref.shape
+def gate_kernel(key_ref, value_ref, query_ref, grad_ref, filter_ref, *refs):
+    out_refs, turn_ref = refs[:-1], refs[-1]
+    blocks, _, channels, block_len = turn_ref.shape
 
     def put(slot, wide):
         turned = wide.T.astype(jnp.bfloat16)
-        out_ref[:, slot] = turned.reshape(blocks, channels, block_len)
+        turn_ref[:, slot] = turned.reshape(blocks, channels, block_len)
 
     put(0, key_ref[...].astype(jnp.float32) * value_ref[...].astype(jnp.float32))
     put(1, filter_ref[...].astype(jnp.float32))
     put(2, query_ref[...].astype(jnp.float32) * grad_ref[...].astype(jnp.float32))
-
-
-def conv_kernel(in_ref, fwd_ref, inv_ref, twid_ref, gates_ref, filt_ref, rows_ref, spec_ref):
-    blocks, signals, channels, block_len = in_ref.shape
+    me = lax.axis_index("ctx")
+    for distance, out_ref in enumerate(out_refs):
+        out_ref[...] = turn_ref[me ^ distance]
+
+
+def conv_kernel(*refs):
+    blocks = lax.axis_size("ctx")
+    in_refs, (fwd_ref, inv_ref, twid_ref) = refs[:blocks], refs[blocks : blocks + 3]
+    gates_refs, filt_refs = refs[blocks + 3 : 2 * blocks + 3], refs[2 * blocks + 3 : 3 * blocks + 3]
+    in_ref, rows_ref, spec_ref = refs[3 * blocks + 3 :]
+    _, signals, channels, block_len = in_ref.shape
+    me = lax.axis_index("ctx")
+    for distance, ref in enumerate(in_refs):
+        in_ref[me ^ distance] = ref[...]
     chunk = min(channels, 16)
     steps = channels // chunk
 
@@ -157,8 +168,9 @@
         preferred_element_type=jnp.float32,
     ).reshape(spec_ref.shape)
 
-    def synthesise(step, out_ref, signal, slot):
-        start = pl.multiple_of(step * chunk, chunk)
+    def synthesise(step, carry):
+        signal = step // steps
+        start = pl.multiple_of((step % steps) * chunk, chunk)
         rows = pl.ds(start, chunk)
         bins = []
         for k in range(blocks + 1):
@@ -172,20 +184,13 @@
                 bins.append((re * cos - im * sin, im * cos + re * sin))
         values = half_spectrum_adjoint(bins)
         for p in range(blocks):
-            out_ref[p, slot, rows, :] = values[p].astype(jnp.bfloat16)
-
-    @pl.loop(0, 2 * steps)
-    def _(step):
-        synthesise(step % steps, gates_ref, step // steps, step // steps)
-
-    @pl.loop(0, steps)
-    def _(step):
-        synthesise(step, filt_ref, 2, 0)
-
-
-def natural(back_ref, slot):
-    blocks, _, channels, block_len = back_ref.shape
-    return back_ref[:, slot].reshape(blocks * channels, block_len).astype(jnp.float32).T
+            in_ref[p, signal, rows, :] = values[p].astype(jnp.bfloat16)
+        return carry
+
+    lax.fori_loop(0, signals * steps, synthesise, 0)
+    for distance in range(blocks):
+        gates_refs[distance][...] = in_ref[me ^ distance, 0:2]
+        filt_refs[distance][...] = in_ref[me ^ distance, 2:3]
 
 
 def term(lhs_ref, weight_refs, group):
@@ -201,29 +206,48 @@
     return total
 
 
-def mate_kernel(back_ref, key_ref, value_ref, grad_ref, wk_ref, wq_ref, wv_ref, lhs_ref, out_ref):
-    conv_out, grad_product = natural(back_ref, 0), natural(back_ref, 1)
+def natural(back_refs, turn_ref):
+    blocks, signals, channels, block_len = turn_ref.shape
+    me = lax.axis_index("ctx")
+    for distance, ref in enumerate(back_refs):
+        turn_ref[me ^ distance] = ref[...]
+    return [
+        turn_ref[:, slot].reshape(blocks * channels, block_len).astype(jnp.float32).T
+        for slot in range(signals)
+    ]
+
+
+def project_kernel(*refs):
+    blocks = lax.axis_size("ctx")
+    back_refs, (key_ref, value_ref, grad_ref) = refs[:blocks], refs[blocks : blocks + 3]
+    weight_refs = refs[blocks + 3 : blocks + 6]
+    mate_ref, far_ref, own_ref, turn_ref, lhs_ref = refs[blocks + 6 :]
+    conv_out, grad_product = natural(back_refs, turn_ref)
     lhs_ref[0] = (grad_product * value_ref[...].astype(jnp.float32)).astype(jnp.bfloat16)
     lhs_ref[1] = (conv_out * grad_ref[...].astype(jnp.float32)).astype(jnp.bfloat16)
     lhs_ref[2] = (grad_product * key_ref[...].astype(jnp.float32)).astype(jnp.bfloat16)
-    me = lax.axis_index("tp")
-    for slot, distance in enumerate((3, 1)):
-        out_ref[slot] = term(lhs_ref, (wk_ref, wq_ref, wv_ref), me ^ distance).astype(jnp.bfloat16)
-
-
-def own_kernel(lhs_ref, wk_ref, wq_ref, wv_ref, far_ref, own_ref):
-    me = lax.axis_index("tp")
-    far_ref[...] = term(lhs_ref, (wk_ref, wq_ref, wv_ref), me ^ 2)
-    own_ref[...] = term(lhs_ref, (wk_ref, wq_ref, wv_ref), me)
-
-
-def turn_kernel(back_ref, out_ref):
-    out_ref[...] = natural(back_ref, 0).astype(jnp.bfloat16)
-
-
-def exchange(block, distance):
-    pairs = [(i, i ^ distance) for i in range(lax.axis_size("tp"))]
-    return lax.ppermute(block, "tp", pairs)
+    group = lax.axis_index("tp")
+    mate_ref[0] = term(lhs_ref, weight_refs, group ^ 3).astype(jnp.bfloat16)
+    mate_ref[1] = term(lhs_ref, weight_refs, group ^ 1).astype(jnp.bfloat16)
+    far_ref[...] = term(lhs_ref, weight_refs, group ^ 2)
+    own_ref[...] = term(lhs_ref, weight_refs, group)
+
+
+def turn_kernel(*refs):
+    back_refs, (out_ref, turn_ref) = refs[:-2], refs[-2:]
+    out_ref[...] = natural(back_refs, turn_ref)[0].astype(jnp.bfloat16)
+
+
+def exchange(block, axis, distance):
+    pairs = [(i, i ^ distance) for i in range(lax.axis_size(axis))]
+    return lax.ppermute(block, axis, pairs)
+
+
+def swap(pieces):
+    moved = list(pieces)
+    for distance in reversed(range(1, len(pieces))):
+        moved[distance] = exchange(pieces[distance], "ctx", distance)
+    return moved
 
 
 def per_device(key_act, value_act, query_act, grad_out, long_filter, w_key, w_query, w_value):
@@ -233,64 +257,64 @@
     channels = width // blocks
     seq_len = blocks * block_len
     part = w_key.shape[0] // groups
-    flops = 2 * block_len * part * 3 * width
+
+    def arrays(count, *shape, dtype=jnp.bfloat16):
+        return [jax.ShapeDtypeStruct(shape, dtype)] * count
 
     sent = pl.pallas_call(
         gate_kernel,
-        out_shape=jax.ShapeDtypeStruct((blocks, 3, channels, block_len), jnp.bfloat16),
+        out_shape=arrays(blocks, 3, channels, block_len),
+        scratch_shapes=[pltpu.VMEM((blocks, 3, channels, block_len), jnp.bfloat16)],
         compiler_params=compiler_params(60),
         name="gate",
     )(key_act, value_act, query_act, grad_out, long_filter)
-    moved = lax.all_to_all(sent, "ctx", split_axis=0, concat_axis=0, tiled=True)
+    moved = swap(sent)
 
     forward, inverse, twiddle = dft_tables(
         blocks, block_len, 1.0 / (math.sqrt(seq_len) * 2 * seq_len)
     )
-    gates, filt = pl.pallas_call(
+    results = pl.pallas_call(
         conv_kernel,
-        out_shape=[
-            jax.ShapeDtypeStruct((blocks, 2, channels, block_len), jnp.bfloat16),
-            jax.ShapeDtypeStruct((blocks, 1, channels, block_len), jnp.bfloat16),
-        ],
+        out_shape=arrays(blocks, 2, channels, block_len) + arrays(blocks, 1, channels, block_len),
         scratch_shapes=[
+            pltpu.VMEM((blocks, 3, channels, block_len), jnp.bfloat16),
             pltpu.VMEM((blocks + 1, 3, channels, 2 * block_len), jnp.bfloat16),
             pltpu.VMEM((blocks + 1, 3, channels, 2 * block_len), jnp.float32),
         ],
-        compiler_params=compiler_params(24),
+        compiler_params=compiler_params(20),
         name="conv",
-    )(moved, forward, inverse, twiddle)
-    back = lax.all_to_all(gates, "ctx", split_axis=0, concat_axis=0, tiled=True)
-    filt, back = lax.optimization_barrier((filt, back))
-    back_filt = lax.all_to_all(filt, "ctx", split_axis=0, concat_axis=0, tiled=True)
-
-    weights = (w_key, w_query, w_value)
-    lhs, to_mate = pl.pallas_call(
-        mate_kernel,
-        out_shape=[
-            jax.ShapeDtypeStruct((3, block_len, width), jnp.bfloat16),
-            jax.ShapeDtypeStruct((2, block_len, part), jnp.bfloat16),
+    )(*moved, forward, inverse, twiddle)
+    back = swap(results[:blocks])
+    filt, back = lax.optimization_barrier((results[blocks:], back))
+    back_filt = swap(filt)
+
+    to_mate, far, own = pl.pallas_call(
+        project_kernel,
+        out_shape=arrays(1, 2, block_len, part) + arrays(2, block_len, part, dtype=jnp.float32),
+        scratch_shapes=[
+            pltpu.VMEM((blocks, 2, channels, block_len), jnp.bfloat16),
+            pltpu.VMEM((3, block_len, width), jnp.bfloat16),
         ],
-        compiler_params=compiler_params(24),
-        cost_estimate=pl.CostEstimate(flops=2 * flops, bytes_accessed=1 << 23, transcendentals=0),
-        name="mate",
-    )(back, key_act, value_act, grad_out, *weights)
-    from_mate = exchange(to_mate, 1)
-    far, own = pl.pallas_call(
-        own_kernel,
-        out_shape=[jax.ShapeDtypeStruct((block_len, part), jnp.float32)] * 2,
-        compiler_params=compiler_params(24),
-        cost_estimate=pl.CostEstimate(flops=2 * flops, bytes_accessed=1 << 23, transcendentals=0),
-        name="own",
-    )(lhs, *weights)
-    from_far = exchange((far + from_mate[0].astype(jnp.float32)).astype(jnp.bfloat16), 2)
+        compiler_params=compiler_params(16),
+        cost_estimate=pl.CostEstimate(
+            flops=2 * block_len * 3 * width * w_key.shape[0],
+            bytes_accessed=1 << 23,
+            transcendentals=0,
+        ),
+        name="project",
+    )(*back, key_act, value_act, grad_out, w_key, w_query, w_value)
+    from_mate = exchange(to_mate, "tp", 1)
+    far = (far + from_mate[0].astype(jnp.float32)).astype(jnp.bfloat16)
+    from_far = exchange(far, "tp", 2)
     near = own + from_mate[1].astype(jnp.float32)
     grad_input = (near + from_far.astype(jnp.float32)).astype(jnp.bfloat16)
     grad_filter = pl.pallas_call(
         turn_kernel,
-        out_shape=jax.ShapeDtypeStruct((block_len, width), jnp.bfloat16),
-        compiler_params=compiler_params(24),
+        out_shape=arrays(1, block_len, width)[0],
+        scratch_shapes=[pltpu.VMEM((blocks, 1, channels, block_len), jnp.bfloat16)],
+        compiler_params=compiler_params(16),
         name="turn",
-    )(back_filt)
+    )(*back_filt)
     return (grad_input, grad_filter)
 
 

time: 77.7 us -> 80.3 us (1.033)
  blocking collectives: 45.2 us -> 0 us
  starting transfers between devices: 5.2 us -> 39.4 us
  waiting for transfers between devices: 6.17 us -> 21.4 us
  other arithmetic: 3.12 us -> 0.88 us
  local copies, waits for them, and re-layouts: 4.81 us -> 7.01 us
  Pallas kernels: 11.9 us -> 10.5 us
    all_to_all x2 -> x0, blocking collectives: 45.2 us -> none  [the longest x1 27.7 us: per_device(): moved = lax.all_to_all(sent, 'ctx', split_axis=0, concat_axis=0, tiled=True)]
    ppermute x2 -> x23, starting transfers between devices: 1.56 us -> 39.4 us  [exchange(): return lax.ppermute(block, axis, pairs)]
    ppermute x2 -> x23, waiting for transfers between devices: 3.57 us -> 21.4 us  [exchange(): return lax.ppermute(block, axis, pairs)]
    all_to_all x1 -> x0, starting transfers between devices: 3.64 us -> none  [per_device(): lax.all_to_all(filt, 'ctx', split_axis=0, concat_axis=0, tiled=True)]
    all_to_all x1 -> x0, waiting for transfers between devices: 2.6 us -> none  [per_device(): lax.all_to_all(filt, 'ctx', split_axis=0, concat_axis=0, tiled=True)]
    unnamed x24 -> x20, local copies, waits for them, and re-layouts: 4.81 us -> 7.01 us
    pallas_call x5 -> x4, Pallas kernels: 11.9 us -> 10.5 us  [the longest x1 5.13 us: per_device(): pl.pallas_call(conv_kernel, out_shape=arrays(blocks, 2, channels, block_l...]
    convert_element_type x1, other arithmetic: 1.21 us -> 0.07 us  [per_device(): far = (far + from_mate[0].astype(jnp.float32)).astype(jnp.bfloat16)]
  transfers between devices with their start and end apart: 3 -> 23, of which waited for: 2 -> 8; matrix products, arithmetic and copies ran while one was open for 2% -> 0% of each run, Pallas kernels for 2% -> 1%
where the time goes in v2:
time: 80.3 us; the launch traced here: 80 us
  starting transfers between devices  39.4 us (49%)
  waiting for transfers between devices  21.4 us (27%)
  Pallas kernels  10.5 us (13%)
  local copies, waits for them, and re-layouts  7.01 us (9%)
  other arithmetic  0.88 us (1%)
    ppermute x23, starting transfers between devices, exchange(): return lax.ppermute(block, axis, pairs)  39.4 us
    ppermute x23, waiting for transfers between devices, exchange(): return lax.ppermute(block, axis, pairs)  21.4 us
    unnamed x20, local copies, waits for them, and re-layouts  7.01 us
    pallas_call x1, Pallas kernels, per_device(): pl.pallas_call(conv_kernel, out_shape=arrays(blocks, 2, channels, block_l...  5.13 us
    pallas_call x1, Pallas kernels, per_device(): pl.pallas_call(gate_kernel, out_shape=arrays(blocks, 3, channels, block_l...  2.58 us
    pallas_call x1, Pallas kernels, per_device(): pl.pallas_call(project_kernel, out_shape=arrays(1, 2, block_len, part) +...  1.88 us
  transfers between devices with their start and end apart: 23, of which 8 were waited for; matrix products, arithmetic and copies ran while one was open for 0% of the time, Pallas kernels for 1%

profile of v2, /device:TPU:0, one launch (start us, length us, event | category | flops | bytes accessed | tf_op | source)
XLA Modules:
  0.0 80.0 jit_solution(14337755749708307273)
XLA Ops:
  0.6 0.0 copy-start.5
  0.6 0.0 copy-start.4
  0.7 0.0 copy-start.3
  0.7 0.0 copy-start
  0.7 2.6 %gate.1 = (bf16[3,64,256]{2,1,0:T(8,128)(2,1)}, bf16[3,64,256]{2,1,0:T(8,128)(2,1)}, bf16[3,64,256]{2,1,0:T(8,128)(2,1)}, bf16[3,64,256]{2,1,0:T(8,128)(2,1)}, b...) custom-call(bf16[256,512]{1,0:T(8,128)(2,1)} %refs_8_.2, ...), custom_call_target="tpu_custom_call" | custom-call | tf_op jit(solution)/shard_map/gate/pallas_call | solution.py:264
  3.3 3.0 %collective-permute-start = (bf16[3,64,256]{2,1,0:T(8,128)(2,1)}, bf16[3,64,256]{2,1,0:T(8,128)(2,1)S(1)}, u32[]{:S(2)}, u32[]{:S(2)}) collective-permute-start(bf16[3,64,256]{2,1,0:T(8,128)(2,1)} %get-tuple-element.46), channel_id=1, source_target_pairs={{0,4},{4,0},{8,12},{12,8},{16,20},{20,16},{24,28},{28,24},{1,5},{5... | collective-permute-start | bytes 294920 | tf_op jit(solution)/shard_map/ppermute | solution.py:243
  6.2 1.6 %collective-permute-start.1 = (bf16[3,64,256]{2,1,0:T(8,128)(2,1)}, bf16[3,64,256]{2,1,0:T(8,128)(2,1)S(1)}, u32[]{:S(2)}, u32[]{:S(2)}) collective-permute-start(bf16[3,64,256]{2,1,0:T(8,128)(2,1)} %get-tuple-element.47), channel_id=1, source_target_pairs={{0,8},{4,12},{8,0},{12,4},{16,24},{20,28},{24,16},{28,20},{1,9},{5... | collective-permute-start | bytes 294920 | tf_op jit(solution)/shard_map/ppermute | solution.py:243
  7.8 0.0 collective-permute-start.2
  7.8 3.0 %collective-permute-start.3 = (bf16[3,64,256]{2,1,0:T(8,128)(2,1)}, bf16[3,64,256]{2,1,0:T(8,128)(2,1)S(1)}, u32[]{:S(2)}, u32[]{:S(2)}) collective-permute-start(bf16[3,64,256]{2,1,0:T(8,128)(2,1)} %get-tuple-element.49), channel_id=1, source_target_pairs={{0,16},{4,20},{8,24},{12,28},{16,0},{20,4},{24,8},{28,12},{1,17},{... | collective-permute-start | bytes 294920 | tf_op jit(solution)/shard_map/ppermute | solution.py:243
  10.8 1.3 %collective-permute-start.4 = (bf16[3,64,256]{2,1,0:T(8,128)(2,1)}, bf16[3,64,256]{2,1,0:T(8,128)(2,1)S(1)}, u32[]{:S(2)}, u32[]{:S(2)}) collective-permute-start(bf16[3,64,256]{2,1,0:T(8,128)(2,1)} %get-tuple-element.50), channel_id=1, source_target_pairs={{0,20},{4,16},{8,28},{12,24},{16,4},{20,0},{24,12},{28,8},{1,21},{... | collective-permute-start | bytes 294920 | tf_op jit(solution)/shard_map/ppermute | solution.py:243
  12.1 0.0 collective-permute-done.refs_1_
  12.1 3.6 %collective-permute-start.5 = (bf16[3,64,256]{2,1,0:T(8,128)(2,1)}, bf16[3,64,256]{2,1,0:T(8,128)(2,1)S(1)}, u32[]{:S(2)}, u32[]{:S(2)}) collective-permute-start(bf16[3,64,256]{2,1,0:T(8,128)(2,1)} %get-tuple-element.51), channel_id=1, source_target_pairs={{0,24},{4,28},{8,16},{12,20},{16,8},{20,12},{24,0},{28,4},{1,25},{... | collective-permute-start | bytes 294920 | tf_op jit(solution)/shard_map/ppermute | solution.py:243
  15.7 0.0 collective-permute-done.1.refs_2_
  15.7 0.0 collective-permute-start.6
  15.7 0.0 collective-permute-done.2.refs_3_
  15.7 0.0 collective-permute-done.3.refs_4_
  15.7 10.5 %collective-permute-done.4.refs_5_ = bf16[3,64,256]{2,1,0:T(8,128)(2,1)S(1)} collective-permute-done((bf16[3,64,256]{2,1,0:T(8,128)(2,1)}, bf16[3,64,256]{2,1,0:T(8,128)(2,1)S(1)}, u32[]{:S(2)}, u32[]{:S(2)}) %collective-permute-start.4) | collective-permute-done | bytes 98336 | tf_op jit(solution)/shard_map/ppermute | solution.py:243
  26.2 0.0 collective-permute-done.5.refs_6_
  26.2 0.0 collective-permute-done.6.refs_7_
  26.2 1.0 %copy-done.6 = bf16[512,512]{1,0:T(8,128)(2,1)S(1)} copy-done((bf16[512,512]{1,0:T(8,128)(2,1)S(1)}, bf16[512,512]{1,0:T(8,128)(2,1)}, u32[]{:S(2)}) %copy-start.6) | copy-done | bytes 524312
  27.2 1.0 %copy-done.7 = bf16[512,512]{1,0:T(8,128)(2,1)S(1)} copy-done((bf16[512,512]{1,0:T(8,128)(2,1)S(1)}, bf16[512,512]{1,0:T(8,128)(2,1)}, u32[]{:S(2)}) %copy-start.7) | copy-done | bytes 524312
  28.3 0.9 %copy-done.8 = bf16[3,64,256]{2,1,0:T(8,128)(2,1)S(1)} copy-done((bf16[3,64,256]{2,1,0:T(8,128)(2,1)S(1)}, bf16[3,64,256]{2,1,0:T(8,128)(2,1)}, u32[]{:S(2)}) %copy-start.8) | copy-done | bytes 98328
  29.2 0.8 %copy-done.9 = f32[4,9,256]{2,1,0:T(8,128)S(1)} copy-done((f32[4,9,256]{2,1,0:T(8,128)S(1)}, f32[4,9,256]{2,1,0:T(8,128)}, u32[]{:S(2)}) %copy-start.9) | copy-done | bytes 36888
  30.0 5.1 %conv.1 = (bf16[2,64,256]{2,1,0:T(8,128)(2,1)S(1)}, bf16[2,64,256]{2,1,0:T(8,128)(2,1)S(1)}, bf16[2,64,256]{2,1,0:T(8,128)(2,1)S(1)}, bf16[2,64,256]{2,1,0:T(8,1...) custom-call(bf16[3,64,256]{2,1,0:T(8,128)(2,1)S(1)} %copy-done.8, ...), custom_call_target="tpu_custom_call" | custom-call | tf_op jit(solution)/shard_map/conv/pallas_call | solution.py:276
  35.2 1.0 %collective-permute-start.7 = (bf16[2,64,256]{2,1,0:T(8,128)(2,1)S(1)}, bf16[2,64,256]{2,1,0:T(8,128)(2,1)S(1)}, u32[]{:S(2)}, u32[]{:S(2)}) collective-permute-start(bf16[2,64,256]{2,1,0:T(8,128)(2,1)S(1)} %get-tuple-element.62), channel_id=1, source_target_pairs={{0,4},{4,0},{8,12},{12,8},{16,20},{20,16},{24,28},{28,24},{1,5},{5... | collective-permute-start | bytes 196616 | tf_op jit(solution)/shard_map/ppermute | solution.py:243
  36.2 3.6 %collective-permute-start.8 = (bf16[2,64,256]{2,1,0:T(8,128)(2,1)S(1)}, bf16[2,64,256]{2,1,0:T(8,128)(2,1)S(1)}, u32[]{:S(2)}, u32[]{:S(2)}) collective-permute-start(bf16[2,64,256]{2,1,0:T(8,128)(2,1)S(1)} %get-tuple-element.63), channel_id=1, source_target_pairs={{0,8},{4,12},{8,0},{12,4},{16,24},{20,28},{24,16},{28,20},{1,9},{5... | collective-permute-start | bytes 196616 | tf_op jit(solution)/shard_map/ppermute | solution.py:243
  39.8 0.9 %collective-permute-start.9 = (bf16[2,64,256]{2,1,0:T(8,128)(2,1)S(1)}, bf16[2,64,256]{2,1,0:T(8,128)(2,1)S(1)}, u32[]{:S(2)}, u32[]{:S(2)}) collective-permute-start(bf16[2,64,256]{2,1,0:T(8,128)(2,1)S(1)} %get-tuple-element.64), channel_id=1, source_target_pairs={{0,12},{4,8},{8,4},{12,0},{16,28},{20,24},{24,20},{28,16},{1,13},{... | collective-permute-start | bytes 196616 | tf_op jit(solution)/shard_map/ppermute | solution.py:243
  40.7 3.2 %collective-permute-start.10 = (bf16[2,64,256]{2,1,0:T(8,128)(2,1)S(1)}, bf16[2,64,256]{2,1,0:T(8,128)(2,1)S(1)}, u32[]{:S(2)}, u32[]{:S(2)}) collective-permute-start(bf16[2,64,256]{2,1,0:T(8,128)(2,1)S(1)} %get-tuple-element.65), channel_id=1, source_target_pairs={{0,16},{4,20},{8,24},{12,28},{16,0},{20,4},{24,8},{28,12},{1,17},{... | collective-permute-start | bytes 196616 | tf_op jit(solution)/shard_map/ppermute | solution.py:243
  43.9 0.0 collective-permute-start.11
  43.9 0.0 collective-permute-done.7.refs_1_
  43.9 2.4 %collective-permute-start.12 = (bf16[2,64,256]{2,1,0:T(8,128)(2,1)S(1)}, bf16[2,64,256]{2,1,0:T(8,128)(2,1)S(1)}, u32[]{:S(2)}, u32[]{:S(2)}) collective-permute-start(bf16[2,64,256]{2,1,0:T(8,128)(2,1)S(1)} %get-tuple-element.67), channel_id=1, source_target_pairs={{0,24},{4,28},{8,16},{12,20},{16,8},{20,12},{24,0},{28,4},{1,25},{... | collective-permute-start | bytes 196616 | tf_op jit(solution)/shard_map/ppermute | solution.py:243
  46.3 0.0 collective-permute-done.8.refs_2_
  46.3 2.4 %collective-permute-start.13 = (bf16[2,64,256]{2,1,0:T(8,128)(2,1)S(1)}, bf16[2,64,256]{2,1,0:T(8,128)(2,1)S(1)}, u32[]{:S(2)}, u32[]{:S(2)}) collective-permute-start(bf16[2,64,256]{2,1,0:T(8,128)(2,1)S(1)} %get-tuple-element.68), channel_id=1, source_target_pairs={{0,28},{4,24},{8,20},{12,16},{16,12},{20,8},{24,4},{28,0},{1,29},{... | collective-permute-start | bytes 196616 | tf_op jit(solution)/shard_map/ppermute | solution.py:243
  48.6 0.0 collective-permute-done.9.refs_3_
  48.6 2.5 %collective-permute-done.10.refs_4_ = bf16[2,64,256]{2,1,0:T(8,128)(2,1)S(1)} collective-permute-done((bf16[2,64,256]{2,1,0:T(8,128)(2,1)S(1)}, bf16[2,64,256]{2,1,0:T(8,128)(2,1)S(1)}, u32[]{:S(2)}, u32[]{:S(2)}) %collective-permute-start.10) | collective-permute-done | bytes 65568 | tf_op jit(solution)/shard_map/ppermute | solution.py:243
  51.1 1.2 %collective-permute-done.11.refs_5_ = bf16[2,64,256]{2,1,0:T(8,128)(2,1)S(1)} collective-permute-done((bf16[2,64,256]{2,1,0:T(8,128)(2,1)S(1)}, bf16[2,64,256]{2,1,0:T(8,128)(2,1)S(1)}, u32[]{:S(2)}, u32[]{:S(2)}) %collective-permute-start.11) | collective-permute-done | bytes 65568 | tf_op jit(solution)/shard_map/ppermute | solution.py:243
  52.3 0.0 collective-permute-done.12.refs_6_
  52.3 1.1 %collective-permute-done.13.refs_7_ = bf16[2,64,256]{2,1,0:T(8,128)(2,1)S(1)} collective-permute-done((bf16[2,64,256]{2,1,0:T(8,128)(2,1)S(1)}, bf16[2,64,256]{2,1,0:T(8,128)(2,1)S(1)}, u32[]{:S(2)}, u32[]{:S(2)}) %collective-permute-start.13) | collective-permute-done | bytes 65568 | tf_op jit(solution)/shard_map/ppermute | solution.py:243
  53.3 0.0 copy-done.5
  53.4 0.0 copy-start.1
  53.4 1.6 %copy-done.1 = bf16[2048,512]{1,0:T(8,128)(2,1)S(1)} copy-done((bf16[2048,512]{1,0:T(8,128)(2,1)S(1)}, bf16[2048,512]{1,0:T(8,128)(2,1)}, u32[]{:S(2)}) %copy-start.1) | copy-done | bytes 2097176
  55.0 1.6 %copy-done.2 = bf16[2048,512]{1,0:T(8,128)(2,1)S(1)} copy-done((bf16[2048,512]{1,0:T(8,128)(2,1)S(1)}, bf16[2048,512]{1,0:T(8,128)(2,1)}, u32[]{:S(2)}) %copy-start.2) | copy-done | bytes 2097176
  56.5 1.9 %project.1 = (bf16[2,256,512]{2,1,0:T(8,128)(2,1)S(1)}, f32[256,512]{1,0:T(8,128)S(1)}, f32[256,512]{1,0:T(8,128)S(1)}) custom-call(bf16[2,64,256]{2,1,0:T(8,128)(2,1)S(1)} %get-tuple-element.69.refs_0_, bf16[2,64,256]{2,1,0:T(8,128)(2,1)S(1)} %collective-permute-done.7.refs_1_, bf16[2,64,256]{2,1,0:T(8,128)(2,1)S(1)} %collective-permute-done.8.refs_2_, ...), custom_call_target="tpu_custom_call" | custom-call | flops 1610612736 | bytes 8388608 | tf_op jit(solution)/shard_map/project/pallas_call | solution.py:291
  58.4 0.1 collective-permute-start.14
  58.5 1.9 %collective-permute-done.14 = bf16[2,256,512]{2,1,0:T(8,128)(2,1)S(1)} collective-permute-done((bf16[2,256,512]{2,1,0:T(8,128)(2,1)S(1)}, bf16[2,256,512]{2,1,0:T(8,128)(2,1)S(1)}, u32[]{:S(2)}, u32[]{:S(2)}) %collective-permute-start.14) | collective-permute-done | bytes 524320 | tf_op jit(solution)/shard_map/ppermute | solution.py:243
  60.4 0.1 fusion
  60.5 1.6 %collective-permute-start.15 = (bf16[256,512]{1,0:T(8,128)(2,1)S(1)}, bf16[256,512]{1,0:T(8,128)(2,1)S(1)}, u32[]{:S(2)}, u32[]{:S(2)}) collective-permute-start(bf16[256,512]{1,0:T(8,128)(2,1)S(1)} %fusion), channel_id=1, source_target_pairs={{0,2},{1,3},{2,0},{3,1},{4,6},{5,7},{6,4},{7,5},{8,10},{9,11},{10,... | collective-permute-start | bytes 786440 | tf_op jit(solution)/shard_map/ppermute | solution.py:243
  62.0 1.5 %collective-permute-start.16 = (bf16[1,64,256]{2,1,0:T(8,128)(2,1)S(1)}, bf16[1,64,256]{2,1,0:T(8,128)(2,1)S(1)}, u32[]{:S(2)}, u32[]{:S(2)}) collective-permute-start(bf16[1,64,256]{2,1,0:T(8,128)(2,1)S(1)} %get-tuple-element.81), channel_id=1, source_target_pairs={{0,4},{4,0},{8,12},{12,8},{16,20},{20,16},{24,28},{28,24},{1,5},{5... | collective-permute-start | bytes 98312 | tf_op jit(solution)/shard_map/ppermute | solution.py:243
  63.5 2.5 %collective-permute-start.17 = (bf16[1,64,256]{2,1,0:T(8,128)(2,1)S(1)}, bf16[1,64,256]{2,1,0:T(8,128)(2,1)S(1)}, u32[]{:S(2)}, u32[]{:S(2)}) collective-permute-start(bf16[1,64,256]{2,1,0:T(8,128)(2,1)S(1)} %get-tuple-element.82), channel_id=1, source_target_pairs={{0,8},{4,12},{8,0},{12,4},{16,24},{20,28},{24,16},{28,20},{1,9},{5... | collective-permute-start | bytes 98312 | tf_op jit(solution)/shard_map/ppermute | solution.py:243
  65.9 0.1 collective-permute-start.18
  66.1 2.7 %collective-permute-start.19 = (bf16[1,64,256]{2,1,0:T(8,128)(2,1)S(1)}, bf16[1,64,256]{2,1,0:T(8,128)(2,1)S(1)}, u32[]{:S(2)}, u32[]{:S(2)}) collective-permute-start(bf16[1,64,256]{2,1,0:T(8,128)(2,1)S(1)} %get-tuple-element.84), channel_id=1, source_target_pairs={{0,16},{4,20},{8,24},{12,28},{16,0},{20,4},{24,8},{28,12},{1,17},{... | collective-permute-start | bytes 98312 | tf_op jit(solution)/shard_map/ppermute | solution.py:243
  68.8 0.0 collective-permute-done.16.refs_1_
  68.8 1.0 %collective-permute-start.20 = (bf16[1,64,256]{2,1,0:T(8,128)(2,1)S(1)}, bf16[1,64,256]{2,1,0:T(8,128)(2,1)S(1)}, u32[]{:S(2)}, u32[]{:S(2)}) collective-permute-start(bf16[1,64,256]{2,1,0:T(8,128)(2,1)S(1)} %get-tuple-element.85), channel_id=1, source_target_pairs={{0,20},{4,16},{8,28},{12,24},{16,4},{20,0},{24,12},{28,8},{1,21},{... | collective-permute-start | bytes 98312 | tf_op jit(solution)/shard_map/ppermute | solution.py:243
  69.8 0.0 collective-permute-done.17.refs_2_
  69.8 1.9 %collective-permute-start.21 = (bf16[1,64,256]{2,1,0:T(8,128)(2,1)S(1)}, bf16[1,64,256]{2,1,0:T(8,128)(2,1)S(1)}, u32[]{:S(2)}, u32[]{:S(2)}) collective-permute-start(bf16[1,64,256]{2,1,0:T(8,128)(2,1)S(1)} %get-tuple-element.86), channel_id=1, source_target_pairs={{0,24},{4,28},{8,16},{12,20},{16,8},{20,12},{24,0},{28,4},{1,25},{... | collective-permute-start | bytes 98312 | tf_op jit(solution)/shard_map/ppermute | solution.py:243
  71.7 0.0 collective-permute-done.18.refs_3_
  71.7 2.3 %collective-permute-start.22 = (bf16[1,64,256]{2,1,0:T(8,128)(2,1)S(1)}, bf16[1,64,256]{2,1,0:T(8,128)(2,1)S(1)}, u32[]{:S(2)}, u32[]{:S(2)}) collective-permute-start(bf16[1,64,256]{2,1,0:T(8,128)(2,1)S(1)} %get-tuple-element.87), channel_id=1, source_target_pairs={{0,28},{4,24},{8,20},{12,16},{16,12},{20,8},{24,4},{28,0},{1,29},{... | collective-permute-start | bytes 98312 | tf_op jit(solution)/shard_map/ppermute | solution.py:243
  74.0 0.0 collective-permute-done.19.refs_4_
  74.0 0.7 collective-permute-done.20.refs_5_
  74.7 1.1 %collective-permute-done.21.refs_6_ = bf16[1,64,256]{2,1,0:T(8,128)(2,1)S(1)} collective-permute-done((bf16[1,64,256]{2,1,0:T(8,128)(2,1)S(1)}, bf16[1,64,256]{2,1,0:T(8,128)(2,1)S(1)}, u32[]{:S(2)}, u32[]{:S(2)}) %collective-permute-start.21) | collective-permute-done | bytes 32800 | tf_op jit(solution)/shard_map/ppermute | solution.py:243
  75.8 2.5 %collective-permute-done.22.refs_7_ = bf16[1,64,256]{2,1,0:T(8,128)(2,1)S(1)} collective-permute-done((bf16[1,64,256]{2,1,0:T(8,128)(2,1)S(1)}, bf16[1,64,256]{2,1,0:T(8,128)(2,1)S(1)}, u32[]{:S(2)}, u32[]{:S(2)}) %collective-permute-start.22) | collective-permute-done | bytes 32800 | tf_op jit(solution)/shard_map/ppermute | solution.py:243
  78.3 0.9 %turn.1 = bf16[256,512]{1,0:T(8,128)(2,1)} custom-call(bf16[1,64,256]{2,1,0:T(8,128)(2,1)S(1)} %get-tuple-element.80.refs_0_, bf16[1,64,256]{2,1,0:T(8,128)(2,1)S(1)} %collective-permute-done.16.refs_1_, bf16[1,64,256]{2,1,0:T(8,128)(2,1)S(1)} %collective-permute-done.17.refs_2_, bf16[1,64,256]{2,1,0:T(8,128)(2,1)S(1)} %collective-permute-done.18.refs_3_, ...), custom_call_target="tpu_custom_call" | custom-call | tf_op jit(solution)/shard_map/turn/pallas_call | solution.py:311
  79.1 0.0 collective-permute-done.15
  79.1 0.8 %fusion.2 = bf16[256,512]{1,0:T(8,128)(2,1)} fusion(f32[256,512]{1,0:T(8,128)S(1)} %get-tuple-element.77, bf16[256,512]{1,0:T(8,128)(2,1)S(1)} %collective-permute-done.15, bf16[2,256,512]{2,1,0:T(8,128)(2,1)S(1)} %collective-permute-done.14), kind=kLoop, calls=%fused_computation.4 | loop fusion | flops 655360 | bytes 1310720 | tf_op jit(solution)/shard_map/convert_element_type | solution.py:310
  (8 shorter events, 0.0 us)
Async XLA Ops:
  0.6 52.7 %copy-start.5 = (bf16[256,512]{1,0:T(8,128)(2,1)S(1)}, bf16[256,512]{1,0:T(8,128)(2,1)}, u32[]{:S(2)}) copy-start(bf16[256,512]{1,0:T(8,128)(2,1)} %refs_10_.2) | copy-start | bytes 786436
  0.6 52.7 %copy-start.4 = (bf16[256,512]{1,0:T(8,128)(2,1)S(1)}, bf16[256,512]{1,0:T(8,128)(2,1)}, u32[]{:S(2)}) copy-start(bf16[256,512]{1,0:T(8,128)(2,1)} %refs_9_.2) | copy-start | bytes 786436
  0.7 52.7 %copy-start.3 = (bf16[256,512]{1,0:T(8,128)(2,1)S(1)}, bf16[256,512]{1,0:T(8,128)(2,1)}, u32[]{:S(2)}) copy-start(bf16[256,512]{1,0:T(8,128)(2,1)} %refs_8_.2) | copy-start | bytes 786436
  0.7 52.7 %copy-start = (bf16[2048,512]{1,0:T(8,128)(2,1)S(1)}, bf16[2048,512]{1,0:T(8,128)(2,1)}, u32[]{:S(2)}) copy-start(bf16[2048,512]{1,0:T(8,128)(2,1)} %refs_11_.1) | copy-start | bytes 6291460
  3.3 8.8 %collective-permute-start = (bf16[3,64,256]{2,1,0:T(8,128)(2,1)}, bf16[3,64,256]{2,1,0:T(8,128)(2,1)S(1)}, u32[]{:S(2)}, u32[]{:S(2)}) collective-permute-start(bf16[3,64,256]{2,1,0:T(8,128)(2,1)} %get-tuple-element.46), channel_id=1, source_target_pairs={{0,4},{4,0},{8,12},{12,8},{16,20},{20,16},{24,28},{28,24},{1,5},{5... | collective-permute-start | bytes 294920 | tf_op jit(solution)/shard_map/ppermute | solution.py:243
  6.2 9.5 %collective-permute-start.1 = (bf16[3,64,256]{2,1,0:T(8,128)(2,1)}, bf16[3,64,256]{2,1,0:T(8,128)(2,1)S(1)}, u32[]{:S(2)}, u32[]{:S(2)}) collective-permute-start(bf16[3,64,256]{2,1,0:T(8,128)(2,1)} %get-tuple-element.47), channel_id=1, source_target_pairs={{0,8},{4,12},{8,0},{12,4},{16,24},{20,28},{24,16},{28,20},{1,9},{5... | collective-permute-start | bytes 294920 | tf_op jit(solution)/shard_map/ppermute | solution.py:243
  7.8 7.9 %collective-permute-start.2 = (bf16[3,64,256]{2,1,0:T(8,128)(2,1)}, bf16[3,64,256]{2,1,0:T(8,128)(2,1)S(1)}, u32[]{:S(2)}, u32[]{:S(2)}) collective-permute-start(bf16[3,64,256]{2,1,0:T(8,128)(2,1)} %get-tuple-element.48), channel_id=1, source_target_pairs={{0,12},{4,8},{8,4},{12,0},{16,28},{20,24},{24,20},{28,16},{1,13},{... | collective-permute-start | bytes 294920 | tf_op jit(solution)/shard_map/ppermute | solution.py:243
  7.8 7.9 %collective-permute-start.3 = (bf16[3,64,256]{2,1,0:T(8,128)(2,1)}, bf16[3,64,256]{2,1,0:T(8,128)(2,1)S(1)}, u32[]{:S(2)}, u32[]{:S(2)}) collective-permute-start(bf16[3,64,256]{2,1,0:T(8,128)(2,1)} %get-tuple-element.49), channel_id=1, source_target_pairs={{0,16},{4,20},{8,24},{12,28},{16,0},{20,4},{24,8},{28,12},{1,17},{... | collective-permute-start | bytes 294920 | tf_op jit(solution)/shard_map/ppermute | solution.py:243
  10.8 15.4 %collective-permute-start.4 = (bf16[3,64,256]{2,1,0:T(8,128)(2,1)}, bf16[3,64,256]{2,1,0:T(8,128)(2,1)S(1)}, u32[]{:S(2)}, u32[]{:S(2)}) collective-permute-start(bf16[3,64,256]{2,1,0:T(8,128)(2,1)} %get-tuple-element.50), channel_id=1, source_target_pairs={{0,20},{4,16},{8,28},{12,24},{16,4},{20,0},{24,12},{28,8},{1,21},{... | collective-permute-start | bytes 294920 | tf_op jit(solution)/shard_map/ppermute | solution.py:243
  12.1 14.1 %collective-permute-start.5 = (bf16[3,64,256]{2,1,0:T(8,128)(2,1)}, bf16[3,64,256]{2,1,0:T(8,128)(2,1)S(1)}, u32[]{:S(2)}, u32[]{:S(2)}) collective-permute-start(bf16[3,64,256]{2,1,0:T(8,128)(2,1)} %get-tuple-element.51), channel_id=1, source_target_pairs={{0,24},{4,28},{8,16},{12,20},{16,8},{20,12},{24,0},{28,4},{1,25},{... | collective-permute-start | bytes 294920 | tf_op jit(solution)/shard_map/ppermute | solution.py:243
  15.7 10.5 %collective-permute-start.6 = (bf16[3,64,256]{2,1,0:T(8,128)(2,1)}, bf16[3,64,256]{2,1,0:T(8,128)(2,1)S(1)}, u32[]{:S(2)}, u32[]{:S(2)}) collective-permute-start(bf16[3,64,256]{2,1,0:T(8,128)(2,1)} %get-tuple-element.52), channel_id=1, source_target_pairs={{0,28},{4,24},{8,20},{12,16},{16,12},{20,8},{24,4},{28,0},{1,29},{... | collective-permute-start | bytes 294920 | tf_op jit(solution)/shard_map/ppermute | solution.py:243
  26.2 1.0 %copy-start.6 = (bf16[512,512]{1,0:T(8,128)(2,1)S(1)}, bf16[512,512]{1,0:T(8,128)(2,1)}, u32[]{:S(2)}) copy-start(bf16[512,512]{1,0:T(8,128)(2,1)} %constant.7.clone.refs_9_) | copy-start | bytes 1572868
  27.2 1.0 %copy-start.7 = (bf16[512,512]{1,0:T(8,128)(2,1)S(1)}, bf16[512,512]{1,0:T(8,128)(2,1)}, u32[]{:S(2)}) copy-start(bf16[512,512]{1,0:T(8,128)(2,1)} %constant.6.clone.refs_8_) | copy-start | bytes 1572868
  28.3 0.9 %copy-start.8 = (bf16[3,64,256]{2,1,0:T(8,128)(2,1)S(1)}, bf16[3,64,256]{2,1,0:T(8,128)(2,1)}, u32[]{:S(2)}) copy-start(bf16[3,64,256]{2,1,0:T(8,128)(2,1)} %get-tuple-element.45.refs_0_) | copy-start | bytes 294916
  29.2 0.8 %copy-start.9 = (f32[4,9,256]{2,1,0:T(8,128)S(1)}, f32[4,9,256]{2,1,0:T(8,128)}, u32[]{:S(2)}) copy-start(f32[4,9,256]{2,1,0:T(8,128)} %constant.8.clone.refs_10_) | copy-start | bytes 110596
  35.2 8.7 %collective-permute-start.7 = (bf16[2,64,256]{2,1,0:T(8,128)(2,1)S(1)}, bf16[2,64,256]{2,1,0:T(8,128)(2,1)S(1)}, u32[]{:S(2)}, u32[]{:S(2)}) collective-permute-start(bf16[2,64,256]{2,1,0:T(8,128)(2,1)S(1)} %get-tuple-element.62), channel_id=1, source_target_pairs={{0,4},{4,0},{8,12},{12,8},{16,20},{20,16},{24,28},{28,24},{1,5},{5... | collective-permute-start | bytes 196616 | tf_op jit(solution)/shard_map/ppermute | solution.py:243
  36.2 10.1 %collective-permute-start.8 = (bf16[2,64,256]{2,1,0:T(8,128)(2,1)S(1)}, bf16[2,64,256]{2,1,0:T(8,128)(2,1)S(1)}, u32[]{:S(2)}, u32[]{:S(2)}) collective-permute-start(bf16[2,64,256]{2,1,0:T(8,128)(2,1)S(1)} %get-tuple-element.63), channel_id=1, source_target_pairs={{0,8},{4,12},{8,0},{12,4},{16,24},{20,28},{24,16},{28,20},{1,9},{5... | collective-permute-start | bytes 196616 | tf_op jit(solution)/shard_map/ppermute | solution.py:243
  39.8 8.9 %collective-permute-start.9 = (bf16[2,64,256]{2,1,0:T(8,128)(2,1)S(1)}, bf16[2,64,256]{2,1,0:T(8,128)(2,1)S(1)}, u32[]{:S(2)}, u32[]{:S(2)}) collective-permute-start(bf16[2,64,256]{2,1,0:T(8,128)(2,1)S(1)} %get-tuple-element.64), channel_id=1, source_target_pairs={{0,12},{4,8},{8,4},{12,0},{16,28},{20,24},{24,20},{28,16},{1,13},{... | collective-permute-start | bytes 196616 | tf_op jit(solution)/shard_map/ppermute | solution.py:243
  40.7 10.4 %collective-permute-start.10 = (bf16[2,64,256]{2,1,0:T(8,128)(2,1)S(1)}, bf16[2,64,256]{2,1,0:T(8,128)(2,1)S(1)}, u32[]{:S(2)}, u32[]{:S(2)}) collective-permute-start(bf16[2,64,256]{2,1,0:T(8,128)(2,1)S(1)} %get-tuple-element.65), channel_id=1, source_target_pairs={{0,16},{4,20},{8,24},{12,28},{16,0},{20,4},{24,8},{28,12},{1,17},{... | collective-permute-start | bytes 196616 | tf_op jit(solution)/shard_map/ppermute | solution.py:243
  43.9 8.4 %collective-permute-start.11 = (bf16[2,64,256]{2,1,0:T(8,128)(2,1)S(1)}, bf16[2,64,256]{2,1,0:T(8,128)(2,1)S(1)}, u32[]{:S(2)}, u32[]{:S(2)}) collective-permute-start(bf16[2,64,256]{2,1,0:T(8,128)(2,1)S(1)} %get-tuple-element.66), channel_id=1, source_target_pairs={{0,20},{4,16},{8,28},{12,24},{16,4},{20,0},{24,12},{28,8},{1,21},{... | collective-permute-start | bytes 196616 | tf_op jit(solution)/shard_map/ppermute | solution.py:243
  43.9 8.4 %collective-permute-start.12 = (bf16[2,64,256]{2,1,0:T(8,128)(2,1)S(1)}, bf16[2,64,256]{2,1,0:T(8,128)(2,1)S(1)}, u32[]{:S(2)}, u32[]{:S(2)}) collective-permute-start(bf16[2,64,256]{2,1,0:T(8,128)(2,1)S(1)} %get-tuple-element.67), channel_id=1, source_target_pairs={{0,24},{4,28},{8,16},{12,20},{16,8},{20,12},{24,0},{28,4},{1,25},{... | collective-permute-start | bytes 196616 | tf_op jit(solution)/shard_map/ppermute | solution.py:243
  46.3 7.1 %collective-permute-start.13 = (bf16[2,64,256]{2,1,0:T(8,128)(2,1)S(1)}, bf16[2,64,256]{2,1,0:T(8,128)(2,1)S(1)}, u32[]{:S(2)}, u32[]{:S(2)}) collective-permute-start(bf16[2,64,256]{2,1,0:T(8,128)(2,1)S(1)} %get-tuple-element.68), channel_id=1, source_target_pairs={{0,28},{4,24},{8,20},{12,16},{16,12},{20,8},{24,4},{28,0},{1,29},{... | collective-permute-start | bytes 196616 | tf_op jit(solution)/shard_map/ppermute | solution.py:243
  53.4 1.6 %copy-start.1 = (bf16[2048,512]{1,0:T(8,128)(2,1)S(1)}, bf16[2048,512]{1,0:T(8,128)(2,1)}, u32[]{:S(2)}) copy-start(bf16[2048,512]{1,0:T(8,128)(2,1)} %refs_12_.1) | copy-start | bytes 6291460
  54.9 1.6 %copy-start.2 = (bf16[2048,512]{1,0:T(8,128)(2,1)S(1)}, bf16[2048,512]{1,0:T(8,128)(2,1)}, u32[]{:S(2)}) copy-start(bf16[2048,512]{1,0:T(8,128)(2,1)} %refs_13_.1) | copy-start | bytes 6291460
  58.4 2.0 %collective-permute-start.14 = (bf16[2,256,512]{2,1,0:T(8,128)(2,1)S(1)}, bf16[2,256,512]{2,1,0:T(8,128)(2,1)S(1)}, u32[]{:S(2)}, u32[]{:S(2)}) collective-permute-start(bf16[2,256,512]{2,1,0:T(8,128)(2,1)S(1)} %get-tuple-element.78), channel_id=1, source_target_pairs={{0,1},{1,0},{2,3},{3,2},{4,5},{5,4},{6,7},{7,6},{8,9},{9,8},{10,11... | collective-permute-start | bytes 1572872 | tf_op jit(solution)/shard_map/ppermute | solution.py:243
  60.5 18.7 %collective-permute-start.15 = (bf16[256,512]{1,0:T(8,128)(2,1)S(1)}, bf16[256,512]{1,0:T(8,128)(2,1)S(1)}, u32[]{:S(2)}, u32[]{:S(2)}) collective-permute-start(bf16[256,512]{1,0:T(8,128)(2,1)S(1)} %fusion), channel_id=1, source_target_pairs={{0,2},{1,3},{2,0},{3,1},{4,6},{5,7},{6,4},{7,5},{8,10},{9,11},{10,... | collective-permute-start | bytes 786440 | tf_op jit(solution)/shard_map/ppermute | solution.py:243
  62.0 6.8 %collective-permute-start.16 = (bf16[1,64,256]{2,1,0:T(8,128)(2,1)S(1)}, bf16[1,64,256]{2,1,0:T(8,128)(2,1)S(1)}, u32[]{:S(2)}, u32[]{:S(2)}) collective-permute-start(bf16[1,64,256]{2,1,0:T(8,128)(2,1)S(1)} %get-tuple-element.81), channel_id=1, source_target_pairs={{0,4},{4,0},{8,12},{12,8},{16,20},{20,16},{24,28},{28,24},{1,5},{5... | collective-permute-start | bytes 98312 | tf_op jit(solution)/shard_map/ppermute | solution.py:243
  63.5 6.3 %collective-permute-start.17 = (bf16[1,64,256]{2,1,0:T(8,128)(2,1)S(1)}, bf16[1,64,256]{2,1,0:T(8,128)(2,1)S(1)}, u32[]{:S(2)}, u32[]{:S(2)}) collective-permute-start(bf16[1,64,256]{2,1,0:T(8,128)(2,1)S(1)} %get-tuple-element.82), channel_id=1, source_target_pairs={{0,8},{4,12},{8,0},{12,4},{16,24},{20,28},{24,16},{28,20},{1,9},{5... | collective-permute-start | bytes 98312 | tf_op jit(solution)/shard_map/ppermute | solution.py:243
  65.9 5.7 %collective-permute-start.18 = (bf16[1,64,256]{2,1,0:T(8,128)(2,1)S(1)}, bf16[1,64,256]{2,1,0:T(8,128)(2,1)S(1)}, u32[]{:S(2)}, u32[]{:S(2)}) collective-permute-start(bf16[1,64,256]{2,1,0:T(8,128)(2,1)S(1)} %get-tuple-element.83), channel_id=1, source_target_pairs={{0,12},{4,8},{8,4},{12,0},{16,28},{20,24},{24,20},{28,16},{1,13},{... | collective-permute-start | bytes 98312 | tf_op jit(solution)/shard_map/ppermute | solution.py:243
  66.1 7.9 %collective-permute-start.19 = (bf16[1,64,256]{2,1,0:T(8,128)(2,1)S(1)}, bf16[1,64,256]{2,1,0:T(8,128)(2,1)S(1)}, u32[]{:S(2)}, u32[]{:S(2)}) collective-permute-start(bf16[1,64,256]{2,1,0:T(8,128)(2,1)S(1)} %get-tuple-element.84), channel_id=1, source_target_pairs={{0,16},{4,20},{8,24},{12,28},{16,0},{20,4},{24,8},{28,12},{1,17},{... | collective-permute-start | bytes 98312 | tf_op jit(solution)/shard_map/ppermute | solution.py:243
  68.8 5.9 %collective-permute-start.20 = (bf16[1,64,256]{2,1,0:T(8,128)(2,1)S(1)}, bf16[1,64,256]{2,1,0:T(8,128)(2,1)S(1)}, u32[]{:S(2)}, u32[]{:S(2)}) collective-permute-start(bf16[1,64,256]{2,1,0:T(8,128)(2,1)S(1)} %get-tuple-element.85), channel_id=1, source_target_pairs={{0,20},{4,16},{8,28},{12,24},{16,4},{20,0},{24,12},{28,8},{1,21},{... | collective-permute-start | bytes 98312 | tf_op jit(solution)/shard_map/ppermute | solution.py:243
  69.8 6.0 %collective-permute-start.21 = (bf16[1,64,256]{2,1,0:T(8,128)(2,1)S(1)}, bf16[1,64,256]{2,1,0:T(8,128)(2,1)S(1)}, u32[]{:S(2)}, u32[]{:S(2)}) collective-permute-start(bf16[1,64,256]{2,1,0:T(8,128)(2,1)S(1)} %get-tuple-element.86), channel_id=1, source_target_pairs={{0,24},{4,28},{8,16},{12,20},{16,8},{20,12},{24,0},{28,4},{1,25},{... | collective-permute-start | bytes 98312 | tf_op jit(solution)/shard_map/ppermute | solution.py:243
  71.7 6.6 %collective-permute-start.22 = (bf16[1,64,256]{2,1,0:T(8,128)(2,1)S(1)}, bf16[1,64,256]{2,1,0:T(8,128)(2,1)S(1)}, u32[]{:S(2)}, u32[]{:S(2)}) collective-permute-start(bf16[1,64,256]{2,1,0:T(8,128)(2,1)S(1)} %get-tuple-element.87), channel_id=1, source_target_pairs={{0,28},{4,24},{8,20},{12,16},{16,12},{20,8},{24,4},{28,0},{1,29},{... | collective-permute-start | bytes 98312 | tf_op jit(solution)/shard_map/ppermute | solution.py:243

commit v3 on v2

--- a/solution.py
+++ b/solution.py
@@ -10,7 +10,7 @@
 
 
 def compiler_params(mib):
-    return pltpu.CompilerParams(vmem_limit_bytes=mib * 1024 * 1024)
+    return pltpu.CompilerParams(vmem_limit_bytes=int(mib * 1024 * 1024))
 
 
 def dft_tables(blocks, block_len, scale):
@@ -85,30 +85,54 @@
     return values
 
 
-def gate_kernel(key_ref, value_ref, query_ref, grad_ref, filter_ref, *refs):
-    out_refs, turn_ref = refs[:-1], refs[-1]
+HBM = pl.BlockSpec(memory_space=pltpu.HBM)
+VMEM = pl.BlockSpec(memory_space=pltpu.VMEM)
+
+
+def far_first(pieces):
+    return zip(reversed(range(len(pieces))), pieces)
+
+
+def fetch(sources, targets, sems):
+    copies = [
+        pltpu.make_async_copy(source, target, sems.at[i])
+        for i, (source, target) in enumerate(zip(sources, targets))
+    ]
+    for copy in copies:
+        copy.start()
+    return copies
+
+
+def gate_kernel(*refs):
+    sources, refs = refs[:5], refs[5:]
+    out_refs, (turn_ref, held_ref, sems) = refs[:-3], refs[-3:]
     blocks, _, channels, block_len = turn_ref.shape
+    filter_copy, *copies = fetch(sources, [held_ref.at[i] for i in range(5)], sems)
 
     def put(slot, wide):
         turned = wide.T.astype(jnp.bfloat16)
         turn_ref[:, slot] = turned.reshape(blocks, channels, block_len)
 
-    put(0, key_ref[...].astype(jnp.float32) * value_ref[...].astype(jnp.float32))
-    put(1, filter_ref[...].astype(jnp.float32))
-    put(2, query_ref[...].astype(jnp.float32) * grad_ref[...].astype(jnp.float32))
+    filter_copy.wait()
+    put(1, held_ref[0].astype(jnp.float32))
+    for copy in copies[:2]:
+        copy.wait()
+    put(0, held_ref[1].astype(jnp.float32) * held_ref[2].astype(jnp.float32))
+    for copy in copies[2:]:
+        copy.wait()
+    put(2, held_ref[3].astype(jnp.float32) * held_ref[4].astype(jnp.float32))
     me = lax.axis_index("ctx")
-    for distance, out_ref in enumerate(out_refs):
+    for distance, out_ref in far_first(out_refs):
         out_ref[...] = turn_ref[me ^ distance]
 
 
 def conv_kernel(*refs):
     blocks = lax.axis_size("ctx")
-    in_refs, (fwd_ref, inv_ref, twid_ref) = refs[:blocks], refs[blocks : blocks + 3]
-    gates_refs, filt_refs = refs[blocks + 3 : 2 * blocks + 3], refs[2 * blocks + 3 : 3 * blocks + 3]
-    in_ref, rows_ref, spec_ref = refs[3 * blocks + 3 :]
+    in_refs, (twid_ref, fwd_ref, inv_ref) = refs[:blocks], refs[blocks : blocks + 3]
+    out_refs, (in_ref, rows_ref, spec_ref) = refs[blocks + 3 : -3], refs[-3:]
     _, signals, channels, block_len = in_ref.shape
     me = lax.axis_index("ctx")
-    for distance, ref in enumerate(in_refs):
+    for distance, ref in far_first(in_refs):
         in_ref[me ^ distance] = ref[...]
     chunk = min(channels, 16)
     steps = channels // chunk
@@ -188,9 +212,8 @@
         return carry
 
     lax.fori_loop(0, signals * steps, synthesise, 0)
-    for distance in range(blocks):
-        gates_refs[distance][...] = in_ref[me ^ distance, 0:2]
-        filt_refs[distance][...] = in_ref[me ^ distance, 2:3]
+    for distance, out_ref in far_first(out_refs):
+        out_ref[...] = in_ref[me ^ distance]
 
 
 def term(lhs_ref, weight_refs, group):
@@ -209,7 +232,7 @@
 def natural(back_refs, turn_ref):
     blocks, signals, channels, block_len = turn_ref.shape
     me = lax.axis_index("ctx")
-    for distance, ref in enumerate(back_refs):
+    for distance, ref in far_first(back_refs):
         turn_ref[me ^ distance] = ref[...]
     return [
         turn_ref[:, slot].reshape(blocks * channels, block_len).astype(jnp.float32).T
@@ -217,25 +240,25 @@
     ]
 
 
-def project_kernel(*refs):
+def mate_kernel(*refs):
     blocks = lax.axis_size("ctx")
     back_refs, (key_ref, value_ref, grad_ref) = refs[:blocks], refs[blocks : blocks + 3]
     weight_refs = refs[blocks + 3 : blocks + 6]
-    mate_ref, far_ref, own_ref, turn_ref, lhs_ref = refs[blocks + 6 :]
-    conv_out, grad_product = natural(back_refs, turn_ref)
+    lhs_ref, out_ref, filt_ref, turn_ref = refs[blocks + 6 :]
+    conv_out, grad_product, grad_filter = natural(back_refs, turn_ref)
     lhs_ref[0] = (grad_product * value_ref[...].astype(jnp.float32)).astype(jnp.bfloat16)
     lhs_ref[1] = (conv_out * grad_ref[...].astype(jnp.float32)).astype(jnp.bfloat16)
     lhs_ref[2] = (grad_product * key_ref[...].astype(jnp.float32)).astype(jnp.bfloat16)
     group = lax.axis_index("tp")
-    mate_ref[0] = term(lhs_ref, weight_refs, group ^ 3).astype(jnp.bfloat16)
-    mate_ref[1] = term(lhs_ref, weight_refs, group ^ 1).astype(jnp.bfloat16)
-    far_ref[...] = term(lhs_ref, weight_refs, group ^ 2)
-    own_ref[...] = term(lhs_ref, weight_refs, group)
-
-
-def turn_kernel(*refs):
-    back_refs, (out_ref, turn_ref) = refs[:-2], refs[-2:]
-    out_ref[...] = natural(back_refs, turn_ref)[0].astype(jnp.bfloat16)
+    out_ref[0] = term(lhs_ref, weight_refs, group ^ 3).astype(jnp.bfloat16)
+    out_ref[1] = term(lhs_ref, weight_refs, group ^ 1).astype(jnp.bfloat16)
+    filt_ref[...] = grad_filter.astype(jnp.bfloat16)
+
+
+def own_kernel(lhs_ref, wk_ref, wq_ref, wv_ref, far_ref, own_ref):
+    group = lax.axis_index("tp")
+    far_ref[...] = term(lhs_ref, (wk_ref, wq_ref, wv_ref), group ^ 2)
+    own_ref[...] = term(lhs_ref, (wk_ref, wq_ref, wv_ref), group)
 
 
 def exchange(block, axis, distance):
@@ -244,10 +267,10 @@
 
 
 def swap(pieces):
-    moved = list(pieces)
-    for distance in reversed(range(1, len(pieces))):
-        moved[distance] = exchange(pieces[distance], "ctx", distance)
-    return moved
+    return [
+        exchange(piece, "ctx", distance) if distance else piece
+        for distance, piece in far_first(pieces)
+    ]
 
 
 def per_device(key_act, value_act, query_act, grad_out, long_filter, w_key, w_query, w_value):
@@ -257,17 +280,26 @@
     channels = width // blocks
     seq_len = blocks * block_len
     part = w_key.shape[0] // groups
+    block_cost = pl.CostEstimate(
+        flops=4 * block_len * 3 * width * part, bytes_accessed=1 << 22, transcendentals=0
+    )
 
     def arrays(count, *shape, dtype=jnp.bfloat16):
         return [jax.ShapeDtypeStruct(shape, dtype)] * count
 
     sent = pl.pallas_call(
         gate_kernel,
+        in_specs=[HBM] * 5,
+        out_specs=[VMEM] * blocks,
         out_shape=arrays(blocks, 3, channels, block_len),
-        scratch_shapes=[pltpu.VMEM((blocks, 3, channels, block_len), jnp.bfloat16)],
-        compiler_params=compiler_params(60),
+        scratch_shapes=[
+            pltpu.VMEM((blocks, 3, channels, block_len), jnp.bfloat16),
+            pltpu.VMEM((5, block_len, width), jnp.bfloat16),
+            pltpu.SemaphoreType.DMA((5,)),
+        ],
+        compiler_params=compiler_params(62),
         name="gate",
-    )(key_act, value_act, query_act, grad_out, long_filter)
+    )(long_filter, key_act, value_act, query_act, grad_out)
     moved = swap(sent)
 
     forward, inverse, twiddle = dft_tables(
@@ -275,7 +307,8 @@
     )
     results = pl.pallas_call(
         conv_kernel,
-        out_shape=arrays(blocks, 2, channels, block_len) + arrays(blocks, 1, channels, block_len),
+        in_specs=[VMEM] * (blocks + 3),
+        out_shape=arrays(blocks, 3, channels, block_len),
         scratch_shapes=[
             pltpu.VMEM((blocks, 3, channels, block_len), jnp.bfloat16),
             pltpu.VMEM((blocks + 1, 3, channels, 2 * block_len), jnp.bfloat16),
@@ -283,38 +316,36 @@
         ],
         compiler_params=compiler_params(20),
         name="conv",
-    )(*moved, forward, inverse, twiddle)
-    back = swap(results[:blocks])
-    filt, back = lax.optimization_barrier((results[blocks:], back))
-    back_filt = swap(filt)
-
-    to_mate, far, own = pl.pallas_call(
-        project_kernel,
-        out_shape=arrays(1, 2, block_len, part) + arrays(2, block_len, part, dtype=jnp.float32),
-        scratch_shapes=[
-            pltpu.VMEM((blocks, 2, channels, block_len), jnp.bfloat16),
-            pltpu.VMEM((3, block_len, width), jnp.bfloat16),
+    )(*moved, twiddle, forward, inverse)
+    back = swap(results)
+
+    weights = (w_key, w_query, w_value)
+    lhs, to_mate, grad_filter = pl.pallas_call(
+        mate_kernel,
+        in_specs=[VMEM] * (blocks + 6),
+        out_shape=[
+            *arrays(1, 3, block_len, width),
+            *arrays(1, 2, block_len, part),
+            *arrays(1, block_len, width),
         ],
+        scratch_shapes=[pltpu.VMEM((blocks, 3, channels, block_len), jnp.bfloat16)],
         compiler_params=compiler_params(16),
-        cost_estimate=pl.CostEstimate(
-            flops=2 * block_len * 3 * width * w_key.shape[0],
-            bytes_accessed=1 << 23,
-            transcendentals=0,
-        ),
-        name="project",
-    )(*back, key_act, value_act, grad_out, w_key, w_query, w_value)
+        cost_estimate=block_cost,
+        name="mate",
+    )(*back, key_act, value_act, grad_out, *weights)
     from_mate = exchange(to_mate, "tp", 1)
+    far, own = pl.pallas_call(
+        own_kernel,
+        in_specs=[VMEM] * 4,
+        out_shape=arrays(2, block_len, part, dtype=jnp.float32),
+        compiler_params=compiler_params(16),
+        cost_estimate=block_cost,
+        name="own",
+    )(lhs, *weights)
     far = (far + from_mate[0].astype(jnp.float32)).astype(jnp.bfloat16)
     from_far = exchange(far, "tp", 2)
     near = own + from_mate[1].astype(jnp.float32)
     grad_input = (near + from_far.astype(jnp.float32)).astype(jnp.bfloat16)
-    grad_filter = pl.pallas_call(
-        turn_kernel,
-        out_shape=arrays(1, block_len, width)[0],
-        scratch_shapes=[pltpu.VMEM((blocks, 1, channels, block_len), jnp.bfloat16)],
-        compiler_params=compiler_params(16),
-        name="turn",
-    )(*back_filt)
     return (grad_input, grad_filter)
 
 

time: 80.3 us -> 72.8 us (0.907)
  starting transfers between devices: 39.4 us -> 34.2 us
  waiting for transfers between devices: 21.4 us -> 16.5 us
  local copies, waits for them, and re-layouts: 7.01 us -> 9.81 us
    ppermute x23 -> x16, starting transfers between devices: 39.4 us -> 34.2 us  [exchange(): return lax.ppermute(block, axis, pairs)]
    ppermute x23 -> x16, waiting for transfers between devices: 21.4 us -> 16.5 us  [exchange(): return lax.ppermute(block, axis, pairs)]
    unnamed x20 -> x26, local copies, waits for them, and re-layouts: 7.01 us -> 9.81 us
  transfers between devices with their start and end apart: 23 -> 16, of which waited for: 8 -> 8; matrix products, arithmetic and copies ran while one was open for 0% -> 0% of each run, Pallas kernels for 1% -> 1%
where the time goes in v3:
time: 72.8 us; the launch traced here: 72.4 us
  starting transfers between devices  34.2 us (47%)
  waiting for transfers between devices  16.5 us (23%)
  Pallas kernels  10.3 us (14%)
  local copies, waits for them, and re-layouts  9.81 us (13%)
  other arithmetic  0.88 us (1%)
  between operations  0.74 us (1%)
    ppermute x16, starting transfers between devices, exchange(): return lax.ppermute(block, axis, pairs)  34.2 us
    ppermute x16, waiting for transfers between devices, exchange(): return lax.ppermute(block, axis, pairs)  16.5 us
    unnamed x26, local copies, waits for them, and re-layouts  9.81 us
    pallas_call x1, Pallas kernels, per_device(): pl.pallas_call(conv_kernel, in_specs=[VMEM] * (blocks + 3), out_shape=arr...  5.13 us
    pallas_call x1, Pallas kernels, per_device(): pl.pallas_call(gate_kernel, in_specs=[HBM] * 5, out_specs=[VMEM] * blocks...  2.4 us
    pallas_call x1, Pallas kernels, per_device(): pl.pallas_call(mate_kernel, in_specs=[VMEM] * (blocks + 6), out_shape=[*a...  1.73 us
  transfers between devices with their start and end apart: 16, of which 8 were waited for; matrix products, arithmetic and copies ran while one was open for 0% of the time, Pallas kernels for 1%

profile of v3, /device:TPU:0, one launch (start us, length us, event | category | flops | bytes accessed | tf_op | source)
XLA Modules:
  0.0 72.4 jit_solution(17567057742492297381)
XLA Ops:
  0.6 0.0 copy-start.8
  0.6 0.0 copy-start.7
  0.7 0.0 copy-start.6
  0.7 2.4 %gate.1 = (bf16[3,64,256]{2,1,0:T(8,128)(2,1)}, bf16[3,64,256]{2,1,0:T(8,128)(2,1)}, bf16[3,64,256]{2,1,0:T(8,128)(2,1)}, bf16[3,64,256]{2,1,0:T(8,128)(2,1)}, b...) custom-call(bf16[256,512]{1,0:T(8,128)(2,1)} %refs_0_.1, ...), custom_call_target="tpu_custom_call" | custom-call | tf_op jit(solution)/shard_map/gate/pallas_call | solution.py:290
  3.1 6.1 %collective-permute-start = (bf16[3,64,256]{2,1,0:T(8,128)(2,1)}, bf16[3,64,256]{2,1,0:T(8,128)(2,1)S(1)}, u32[]{:S(2)}, u32[]{:S(2)}) collective-permute-start(bf16[3,64,256]{2,1,0:T(8,128)(2,1)} %get-tuple-element.23), channel_id=1, source_target_pairs={{0,28},{4,24},{8,20},{12,16},{16,12},{20,8},{24,4},{28,0},{1,29},{... | collective-permute-start | bytes 294920 | tf_op jit(solution)/shard_map/ppermute | solution.py:266
  9.1 0.2 collective-permute-start.1
  9.4 0.7 %collective-permute-start.2 = (bf16[3,64,256]{2,1,0:T(8,128)(2,1)}, bf16[3,64,256]{2,1,0:T(8,128)(2,1)S(1)}, u32[]{:S(2)}, u32[]{:S(2)}) collective-permute-start(bf16[3,64,256]{2,1,0:T(8,128)(2,1)} %get-tuple-element.25), channel_id=1, source_target_pairs={{0,20},{4,16},{8,28},{12,24},{16,4},{20,0},{24,12},{28,8},{1,21},{... | collective-permute-start | bytes 294920 | tf_op jit(solution)/shard_map/ppermute | solution.py:266
  10.1 2.0 %collective-permute-start.3 = (bf16[3,64,256]{2,1,0:T(8,128)(2,1)}, bf16[3,64,256]{2,1,0:T(8,128)(2,1)S(1)}, u32[]{:S(2)}, u32[]{:S(2)}) collective-permute-start(bf16[3,64,256]{2,1,0:T(8,128)(2,1)} %get-tuple-element.26), channel_id=1, source_target_pairs={{0,16},{4,20},{8,24},{12,28},{16,0},{20,4},{24,8},{28,12},{1,17},{... | collective-permute-start | bytes 294920 | tf_op jit(solution)/shard_map/ppermute | solution.py:266
  12.1 2.3 %collective-permute-start.4 = (bf16[3,64,256]{2,1,0:T(8,128)(2,1)}, bf16[3,64,256]{2,1,0:T(8,128)(2,1)S(1)}, u32[]{:S(2)}, u32[]{:S(2)}) collective-permute-start(bf16[3,64,256]{2,1,0:T(8,128)(2,1)} %get-tuple-element.27), channel_id=1, source_target_pairs={{0,12},{4,8},{8,4},{12,0},{16,28},{20,24},{24,20},{28,16},{1,13},{... | collective-permute-start | bytes 294920 | tf_op jit(solution)/shard_map/ppermute | solution.py:266
  14.4 0.0 collective-permute-done.refs_0_
  14.4 6.8 %collective-permute-start.5 = (bf16[3,64,256]{2,1,0:T(8,128)(2,1)}, bf16[3,64,256]{2,1,0:T(8,128)(2,1)S(1)}, u32[]{:S(2)}, u32[]{:S(2)}) collective-permute-start(bf16[3,64,256]{2,1,0:T(8,128)(2,1)} %get-tuple-element.28), channel_id=1, source_target_pairs={{0,8},{4,12},{8,0},{12,4},{16,24},{20,28},{24,16},{28,20},{1,9},{5... | collective-permute-start | bytes 294920 | tf_op jit(solution)/shard_map/ppermute | solution.py:266
  21.2 0.0 collective-permute-done.1.refs_1_
  21.2 1.0 %collective-permute-start.6 = (bf16[3,64,256]{2,1,0:T(8,128)(2,1)}, bf16[3,64,256]{2,1,0:T(8,128)(2,1)S(1)}, u32[]{:S(2)}, u32[]{:S(2)}) collective-permute-start(bf16[3,64,256]{2,1,0:T(8,128)(2,1)} %get-tuple-element.29), channel_id=1, source_target_pairs={{0,4},{4,0},{8,12},{12,8},{16,20},{20,16},{24,28},{28,24},{1,5},{5... | collective-permute-start | bytes 294920 | tf_op jit(solution)/shard_map/ppermute | solution.py:266
  22.2 2.8 %collective-permute-done.2.refs_2_ = bf16[3,64,256]{2,1,0:T(8,128)(2,1)S(1)} collective-permute-done((bf16[3,64,256]{2,1,0:T(8,128)(2,1)}, bf16[3,64,256]{2,1,0:T(8,128)(2,1)S(1)}, u32[]{:S(2)}, u32[]{:S(2)}) %collective-permute-start.2) | collective-permute-done | bytes 98336 | tf_op jit(solution)/shard_map/ppermute | solution.py:266
  25.0 1.1 %collective-permute-done.3.refs_3_ = bf16[3,64,256]{2,1,0:T(8,128)(2,1)S(1)} collective-permute-done((bf16[3,64,256]{2,1,0:T(8,128)(2,1)}, bf16[3,64,256]{2,1,0:T(8,128)(2,1)S(1)}, u32[]{:S(2)}, u32[]{:S(2)}) %collective-permute-start.3) | collective-permute-done | bytes 98336 | tf_op jit(solution)/shard_map/ppermute | solution.py:266
  26.1 0.0 collective-permute-done.4.refs_4_
  26.1 0.9 %collective-permute-done.5.refs_5_ = bf16[3,64,256]{2,1,0:T(8,128)(2,1)S(1)} collective-permute-done((bf16[3,64,256]{2,1,0:T(8,128)(2,1)}, bf16[3,64,256]{2,1,0:T(8,128)(2,1)S(1)}, u32[]{:S(2)}, u32[]{:S(2)}) %collective-permute-start.5) | collective-permute-done | bytes 98336 | tf_op jit(solution)/shard_map/ppermute | solution.py:266
  27.1 0.0 collective-permute-done.6.refs_6_
  27.1 0.0 copy-start.9
  27.1 1.0 %copy-done.9 = bf16[512,512]{1,0:T(8,128)(2,1)S(1)} copy-done((bf16[512,512]{1,0:T(8,128)(2,1)S(1)}, bf16[512,512]{1,0:T(8,128)(2,1)}, u32[]{:S(2)}) %copy-start.9) | copy-done | bytes 524312
  28.1 0.0 copy-start.10
  28.1 1.0 %copy-done.10 = bf16[512,512]{1,0:T(8,128)(2,1)S(1)} copy-done((bf16[512,512]{1,0:T(8,128)(2,1)S(1)}, bf16[512,512]{1,0:T(8,128)(2,1)}, u32[]{:S(2)}) %copy-start.10) | copy-done | bytes 524312
  29.2 0.0 copy-start.11
  29.2 0.9 %copy-done.11 = bf16[3,64,256]{2,1,0:T(8,128)(2,1)S(1)} copy-done((bf16[3,64,256]{2,1,0:T(8,128)(2,1)S(1)}, bf16[3,64,256]{2,1,0:T(8,128)(2,1)}, u32[]{:S(2)}) %copy-start.11) | copy-done | bytes 98328
  30.1 0.0 copy-start.12
  30.1 0.8 %copy-done.12 = f32[4,9,256]{2,1,0:T(8,128)S(1)} copy-done((f32[4,9,256]{2,1,0:T(8,128)S(1)}, f32[4,9,256]{2,1,0:T(8,128)}, u32[]{:S(2)}) %copy-start.12) | copy-done | bytes 36888
  30.9 5.1 %conv.1 = (bf16[3,64,256]{2,1,0:T(8,128)(2,1)S(1)}, bf16[3,64,256]{2,1,0:T(8,128)(2,1)S(1)}, bf16[3,64,256]{2,1,0:T(8,128)(2,1)S(1)}, bf16[3,64,256]{2,1,0:T(8,1...) custom-call(bf16[3,64,256]{2,1,0:T(8,128)(2,1)S(1)} %collective-perm, ...), custom_call_target="tpu_custom_call" | custom-call | tf_op jit(solution)/shard_map/conv/pallas_call | solution.py:308
  36.1 2.6 %collective-permute-start.7 = (bf16[3,64,256]{2,1,0:T(8,128)(2,1)S(1)}, bf16[3,64,256]{2,1,0:T(8,128)(2,1)S(1)}, u32[]{:S(2)}, u32[]{:S(2)}) collective-permute-start(bf16[3,64,256]{2,1,0:T(8,128)(2,1)S(1)} %get-tuple-element.31), channel_id=1, source_target_pairs={{0,28},{4,24},{8,20},{12,16},{16,12},{20,8},{24,4},{28,0},{1,29},{... | collective-permute-start | bytes 294920 | tf_op jit(solution)/shard_map/ppermute | solution.py:266
  38.7 1.2 %collective-permute-start.8 = (bf16[3,64,256]{2,1,0:T(8,128)(2,1)S(1)}, bf16[3,64,256]{2,1,0:T(8,128)(2,1)S(1)}, u32[]{:S(2)}, u32[]{:S(2)}) collective-permute-start(bf16[3,64,256]{2,1,0:T(8,128)(2,1)S(1)} %get-tuple-element.32), channel_id=1, source_target_pairs={{0,24},{4,28},{8,16},{12,20},{16,8},{20,12},{24,0},{28,4},{1,25},{... | collective-permute-start | bytes 294920 | tf_op jit(solution)/shard_map/ppermute | solution.py:266
  39.9 1.4 %collective-permute-start.9 = (bf16[3,64,256]{2,1,0:T(8,128)(2,1)S(1)}, bf16[3,64,256]{2,1,0:T(8,128)(2,1)S(1)}, u32[]{:S(2)}, u32[]{:S(2)}) collective-permute-start(bf16[3,64,256]{2,1,0:T(8,128)(2,1)S(1)} %get-tuple-element.33), channel_id=1, source_target_pairs={{0,20},{4,16},{8,28},{12,24},{16,4},{20,0},{24,12},{28,8},{1,21},{... | collective-permute-start | bytes 294920 | tf_op jit(solution)/shard_map/ppermute | solution.py:266
  41.3 2.4 %collective-permute-start.10 = (bf16[3,64,256]{2,1,0:T(8,128)(2,1)S(1)}, bf16[3,64,256]{2,1,0:T(8,128)(2,1)S(1)}, u32[]{:S(2)}, u32[]{:S(2)}) collective-permute-start(bf16[3,64,256]{2,1,0:T(8,128)(2,1)S(1)} %get-tuple-element.34), channel_id=1, source_target_pairs={{0,16},{4,20},{8,24},{12,28},{16,0},{20,4},{24,8},{28,12},{1,17},{... | collective-permute-start | bytes 294920 | tf_op jit(solution)/shard_map/ppermute | solution.py:266
  43.8 0.2 collective-permute-start.11
  44.0 0.6 collective-permute-done.7.refs_0_
  44.6 4.6 %collective-permute-start.12 = (bf16[3,64,256]{2,1,0:T(8,128)(2,1)S(1)}, bf16[3,64,256]{2,1,0:T(8,128)(2,1)S(1)}, u32[]{:S(2)}, u32[]{:S(2)}) collective-permute-start(bf16[3,64,256]{2,1,0:T(8,128)(2,1)S(1)} %get-tuple-element.36), channel_id=1, source_target_pairs={{0,8},{4,12},{8,0},{12,4},{16,24},{20,28},{24,16},{28,20},{1,9},{5... | collective-permute-start | bytes 294920 | tf_op jit(solution)/shard_map/ppermute | solution.py:266
  49.2 0.0 collective-permute-done.8.refs_1_
  49.2 1.1 %collective-permute-start.13 = (bf16[3,64,256]{2,1,0:T(8,128)(2,1)S(1)}, bf16[3,64,256]{2,1,0:T(8,128)(2,1)S(1)}, u32[]{:S(2)}, u32[]{:S(2)}) collective-permute-start(bf16[3,64,256]{2,1,0:T(8,128)(2,1)S(1)} %get-tuple-element.37), channel_id=1, source_target_pairs={{0,4},{4,0},{8,12},{12,8},{16,20},{20,16},{24,28},{28,24},{1,5},{5... | collective-permute-start | bytes 294920 | tf_op jit(solution)/shard_map/ppermute | solution.py:266
  50.2 3.6 %collective-permute-done.9.refs_2_ = bf16[3,64,256]{2,1,0:T(8,128)(2,1)S(1)} collective-permute-done((bf16[3,64,256]{2,1,0:T(8,128)(2,1)S(1)}, bf16[3,64,256]{2,1,0:T(8,128)(2,1)S(1)}, u32[]{:S(2)}, u32[]{:S(2)}) %collective-permute-start.9) | collective-permute-done | bytes 98336 | tf_op jit(solution)/shard_map/ppermute | solution.py:266
  53.8 0.1 collective-permute-done.10.refs_3_
  54.0 0.0 collective-permute-done.11.refs_4_
  54.0 0.7 %collective-permute-done.12.refs_5_ = bf16[3,64,256]{2,1,0:T(8,128)(2,1)S(1)} collective-permute-done((bf16[3,64,256]{2,1,0:T(8,128)(2,1)S(1)}, bf16[3,64,256]{2,1,0:T(8,128)(2,1)S(1)}, u32[]{:S(2)}, u32[]{:S(2)}) %collective-permute-start.12) | collective-permute-done | bytes 98336 | tf_op jit(solution)/shard_map/ppermute | solution.py:266
  54.7 0.0 collective-permute-done.13.refs_6_
  54.7 0.0 copy-done.8
  54.7 0.0 copy-done.7
  54.7 0.0 copy-done.6
  54.7 0.0 copy-start
  54.7 1.6 %copy-done = bf16[2048,512]{1,0:T(8,128)(2,1)S(1)} copy-done((bf16[2048,512]{1,0:T(8,128)(2,1)S(1)}, bf16[2048,512]{1,0:T(8,128)(2,1)}, u32[]{:S(2)}) %copy-start) | copy-done | bytes 2097176
  56.3 0.0 copy-start.2
  56.3 1.6 %copy-done.2 = bf16[2048,512]{1,0:T(8,128)(2,1)S(1)} copy-done((bf16[2048,512]{1,0:T(8,128)(2,1)S(1)}, bf16[2048,512]{1,0:T(8,128)(2,1)}, u32[]{:S(2)}) %copy-start.2) | copy-done | bytes 2097176
  57.9 0.0 copy-start.4
  57.9 1.6 %copy-done.4 = bf16[2048,512]{1,0:T(8,128)(2,1)S(1)} copy-done((bf16[2048,512]{1,0:T(8,128)(2,1)S(1)}, bf16[2048,512]{1,0:T(8,128)(2,1)}, u32[]{:S(2)}) %copy-start.4) | copy-done | bytes 2097176
  59.5 0.0 copy-start.1
  59.5 0.0 copy-start.3
  59.5 0.0 copy-start.5
  59.5 1.7 %mate.1 = (bf16[3,256,512]{2,1,0:T(8,128)(2,1)S(1)}, bf16[2,256,512]{2,1,0:T(8,128)(2,1)S(1)}, bf16[256,512]{1,0:T(8,128)(2,1)}) custom-call(bf16[3,64,256]{2,1,0:T(8,128)(2,1)S(1)} %collective-permute-done.7.refs_0_, bf16[3,64,256]{2,1,0:T(8,128)(2,1)S(1)} %collective-permute-done.8.refs_1_, bf16[3,64,256]{2,1,0:T(8,128)(2,1)S(1)} %collective-permute-done.9.refs_2_, ...), custom_call_target="tpu_custom_call" | custom-call | flops 805306368 | bytes 4194304 | tf_op jit(solution)/shard_map/mate/pallas_call | solution.py:323
  61.2 0.0 collective-permute-start.14
  61.2 0.0 copy-done.1
  61.2 0.6 copy-done.3
  61.8 0.6 copy-done.5
  62.4 1.0 %own.1 = (f32[256,512]{1,0:T(8,128)S(1)}, f32[256,512]{1,0:T(8,128)S(1)}) custom-call(bf16[3,256,512]{2,1,0:T(8,128)(2,1)S(1)} %get-tuple-element.39.lhs_ref, bf16[2048,512]{1,0:T(8,128)(2,1)S(1)} %copy-done.1, bf16[2048,512]{1,0:T(8,128)(2,1)S(1)} %copy-done.3, bf16[2048,512]{1,0:T(8,128)(2,1)S(1)} %copy-done.5), custom_call_target="tpu_custom_call" | custom-call | flops 805306368 | bytes 4194304 | tf_op jit(solution)/shard_map/own/pallas_call | solution.py:337
  63.5 0.0 collective-permute-done.14
  63.5 0.1 fusion
  63.5 1.6 %collective-permute-start.15 = (bf16[256,512]{1,0:T(8,128)(2,1)S(1)}, bf16[256,512]{1,0:T(8,128)(2,1)S(1)}, u32[]{:S(2)}, u32[]{:S(2)}) collective-permute-start(bf16[256,512]{1,0:T(8,128)(2,1)S(1)} %fusion), channel_id=1, source_target_pairs={{0,2},{1,3},{2,0},{3,1},{4,6},{5,7},{6,4},{7,5},{8,10},{9,11},{10,... | collective-permute-start | bytes 786440 | tf_op jit(solution)/shard_map/ppermute | solution.py:266
  65.1 6.5 %collective-permute-done.15 = bf16[256,512]{1,0:T(8,128)(2,1)S(1)} collective-permute-done((bf16[256,512]{1,0:T(8,128)(2,1)S(1)}, bf16[256,512]{1,0:T(8,128)(2,1)S(1)}, u32[]{:S(2)}, u32[]{:S(2)}) %collective-permute-start.15) | collective-permute-done | bytes 262176 | tf_op jit(solution)/shard_map/ppermute | solution.py:266
  71.6 0.8 %fusion.2 = bf16[256,512]{1,0:T(8,128)(2,1)} fusion(f32[256,512]{1,0:T(8,128)S(1)} %get-tuple-element.40, bf16[256,512]{1,0:T(8,128)(2,1)S(1)} %collective-permute-done.15, bf16[2,256,512]{2,1,0:T(8,128)(2,1)S(1)} %collective-permute-done.14), kind=kLoop, calls=%fused_computation.4 | loop fusion | flops 655360 | bytes 1310720 | tf_op jit(solution)/shard_map/convert_element_type | solution.py:348
Async XLA Ops:
  0.6 54.1 %copy-start.8 = (bf16[256,512]{1,0:T(8,128)(2,1)S(1)}, bf16[256,512]{1,0:T(8,128)(2,1)}, u32[]{:S(2)}) copy-start(bf16[256,512]{1,0:T(8,128)(2,1)} %refs_10_.2) | copy-start | bytes 786436
  0.6 54.1 %copy-start.7 = (bf16[256,512]{1,0:T(8,128)(2,1)S(1)}, bf16[256,512]{1,0:T(8,128)(2,1)}, u32[]{:S(2)}) copy-start(bf16[256,512]{1,0:T(8,128)(2,1)} %refs_9_.2) | copy-start | bytes 786436
  0.7 54.0 %copy-start.6 = (bf16[256,512]{1,0:T(8,128)(2,1)S(1)}, bf16[256,512]{1,0:T(8,128)(2,1)}, u32[]{:S(2)}) copy-start(bf16[256,512]{1,0:T(8,128)(2,1)} %refs_8_.2) | copy-start | bytes 786436
  3.1 11.4 %collective-permute-start = (bf16[3,64,256]{2,1,0:T(8,128)(2,1)}, bf16[3,64,256]{2,1,0:T(8,128)(2,1)S(1)}, u32[]{:S(2)}, u32[]{:S(2)}) collective-permute-start(bf16[3,64,256]{2,1,0:T(8,128)(2,1)} %get-tuple-element.23), channel_id=1, source_target_pairs={{0,28},{4,24},{8,20},{12,16},{16,12},{20,8},{24,4},{28,0},{1,29},{... | collective-permute-start | bytes 294920 | tf_op jit(solution)/shard_map/ppermute | solution.py:266
  9.1 12.1 %collective-permute-start.1 = (bf16[3,64,256]{2,1,0:T(8,128)(2,1)}, bf16[3,64,256]{2,1,0:T(8,128)(2,1)S(1)}, u32[]{:S(2)}, u32[]{:S(2)}) collective-permute-start(bf16[3,64,256]{2,1,0:T(8,128)(2,1)} %get-tuple-element.24), channel_id=1, source_target_pairs={{0,24},{4,28},{8,16},{12,20},{16,8},{20,12},{24,0},{28,4},{1,25},{... | collective-permute-start | bytes 294920 | tf_op jit(solution)/shard_map/ppermute | solution.py:266
  9.4 15.6 %collective-permute-start.2 = (bf16[3,64,256]{2,1,0:T(8,128)(2,1)}, bf16[3,64,256]{2,1,0:T(8,128)(2,1)S(1)}, u32[]{:S(2)}, u32[]{:S(2)}) collective-permute-start(bf16[3,64,256]{2,1,0:T(8,128)(2,1)} %get-tuple-element.25), channel_id=1, source_target_pairs={{0,20},{4,16},{8,28},{12,24},{16,4},{20,0},{24,12},{28,8},{1,21},{... | collective-permute-start | bytes 294920 | tf_op jit(solution)/shard_map/ppermute | solution.py:266
  10.1 16.0 %collective-permute-start.3 = (bf16[3,64,256]{2,1,0:T(8,128)(2,1)}, bf16[3,64,256]{2,1,0:T(8,128)(2,1)S(1)}, u32[]{:S(2)}, u32[]{:S(2)}) collective-permute-start(bf16[3,64,256]{2,1,0:T(8,128)(2,1)} %get-tuple-element.26), channel_id=1, source_target_pairs={{0,16},{4,20},{8,24},{12,28},{16,0},{20,4},{24,8},{28,12},{1,17},{... | collective-permute-start | bytes 294920 | tf_op jit(solution)/shard_map/ppermute | solution.py:266
  12.1 14.0 %collective-permute-start.4 = (bf16[3,64,256]{2,1,0:T(8,128)(2,1)}, bf16[3,64,256]{2,1,0:T(8,128)(2,1)S(1)}, u32[]{:S(2)}, u32[]{:S(2)}) collective-permute-start(bf16[3,64,256]{2,1,0:T(8,128)(2,1)} %get-tuple-element.27), channel_id=1, source_target_pairs={{0,12},{4,8},{8,4},{12,0},{16,28},{20,24},{24,20},{28,16},{1,13},{... | collective-permute-start | bytes 294920 | tf_op jit(solution)/shard_map/ppermute | solution.py:266
  14.4 12.7 %collective-permute-start.5 = (bf16[3,64,256]{2,1,0:T(8,128)(2,1)}, bf16[3,64,256]{2,1,0:T(8,128)(2,1)S(1)}, u32[]{:S(2)}, u32[]{:S(2)}) collective-permute-start(bf16[3,64,256]{2,1,0:T(8,128)(2,1)} %get-tuple-element.28), channel_id=1, source_target_pairs={{0,8},{4,12},{8,0},{12,4},{16,24},{20,28},{24,16},{28,20},{1,9},{5... | collective-permute-start | bytes 294920 | tf_op jit(solution)/shard_map/ppermute | solution.py:266
  21.2 5.9 %collective-permute-start.6 = (bf16[3,64,256]{2,1,0:T(8,128)(2,1)}, bf16[3,64,256]{2,1,0:T(8,128)(2,1)S(1)}, u32[]{:S(2)}, u32[]{:S(2)}) collective-permute-start(bf16[3,64,256]{2,1,0:T(8,128)(2,1)} %get-tuple-element.29), channel_id=1, source_target_pairs={{0,4},{4,0},{8,12},{12,8},{16,20},{20,16},{24,28},{28,24},{1,5},{5... | collective-permute-start | bytes 294920 | tf_op jit(solution)/shard_map/ppermute | solution.py:266
  27.1 1.0 %copy-start.9 = (bf16[512,512]{1,0:T(8,128)(2,1)S(1)}, bf16[512,512]{1,0:T(8,128)(2,1)}, u32[]{:S(2)}) copy-start(bf16[512,512]{1,0:T(8,128)(2,1)} %constant.7.clone.refs_10_) | copy-start | bytes 1572868
  28.1 1.0 %copy-start.10 = (bf16[512,512]{1,0:T(8,128)(2,1)S(1)}, bf16[512,512]{1,0:T(8,128)(2,1)}, u32[]{:S(2)}) copy-start(bf16[512,512]{1,0:T(8,128)(2,1)} %constant.6.clone.refs_9_) | copy-start | bytes 1572868
  29.2 0.9 %copy-start.11 = (bf16[3,64,256]{2,1,0:T(8,128)(2,1)S(1)}, bf16[3,64,256]{2,1,0:T(8,128)(2,1)}, u32[]{:S(2)}) copy-start(bf16[3,64,256]{2,1,0:T(8,128)(2,1)} %get-tuple-element.30.refs_7_) | copy-start | bytes 294916
  30.1 0.8 %copy-start.12 = (f32[4,9,256]{2,1,0:T(8,128)S(1)}, f32[4,9,256]{2,1,0:T(8,128)}, u32[]{:S(2)}) copy-start(f32[4,9,256]{2,1,0:T(8,128)} %constant.8.clone.refs_8_) | copy-start | bytes 110596
  36.1 8.5 %collective-permute-start.7 = (bf16[3,64,256]{2,1,0:T(8,128)(2,1)S(1)}, bf16[3,64,256]{2,1,0:T(8,128)(2,1)S(1)}, u32[]{:S(2)}, u32[]{:S(2)}) collective-permute-start(bf16[3,64,256]{2,1,0:T(8,128)(2,1)S(1)} %get-tuple-element.31), channel_id=1, source_target_pairs={{0,28},{4,24},{8,20},{12,16},{16,12},{20,8},{24,4},{28,0},{1,29},{... | collective-permute-start | bytes 294920 | tf_op jit(solution)/shard_map/ppermute | solution.py:266
  38.7 10.5 %collective-permute-start.8 = (bf16[3,64,256]{2,1,0:T(8,128)(2,1)S(1)}, bf16[3,64,256]{2,1,0:T(8,128)(2,1)S(1)}, u32[]{:S(2)}, u32[]{:S(2)}) collective-permute-start(bf16[3,64,256]{2,1,0:T(8,128)(2,1)S(1)} %get-tuple-element.32), channel_id=1, source_target_pairs={{0,24},{4,28},{8,16},{12,20},{16,8},{20,12},{24,0},{28,4},{1,25},{... | collective-permute-start | bytes 294920 | tf_op jit(solution)/shard_map/ppermute | solution.py:266
  39.9 14.0 %collective-permute-start.9 = (bf16[3,64,256]{2,1,0:T(8,128)(2,1)S(1)}, bf16[3,64,256]{2,1,0:T(8,128)(2,1)S(1)}, u32[]{:S(2)}, u32[]{:S(2)}) collective-permute-start(bf16[3,64,256]{2,1,0:T(8,128)(2,1)S(1)} %get-tuple-element.33), channel_id=1, source_target_pairs={{0,20},{4,16},{8,28},{12,24},{16,4},{20,0},{24,12},{28,8},{1,21},{... | collective-permute-start | bytes 294920 | tf_op jit(solution)/shard_map/ppermute | solution.py:266
  41.3 12.6 %collective-permute-start.10 = (bf16[3,64,256]{2,1,0:T(8,128)(2,1)S(1)}, bf16[3,64,256]{2,1,0:T(8,128)(2,1)S(1)}, u32[]{:S(2)}, u32[]{:S(2)}) collective-permute-start(bf16[3,64,256]{2,1,0:T(8,128)(2,1)S(1)} %get-tuple-element.34), channel_id=1, source_target_pairs={{0,16},{4,20},{8,24},{12,28},{16,0},{20,4},{24,8},{28,12},{1,17},{... | collective-permute-start | bytes 294920 | tf_op jit(solution)/shard_map/ppermute | solution.py:266
  43.8 10.2 %collective-permute-start.11 = (bf16[3,64,256]{2,1,0:T(8,128)(2,1)S(1)}, bf16[3,64,256]{2,1,0:T(8,128)(2,1)S(1)}, u32[]{:S(2)}, u32[]{:S(2)}) collective-permute-start(bf16[3,64,256]{2,1,0:T(8,128)(2,1)S(1)} %get-tuple-element.35), channel_id=1, source_target_pairs={{0,12},{4,8},{8,4},{12,0},{16,28},{20,24},{24,20},{28,16},{1,13},{... | collective-permute-start | bytes 294920 | tf_op jit(solution)/shard_map/ppermute | solution.py:266
  44.6 10.1 %collective-permute-start.12 = (bf16[3,64,256]{2,1,0:T(8,128)(2,1)S(1)}, bf16[3,64,256]{2,1,0:T(8,128)(2,1)S(1)}, u32[]{:S(2)}, u32[]{:S(2)}) collective-permute-start(bf16[3,64,256]{2,1,0:T(8,128)(2,1)S(1)} %get-tuple-element.36), channel_id=1, source_target_pairs={{0,8},{4,12},{8,0},{12,4},{16,24},{20,28},{24,16},{28,20},{1,9},{5... | collective-permute-start | bytes 294920 | tf_op jit(solution)/shard_map/ppermute | solution.py:266
  49.2 5.5 %collective-permute-start.13 = (bf16[3,64,256]{2,1,0:T(8,128)(2,1)S(1)}, bf16[3,64,256]{2,1,0:T(8,128)(2,1)S(1)}, u32[]{:S(2)}, u32[]{:S(2)}) collective-permute-start(bf16[3,64,256]{2,1,0:T(8,128)(2,1)S(1)} %get-tuple-element.37), channel_id=1, source_target_pairs={{0,4},{4,0},{8,12},{12,8},{16,20},{20,16},{24,28},{28,24},{1,5},{5... | collective-permute-start | bytes 294920 | tf_op jit(solution)/shard_map/ppermute | solution.py:266
  54.7 1.6 %copy-start = (bf16[2048,512]{1,0:T(8,128)(2,1)S(1)}, bf16[2048,512]{1,0:T(8,128)(2,1)}, u32[]{:S(2)}) copy-start(bf16[2048,512]{1,0:T(8,128)(2,1)} %wk_ref.1) | copy-start | bytes 6291460
  56.3 1.6 %copy-start.2 = (bf16[2048,512]{1,0:T(8,128)(2,1)S(1)}, bf16[2048,512]{1,0:T(8,128)(2,1)}, u32[]{:S(2)}) copy-start(bf16[2048,512]{1,0:T(8,128)(2,1)} %wq_ref.1) | copy-start | bytes 6291460
  57.9 1.6 %copy-start.4 = (bf16[2048,512]{1,0:T(8,128)(2,1)S(1)}, bf16[2048,512]{1,0:T(8,128)(2,1)}, u32[]{:S(2)}) copy-start(bf16[2048,512]{1,0:T(8,128)(2,1)} %wv_ref.1) | copy-start | bytes 6291460
  59.5 1.7 %copy-start.1 = (bf16[2048,512]{1,0:T(8,128)(2,1)S(1)}, bf16[2048,512]{1,0:T(8,128)(2,1)}, u32[]{:S(2)}) copy-start(bf16[2048,512]{1,0:T(8,128)(2,1)} %wk_ref.1) | copy-start | bytes 6291460
  59.5 2.3 %copy-start.3 = (bf16[2048,512]{1,0:T(8,128)(2,1)S(1)}, bf16[2048,512]{1,0:T(8,128)(2,1)}, u32[]{:S(2)}) copy-start(bf16[2048,512]{1,0:T(8,128)(2,1)} %wq_ref.1) | copy-start | bytes 6291460
  59.5 2.9 %copy-start.5 = (bf16[2048,512]{1,0:T(8,128)(2,1)S(1)}, bf16[2048,512]{1,0:T(8,128)(2,1)}, u32[]{:S(2)}) copy-start(bf16[2048,512]{1,0:T(8,128)(2,1)} %wv_ref.1) | copy-start | bytes 6291460
  61.2 2.2 %collective-permute-start.14 = (bf16[2,256,512]{2,1,0:T(8,128)(2,1)S(1)}, bf16[2,256,512]{2,1,0:T(8,128)(2,1)S(1)}, u32[]{:S(2)}, u32[]{:S(2)}) collective-permute-start(bf16[2,256,512]{2,1,0:T(8,128)(2,1)S(1)} %get-tuple-element.41), channel_id=1, source_target_pairs={{0,1},{1,0},{2,3},{3,2},{4,5},{5,4},{6,7},{7,6},{8,9},{9,8},{10,11... | collective-permute-start | bytes 1572872 | tf_op jit(solution)/shard_map/ppermute | solution.py:266
  63.5 8.1 %collective-permute-start.15 = (bf16[256,512]{1,0:T(8,128)(2,1)S(1)}, bf16[256,512]{1,0:T(8,128)(2,1)S(1)}, u32[]{:S(2)}, u32[]{:S(2)}) collective-permute-start(bf16[256,512]{1,0:T(8,128)(2,1)S(1)} %fusion), channel_id=1, source_target_pairs={{0,2},{1,3},{2,0},{3,1},{4,6},{5,7},{6,4},{7,5},{8,10},{9,11},{10,... | collective-permute-start | bytes 786440 | tf_op jit(solution)/shard_map/ppermute | solution.py:266

commit v4 on v3

--- a/solution.py
+++ b/solution.py
@@ -89,6 +89,10 @@
 VMEM = pl.BlockSpec(memory_space=pltpu.VMEM)
 
 
+def in_hbm(*arrays):
+    return [pltpu.with_memory_space_constraint(array, pltpu.HBM) for array in arrays]
+
+
 def far_first(pieces):
     return zip(reversed(range(len(pieces))), pieces)
 
@@ -128,12 +132,14 @@
 
 def conv_kernel(*refs):
     blocks = lax.axis_size("ctx")
-    in_refs, (twid_ref, fwd_ref, inv_ref) = refs[:blocks], refs[blocks : blocks + 3]
-    out_refs, (in_ref, rows_ref, spec_ref) = refs[blocks + 3 : -3], refs[-3:]
+    in_refs, tables, out_refs = refs[:blocks], refs[blocks : blocks + 3], refs[blocks + 3 : -7]
+    in_ref, rows_ref, spec_ref, twid_ref, fwd_ref, inv_ref, sems = refs[-7:]
+    twid_copy, fwd_copy, inv_copy = fetch(tables, (twid_ref, fwd_ref, inv_ref), sems)
     _, signals, channels, block_len = in_ref.shape
     me = lax.axis_index("ctx")
     for distance, ref in far_first(in_refs):
         in_ref[me ^ distance] = ref[...]
+    twid_copy.wait()
     chunk = min(channels, 16)
     steps = channels // chunk
 
@@ -159,6 +165,8 @@
         return carry
 
     lax.fori_loop(0, signals * steps, analyse, 0)
+    fwd_copy.wait()
+    inv_copy.wait()
 
     total = (blocks + 1) * signals * channels
     spec_ref[...] = jnp.dot(
@@ -240,6 +248,12 @@
     ]
 
 
+def hold_kernel(*refs):
+    count = len(refs) // 2
+    for copy in fetch(refs[:count], refs[count : 2 * count], refs[-1]):
+        copy.wait()
+
+
 def mate_kernel(*refs):
     blocks = lax.axis_size("ctx")
     back_refs, (key_ref, value_ref, grad_ref) = refs[:blocks], refs[blocks : blocks + 3]
@@ -285,21 +299,20 @@
     )
 
     def arrays(count, *shape, dtype=jnp.bfloat16):
-        return [jax.ShapeDtypeStruct(shape, dtype)] * count
+        return [pltpu.VMEM(shape, dtype)] * count
 
     sent = pl.pallas_call(
         gate_kernel,
         in_specs=[HBM] * 5,
-        out_specs=[VMEM] * blocks,
         out_shape=arrays(blocks, 3, channels, block_len),
         scratch_shapes=[
             pltpu.VMEM((blocks, 3, channels, block_len), jnp.bfloat16),
             pltpu.VMEM((5, block_len, width), jnp.bfloat16),
             pltpu.SemaphoreType.DMA((5,)),
         ],
-        compiler_params=compiler_params(62),
+        compiler_params=compiler_params(12),
         name="gate",
-    )(long_filter, key_act, value_act, query_act, grad_out)
+    )(*in_hbm(long_filter, key_act, value_act, query_act, grad_out))
     moved = swap(sent)
 
     forward, inverse, twiddle = dft_tables(
@@ -307,32 +320,47 @@
     )
     results = pl.pallas_call(
         conv_kernel,
-        in_specs=[VMEM] * (blocks + 3),
+        in_specs=[VMEM] * blocks + [HBM] * 3,
         out_shape=arrays(blocks, 3, channels, block_len),
         scratch_shapes=[
             pltpu.VMEM((blocks, 3, channels, block_len), jnp.bfloat16),
             pltpu.VMEM((blocks + 1, 3, channels, 2 * block_len), jnp.bfloat16),
             pltpu.VMEM((blocks + 1, 3, channels, 2 * block_len), jnp.float32),
+            pltpu.VMEM(twiddle.shape, jnp.float32),
+            pltpu.VMEM(forward.shape, jnp.bfloat16),
+            pltpu.VMEM(inverse.shape, jnp.bfloat16),
+            pltpu.SemaphoreType.DMA((3,)),
         ],
         compiler_params=compiler_params(20),
         name="conv",
-    )(*moved, twiddle, forward, inverse)
+    )(*moved, *in_hbm(twiddle, forward, inverse))
     back = swap(results)
 
-    weights = (w_key, w_query, w_value)
+    held = (key_act, value_act, grad_out, w_key, w_query, w_value)
+    held, _ = lax.optimization_barrier((held, results[0]))
+    held = pl.pallas_call(
+        hold_kernel,
+        in_specs=[HBM] * len(held),
+        out_shape=[pltpu.VMEM(array.shape, array.dtype) for array in held],
+        scratch_shapes=[pltpu.SemaphoreType.DMA((len(held),))],
+        compiler_params=compiler_params(12),
+        cost_estimate=pl.CostEstimate(flops=0, bytes_accessed=1 << 23, transcendentals=0),
+        name="hold",
+    )(*in_hbm(*held))
+    weights = held[3:]
     lhs, to_mate, grad_filter = pl.pallas_call(
         mate_kernel,
         in_specs=[VMEM] * (blocks + 6),
         out_shape=[
             *arrays(1, 3, block_len, width),
             *arrays(1, 2, block_len, part),
-            *arrays(1, block_len, width),
+            jax.ShapeDtypeStruct((block_len, width), jnp.bfloat16),
         ],
         scratch_shapes=[pltpu.VMEM((blocks, 3, channels, block_len), jnp.bfloat16)],
         compiler_params=compiler_params(16),
         cost_estimate=block_cost,
         name="mate",
-    )(*back, key_act, value_act, grad_out, *weights)
+    )(*back, *held)
     from_mate = exchange(to_mate, "tp", 1)
     far, own = pl.pallas_call(
         own_kernel,

time: 72.8 us -> 65.4 us (0.90)
  local copies, waits for them, and re-layouts: 9.81 us -> 0 us
  Pallas kernels: 10.3 us -> 13.4 us
  starting transfers between devices: 34.2 us -> 32.8 us
  waiting for transfers between devices: 16.5 us -> 17.5 us
    unnamed x26 -> x0, local copies, waits for them, and re-layouts: 9.81 us -> none
    pallas_call x2 -> x3, Pallas kernels: 7.53 us -> 10.6 us  [the longest x1 5.97 us: per_device(): pl.pallas_call(conv_kernel, in_specs=[VMEM] * blocks + [HBM] * 3, out_sha...]
    ppermute x16, starting transfers between devices: 34.2 us -> 32.8 us  [exchange(): return lax.ppermute(block, axis, pairs)]
    ppermute x16, waiting for transfers between devices: 16.5 us -> 17.5 us  [exchange(): return lax.ppermute(block, axis, pairs)]
  transfers between devices with their start and end apart: 16 -> 16, of which waited for: 8 -> 7; matrix products, arithmetic and copies ran while one was open for 0% -> 0% of each run, Pallas kernels for 1% -> 6%
where the time goes in v4:
time: 65.4 us; the launch traced here: 65.2 us
  starting transfers between devices  32.8 us (50%)
  waiting for transfers between devices  17.5 us (27%)
  Pallas kernels  13.4 us (20%)
  other arithmetic  0.88 us (1%)
  between operations  0.71 us (1%)
    ppermute x16, starting transfers between devices, exchange(): return lax.ppermute(block, axis, pairs)  32.8 us
    ppermute x16, waiting for transfers between devices, exchange(): return lax.ppermute(block, axis, pairs)  17.5 us
    pallas_call x1, Pallas kernels, per_device(): pl.pallas_call(conv_kernel, in_specs=[VMEM] * blocks + [HBM] * 3, out_sha...  5.97 us
    pallas_call x1, Pallas kernels, per_device(): pl.pallas_call(hold_kernel, in_specs=[HBM] * len(held), out_shape=[pltpu....  3.17 us
    pallas_call x1, Pallas kernels, per_device(): pl.pallas_call(mate_kernel, in_specs=[VMEM] * (blocks + 6), out_shape=[*a...  1.74 us
    pallas_call x1, Pallas kernels, per_device(): pl.pallas_call(gate_kernel, in_specs=[HBM] * 5, out_shape=arrays(blocks,...  1.5 us
  transfers between devices with their start and end apart: 16, of which 7 were waited for; matrix products, arithmetic and copies ran while one was open for 0% of the time, Pallas kernels for 6%

profile of v4, /device:TPU:0, one launch (start us, length us, event | category | flops | bytes accessed | tf_op | source)
XLA Modules:
  0.0 65.2 jit_solution(2377739525572243166)
XLA Ops:
  0.6 1.5 %gate.1 = (bf16[3,64,256]{2,1,0:T(8,128)(2,1)S(1)}, bf16[3,64,256]{2,1,0:T(8,128)(2,1)S(1)}, bf16[3,64,256]{2,1,0:T(8,128)(2,1)S(1)}, bf16[3,64,256]{2,1,0:T(8,1...) custom-call(bf16[256,512]{1,0:T(8,128)(2,1)} %refs_0_.1, ...), custom_call_target="tpu_custom_call" | custom-call | tf_op jit(solution)/shard_map/gate/pallas_call | solution.py:304
  2.1 6.1 %collective-permute-start = (bf16[3,64,256]{2,1,0:T(8,128)(2,1)S(1)}, bf16[3,64,256]{2,1,0:T(8,128)(2,1)S(1)}, u32[]{:S(2)}, u32[]{:S(2)}) collective-permute-start(bf16[3,64,256]{2,1,0:T(8,128)(2,1)S(1)} %get-tuple-element.35), channel_id=1, source_target_pairs={{0,28},{4,24},{8,20},{12,16},{16,12},{20,8},{24,4},{28,0},{1,29},{... | collective-permute-start | bytes 294920 | tf_op jit(solution)/shard_map/ppermute | solution.py:280
  8.2 0.2 collective-permute-start.1
  8.4 0.7 %collective-permute-start.2 = (bf16[3,64,256]{2,1,0:T(8,128)(2,1)S(1)}, bf16[3,64,256]{2,1,0:T(8,128)(2,1)S(1)}, u32[]{:S(2)}, u32[]{:S(2)}) collective-permute-start(bf16[3,64,256]{2,1,0:T(8,128)(2,1)S(1)} %get-tuple-element.37), channel_id=1, source_target_pairs={{0,20},{4,16},{8,28},{12,24},{16,4},{20,0},{24,12},{28,8},{1,21},{... | collective-permute-start | bytes 294920 | tf_op jit(solution)/shard_map/ppermute | solution.py:280
  9.2 2.0 %collective-permute-start.3 = (bf16[3,64,256]{2,1,0:T(8,128)(2,1)S(1)}, bf16[3,64,256]{2,1,0:T(8,128)(2,1)S(1)}, u32[]{:S(2)}, u32[]{:S(2)}) collective-permute-start(bf16[3,64,256]{2,1,0:T(8,128)(2,1)S(1)} %get-tuple-element.38), channel_id=1, source_target_pairs={{0,16},{4,20},{8,24},{12,28},{16,0},{20,4},{24,8},{28,12},{1,17},{... | collective-permute-start | bytes 294920 | tf_op jit(solution)/shard_map/ppermute | solution.py:280
  11.2 2.3 %collective-permute-start.4 = (bf16[3,64,256]{2,1,0:T(8,128)(2,1)S(1)}, bf16[3,64,256]{2,1,0:T(8,128)(2,1)S(1)}, u32[]{:S(2)}, u32[]{:S(2)}) collective-permute-start(bf16[3,64,256]{2,1,0:T(8,128)(2,1)S(1)} %get-tuple-element.39), channel_id=1, source_target_pairs={{0,12},{4,8},{8,4},{12,0},{16,28},{20,24},{24,20},{28,16},{1,13},{... | collective-permute-start | bytes 294920 | tf_op jit(solution)/shard_map/ppermute | solution.py:280
  13.5 0.0 collective-permute-done.refs_0_
  13.5 6.6 %collective-permute-start.5 = (bf16[3,64,256]{2,1,0:T(8,128)(2,1)S(1)}, bf16[3,64,256]{2,1,0:T(8,128)(2,1)S(1)}, u32[]{:S(2)}, u32[]{:S(2)}) collective-permute-start(bf16[3,64,256]{2,1,0:T(8,128)(2,1)S(1)} %get-tuple-element.40), channel_id=1, source_target_pairs={{0,8},{4,12},{8,0},{12,4},{16,24},{20,28},{24,16},{28,20},{1,9},{5... | collective-permute-start | bytes 294920 | tf_op jit(solution)/shard_map/ppermute | solution.py:280
  20.1 0.0 collective-permute-done.1.refs_1_
  20.1 1.0 %collective-permute-start.6 = (bf16[3,64,256]{2,1,0:T(8,128)(2,1)S(1)}, bf16[3,64,256]{2,1,0:T(8,128)(2,1)S(1)}, u32[]{:S(2)}, u32[]{:S(2)}) collective-permute-start(bf16[3,64,256]{2,1,0:T(8,128)(2,1)S(1)} %get-tuple-element.41), channel_id=1, source_target_pairs={{0,4},{4,0},{8,12},{12,8},{16,20},{20,16},{24,28},{28,24},{1,5},{5... | collective-permute-start | bytes 294920 | tf_op jit(solution)/shard_map/ppermute | solution.py:280
  21.0 2.8 %collective-permute-done.2.refs_2_ = bf16[3,64,256]{2,1,0:T(8,128)(2,1)S(1)} collective-permute-done((bf16[3,64,256]{2,1,0:T(8,128)(2,1)S(1)}, bf16[3,64,256]{2,1,0:T(8,128)(2,1)S(1)}, u32[]{:S(2)}, u32[]{:S(2)}) %collective-permute-start.2) | collective-permute-done | bytes 98336 | tf_op jit(solution)/shard_map/ppermute | solution.py:280
  23.9 1.1 %collective-permute-done.3.refs_3_ = bf16[3,64,256]{2,1,0:T(8,128)(2,1)S(1)} collective-permute-done((bf16[3,64,256]{2,1,0:T(8,128)(2,1)S(1)}, bf16[3,64,256]{2,1,0:T(8,128)(2,1)S(1)}, u32[]{:S(2)}, u32[]{:S(2)}) %collective-permute-start.3) | collective-permute-done | bytes 98336 | tf_op jit(solution)/shard_map/ppermute | solution.py:280
  25.0 0.0 collective-permute-done.4.refs_4_
  25.0 0.9 %collective-permute-done.5.refs_5_ = bf16[3,64,256]{2,1,0:T(8,128)(2,1)S(1)} collective-permute-done((bf16[3,64,256]{2,1,0:T(8,128)(2,1)S(1)}, bf16[3,64,256]{2,1,0:T(8,128)(2,1)S(1)}, u32[]{:S(2)}, u32[]{:S(2)}) %collective-permute-start.5) | collective-permute-done | bytes 98336 | tf_op jit(solution)/shard_map/ppermute | solution.py:280
  26.0 0.0 collective-permute-done.6.refs_6_
  26.0 6.0 %conv.1 = (bf16[3,64,256]{2,1,0:T(8,128)(2,1)S(1)}, bf16[3,64,256]{2,1,0:T(8,128)(2,1)S(1)}, bf16[3,64,256]{2,1,0:T(8,128)(2,1)S(1)}, bf16[3,64,256]{2,1,0:T(8,1...) custom-call(bf16[3,64,256]{2,1,0:T(8,128)(2,1)S(1)} %collective-perm, ...), custom_call_target="tpu_custom_call" | custom-call | tf_op jit(solution)/shard_map/conv/pallas_call | solution.py:321
  31.9 2.5 %collective-permute-start.8 = (bf16[3,64,256]{2,1,0:T(8,128)(2,1)S(1)}, bf16[3,64,256]{2,1,0:T(8,128)(2,1)S(1)}, u32[]{:S(2)}, u32[]{:S(2)}) collective-permute-start(bf16[3,64,256]{2,1,0:T(8,128)(2,1)S(1)} %get-tuple-element.44), channel_id=1, source_target_pairs={{0,24},{4,28},{8,16},{12,20},{16,8},{20,12},{24,0},{28,4},{1,25},{... | collective-permute-start | bytes 294920 | tf_op jit(solution)/shard_map/ppermute | solution.py:280
  34.4 0.0 collective-permute-start.9
  34.4 2.9 %collective-permute-start.10 = (bf16[3,64,256]{2,1,0:T(8,128)(2,1)S(1)}, bf16[3,64,256]{2,1,0:T(8,128)(2,1)S(1)}, u32[]{:S(2)}, u32[]{:S(2)}) collective-permute-start(bf16[3,64,256]{2,1,0:T(8,128)(2,1)S(1)} %get-tuple-element.46), channel_id=1, source_target_pairs={{0,16},{4,20},{8,24},{12,28},{16,0},{20,4},{24,8},{28,12},{1,17},{... | collective-permute-start | bytes 294920 | tf_op jit(solution)/shard_map/ppermute | solution.py:280
  37.3 1.1 %collective-permute-start.11 = (bf16[3,64,256]{2,1,0:T(8,128)(2,1)S(1)}, bf16[3,64,256]{2,1,0:T(8,128)(2,1)S(1)}, u32[]{:S(2)}, u32[]{:S(2)}) collective-permute-start(bf16[3,64,256]{2,1,0:T(8,128)(2,1)S(1)} %get-tuple-element.47), channel_id=1, source_target_pairs={{0,12},{4,8},{8,4},{12,0},{16,28},{20,24},{24,20},{28,16},{1,13},{... | collective-permute-start | bytes 294920 | tf_op jit(solution)/shard_map/ppermute | solution.py:280
  38.5 1.8 %collective-permute-start.12 = (bf16[3,64,256]{2,1,0:T(8,128)(2,1)S(1)}, bf16[3,64,256]{2,1,0:T(8,128)(2,1)S(1)}, u32[]{:S(2)}, u32[]{:S(2)}) collective-permute-start(bf16[3,64,256]{2,1,0:T(8,128)(2,1)S(1)} %get-tuple-element.48), channel_id=1, source_target_pairs={{0,8},{4,12},{8,0},{12,4},{16,24},{20,28},{24,16},{28,20},{1,9},{5... | collective-permute-start | bytes 294920 | tf_op jit(solution)/shard_map/ppermute | solution.py:280
  40.3 0.0 collective-permute-done.8.refs_1_
  40.3 0.5 collective-permute-start.13
  40.8 4.1 %collective-permute-done.9.refs_2_ = bf16[3,64,256]{2,1,0:T(8,128)(2,1)S(1)} collective-permute-done((bf16[3,64,256]{2,1,0:T(8,128)(2,1)S(1)}, bf16[3,64,256]{2,1,0:T(8,128)(2,1)S(1)}, u32[]{:S(2)}, u32[]{:S(2)}) %collective-permute-start.9) | collective-permute-done | bytes 98336 | tf_op jit(solution)/shard_map/ppermute | solution.py:280
  45.0 3.4 %collective-permute-start.7 = (bf16[3,64,256]{2,1,0:T(8,128)(2,1)S(1)}, bf16[3,64,256]{2,1,0:T(8,128)(2,1)S(1)}, u32[]{:S(2)}, u32[]{:S(2)}) collective-permute-start(bf16[3,64,256]{2,1,0:T(8,128)(2,1)S(1)} %get-tuple-element.43), channel_id=1, source_target_pairs={{0,28},{4,24},{8,20},{12,16},{16,12},{20,8},{24,4},{28,0},{1,29},{... | collective-permute-start | bytes 294920 | tf_op jit(solution)/shard_map/ppermute | solution.py:280
  48.4 3.2 %hold.1 = (bf16[256,512]{1,0:T(8,128)(2,1)S(1)}, bf16[256,512]{1,0:T(8,128)(2,1)S(1)}, bf16[256,512]{1,0:T(8,128)(2,1)S(1)}, bf16[2048,512]{1,0:T(8,128)(2,1)S(1...) custom-call(bf16[256,512]{1,0:T(8,128)(2,1)} %refs_0_.2, bf16[256,512]{1,0:T(8,128)(2,1)} %refs_1_.2, ...), custom_call_target="tpu_custom_call" | custom-call | bytes 8388608 | tf_op jit(solution)/shard_map/hold/pallas_call | solution.py:341
  51.6 0.0 collective-permute-done.10.refs_3_
  51.6 0.0 collective-permute-done.11.refs_4_
  51.6 0.0 collective-permute-done.12.refs_5_
  51.6 0.0 collective-permute-done.13.refs_6_
  51.6 0.7 %collective-permute-done.7.refs_0_ = bf16[3,64,256]{2,1,0:T(8,128)(2,1)S(1)} collective-permute-done((bf16[3,64,256]{2,1,0:T(8,128)(2,1)S(1)}, bf16[3,64,256]{2,1,0:T(8,128)(2,1)S(1)}, u32[]{:S(2)}, u32[]{:S(2)}) %collective-permute-start.7) | collective-permute-done | bytes 98336 | tf_op jit(solution)/shard_map/ppermute | solution.py:280
  52.3 1.7 %mate.1 = (bf16[3,256,512]{2,1,0:T(8,128)(2,1)S(1)}, bf16[2,256,512]{2,1,0:T(8,128)(2,1)S(1)}, bf16[256,512]{1,0:T(8,128)(2,1)}) custom-call(bf16[3,64,256]{2,1,0:T(8,128)(2,1)S(1)} %collective-permute-done.7.refs_0_, bf16[3,64,256]{2,1,0:T(8,128)(2,1)S(1)} %collective-permute-done.8.refs_1_, bf16[3,64,256]{2,1,0:T(8,128)(2,1)S(1)} %collective-permute-done.9.refs_2_, ...), custom_call_target="tpu_custom_call" | custom-call | flops 805306368 | bytes 4194304 | tf_op jit(solution)/shard_map/mate/pallas_call | solution.py:351
  54.0 0.0 collective-permute-start.14
  54.0 1.0 %own.1 = (f32[256,512]{1,0:T(8,128)S(1)}, f32[256,512]{1,0:T(8,128)S(1)}) custom-call(bf16[3,256,512]{2,1,0:T(8,128)(2,1)S(1)} %get-tuple-element.63.lhs_ref, bf16[2048,512]{1,0:T(8,128)(2,1)S(1)} %get-tuple-element.60.refs_11_.wk_ref, bf16[2048,512]{1,0:T(8,128)(2,1)S(1)} %get-tuple-element.61.refs_12_.wq_ref, ...), custom_call_target="tpu_custom_call" | custom-call | flops 805306368 | bytes 4194304 | tf_op jit(solution)/shard_map/own/pallas_call | solution.py:365
  55.0 0.9 %collective-permute-done.14 = bf16[2,256,512]{2,1,0:T(8,128)(2,1)S(1)} collective-permute-done((bf16[2,256,512]{2,1,0:T(8,128)(2,1)S(1)}, bf16[2,256,512]{2,1,0:T(8,128)(2,1)S(1)}, u32[]{:S(2)}, u32[]{:S(2)}) %collective-permute-start.14) | collective-permute-done | bytes 524320 | tf_op jit(solution)/shard_map/ppermute | solution.py:280
  55.9 0.1 fusion
  56.0 1.6 %collective-permute-start.15 = (bf16[256,512]{1,0:T(8,128)(2,1)S(1)}, bf16[256,512]{1,0:T(8,128)(2,1)S(1)}, u32[]{:S(2)}, u32[]{:S(2)}) collective-permute-start(bf16[256,512]{1,0:T(8,128)(2,1)S(1)} %fusion), channel_id=1, source_target_pairs={{0,2},{1,3},{2,0},{3,1},{4,6},{5,7},{6,4},{7,5},{8,10},{9,11},{10,... | collective-permute-start | bytes 786440 | tf_op jit(solution)/shard_map/ppermute | solution.py:280
  57.6 6.9 %collective-permute-done.15 = bf16[256,512]{1,0:T(8,128)(2,1)S(1)} collective-permute-done((bf16[256,512]{1,0:T(8,128)(2,1)S(1)}, bf16[256,512]{1,0:T(8,128)(2,1)S(1)}, u32[]{:S(2)}, u32[]{:S(2)}) %collective-permute-start.15) | collective-permute-done | bytes 262176 | tf_op jit(solution)/shard_map/ppermute | solution.py:280
  64.4 0.8 %fusion.2 = bf16[256,512]{1,0:T(8,128)(2,1)} fusion(f32[256,512]{1,0:T(8,128)S(1)} %get-tuple-element.64, bf16[256,512]{1,0:T(8,128)(2,1)S(1)} %collective-permute-done.15, bf16[2,256,512]{2,1,0:T(8,128)(2,1)S(1)} %collective-permute-done.14), kind=kLoop, calls=%fused_computation.4 | loop fusion | flops 655360 | bytes 1310720 | tf_op jit(solution)/shard_map/convert_element_type | solution.py:376
Async XLA Ops:
  2.1 11.4 %collective-permute-start = (bf16[3,64,256]{2,1,0:T(8,128)(2,1)S(1)}, bf16[3,64,256]{2,1,0:T(8,128)(2,1)S(1)}, u32[]{:S(2)}, u32[]{:S(2)}) collective-permute-start(bf16[3,64,256]{2,1,0:T(8,128)(2,1)S(1)} %get-tuple-element.35), channel_id=1, source_target_pairs={{0,28},{4,24},{8,20},{12,16},{16,12},{20,8},{24,4},{28,0},{1,29},{... | collective-permute-start | bytes 294920 | tf_op jit(solution)/shard_map/ppermute | solution.py:280
  8.2 11.9 %collective-permute-start.1 = (bf16[3,64,256]{2,1,0:T(8,128)(2,1)S(1)}, bf16[3,64,256]{2,1,0:T(8,128)(2,1)S(1)}, u32[]{:S(2)}, u32[]{:S(2)}) collective-permute-start(bf16[3,64,256]{2,1,0:T(8,128)(2,1)S(1)} %get-tuple-element.36), channel_id=1, source_target_pairs={{0,24},{4,28},{8,16},{12,20},{16,8},{20,12},{24,0},{28,4},{1,25},{... | collective-permute-start | bytes 294920 | tf_op jit(solution)/shard_map/ppermute | solution.py:280
  8.4 15.4 %collective-permute-start.2 = (bf16[3,64,256]{2,1,0:T(8,128)(2,1)S(1)}, bf16[3,64,256]{2,1,0:T(8,128)(2,1)S(1)}, u32[]{:S(2)}, u32[]{:S(2)}) collective-permute-start(bf16[3,64,256]{2,1,0:T(8,128)(2,1)S(1)} %get-tuple-element.37), channel_id=1, source_target_pairs={{0,20},{4,16},{8,28},{12,24},{16,4},{20,0},{24,12},{28,8},{1,21},{... | collective-permute-start | bytes 294920 | tf_op jit(solution)/shard_map/ppermute | solution.py:280
  9.2 15.8 %collective-permute-start.3 = (bf16[3,64,256]{2,1,0:T(8,128)(2,1)S(1)}, bf16[3,64,256]{2,1,0:T(8,128)(2,1)S(1)}, u32[]{:S(2)}, u32[]{:S(2)}) collective-permute-start(bf16[3,64,256]{2,1,0:T(8,128)(2,1)S(1)} %get-tuple-element.38), channel_id=1, source_target_pairs={{0,16},{4,20},{8,24},{12,28},{16,0},{20,4},{24,8},{28,12},{1,17},{... | collective-permute-start | bytes 294920 | tf_op jit(solution)/shard_map/ppermute | solution.py:280
  11.2 13.8 %collective-permute-start.4 = (bf16[3,64,256]{2,1,0:T(8,128)(2,1)S(1)}, bf16[3,64,256]{2,1,0:T(8,128)(2,1)S(1)}, u32[]{:S(2)}, u32[]{:S(2)}) collective-permute-start(bf16[3,64,256]{2,1,0:T(8,128)(2,1)S(1)} %get-tuple-element.39), channel_id=1, source_target_pairs={{0,12},{4,8},{8,4},{12,0},{16,28},{20,24},{24,20},{28,16},{1,13},{... | collective-permute-start | bytes 294920 | tf_op jit(solution)/shard_map/ppermute | solution.py:280
  13.5 12.5 %collective-permute-start.5 = (bf16[3,64,256]{2,1,0:T(8,128)(2,1)S(1)}, bf16[3,64,256]{2,1,0:T(8,128)(2,1)S(1)}, u32[]{:S(2)}, u32[]{:S(2)}) collective-permute-start(bf16[3,64,256]{2,1,0:T(8,128)(2,1)S(1)} %get-tuple-element.40), channel_id=1, source_target_pairs={{0,8},{4,12},{8,0},{12,4},{16,24},{20,28},{24,16},{28,20},{1,9},{5... | collective-permute-start | bytes 294920 | tf_op jit(solution)/shard_map/ppermute | solution.py:280
  20.1 5.9 %collective-permute-start.6 = (bf16[3,64,256]{2,1,0:T(8,128)(2,1)S(1)}, bf16[3,64,256]{2,1,0:T(8,128)(2,1)S(1)}, u32[]{:S(2)}, u32[]{:S(2)}) collective-permute-start(bf16[3,64,256]{2,1,0:T(8,128)(2,1)S(1)} %get-tuple-element.41), channel_id=1, source_target_pairs={{0,4},{4,0},{8,12},{12,8},{16,20},{20,16},{24,28},{28,24},{1,5},{5... | collective-permute-start | bytes 294920 | tf_op jit(solution)/shard_map/ppermute | solution.py:280
  31.9 8.4 %collective-permute-start.8 = (bf16[3,64,256]{2,1,0:T(8,128)(2,1)S(1)}, bf16[3,64,256]{2,1,0:T(8,128)(2,1)S(1)}, u32[]{:S(2)}, u32[]{:S(2)}) collective-permute-start(bf16[3,64,256]{2,1,0:T(8,128)(2,1)S(1)} %get-tuple-element.44), channel_id=1, source_target_pairs={{0,24},{4,28},{8,16},{12,20},{16,8},{20,12},{24,0},{28,4},{1,25},{... | collective-permute-start | bytes 294920 | tf_op jit(solution)/shard_map/ppermute | solution.py:280
  34.4 10.5 %collective-permute-start.9 = (bf16[3,64,256]{2,1,0:T(8,128)(2,1)S(1)}, bf16[3,64,256]{2,1,0:T(8,128)(2,1)S(1)}, u32[]{:S(2)}, u32[]{:S(2)}) collective-permute-start(bf16[3,64,256]{2,1,0:T(8,128)(2,1)S(1)} %get-tuple-element.45), channel_id=1, source_target_pairs={{0,20},{4,16},{8,28},{12,24},{16,4},{20,0},{24,12},{28,8},{1,21},{... | collective-permute-start | bytes 294920 | tf_op jit(solution)/shard_map/ppermute | solution.py:280
  34.4 17.1 %collective-permute-start.10 = (bf16[3,64,256]{2,1,0:T(8,128)(2,1)S(1)}, bf16[3,64,256]{2,1,0:T(8,128)(2,1)S(1)}, u32[]{:S(2)}, u32[]{:S(2)}) collective-permute-start(bf16[3,64,256]{2,1,0:T(8,128)(2,1)S(1)} %get-tuple-element.46), channel_id=1, source_target_pairs={{0,16},{4,20},{8,24},{12,28},{16,0},{20,4},{24,8},{28,12},{1,17},{... | collective-permute-start | bytes 294920 | tf_op jit(solution)/shard_map/ppermute | solution.py:280
  37.3 14.2 %collective-permute-start.11 = (bf16[3,64,256]{2,1,0:T(8,128)(2,1)S(1)}, bf16[3,64,256]{2,1,0:T(8,128)(2,1)S(1)}, u32[]{:S(2)}, u32[]{:S(2)}) collective-permute-start(bf16[3,64,256]{2,1,0:T(8,128)(2,1)S(1)} %get-tuple-element.47), channel_id=1, source_target_pairs={{0,12},{4,8},{8,4},{12,0},{16,28},{20,24},{24,20},{28,16},{1,13},{... | collective-permute-start | bytes 294920 | tf_op jit(solution)/shard_map/ppermute | solution.py:280
  38.5 13.1 %collective-permute-start.12 = (bf16[3,64,256]{2,1,0:T(8,128)(2,1)S(1)}, bf16[3,64,256]{2,1,0:T(8,128)(2,1)S(1)}, u32[]{:S(2)}, u32[]{:S(2)}) collective-permute-start(bf16[3,64,256]{2,1,0:T(8,128)(2,1)S(1)} %get-tuple-element.48), channel_id=1, source_target_pairs={{0,8},{4,12},{8,0},{12,4},{16,24},{20,28},{24,16},{28,20},{1,9},{5... | collective-permute-start | bytes 294920 | tf_op jit(solution)/shard_map/ppermute | solution.py:280
  40.3 11.3 %collective-permute-start.13 = (bf16[3,64,256]{2,1,0:T(8,128)(2,1)S(1)}, bf16[3,64,256]{2,1,0:T(8,128)(2,1)S(1)}, u32[]{:S(2)}, u32[]{:S(2)}) collective-permute-start(bf16[3,64,256]{2,1,0:T(8,128)(2,1)S(1)} %get-tuple-element.49), channel_id=1, source_target_pairs={{0,4},{4,0},{8,12},{12,8},{16,20},{20,16},{24,28},{28,24},{1,5},{5... | collective-permute-start | bytes 294920 | tf_op jit(solution)/shard_map/ppermute | solution.py:280
  45.0 7.3 %collective-permute-start.7 = (bf16[3,64,256]{2,1,0:T(8,128)(2,1)S(1)}, bf16[3,64,256]{2,1,0:T(8,128)(2,1)S(1)}, u32[]{:S(2)}, u32[]{:S(2)}) collective-permute-start(bf16[3,64,256]{2,1,0:T(8,128)(2,1)S(1)} %get-tuple-element.43), channel_id=1, source_target_pairs={{0,28},{4,24},{8,20},{12,16},{16,12},{20,8},{24,4},{28,0},{1,29},{... | collective-permute-start | bytes 294920 | tf_op jit(solution)/shard_map/ppermute | solution.py:280
  54.0 1.9 %collective-permute-start.14 = (bf16[2,256,512]{2,1,0:T(8,128)(2,1)S(1)}, bf16[2,256,512]{2,1,0:T(8,128)(2,1)S(1)}, u32[]{:S(2)}, u32[]{:S(2)}) collective-permute-start(bf16[2,256,512]{2,1,0:T(8,128)(2,1)S(1)} %get-tuple-element.65), channel_id=1, source_target_pairs={{0,1},{1,0},{2,3},{3,2},{4,5},{5,4},{6,7},{7,6},{8,9},{9,8},{10,11... | collective-permute-start | bytes 1572872 | tf_op jit(solution)/shard_map/ppermute | solution.py:280
  56.0 8.4 %collective-permute-start.15 = (bf16[256,512]{1,0:T(8,128)(2,1)S(1)}, bf16[256,512]{1,0:T(8,128)(2,1)S(1)}, u32[]{:S(2)}, u32[]{:S(2)}) collective-permute-start(bf16[256,512]{1,0:T(8,128)(2,1)S(1)} %fusion), channel_id=1, source_target_pairs={{0,2},{1,3},{2,0},{3,1},{4,6},{5,7},{6,4},{7,5},{8,10},{9,11},{10,... | collective-permute-start | bytes 786440 | tf_op jit(solution)/shard_map/ppermute | solution.py:280

commit v5 on v4

--- a/solution.py
+++ b/solution.py
@@ -135,91 +135,103 @@
     in_refs, tables, out_refs = refs[:blocks], refs[blocks : blocks + 3], refs[blocks + 3 : -7]
     in_ref, rows_ref, spec_ref, twid_ref, fwd_ref, inv_ref, sems = refs[-7:]
     twid_copy, fwd_copy, inv_copy = fetch(tables, (twid_ref, fwd_ref, inv_ref), sems)
-    _, signals, channels, block_len = in_ref.shape
+    groups, bins_count, signals, chunk, _ = rows_ref.shape
+    block_len = in_ref.shape[-1]
     me = lax.axis_index("ctx")
     for distance, ref in far_first(in_refs):
         in_ref[me ^ distance] = ref[...]
     twid_copy.wait()
-    chunk = min(channels, 16)
-    steps = channels // chunk
-
-    def analyse(step, carry):
-        signal = step // steps
-        start = pl.multiple_of((step % steps) * chunk, chunk)
-        values = [
-            in_ref[p, signal, pl.ds(start, chunk), :].astype(jnp.float32) for p in range(blocks)
-        ]
-        bins = half_spectrum(values)
-        for k in range(blocks + 1):
-            re, im = bins[k]
-            if k == 0:
-                im = jnp.zeros_like(re)
-            else:
+
+    def each(count, body):
+        if blocks <= 8:
+            for i in range(count):
+                body(i)
+        else:
+            pl.loop(0, count)(body)
+
+    def put(group, k, slot, re, im):
+        rows_ref[group, k, slot, :, :block_len] = re.astype(jnp.bfloat16)
+        rows_ref[group, k, slot, :, block_len:] = im.astype(jnp.bfloat16)
+
+    def get(group, k, slot):
+        return spec_ref[group, k, slot, :, :block_len], spec_ref[group, k, slot, :, block_len:]
+
+    def analyse(group):
+        rows = pl.ds(group * chunk, chunk)
+
+        def one(signal):
+            bins = half_spectrum(
+                [in_ref[p, signal, rows, :].astype(jnp.float32) for p in range(blocks)]
+            )
+            for k, (re, im) in enumerate(bins):
                 cos, sin = twid_ref[0, k : k + 1, :], twid_ref[1, k : k + 1, :]
-                if im is None:
-                    re, im = re * cos, -(re * sin)
+                if k == 0:
+                    put(group, k, signal, re, jnp.zeros_like(re))
+                elif im is None:
+                    put(group, k, signal, re * cos, -(re * sin))
                 else:
-                    re, im = re * cos + im * sin, im * cos - re * sin
-            rows_ref[k, signal, pl.ds(start, chunk), :block_len] = re.astype(jnp.bfloat16)
-            rows_ref[k, signal, pl.ds(start, chunk), block_len:] = im.astype(jnp.bfloat16)
-        return carry
-
-    lax.fori_loop(0, signals * steps, analyse, 0)
-    fwd_copy.wait()
-    inv_copy.wait()
-
-    total = (blocks + 1) * signals * channels
-    spec_ref[...] = jnp.dot(
-        rows_ref[...].reshape(total, 2 * block_len),
-        fwd_ref[...],
-        preferred_element_type=jnp.float32,
-    ).reshape(spec_ref.shape)
-
-    def combine(step, carry):
-        k = step // steps
-        start = pl.multiple_of((step % steps) * chunk, chunk)
-        rows = pl.ds(start, chunk)
-        prod_re, prod_im = spec_ref[k, 0, rows, :block_len], spec_ref[k, 0, rows, block_len:]
-        kern_re, kern_im = spec_ref[k, 1, rows, :block_len], spec_ref[k, 1, rows, block_len:]
-        grad_re, grad_im = spec_ref[k, 2, rows, :block_len], spec_ref[k, 2, rows, block_len:]
-
-        def put(slot, re, im):
-            rows_ref[k, slot, rows, :block_len] = re.astype(jnp.bfloat16)
-            rows_ref[k, slot, rows, block_len:] = im.astype(jnp.bfloat16)
-
-        put(0, prod_re * kern_re - prod_im * kern_im, prod_re * kern_im + prod_im * kern_re)
-        put(1, grad_re * kern_re + grad_im * kern_im, grad_im * kern_re - grad_re * kern_im)
-        put(2, grad_re * prod_re + grad_im * prod_im, grad_im * prod_re - grad_re * prod_im)
-        return carry
-
-    lax.fori_loop(0, (blocks + 1) * steps, combine, 0)
-
-    spec_ref[...] = jnp.dot(
-        rows_ref[...].reshape(total, 2 * block_len),
-        inv_ref[...],
-        preferred_element_type=jnp.float32,
-    ).reshape(spec_ref.shape)
-
-    def synthesise(step, carry):
-        signal = step // steps
-        start = pl.multiple_of((step % steps) * chunk, chunk)
-        rows = pl.ds(start, chunk)
-        bins = []
-        for k in range(blocks + 1):
-            re, im = spec_ref[k, signal, rows, :block_len], spec_ref[k, signal, rows, block_len:]
-            cos, sin = twid_ref[2, k : k + 1, :], twid_ref[3, k : k + 1, :]
-            if k == 0:
-                bins.append((re * cos, None))
-            elif k == blocks:
-                bins.append((re * cos - im * sin, None))
-            else:
-                bins.append((re * cos - im * sin, im * cos + re * sin))
-        values = half_spectrum_adjoint(bins)
-        for p in range(blocks):
-            in_ref[p, signal, rows, :] = values[p].astype(jnp.bfloat16)
-        return carry
-
-    lax.fori_loop(0, signals * steps, synthesise, 0)
+                    put(group, k, signal, re * cos + im * sin, im * cos - re * sin)
+
+        each(signals, one)
+
+    def transform(group, table_ref):
+        spec_ref[group] = jnp.dot(
+            rows_ref[group].reshape(bins_count * signals * chunk, 2 * block_len),
+            table_ref[...],
+            preferred_element_type=jnp.float32,
+        ).reshape(spec_ref.shape[1:])
+
+    def forward(group):
+        if group == 0:
+            fwd_copy.wait()
+        transform(group, fwd_ref)
+
+    def combine(group):
+        def one(k):
+            prod_re, prod_im = get(group, k, 0)
+            kern_re, kern_im = get(group, k, 1)
+            grad_re, grad_im = get(group, k, 2)
+            conv_re = prod_re * kern_re - prod_im * kern_im
+            conv_im = prod_re * kern_im + prod_im * kern_re
+            back_re = grad_re * kern_re + grad_im * kern_im
+            back_im = grad_im * kern_re - grad_re * kern_im
+            filt_re = grad_re * prod_re + grad_im * prod_im
+            filt_im = grad_im * prod_re - grad_re * prod_im
+            put(group, k, 0, conv_re, conv_im)
+            put(group, k, 1, back_re, back_im)
+            put(group, k, 2, filt_re, filt_im)
+
+        each(bins_count, one)
+
+    def inverse(group):
+        if group == 0:
+            inv_copy.wait()
+        transform(group, inv_ref)
+
+    def synthesise(group):
+        rows = pl.ds(group * chunk, chunk)
+
+        def one(signal):
+            bins = []
+            for k in range(bins_count):
+                re, im = get(group, k, signal)
+                cos, sin = twid_ref[2, k : k + 1, :], twid_ref[3, k : k + 1, :]
+                if k == 0:
+                    bins.append((re * cos, None))
+                elif k == blocks:
+                    bins.append((re * cos - im * sin, None))
+                else:
+                    bins.append((re * cos - im * sin, im * cos + re * sin))
+            for p, value in enumerate(half_spectrum_adjoint(bins)):
+                in_ref[p, signal, rows, :] = value.astype(jnp.bfloat16)
+
+        each(signals, one)
+
+    stages = (analyse, forward, combine, inverse, synthesise)
+    for step in range(groups + len(stages) - 1):
+        for depth, stage in reversed(list(enumerate(stages))):
+            if 0 <= step - depth < groups:
+                stage(step - depth)
     for distance, out_ref in far_first(out_refs):
         out_ref[...] = in_ref[me ^ distance]
 
@@ -237,14 +249,15 @@
     return total
 
 
-def natural(back_refs, turn_ref):
-    blocks, signals, channels, block_len = turn_ref.shape
+def natural(back_refs, turn_ref, slots):
+    blocks, _, channels, block_len = turn_ref.shape
     me = lax.axis_index("ctx")
     for distance, ref in far_first(back_refs):
-        turn_ref[me ^ distance] = ref[...]
+        for i, slot in enumerate(slots):
+            turn_ref[me ^ distance, i] = ref[slot]
     return [
-        turn_ref[:, slot].reshape(blocks * channels, block_len).astype(jnp.float32).T
-        for slot in range(signals)
+        turn_ref[:, i].reshape(blocks * channels, block_len).astype(jnp.float32).T
+        for i in range(len(slots))
     ]
 
 
@@ -258,21 +271,25 @@
     blocks = lax.axis_size("ctx")
     back_refs, (key_ref, value_ref, grad_ref) = refs[:blocks], refs[blocks : blocks + 3]
     weight_refs = refs[blocks + 3 : blocks + 6]
-    lhs_ref, out_ref, filt_ref, turn_ref = refs[blocks + 6 :]
-    conv_out, grad_product, grad_filter = natural(back_refs, turn_ref)
+    lhs_ref, out_ref, turn_ref = refs[blocks + 6 :]
+    conv_out, grad_product = natural(back_refs, turn_ref, (0, 1))
     lhs_ref[0] = (grad_product * value_ref[...].astype(jnp.float32)).astype(jnp.bfloat16)
     lhs_ref[1] = (conv_out * grad_ref[...].astype(jnp.float32)).astype(jnp.bfloat16)
     lhs_ref[2] = (grad_product * key_ref[...].astype(jnp.float32)).astype(jnp.bfloat16)
+    out_ref[...] = term(lhs_ref, weight_refs, lax.axis_index("tp") ^ 3).astype(jnp.bfloat16)
+
+
+def own_kernel(lhs_ref, wk_ref, wq_ref, wv_ref, far_ref, near_ref, own_ref):
     group = lax.axis_index("tp")
-    out_ref[0] = term(lhs_ref, weight_refs, group ^ 3).astype(jnp.bfloat16)
-    out_ref[1] = term(lhs_ref, weight_refs, group ^ 1).astype(jnp.bfloat16)
-    filt_ref[...] = grad_filter.astype(jnp.bfloat16)
-
-
-def own_kernel(lhs_ref, wk_ref, wq_ref, wv_ref, far_ref, own_ref):
-    group = lax.axis_index("tp")
-    far_ref[...] = term(lhs_ref, (wk_ref, wq_ref, wv_ref), group ^ 2)
-    own_ref[...] = term(lhs_ref, (wk_ref, wq_ref, wv_ref), group)
+    weight_refs = (wk_ref, wq_ref, wv_ref)
+    far_ref[...] = term(lhs_ref, weight_refs, group ^ 2)
+    near_ref[...] = term(lhs_ref, weight_refs, group ^ 1).astype(jnp.bfloat16)
+    own_ref[...] = term(lhs_ref, weight_refs, group)
+
+
+def turn_kernel(*refs):
+    back_refs, (out_ref, turn_ref) = refs[:-2], refs[-2:]
+    out_ref[...] = natural(back_refs, turn_ref, (2,))[0].astype(jnp.bfloat16)
 
 
 def exchange(block, axis, distance):
@@ -292,6 +309,7 @@
     groups = lax.axis_size("tp")
     block_len, width = key_act.shape
     channels = width // blocks
+    chunk = min(channels, 16)
     seq_len = blocks * block_len
     part = w_key.shape[0] // groups
     block_cost = pl.CostEstimate(
@@ -324,8 +342,8 @@
         out_shape=arrays(blocks, 3, channels, block_len),
         scratch_shapes=[
             pltpu.VMEM((blocks, 3, channels, block_len), jnp.bfloat16),
-            pltpu.VMEM((blocks + 1, 3, channels, 2 * block_len), jnp.bfloat16),
-            pltpu.VMEM((blocks + 1, 3, channels, 2 * block_len), jnp.float32),
+            pltpu.VMEM((channels // chunk, blocks + 1, 3, chunk, 2 * block_len), jnp.bfloat16),
+            pltpu.VMEM((channels // chunk, blocks + 1, 3, chunk, 2 * block_len), jnp.float32),
             pltpu.VMEM(twiddle.shape, jnp.float32),
             pltpu.VMEM(forward.shape, jnp.bfloat16),
             pltpu.VMEM(inverse.shape, jnp.bfloat16),
@@ -337,7 +355,7 @@
     back = swap(results)
 
     held = (key_act, value_act, grad_out, w_key, w_query, w_value)
-    held, _ = lax.optimization_barrier((held, results[0]))
+    held, _ = lax.optimization_barrier((held, results[-1]))
     held = pl.pallas_call(
         hold_kernel,
         in_specs=[HBM] * len(held),
@@ -348,32 +366,43 @@
         name="hold",
     )(*in_hbm(*held))
     weights = held[3:]
-    lhs, to_mate, grad_filter = pl.pallas_call(
+    lhs, to_mate = pl.pallas_call(
         mate_kernel,
         in_specs=[VMEM] * (blocks + 6),
-        out_shape=[
-            *arrays(1, 3, block_len, width),
-            *arrays(1, 2, block_len, part),
-            jax.ShapeDtypeStruct((block_len, width), jnp.bfloat16),
-        ],
-        scratch_shapes=[pltpu.VMEM((blocks, 3, channels, block_len), jnp.bfloat16)],
+        out_shape=arrays(1, 3, block_len, width) + arrays(1, block_len, part),
+        scratch_shapes=[pltpu.VMEM((blocks, 2, channels, block_len), jnp.bfloat16)],
         compiler_params=compiler_params(16),
         cost_estimate=block_cost,
         name="mate",
     )(*back, *held)
     from_mate = exchange(to_mate, "tp", 1)
-    far, own = pl.pallas_call(
+    far, near, own = pl.pallas_call(
         own_kernel,
         in_specs=[VMEM] * 4,
-        out_shape=arrays(2, block_len, part, dtype=jnp.float32),
+        out_shape=[
+            *arrays(1, block_len, part, dtype=jnp.float32),
+            *arrays(1, block_len, part),
+            *arrays(1, block_len, part, dtype=jnp.float32),
+        ],
         compiler_params=compiler_params(16),
         cost_estimate=block_cost,
         name="own",
     )(lhs, *weights)
-    far = (far + from_mate[0].astype(jnp.float32)).astype(jnp.bfloat16)
+    far = (far + from_mate.astype(jnp.float32)).astype(jnp.bfloat16)
+    far, near, back = lax.optimization_barrier((far, near, back))
     from_far = exchange(far, "tp", 2)
-    near = own + from_mate[1].astype(jnp.float32)
-    grad_input = (near + from_far.astype(jnp.float32)).astype(jnp.bfloat16)
+    from_near = exchange(near, "tp", 1)
+    grad_filter = pl.pallas_call(
+        turn_kernel,
+        in_specs=[VMEM] * blocks,
+        out_shape=jax.ShapeDtypeStruct((block_len, width), jnp.bfloat16),
+        scratch_shapes=[pltpu.VMEM((blocks, 1, channels, block_len), jnp.bfloat16)],
+        compiler_params=compiler_params(16),
+        cost_estimate=block_cost,
+        name="turn",
+    )(*back)
+    total = from_far.astype(jnp.float32) + from_near.astype(jnp.float32) + own
+    grad_input = total.astype(jnp.bfloat16)
     return (grad_input, grad_filter)
 
 

time: 65.4 us -> 60.6 us (0.927)
  waiting for transfers between devices: 17.5 us -> 13.2 us
  Pallas kernels: 13.4 us -> 12 us
  starting transfers between devices: 32.8 us -> 33.6 us
    ppermute x16 -> x17, waiting for transfers between devices: 17.5 us -> 13.2 us  [exchange(): return lax.ppermute(block, axis, pairs)]
    pallas_call x1, Pallas kernels: 5.97 us -> 4.41 us  [per_device(): pl.pallas_call(conv_kernel, in_specs=[VMEM] * blocks + [HBM] * 3, out_sha...]
    ppermute x16 -> x17, starting transfers between devices: 32.8 us -> 33.6 us  [exchange(): return lax.ppermute(block, axis, pairs)]
    pallas_call x2 -> x3, Pallas kernels: 2.74 us -> 2.95 us  [the longest x1 1.42 us: per_device(): pl.pallas_call(own_kernel, in_specs=[VMEM] * 4, out_shape=[*arrays(1, blo...]
  transfers between devices with their start and end apart: 16 -> 17, of which waited for: 7 -> 9; matrix products, arithmetic and copies ran while one was open for 0% -> 0% of each run, Pallas kernels for 6% -> 9%
where the time goes in v5:
time: 60.6 us; the launch traced here: 60.4 us
  starting transfers between devices  33.6 us (55%)
  waiting for transfers between devices  13.2 us (22%)
  Pallas kernels  12 us (20%)
  other arithmetic  0.87 us (1%)
  between operations  0.7 us (1%)
    ppermute x17, starting transfers between devices, exchange(): return lax.ppermute(block, axis, pairs)  33.6 us
    ppermute x17, waiting for transfers between devices, exchange(): return lax.ppermute(block, axis, pairs)  13.2 us
    pallas_call x1, Pallas kernels, per_device(): pl.pallas_call(conv_kernel, in_specs=[VMEM] * blocks + [HBM] * 3, out_sha...  4.41 us
    pallas_call x1, Pallas kernels, per_device(): pl.pallas_call(hold_kernel, in_specs=[HBM] * len(held), out_shape=[pltpu....  3.17 us
    pallas_call x1, Pallas kernels, per_device(): pl.pallas_call(gate_kernel, in_specs=[HBM] * 5, out_shape=arrays(blocks,...  1.5 us
    pallas_call x1, Pallas kernels, per_device(): pl.pallas_call(own_kernel, in_specs=[VMEM] * 4, out_shape=[*arrays(1, blo...  1.42 us
  transfers between devices with their start and end apart: 17, of which 9 were waited for; matrix products, arithmetic and copies ran while one was open for 0% of the time, Pallas kernels for 9%

profile of v5, /device:TPU:0, one launch (start us, length us, event | category | flops | bytes accessed | tf_op | source)
XLA Modules:
  0.0 60.4 jit_solution(15462208738129751274)
XLA Ops:
  0.6 1.5 %gate.1 = (bf16[3,64,256]{2,1,0:T(8,128)(2,1)S(1)}, bf16[3,64,256]{2,1,0:T(8,128)(2,1)S(1)}, bf16[3,64,256]{2,1,0:T(8,128)(2,1)S(1)}, bf16[3,64,256]{2,1,0:T(8,1...) custom-call(bf16[256,512]{1,0:T(8,128)(2,1)} %refs_0_.1, ...), custom_call_target="tpu_custom_call" | custom-call | tf_op jit(solution)/shard_map/gate/pallas_call | solution.py:322
  2.1 6.1 %collective-permute-start = (bf16[3,64,256]{2,1,0:T(8,128)(2,1)S(1)}, bf16[3,64,256]{2,1,0:T(8,128)(2,1)S(1)}, u32[]{:S(2)}, u32[]{:S(2)}) collective-permute-start(bf16[3,64,256]{2,1,0:T(8,128)(2,1)S(1)} %get-tuple-element.45), channel_id=1, source_target_pairs={{0,28},{4,24},{8,20},{12,16},{16,12},{20,8},{24,4},{28,0},{1,29},{... | collective-permute-start | bytes 294920 | tf_op jit(solution)/shard_map/ppermute | solution.py:297
  8.2 0.2 collective-permute-start.1
  8.4 0.7 %collective-permute-start.2 = (bf16[3,64,256]{2,1,0:T(8,128)(2,1)S(1)}, bf16[3,64,256]{2,1,0:T(8,128)(2,1)S(1)}, u32[]{:S(2)}, u32[]{:S(2)}) collective-permute-start(bf16[3,64,256]{2,1,0:T(8,128)(2,1)S(1)} %get-tuple-element.47), channel_id=1, source_target_pairs={{0,20},{4,16},{8,28},{12,24},{16,4},{20,0},{24,12},{28,8},{1,21},{... | collective-permute-start | bytes 294920 | tf_op jit(solution)/shard_map/ppermute | solution.py:297
  9.2 2.0 %collective-permute-start.3 = (bf16[3,64,256]{2,1,0:T(8,128)(2,1)S(1)}, bf16[3,64,256]{2,1,0:T(8,128)(2,1)S(1)}, u32[]{:S(2)}, u32[]{:S(2)}) collective-permute-start(bf16[3,64,256]{2,1,0:T(8,128)(2,1)S(1)} %get-tuple-element.48), channel_id=1, source_target_pairs={{0,16},{4,20},{8,24},{12,28},{16,0},{20,4},{24,8},{28,12},{1,17},{... | collective-permute-start | bytes 294920 | tf_op jit(solution)/shard_map/ppermute | solution.py:297
  11.2 2.3 %collective-permute-start.4 = (bf16[3,64,256]{2,1,0:T(8,128)(2,1)S(1)}, bf16[3,64,256]{2,1,0:T(8,128)(2,1)S(1)}, u32[]{:S(2)}, u32[]{:S(2)}) collective-permute-start(bf16[3,64,256]{2,1,0:T(8,128)(2,1)S(1)} %get-tuple-element.49), channel_id=1, source_target_pairs={{0,12},{4,8},{8,4},{12,0},{16,28},{20,24},{24,20},{28,16},{1,13},{... | collective-permute-start | bytes 294920 | tf_op jit(solution)/shard_map/ppermute | solution.py:297
  13.5 0.0 collective-permute-done.refs_0_
  13.5 6.6 %collective-permute-start.5 = (bf16[3,64,256]{2,1,0:T(8,128)(2,1)S(1)}, bf16[3,64,256]{2,1,0:T(8,128)(2,1)S(1)}, u32[]{:S(2)}, u32[]{:S(2)}) collective-permute-start(bf16[3,64,256]{2,1,0:T(8,128)(2,1)S(1)} %get-tuple-element.50), channel_id=1, source_target_pairs={{0,8},{4,12},{8,0},{12,4},{16,24},{20,28},{24,16},{28,20},{1,9},{5... | collective-permute-start | bytes 294920 | tf_op jit(solution)/shard_map/ppermute | solution.py:297
  20.1 0.0 collective-permute-done.1.refs_1_
  20.1 1.0 %collective-permute-start.6 = (bf16[3,64,256]{2,1,0:T(8,128)(2,1)S(1)}, bf16[3,64,256]{2,1,0:T(8,128)(2,1)S(1)}, u32[]{:S(2)}, u32[]{:S(2)}) collective-permute-start(bf16[3,64,256]{2,1,0:T(8,128)(2,1)S(1)} %get-tuple-element.51), channel_id=1, source_target_pairs={{0,4},{4,0},{8,12},{12,8},{16,20},{20,16},{24,28},{28,24},{1,5},{5... | collective-permute-start | bytes 294920 | tf_op jit(solution)/shard_map/ppermute | solution.py:297
  21.0 2.8 %collective-permute-done.2.refs_2_ = bf16[3,64,256]{2,1,0:T(8,128)(2,1)S(1)} collective-permute-done((bf16[3,64,256]{2,1,0:T(8,128)(2,1)S(1)}, bf16[3,64,256]{2,1,0:T(8,128)(2,1)S(1)}, u32[]{:S(2)}, u32[]{:S(2)}) %collective-permute-start.2) | collective-permute-done | bytes 98336 | tf_op jit(solution)/shard_map/ppermute | solution.py:297
  23.9 1.1 %collective-permute-done.3.refs_3_ = bf16[3,64,256]{2,1,0:T(8,128)(2,1)S(1)} collective-permute-done((bf16[3,64,256]{2,1,0:T(8,128)(2,1)S(1)}, bf16[3,64,256]{2,1,0:T(8,128)(2,1)S(1)}, u32[]{:S(2)}, u32[]{:S(2)}) %collective-permute-start.3) | collective-permute-done | bytes 98336 | tf_op jit(solution)/shard_map/ppermute | solution.py:297
  25.0 0.0 collective-permute-done.4.refs_4_
  25.0 0.9 %collective-permute-done.5.refs_5_ = bf16[3,64,256]{2,1,0:T(8,128)(2,1)S(1)} collective-permute-done((bf16[3,64,256]{2,1,0:T(8,128)(2,1)S(1)}, bf16[3,64,256]{2,1,0:T(8,128)(2,1)S(1)}, u32[]{:S(2)}, u32[]{:S(2)}) %collective-permute-start.5) | collective-permute-done | bytes 98336 | tf_op jit(solution)/shard_map/ppermute | solution.py:297
  26.0 0.0 collective-permute-done.6.refs_6_
  26.0 4.4 %conv.1 = (bf16[3,64,256]{2,1,0:T(8,128)(2,1)S(1)}, bf16[3,64,256]{2,1,0:T(8,128)(2,1)S(1)}, bf16[3,64,256]{2,1,0:T(8,128)(2,1)S(1)}, bf16[3,64,256]{2,1,0:T(8,1...) custom-call(bf16[3,64,256]{2,1,0:T(8,128)(2,1)S(1)} %collective-perm, ...), custom_call_target="tpu_custom_call" | custom-call | tf_op jit(solution)/shard_map/conv/pallas_call | solution.py:339
  30.4 2.5 %collective-permute-start.7 = (bf16[3,64,256]{2,1,0:T(8,128)(2,1)S(1)}, bf16[3,64,256]{2,1,0:T(8,128)(2,1)S(1)}, u32[]{:S(2)}, u32[]{:S(2)}) collective-permute-start(bf16[3,64,256]{2,1,0:T(8,128)(2,1)S(1)} %get-tuple-element.53), channel_id=1, source_target_pairs={{0,28},{4,24},{8,20},{12,16},{16,12},{20,8},{24,4},{28,0},{1,29},{... | collective-permute-start | bytes 294920 | tf_op jit(solution)/shard_map/ppermute | solution.py:297
  32.9 1.3 %collective-permute-start.8 = (bf16[3,64,256]{2,1,0:T(8,128)(2,1)S(1)}, bf16[3,64,256]{2,1,0:T(8,128)(2,1)S(1)}, u32[]{:S(2)}, u32[]{:S(2)}) collective-permute-start(bf16[3,64,256]{2,1,0:T(8,128)(2,1)S(1)} %get-tuple-element.54), channel_id=1, source_target_pairs={{0,24},{4,28},{8,16},{12,20},{16,8},{20,12},{24,0},{28,4},{1,25},{... | collective-permute-start | bytes 294920 | tf_op jit(solution)/shard_map/ppermute | solution.py:297
  34.2 1.2 %collective-permute-start.9 = (bf16[3,64,256]{2,1,0:T(8,128)(2,1)S(1)}, bf16[3,64,256]{2,1,0:T(8,128)(2,1)S(1)}, u32[]{:S(2)}, u32[]{:S(2)}) collective-permute-start(bf16[3,64,256]{2,1,0:T(8,128)(2,1)S(1)} %get-tuple-element.55), channel_id=1, source_target_pairs={{0,20},{4,16},{8,28},{12,24},{16,4},{20,0},{24,12},{28,8},{1,21},{... | collective-permute-start | bytes 294920 | tf_op jit(solution)/shard_map/ppermute | solution.py:297
  35.4 2.7 %collective-permute-start.10 = (bf16[3,64,256]{2,1,0:T(8,128)(2,1)S(1)}, bf16[3,64,256]{2,1,0:T(8,128)(2,1)S(1)}, u32[]{:S(2)}, u32[]{:S(2)}) collective-permute-start(bf16[3,64,256]{2,1,0:T(8,128)(2,1)S(1)} %get-tuple-element.56), channel_id=1, source_target_pairs={{0,16},{4,20},{8,24},{12,28},{16,0},{20,4},{24,8},{28,12},{1,17},{... | collective-permute-start | bytes 294920 | tf_op jit(solution)/shard_map/ppermute | solution.py:297
  38.1 0.1 collective-permute-start.11
  38.2 0.7 %collective-permute-done.7.refs_0_ = bf16[3,64,256]{2,1,0:T(8,128)(2,1)S(1)} collective-permute-done((bf16[3,64,256]{2,1,0:T(8,128)(2,1)S(1)}, bf16[3,64,256]{2,1,0:T(8,128)(2,1)S(1)}, u32[]{:S(2)}, u32[]{:S(2)}) %collective-permute-start.7) | collective-permute-done | bytes 98336 | tf_op jit(solution)/shard_map/ppermute | solution.py:297
  38.9 3.8 %collective-permute-start.12 = (bf16[3,64,256]{2,1,0:T(8,128)(2,1)S(1)}, bf16[3,64,256]{2,1,0:T(8,128)(2,1)S(1)}, u32[]{:S(2)}, u32[]{:S(2)}) collective-permute-start(bf16[3,64,256]{2,1,0:T(8,128)(2,1)S(1)} %get-tuple-element.58), channel_id=1, source_target_pairs={{0,8},{4,12},{8,0},{12,4},{16,24},{20,28},{24,16},{28,20},{1,9},{5... | collective-permute-start | bytes 294920 | tf_op jit(solution)/shard_map/ppermute | solution.py:297
  42.7 0.0 collective-permute-done.8.refs_1_
  42.7 1.3 %collective-permute-start.13 = (bf16[3,64,256]{2,1,0:T(8,128)(2,1)S(1)}, bf16[3,64,256]{2,1,0:T(8,128)(2,1)S(1)}, u32[]{:S(2)}, u32[]{:S(2)}) collective-permute-start(bf16[3,64,256]{2,1,0:T(8,128)(2,1)S(1)} %get-tuple-element.59), channel_id=1, source_target_pairs={{0,4},{4,0},{8,12},{12,8},{16,20},{20,16},{24,28},{28,24},{1,5},{5... | collective-permute-start | bytes 294920 | tf_op jit(solution)/shard_map/ppermute | solution.py:297
  44.0 3.2 %hold.1 = (bf16[256,512]{1,0:T(8,128)(2,1)S(1)}, bf16[256,512]{1,0:T(8,128)(2,1)S(1)}, bf16[256,512]{1,0:T(8,128)(2,1)S(1)}, bf16[2048,512]{1,0:T(8,128)(2,1)S(1...) custom-call(bf16[256,512]{1,0:T(8,128)(2,1)} %refs_0_.2, bf16[256,512]{1,0:T(8,128)(2,1)} %refs_1_.2, ...), custom_call_target="tpu_custom_call" | custom-call | bytes 8388608 | tf_op jit(solution)/shard_map/hold/pallas_call | solution.py:359
  47.2 0.8 %collective-permute-done.9.refs_2_ = bf16[3,64,256]{2,1,0:T(8,128)(2,1)S(1)} collective-permute-done((bf16[3,64,256]{2,1,0:T(8,128)(2,1)S(1)}, bf16[3,64,256]{2,1,0:T(8,128)(2,1)S(1)}, u32[]{:S(2)}, u32[]{:S(2)}) %collective-permute-start.9) | collective-permute-done | bytes 98336 | tf_op jit(solution)/shard_map/ppermute | solution.py:297
  48.0 0.1 collective-permute-done.10.refs_3_
  48.1 0.0 collective-permute-done.11.refs_4_
  48.1 0.5 collective-permute-done.12.refs_5_
  48.5 0.0 collective-permute-done.13.refs_6_
  48.5 0.7 %mate.1 = (bf16[3,256,512]{2,1,0:T(8,128)(2,1)S(1)}, bf16[256,512]{1,0:T(8,128)(2,1)S(1)}) custom-call(bf16[3,64,256]{2,1,0:T(8,128)(2,1)S(1)} %collective-permute-done.7.refs_0_, bf16[3,64,256]{2,1,0:T(8,128)(2,1)S(1)} %collective-permute-done.8.refs_1_, bf16[3,64,256]{2,1,0:T(8,128)(2,1)S(1)} %collective-permute-done.9.refs_2_, ...), custom_call_target="tpu_custom_call" | custom-call | flops 805306368 | bytes 4194304 | tf_op jit(solution)/shard_map/mate/pallas_call | solution.py:369
  49.2 0.1 collective-permute-start.14
  49.3 1.4 %own.1 = (f32[256,512]{1,0:T(8,128)S(1)}, bf16[256,512]{1,0:T(8,128)(2,1)S(1)}, f32[256,512]{1,0:T(8,128)S(1)}) custom-call(bf16[3,256,512]{2,1,0:T(8,128)(2,1)S(1)} %get-tuple-element.73.lhs_ref, bf16[2048,512]{1,0:T(8,128)(2,1)S(1)} %get-tuple-element.70.refs_11_.wk_ref, bf16[2048,512]{1,0:T(8,128)(2,1)S(1)} %get-tuple-element.71.refs_12_.wq_ref, ...), custom_call_target="tpu_custom_call" | custom-call | flops 805306368 | bytes 4194304 | tf_op jit(solution)/shard_map/own/pallas_call | solution.py:379
  50.7 0.1 collective-permute-done.14
  50.8 0.1 add_convert_fusion.1
  50.9 1.6 %collective-permute-start.15 = (bf16[256,512]{1,0:T(8,128)(2,1)S(1)}, bf16[256,512]{1,0:T(8,128)(2,1)S(1)}, u32[]{:S(2)}, u32[]{:S(2)}) collective-permute-start(bf16[256,512]{1,0:T(8,128)(2,1)S(1)} %add_convert_fusion.1), channel_id=1, source_target_pairs={{0,2},{1,3},{2,0},{3,1},{4,6},{5,7},{6,4},{7,5},{8,10},{9,11},{10,... | collective-permute-start | bytes 786440 | tf_op jit(solution)/shard_map/ppermute | solution.py:297
  52.4 0.1 collective-permute-start.16
  52.6 0.9 %turn.1 = bf16[256,512]{1,0:T(8,128)(2,1)} custom-call(bf16[3,64,256]{2,1,0:T(8,128)(2,1)S(1)} %collective-permute-done.7.refs_0_, bf16[3,64,256]{2,1,0:T(8,128)(2,1)S(1)} %collective-permute-done.8.refs_1_, bf16[3,64,256]{2,1,0:T(8,128)(2,1)S(1)} %collective-permute-done.9.refs_2_, bf16[3,64,256]{2,1,0:T(8,128)(2,1)S(1)} %collective-permute-done.10.refs_3_, ...), custom_call_target="tpu_custom_call" | custom-call | flops 805306368 | bytes 4194304 | tf_op jit(solution)/shard_map/turn/pallas_call | solution.py:395
  53.5 6.1 %collective-permute-done.15 = bf16[256,512]{1,0:T(8,128)(2,1)S(1)} collective-permute-done((bf16[256,512]{1,0:T(8,128)(2,1)S(1)}, bf16[256,512]{1,0:T(8,128)(2,1)S(1)}, u32[]{:S(2)}, u32[]{:S(2)}) %collective-permute-start.15) | collective-permute-done | bytes 262176 | tf_op jit(solution)/shard_map/ppermute | solution.py:297
  59.6 0.0 collective-permute-done.16
  59.6 0.8 %add_convert_fusion = bf16[256,512]{1,0:T(8,128)(2,1)} fusion(f32[256,512]{1,0:T(8,128)S(1)} %get-tuple-element.79, bf16[256,512]{1,0:T(8,128)(2,1)S(1)} %collective-permute-done.16, bf16[256,512]{1,0:T(8,128)(2,1)S(1)} %collective-permute-done.15), kind=kLoop, calls=%fused_computation | loop fusion | flops 655360 | bytes 1310720 | tf_op jit(solution)/shard_map/convert_element_type | solution.py:405
Async XLA Ops:
  2.1 11.4 %collective-permute-start = (bf16[3,64,256]{2,1,0:T(8,128)(2,1)S(1)}, bf16[3,64,256]{2,1,0:T(8,128)(2,1)S(1)}, u32[]{:S(2)}, u32[]{:S(2)}) collective-permute-start(bf16[3,64,256]{2,1,0:T(8,128)(2,1)S(1)} %get-tuple-element.45), channel_id=1, source_target_pairs={{0,28},{4,24},{8,20},{12,16},{16,12},{20,8},{24,4},{28,0},{1,29},{... | collective-permute-start | bytes 294920 | tf_op jit(solution)/shard_map/ppermute | solution.py:297
  8.2 11.9 %collective-permute-start.1 = (bf16[3,64,256]{2,1,0:T(8,128)(2,1)S(1)}, bf16[3,64,256]{2,1,0:T(8,128)(2,1)S(1)}, u32[]{:S(2)}, u32[]{:S(2)}) collective-permute-start(bf16[3,64,256]{2,1,0:T(8,128)(2,1)S(1)} %get-tuple-element.46), channel_id=1, source_target_pairs={{0,24},{4,28},{8,16},{12,20},{16,8},{20,12},{24,0},{28,4},{1,25},{... | collective-permute-start | bytes 294920 | tf_op jit(solution)/shard_map/ppermute | solution.py:297
  8.4 15.4 %collective-permute-start.2 = (bf16[3,64,256]{2,1,0:T(8,128)(2,1)S(1)}, bf16[3,64,256]{2,1,0:T(8,128)(2,1)S(1)}, u32[]{:S(2)}, u32[]{:S(2)}) collective-permute-start(bf16[3,64,256]{2,1,0:T(8,128)(2,1)S(1)} %get-tuple-element.47), channel_id=1, source_target_pairs={{0,20},{4,16},{8,28},{12,24},{16,4},{20,0},{24,12},{28,8},{1,21},{... | collective-permute-start | bytes 294920 | tf_op jit(solution)/shard_map/ppermute | solution.py:297
  9.2 15.8 %collective-permute-start.3 = (bf16[3,64,256]{2,1,0:T(8,128)(2,1)S(1)}, bf16[3,64,256]{2,1,0:T(8,128)(2,1)S(1)}, u32[]{:S(2)}, u32[]{:S(2)}) collective-permute-start(bf16[3,64,256]{2,1,0:T(8,128)(2,1)S(1)} %get-tuple-element.48), channel_id=1, source_target_pairs={{0,16},{4,20},{8,24},{12,28},{16,0},{20,4},{24,8},{28,12},{1,17},{... | collective-permute-start | bytes 294920 | tf_op jit(solution)/shard_map/ppermute | solution.py:297
  11.2 13.8 %collective-permute-start.4 = (bf16[3,64,256]{2,1,0:T(8,128)(2,1)S(1)}, bf16[3,64,256]{2,1,0:T(8,128)(2,1)S(1)}, u32[]{:S(2)}, u32[]{:S(2)}) collective-permute-start(bf16[3,64,256]{2,1,0:T(8,128)(2,1)S(1)} %get-tuple-element.49), channel_id=1, source_target_pairs={{0,12},{4,8},{8,4},{12,0},{16,28},{20,24},{24,20},{28,16},{1,13},{... | collective-permute-start | bytes 294920 | tf_op jit(solution)/shard_map/ppermute | solution.py:297
  13.5 12.5 %collective-permute-start.5 = (bf16[3,64,256]{2,1,0:T(8,128)(2,1)S(1)}, bf16[3,64,256]{2,1,0:T(8,128)(2,1)S(1)}, u32[]{:S(2)}, u32[]{:S(2)}) collective-permute-start(bf16[3,64,256]{2,1,0:T(8,128)(2,1)S(1)} %get-tuple-element.50), channel_id=1, source_target_pairs={{0,8},{4,12},{8,0},{12,4},{16,24},{20,28},{24,16},{28,20},{1,9},{5... | collective-permute-start | bytes 294920 | tf_op jit(solution)/shard_map/ppermute | solution.py:297
  20.1 5.9 %collective-permute-start.6 = (bf16[3,64,256]{2,1,0:T(8,128)(2,1)S(1)}, bf16[3,64,256]{2,1,0:T(8,128)(2,1)S(1)}, u32[]{:S(2)}, u32[]{:S(2)}) collective-permute-start(bf16[3,64,256]{2,1,0:T(8,128)(2,1)S(1)} %get-tuple-element.51), channel_id=1, source_target_pairs={{0,4},{4,0},{8,12},{12,8},{16,20},{20,16},{24,28},{28,24},{1,5},{5... | collective-permute-start | bytes 294920 | tf_op jit(solution)/shard_map/ppermute | solution.py:297
  30.4 8.5 %collective-permute-start.7 = (bf16[3,64,256]{2,1,0:T(8,128)(2,1)S(1)}, bf16[3,64,256]{2,1,0:T(8,128)(2,1)S(1)}, u32[]{:S(2)}, u32[]{:S(2)}) collective-permute-start(bf16[3,64,256]{2,1,0:T(8,128)(2,1)S(1)} %get-tuple-element.53), channel_id=1, source_target_pairs={{0,28},{4,24},{8,20},{12,16},{16,12},{20,8},{24,4},{28,0},{1,29},{... | collective-permute-start | bytes 294920 | tf_op jit(solution)/shard_map/ppermute | solution.py:297
  32.9 9.8 %collective-permute-start.8 = (bf16[3,64,256]{2,1,0:T(8,128)(2,1)S(1)}, bf16[3,64,256]{2,1,0:T(8,128)(2,1)S(1)}, u32[]{:S(2)}, u32[]{:S(2)}) collective-permute-start(bf16[3,64,256]{2,1,0:T(8,128)(2,1)S(1)} %get-tuple-element.54), channel_id=1, source_target_pairs={{0,24},{4,28},{8,16},{12,20},{16,8},{20,12},{24,0},{28,4},{1,25},{... | collective-permute-start | bytes 294920 | tf_op jit(solution)/shard_map/ppermute | solution.py:297
  34.2 13.7 %collective-permute-start.9 = (bf16[3,64,256]{2,1,0:T(8,128)(2,1)S(1)}, bf16[3,64,256]{2,1,0:T(8,128)(2,1)S(1)}, u32[]{:S(2)}, u32[]{:S(2)}) collective-permute-start(bf16[3,64,256]{2,1,0:T(8,128)(2,1)S(1)} %get-tuple-element.55), channel_id=1, source_target_pairs={{0,20},{4,16},{8,28},{12,24},{16,4},{20,0},{24,12},{28,8},{1,21},{... | collective-permute-start | bytes 294920 | tf_op jit(solution)/shard_map/ppermute | solution.py:297
  35.4 12.6 %collective-permute-start.10 = (bf16[3,64,256]{2,1,0:T(8,128)(2,1)S(1)}, bf16[3,64,256]{2,1,0:T(8,128)(2,1)S(1)}, u32[]{:S(2)}, u32[]{:S(2)}) collective-permute-start(bf16[3,64,256]{2,1,0:T(8,128)(2,1)S(1)} %get-tuple-element.56), channel_id=1, source_target_pairs={{0,16},{4,20},{8,24},{12,28},{16,0},{20,4},{24,8},{28,12},{1,17},{... | collective-permute-start | bytes 294920 | tf_op jit(solution)/shard_map/ppermute | solution.py:297
  38.1 10.0 %collective-permute-start.11 = (bf16[3,64,256]{2,1,0:T(8,128)(2,1)S(1)}, bf16[3,64,256]{2,1,0:T(8,128)(2,1)S(1)}, u32[]{:S(2)}, u32[]{:S(2)}) collective-permute-start(bf16[3,64,256]{2,1,0:T(8,128)(2,1)S(1)} %get-tuple-element.57), channel_id=1, source_target_pairs={{0,12},{4,8},{8,4},{12,0},{16,28},{20,24},{24,20},{28,16},{1,13},{... | collective-permute-start | bytes 294920 | tf_op jit(solution)/shard_map/ppermute | solution.py:297
  38.9 9.6 %collective-permute-start.12 = (bf16[3,64,256]{2,1,0:T(8,128)(2,1)S(1)}, bf16[3,64,256]{2,1,0:T(8,128)(2,1)S(1)}, u32[]{:S(2)}, u32[]{:S(2)}) collective-permute-start(bf16[3,64,256]{2,1,0:T(8,128)(2,1)S(1)} %get-tuple-element.58), channel_id=1, source_target_pairs={{0,8},{4,12},{8,0},{12,4},{16,24},{20,28},{24,16},{28,20},{1,9},{5... | collective-permute-start | bytes 294920 | tf_op jit(solution)/shard_map/ppermute | solution.py:297
  42.7 5.8 %collective-permute-start.13 = (bf16[3,64,256]{2,1,0:T(8,128)(2,1)S(1)}, bf16[3,64,256]{2,1,0:T(8,128)(2,1)S(1)}, u32[]{:S(2)}, u32[]{:S(2)}) collective-permute-start(bf16[3,64,256]{2,1,0:T(8,128)(2,1)S(1)} %get-tuple-element.59), channel_id=1, source_target_pairs={{0,4},{4,0},{8,12},{12,8},{16,20},{20,16},{24,28},{28,24},{1,5},{5... | collective-permute-start | bytes 294920 | tf_op jit(solution)/shard_map/ppermute | solution.py:297
  49.2 1.6 %collective-permute-start.14 = (bf16[256,512]{1,0:T(8,128)(2,1)S(1)}, bf16[256,512]{1,0:T(8,128)(2,1)S(1)}, u32[]{:S(2)}, u32[]{:S(2)}) collective-permute-start(bf16[256,512]{1,0:T(8,128)(2,1)S(1)} %get-tuple-element.75), channel_id=1, source_target_pairs={{0,1},{1,0},{2,3},{3,2},{4,5},{5,4},{6,7},{7,6},{8,9},{9,8},{10,11... | collective-permute-start | bytes 786440 | tf_op jit(solution)/shard_map/ppermute | solution.py:297
  50.9 8.7 %collective-permute-start.15 = (bf16[256,512]{1,0:T(8,128)(2,1)S(1)}, bf16[256,512]{1,0:T(8,128)(2,1)S(1)}, u32[]{:S(2)}, u32[]{:S(2)}) collective-permute-start(bf16[256,512]{1,0:T(8,128)(2,1)S(1)} %add_convert_fusion.1), channel_id=1, source_target_pairs={{0,2},{1,3},{2,0},{3,1},{4,6},{5,7},{6,4},{7,5},{8,10},{9,11},{10,... | collective-permute-start | bytes 786440 | tf_op jit(solution)/shard_map/ppermute | solution.py:297
  52.4 7.1 %collective-permute-start.16 = (bf16[256,512]{1,0:T(8,128)(2,1)S(1)}, bf16[256,512]{1,0:T(8,128)(2,1)S(1)}, u32[]{:S(2)}, u32[]{:S(2)}) collective-permute-start(bf16[256,512]{1,0:T(8,128)(2,1)S(1)} %get-tuple-element.78), channel_id=1, source_target_pairs={{0,1},{1,0},{2,3},{3,2},{4,5},{5,4},{6,7},{7,6},{8,9},{9,8},{10,11... | collective-permute-start | bytes 786440 | tf_op jit(solution)/shard_map/ppermute | solution.py:297

commit v6 on v5

--- a/solution.py
+++ b/solution.py
@@ -93,8 +93,10 @@
     return [pltpu.with_memory_space_constraint(array, pltpu.HBM) for array in arrays]
 
 
-def far_first(pieces):
-    return zip(reversed(range(len(pieces))), pieces)
+def by_distance(pieces):
+    last = len(pieces) - 1
+    order = [last - i // 2 if i % 2 == 0 else 1 + i // 2 for i in range(last)]
+    return zip([*order, 0], pieces)
 
 
 def fetch(sources, targets, sems):
@@ -126,19 +128,22 @@
         copy.wait()
     put(2, held_ref[3].astype(jnp.float32) * held_ref[4].astype(jnp.float32))
     me = lax.axis_index("ctx")
-    for distance, out_ref in far_first(out_refs):
+    for distance, out_ref in by_distance(out_refs):
         out_ref[...] = turn_ref[me ^ distance]
 
 
 def conv_kernel(*refs):
     blocks = lax.axis_size("ctx")
-    in_refs, tables, out_refs = refs[:blocks], refs[blocks : blocks + 3], refs[blocks + 3 : -7]
-    in_ref, rows_ref, spec_ref, twid_ref, fwd_ref, inv_ref, sems = refs[-7:]
-    twid_copy, fwd_copy, inv_copy = fetch(tables, (twid_ref, fwd_ref, inv_ref), sems)
+    in_refs, sources, refs = refs[:blocks], refs[blocks : blocks + 9], refs[blocks + 9 :]
+    out_refs, held_refs = refs[:blocks], refs[blocks : blocks + 6]
+    in_ref, rows_ref, spec_ref, twid_ref, fwd_ref, inv_ref, sems = refs[blocks + 6 :]
+    twid_copy, fwd_copy, inv_copy, *held_copies = fetch(
+        sources, (twid_ref, fwd_ref, inv_ref, *held_refs), sems
+    )
     groups, bins_count, signals, chunk, _ = rows_ref.shape
     block_len = in_ref.shape[-1]
     me = lax.axis_index("ctx")
-    for distance, ref in far_first(in_refs):
+    for distance, ref in by_distance(in_refs):
         in_ref[me ^ distance] = ref[...]
     twid_copy.wait()
 
@@ -232,8 +237,10 @@
         for depth, stage in reversed(list(enumerate(stages))):
             if 0 <= step - depth < groups:
                 stage(step - depth)
-    for distance, out_ref in far_first(out_refs):
+    for distance, out_ref in by_distance(out_refs):
         out_ref[...] = in_ref[me ^ distance]
+    for copy in held_copies:
+        copy.wait()
 
 
 def term(lhs_ref, weight_refs, group):
@@ -252,19 +259,13 @@
 def natural(back_refs, turn_ref, slots):
     blocks, _, channels, block_len = turn_ref.shape
     me = lax.axis_index("ctx")
-    for distance, ref in far_first(back_refs):
+    for distance, ref in by_distance(back_refs):
         for i, slot in enumerate(slots):
             turn_ref[me ^ distance, i] = ref[slot]
     return [
         turn_ref[:, i].reshape(blocks * channels, block_len).astype(jnp.float32).T
         for i in range(len(slots))
     ]
-
-
-def hold_kernel(*refs):
-    count = len(refs) // 2
-    for copy in fetch(refs[:count], refs[count : 2 * count], refs[-1]):
-        copy.wait()
 
 
 def mate_kernel(*refs):
@@ -279,12 +280,14 @@
     out_ref[...] = term(lhs_ref, weight_refs, lax.axis_index("tp") ^ 3).astype(jnp.bfloat16)
 
 
-def own_kernel(lhs_ref, wk_ref, wq_ref, wv_ref, far_ref, near_ref, own_ref):
+def far_kernel(lhs_ref, wk_ref, wq_ref, wv_ref, far_ref, near_ref):
     group = lax.axis_index("tp")
-    weight_refs = (wk_ref, wq_ref, wv_ref)
-    far_ref[...] = term(lhs_ref, weight_refs, group ^ 2)
-    near_ref[...] = term(lhs_ref, weight_refs, group ^ 1).astype(jnp.bfloat16)
-    own_ref[...] = term(lhs_ref, weight_refs, group)
+    far_ref[...] = term(lhs_ref, (wk_ref, wq_ref, wv_ref), group ^ 2)
+    near_ref[...] = term(lhs_ref, (wk_ref, wq_ref, wv_ref), group ^ 1).astype(jnp.bfloat16)
+
+
+def own_kernel(lhs_ref, wk_ref, wq_ref, wv_ref, own_ref):
+    own_ref[...] = term(lhs_ref, (wk_ref, wq_ref, wv_ref), lax.axis_index("tp"))
 
 
 def turn_kernel(*refs):
@@ -300,7 +303,7 @@
 def swap(pieces):
     return [
         exchange(piece, "ctx", distance) if distance else piece
-        for distance, piece in far_first(pieces)
+        for distance, piece in by_distance(pieces)
     ]
 
 
@@ -336,35 +339,24 @@
     forward, inverse, twiddle = dft_tables(
         blocks, block_len, 1.0 / (math.sqrt(seq_len) * 2 * seq_len)
     )
+    tables = (twiddle, forward, inverse)
+    held = (key_act, value_act, grad_out, w_key, w_query, w_value)
     results = pl.pallas_call(
         conv_kernel,
-        in_specs=[VMEM] * blocks + [HBM] * 3,
-        out_shape=arrays(blocks, 3, channels, block_len),
+        in_specs=[VMEM] * blocks + [HBM] * 9,
+        out_shape=arrays(blocks, 3, channels, block_len)
+        + [pltpu.VMEM(array.shape, array.dtype) for array in held],
         scratch_shapes=[
             pltpu.VMEM((blocks, 3, channels, block_len), jnp.bfloat16),
             pltpu.VMEM((channels // chunk, blocks + 1, 3, chunk, 2 * block_len), jnp.bfloat16),
             pltpu.VMEM((channels // chunk, blocks + 1, 3, chunk, 2 * block_len), jnp.float32),
-            pltpu.VMEM(twiddle.shape, jnp.float32),
-            pltpu.VMEM(forward.shape, jnp.bfloat16),
-            pltpu.VMEM(inverse.shape, jnp.bfloat16),
-            pltpu.SemaphoreType.DMA((3,)),
+            *[pltpu.VMEM(array.shape, array.dtype) for array in tables],
+            pltpu.SemaphoreType.DMA((9,)),
         ],
-        compiler_params=compiler_params(20),
+        compiler_params=compiler_params(28),
         name="conv",
-    )(*moved, *in_hbm(twiddle, forward, inverse))
-    back = swap(results)
-
-    held = (key_act, value_act, grad_out, w_key, w_query, w_value)
-    held, _ = lax.optimization_barrier((held, results[-1]))
-    held = pl.pallas_call(
-        hold_kernel,
-        in_specs=[HBM] * len(held),
-        out_shape=[pltpu.VMEM(array.shape, array.dtype) for array in held],
-        scratch_shapes=[pltpu.SemaphoreType.DMA((len(held),))],
-        compiler_params=compiler_params(12),
-        cost_estimate=pl.CostEstimate(flops=0, bytes_accessed=1 << 23, transcendentals=0),
-        name="hold",
-    )(*in_hbm(*held))
+    )(*moved, *in_hbm(*tables, *held))
+    back, held = swap(results[:blocks]), results[blocks:]
     weights = held[3:]
     lhs, to_mate = pl.pallas_call(
         mate_kernel,
@@ -376,20 +368,16 @@
         name="mate",
     )(*back, *held)
     from_mate = exchange(to_mate, "tp", 1)
-    far, near, own = pl.pallas_call(
-        own_kernel,
+    far, near = pl.pallas_call(
+        far_kernel,
         in_specs=[VMEM] * 4,
-        out_shape=[
-            *arrays(1, block_len, part, dtype=jnp.float32),
-            *arrays(1, block_len, part),
-            *arrays(1, block_len, part, dtype=jnp.float32),
-        ],
+        out_shape=arrays(1, block_len, part, dtype=jnp.float32) + arrays(1, block_len, part),
         compiler_params=compiler_params(16),
         cost_estimate=block_cost,
-        name="own",
+        name="far",
     )(lhs, *weights)
     far = (far + from_mate.astype(jnp.float32)).astype(jnp.bfloat16)
-    far, near, back = lax.optimization_barrier((far, near, back))
+    far, near, lhs, back = lax.optimization_barrier((far, near, lhs, back))
     from_far = exchange(far, "tp", 2)
     from_near = exchange(near, "tp", 1)
     grad_filter = pl.pallas_call(
@@ -401,6 +389,14 @@
         cost_estimate=block_cost,
         name="turn",
     )(*back)
+    own = pl.pallas_call(
+        own_kernel,
+        in_specs=[VMEM] * 4,
+        out_shape=arrays(1, block_len, part, dtype=jnp.float32)[0],
+        compiler_params=compiler_params(16),
+        cost_estimate=block_cost,
+        name="own",
+    )(lhs, *weights)
     total = from_far.astype(jnp.float32) + from_near.astype(jnp.float32) + own
     grad_input = total.astype(jnp.bfloat16)
     return (grad_input, grad_filter)

time: 60.6 us -> 59.2 us (0.977)
  waiting for transfers between devices: 13.2 us -> 20.3 us
  starting transfers between devices: 33.6 us -> 28 us
  Pallas kernels: 12 us -> 9.13 us
    ppermute x17, waiting for transfers between devices: 13.2 us -> 20.3 us  [exchange(): return lax.ppermute(block, axis, pairs)]
    ppermute x17, starting transfers between devices: 33.6 us -> 28 us  [exchange(): return lax.ppermute(block, axis, pairs)]
    pallas_call x3, Pallas kernels: 8.99 us -> 6.09 us  [the longest x1 4.48 us: per_device(): pl.pallas_call(conv_kernel, in_specs=[VMEM] * blocks + [HBM] * 9, out_sha...]
  transfers between devices with their start and end apart: 17 -> 17, of which waited for: 9 -> 8; matrix products, arithmetic and copies ran while one was open for 0% -> 0% of each run, Pallas kernels for 9% -> 4%
where the time goes in v6:
time: 59.2 us; the launch traced here: 59 us
  starting transfers between devices  28 us (47%)
  waiting for transfers between devices  20.3 us (34%)
  Pallas kernels  9.13 us (15%)
  other arithmetic  0.87 us (1%)
  between operations  0.7 us (1%)
    ppermute x17, starting transfers between devices, exchange(): return lax.ppermute(block, axis, pairs)  28 us
    ppermute x17, waiting for transfers between devices, exchange(): return lax.ppermute(block, axis, pairs)  20.3 us
    pallas_call x1, Pallas kernels, per_device(): pl.pallas_call(conv_kernel, in_specs=[VMEM] * blocks + [HBM] * 9, out_sha...  4.48 us
    pallas_call x1, Pallas kernels, per_device(): pl.pallas_call(gate_kernel, in_specs=[HBM] * 5, out_shape=arrays(blocks,...  1.5 us
  transfers between devices with their start and end apart: 17, of which 8 were waited for; matrix products, arithmetic and copies ran while one was open for 0% of the time, Pallas kernels for 4%

profile of v6, /device:TPU:0, one launch (start us, length us, event | category | flops | bytes accessed | tf_op | source)
XLA Modules:
  0.0 59.0 jit_solution(5425285891079452059)
XLA Ops:
  0.6 1.5 %gate.1 = (bf16[3,64,256]{2,1,0:T(8,128)(2,1)S(1)}, bf16[3,64,256]{2,1,0:T(8,128)(2,1)S(1)}, bf16[3,64,256]{2,1,0:T(8,128)(2,1)S(1)}, bf16[3,64,256]{2,1,0:T(8,1...) custom-call(bf16[256,512]{1,0:T(8,128)(2,1)} %refs_0_.1, ...), custom_call_target="tpu_custom_call" | custom-call | tf_op jit(solution)/shard_map/gate/pallas_call | solution.py:325
  2.1 6.1 %collective-permute-start = (bf16[3,64,256]{2,1,0:T(8,128)(2,1)S(1)}, bf16[3,64,256]{2,1,0:T(8,128)(2,1)S(1)}, u32[]{:S(2)}, u32[]{:S(2)}) collective-permute-start(bf16[3,64,256]{2,1,0:T(8,128)(2,1)S(1)} %get-tuple-element.39), channel_id=1, source_target_pairs={{0,28},{4,24},{8,20},{12,16},{16,12},{20,8},{24,4},{28,0},{1,29},{... | collective-permute-start | bytes 294920 | tf_op jit(solution)/shard_map/ppermute | solution.py:300
  8.2 0.5 collective-permute-start.1
  8.7 0.1 collective-permute-start.2
  8.9 0.0 collective-permute-start.3
  8.9 5.2 %collective-permute-start.4 = (bf16[3,64,256]{2,1,0:T(8,128)(2,1)S(1)}, bf16[3,64,256]{2,1,0:T(8,128)(2,1)S(1)}, u32[]{:S(2)}, u32[]{:S(2)}) collective-permute-start(bf16[3,64,256]{2,1,0:T(8,128)(2,1)S(1)} %get-tuple-element.43), channel_id=1, source_target_pairs={{0,20},{4,16},{8,28},{12,24},{16,4},{20,0},{24,12},{28,8},{1,21},{... | collective-permute-start | bytes 294920 | tf_op jit(solution)/shard_map/ppermute | solution.py:300
  14.1 0.0 collective-permute-done.refs_0_
  14.1 1.7 %collective-permute-start.5 = (bf16[3,64,256]{2,1,0:T(8,128)(2,1)S(1)}, bf16[3,64,256]{2,1,0:T(8,128)(2,1)S(1)}, u32[]{:S(2)}, u32[]{:S(2)}) collective-permute-start(bf16[3,64,256]{2,1,0:T(8,128)(2,1)S(1)} %get-tuple-element.44), channel_id=1, source_target_pairs={{0,12},{4,8},{8,4},{12,0},{16,28},{20,24},{24,20},{28,16},{1,13},{... | collective-permute-start | bytes 294920 | tf_op jit(solution)/shard_map/ppermute | solution.py:300
  15.7 0.0 collective-permute-done.1.refs_1_
  15.7 1.5 %collective-permute-start.6 = (bf16[3,64,256]{2,1,0:T(8,128)(2,1)S(1)}, bf16[3,64,256]{2,1,0:T(8,128)(2,1)S(1)}, u32[]{:S(2)}, u32[]{:S(2)}) collective-permute-start(bf16[3,64,256]{2,1,0:T(8,128)(2,1)S(1)} %get-tuple-element.45), channel_id=1, source_target_pairs={{0,16},{4,20},{8,24},{12,28},{16,0},{20,4},{24,8},{28,12},{1,17},{... | collective-permute-start | bytes 294920 | tf_op jit(solution)/shard_map/ppermute | solution.py:300
  17.3 0.0 collective-permute-done.2.refs_2_
  17.3 0.0 collective-permute-done.3.refs_3_
  17.3 5.2 %collective-permute-done.4.refs_4_ = bf16[3,64,256]{2,1,0:T(8,128)(2,1)S(1)} collective-permute-done((bf16[3,64,256]{2,1,0:T(8,128)(2,1)S(1)}, bf16[3,64,256]{2,1,0:T(8,128)(2,1)S(1)}, u32[]{:S(2)}, u32[]{:S(2)}) %collective-permute-start.4) | collective-permute-done | bytes 98336 | tf_op jit(solution)/shard_map/ppermute | solution.py:300
  22.5 0.0 collective-permute-done.5.refs_5_
  22.5 2.4 %collective-permute-done.6.refs_6_ = bf16[3,64,256]{2,1,0:T(8,128)(2,1)S(1)} collective-permute-done((bf16[3,64,256]{2,1,0:T(8,128)(2,1)S(1)}, bf16[3,64,256]{2,1,0:T(8,128)(2,1)S(1)}, u32[]{:S(2)}, u32[]{:S(2)}) %collective-permute-start.6) | collective-permute-done | bytes 98336 | tf_op jit(solution)/shard_map/ppermute | solution.py:300
  24.9 4.5 %conv.1 = (bf16[3,64,256]{2,1,0:T(8,128)(2,1)S(1)}, bf16[3,64,256]{2,1,0:T(8,128)(2,1)S(1)}, bf16[3,64,256]{2,1,0:T(8,128)(2,1)S(1)}, bf16[3,64,256]{2,1,0:T(8,1...) custom-call(bf16[3,64,256]{2,1,0:T(8,128)(2,1)S(1)} %collective-perm, ...), custom_call_target="tpu_custom_call" | custom-call | tf_op jit(solution)/shard_map/conv/pallas_call | solution.py:344
  29.4 2.6 %collective-permute-start.7 = (bf16[3,64,256]{2,1,0:T(8,128)(2,1)S(1)}, bf16[3,64,256]{2,1,0:T(8,128)(2,1)S(1)}, u32[]{:S(2)}, u32[]{:S(2)}) collective-permute-start(bf16[3,64,256]{2,1,0:T(8,128)(2,1)S(1)} %get-tuple-element.47), channel_id=1, source_target_pairs={{0,28},{4,24},{8,20},{12,16},{16,12},{20,8},{24,4},{28,0},{1,29},{... | collective-permute-start | bytes 294920 | tf_op jit(solution)/shard_map/ppermute | solution.py:300
  32.0 1.5 %collective-permute-start.8 = (bf16[3,64,256]{2,1,0:T(8,128)(2,1)S(1)}, bf16[3,64,256]{2,1,0:T(8,128)(2,1)S(1)}, u32[]{:S(2)}, u32[]{:S(2)}) collective-permute-start(bf16[3,64,256]{2,1,0:T(8,128)(2,1)S(1)} %get-tuple-element.48), channel_id=1, source_target_pairs={{0,4},{4,0},{8,12},{12,8},{16,20},{20,16},{24,28},{28,24},{1,5},{5... | collective-permute-start | bytes 294920 | tf_op jit(solution)/shard_map/ppermute | solution.py:300
  33.4 1.3 %collective-permute-start.9 = (bf16[3,64,256]{2,1,0:T(8,128)(2,1)S(1)}, bf16[3,64,256]{2,1,0:T(8,128)(2,1)S(1)}, u32[]{:S(2)}, u32[]{:S(2)}) collective-permute-start(bf16[3,64,256]{2,1,0:T(8,128)(2,1)S(1)} %get-tuple-element.49), channel_id=1, source_target_pairs={{0,24},{4,28},{8,16},{12,20},{16,8},{20,12},{24,0},{28,4},{1,25},{... | collective-permute-start | bytes 294920 | tf_op jit(solution)/shard_map/ppermute | solution.py:300
  34.7 0.0 collective-permute-start.10
  34.7 3.1 %collective-permute-start.11 = (bf16[3,64,256]{2,1,0:T(8,128)(2,1)S(1)}, bf16[3,64,256]{2,1,0:T(8,128)(2,1)S(1)}, u32[]{:S(2)}, u32[]{:S(2)}) collective-permute-start(bf16[3,64,256]{2,1,0:T(8,128)(2,1)S(1)} %get-tuple-element.51), channel_id=1, source_target_pairs={{0,20},{4,16},{8,28},{12,24},{16,4},{20,0},{24,12},{28,8},{1,21},{... | collective-permute-start | bytes 294920 | tf_op jit(solution)/shard_map/ppermute | solution.py:300
  37.8 0.0 collective-permute-done.7.refs_0_
  37.8 0.9 %collective-permute-start.12 = (bf16[3,64,256]{2,1,0:T(8,128)(2,1)S(1)}, bf16[3,64,256]{2,1,0:T(8,128)(2,1)S(1)}, u32[]{:S(2)}, u32[]{:S(2)}) collective-permute-start(bf16[3,64,256]{2,1,0:T(8,128)(2,1)S(1)} %get-tuple-element.52), channel_id=1, source_target_pairs={{0,12},{4,8},{8,4},{12,0},{16,28},{20,24},{24,20},{28,16},{1,13},{... | collective-permute-start | bytes 294920 | tf_op jit(solution)/shard_map/ppermute | solution.py:300
  38.7 0.0 collective-permute-done.8.refs_1_
  38.7 2.0 %collective-permute-start.13 = (bf16[3,64,256]{2,1,0:T(8,128)(2,1)S(1)}, bf16[3,64,256]{2,1,0:T(8,128)(2,1)S(1)}, u32[]{:S(2)}, u32[]{:S(2)}) collective-permute-start(bf16[3,64,256]{2,1,0:T(8,128)(2,1)S(1)} %get-tuple-element.53), channel_id=1, source_target_pairs={{0,16},{4,20},{8,24},{12,28},{16,0},{20,4},{24,8},{28,12},{1,17},{... | collective-permute-start | bytes 294920 | tf_op jit(solution)/shard_map/ppermute | solution.py:300
  40.7 0.3 collective-permute-done.9.refs_2_
  41.0 2.5 %collective-permute-done.10.refs_3_ = bf16[3,64,256]{2,1,0:T(8,128)(2,1)S(1)} collective-permute-done((bf16[3,64,256]{2,1,0:T(8,128)(2,1)S(1)}, bf16[3,64,256]{2,1,0:T(8,128)(2,1)S(1)}, u32[]{:S(2)}, u32[]{:S(2)}) %collective-permute-start.10) | collective-permute-done | bytes 98336 | tf_op jit(solution)/shard_map/ppermute | solution.py:300
  43.5 0.0 collective-permute-done.11.refs_4_
  43.5 2.0 %collective-permute-done.12.refs_5_ = bf16[3,64,256]{2,1,0:T(8,128)(2,1)S(1)} collective-permute-done((bf16[3,64,256]{2,1,0:T(8,128)(2,1)S(1)}, bf16[3,64,256]{2,1,0:T(8,128)(2,1)S(1)}, u32[]{:S(2)}, u32[]{:S(2)}) %collective-permute-start.12) | collective-permute-done | bytes 98336 | tf_op jit(solution)/shard_map/ppermute | solution.py:300
  45.5 2.0 %collective-permute-done.13.refs_6_ = bf16[3,64,256]{2,1,0:T(8,128)(2,1)S(1)} collective-permute-done((bf16[3,64,256]{2,1,0:T(8,128)(2,1)S(1)}, bf16[3,64,256]{2,1,0:T(8,128)(2,1)S(1)}, u32[]{:S(2)}, u32[]{:S(2)}) %collective-permute-start.13) | collective-permute-done | bytes 98336 | tf_op jit(solution)/shard_map/ppermute | solution.py:300
  47.4 0.7 %mate.1 = (bf16[3,256,512]{2,1,0:T(8,128)(2,1)S(1)}, bf16[256,512]{1,0:T(8,128)(2,1)S(1)}) custom-call(bf16[3,64,256]{2,1,0:T(8,128)(2,1)S(1)} %collective-permute-done.7.refs_0_, bf16[3,64,256]{2,1,0:T(8,128)(2,1)S(1)} %collective-permute-done.8.refs_1_, bf16[3,64,256]{2,1,0:T(8,128)(2,1)S(1)} %collective-permute-done.9.refs_2_, ...), custom_call_target="tpu_custom_call" | custom-call | flops 805306368 | bytes 4194304 | tf_op jit(solution)/shard_map/mate/pallas_call | solution.py:361
  48.1 0.1 collective-permute-start.14
  48.2 1.0 %far.1 = (f32[256,512]{1,0:T(8,128)S(1)}, bf16[256,512]{1,0:T(8,128)(2,1)S(1)}) custom-call(bf16[3,256,512]{2,1,0:T(8,128)(2,1)S(1)} %get-tuple-element.67.lhs_ref, bf16[2048,512]{1,0:T(8,128)(2,1)S(1)} %get-tuple-element.58.refs_11_.wk_ref, bf16[2048,512]{1,0:T(8,128)(2,1)S(1)} %get-tuple-element.59.refs_12_.wq_ref, ...), custom_call_target="tpu_custom_call" | custom-call | flops 805306368 | bytes 4194304 | tf_op jit(solution)/shard_map/far/pallas_call | solution.py:371
  49.2 0.5 collective-permute-done.14
  49.7 0.1 add_convert_fusion.1
  49.8 1.6 %collective-permute-start.15 = (bf16[256,512]{1,0:T(8,128)(2,1)S(1)}, bf16[256,512]{1,0:T(8,128)(2,1)S(1)}, u32[]{:S(2)}, u32[]{:S(2)}) collective-permute-start(bf16[256,512]{1,0:T(8,128)(2,1)S(1)} %add_convert_fusion.1), channel_id=1, source_target_pairs={{0,2},{1,3},{2,0},{3,1},{4,6},{5,7},{6,4},{7,5},{8,10},{9,11},{10,... | collective-permute-start | bytes 786440 | tf_op jit(solution)/shard_map/ppermute | solution.py:300
  51.3 0.0 collective-permute-start.16
  51.3 0.6 %own.1 = f32[256,512]{1,0:T(8,128)S(1)} custom-call(bf16[3,256,512]{2,1,0:T(8,128)(2,1)S(1)} %get-tuple-element.67.lhs_ref, bf16[2048,512]{1,0:T(8,128)(2,1)S(1)} %get-tuple-element.58.refs_11_.wk_ref, bf16[2048,512]{1,0:T(8,128)(2,1)S(1)} %get-tuple-element.59.refs_12_.wq_ref, bf16[2048,512]{1,0:T(8,128)(2,1)S(1)} %get-tuple-element.60.refs_13_.wv_ref), custom_call_target="tpu_custom_call" | custom-call | flops 805306368 | bytes 4194304 | tf_op jit(solution)/shard_map/own/pallas_call | solution.py:392
  51.9 0.9 %turn.1 = bf16[256,512]{1,0:T(8,128)(2,1)} custom-call(bf16[3,64,256]{2,1,0:T(8,128)(2,1)S(1)} %collective-permute-done.7.refs_0_, bf16[3,64,256]{2,1,0:T(8,128)(2,1)S(1)} %collective-permute-done.8.refs_1_, bf16[3,64,256]{2,1,0:T(8,128)(2,1)S(1)} %collective-permute-done.9.refs_2_, bf16[3,64,256]{2,1,0:T(8,128)(2,1)S(1)} %collective-permute-done.10.refs_3_, ...), custom_call_target="tpu_custom_call" | custom-call | flops 805306368 | bytes 4194304 | tf_op jit(solution)/shard_map/turn/pallas_call | solution.py:383
  52.8 5.4 %collective-permute-done.15 = bf16[256,512]{1,0:T(8,128)(2,1)S(1)} collective-permute-done((bf16[256,512]{1,0:T(8,128)(2,1)S(1)}, bf16[256,512]{1,0:T(8,128)(2,1)S(1)}, u32[]{:S(2)}, u32[]{:S(2)}) %collective-permute-start.15) | collective-permute-done | bytes 262176 | tf_op jit(solution)/shard_map/ppermute | solution.py:300
  58.2 0.0 collective-permute-done.16
  58.2 0.8 %add_convert_fusion = bf16[256,512]{1,0:T(8,128)(2,1)} fusion(f32[256,512]{1,0:T(8,128)S(1)} %own.1, bf16[256,512]{1,0:T(8,128)(2,1)S(1)} %collective-permute-done.16, bf16[256,512]{1,0:T(8,128)(2,1)S(1)} %collective-permute-done.15), kind=kLoop, calls=%fused_computation | loop fusion | flops 655360 | bytes 1310720 | tf_op jit(solution)/shard_map/convert_element_type | solution.py:401
Async XLA Ops:
  2.1 11.9 %collective-permute-start = (bf16[3,64,256]{2,1,0:T(8,128)(2,1)S(1)}, bf16[3,64,256]{2,1,0:T(8,128)(2,1)S(1)}, u32[]{:S(2)}, u32[]{:S(2)}) collective-permute-start(bf16[3,64,256]{2,1,0:T(8,128)(2,1)S(1)} %get-tuple-element.39), channel_id=1, source_target_pairs={{0,28},{4,24},{8,20},{12,16},{16,12},{20,8},{24,4},{28,0},{1,29},{... | collective-permute-start | bytes 294920 | tf_op jit(solution)/shard_map/ppermute | solution.py:300
  8.2 7.5 %collective-permute-start.1 = (bf16[3,64,256]{2,1,0:T(8,128)(2,1)S(1)}, bf16[3,64,256]{2,1,0:T(8,128)(2,1)S(1)}, u32[]{:S(2)}, u32[]{:S(2)}) collective-permute-start(bf16[3,64,256]{2,1,0:T(8,128)(2,1)S(1)} %get-tuple-element.40), channel_id=1, source_target_pairs={{0,4},{4,0},{8,12},{12,8},{16,20},{20,16},{24,28},{28,24},{1,5},{5... | collective-permute-start | bytes 294920 | tf_op jit(solution)/shard_map/ppermute | solution.py:300
  8.7 8.5 %collective-permute-start.2 = (bf16[3,64,256]{2,1,0:T(8,128)(2,1)S(1)}, bf16[3,64,256]{2,1,0:T(8,128)(2,1)S(1)}, u32[]{:S(2)}, u32[]{:S(2)}) collective-permute-start(bf16[3,64,256]{2,1,0:T(8,128)(2,1)S(1)} %get-tuple-element.41), channel_id=1, source_target_pairs={{0,24},{4,28},{8,16},{12,20},{16,8},{20,12},{24,0},{28,4},{1,25},{... | collective-permute-start | bytes 294920 | tf_op jit(solution)/shard_map/ppermute | solution.py:300
  8.9 8.4 %collective-permute-start.3 = (bf16[3,64,256]{2,1,0:T(8,128)(2,1)S(1)}, bf16[3,64,256]{2,1,0:T(8,128)(2,1)S(1)}, u32[]{:S(2)}, u32[]{:S(2)}) collective-permute-start(bf16[3,64,256]{2,1,0:T(8,128)(2,1)S(1)} %get-tuple-element.42), channel_id=1, source_target_pairs={{0,8},{4,12},{8,0},{12,4},{16,24},{20,28},{24,16},{28,20},{1,9},{5... | collective-permute-start | bytes 294920 | tf_op jit(solution)/shard_map/ppermute | solution.py:300
  8.9 13.6 %collective-permute-start.4 = (bf16[3,64,256]{2,1,0:T(8,128)(2,1)S(1)}, bf16[3,64,256]{2,1,0:T(8,128)(2,1)S(1)}, u32[]{:S(2)}, u32[]{:S(2)}) collective-permute-start(bf16[3,64,256]{2,1,0:T(8,128)(2,1)S(1)} %get-tuple-element.43), channel_id=1, source_target_pairs={{0,20},{4,16},{8,28},{12,24},{16,4},{20,0},{24,12},{28,8},{1,21},{... | collective-permute-start | bytes 294920 | tf_op jit(solution)/shard_map/ppermute | solution.py:300
  14.1 8.4 %collective-permute-start.5 = (bf16[3,64,256]{2,1,0:T(8,128)(2,1)S(1)}, bf16[3,64,256]{2,1,0:T(8,128)(2,1)S(1)}, u32[]{:S(2)}, u32[]{:S(2)}) collective-permute-start(bf16[3,64,256]{2,1,0:T(8,128)(2,1)S(1)} %get-tuple-element.44), channel_id=1, source_target_pairs={{0,12},{4,8},{8,4},{12,0},{16,28},{20,24},{24,20},{28,16},{1,13},{... | collective-permute-start | bytes 294920 | tf_op jit(solution)/shard_map/ppermute | solution.py:300
  15.7 9.2 %collective-permute-start.6 = (bf16[3,64,256]{2,1,0:T(8,128)(2,1)S(1)}, bf16[3,64,256]{2,1,0:T(8,128)(2,1)S(1)}, u32[]{:S(2)}, u32[]{:S(2)}) collective-permute-start(bf16[3,64,256]{2,1,0:T(8,128)(2,1)S(1)} %get-tuple-element.45), channel_id=1, source_target_pairs={{0,16},{4,20},{8,24},{12,28},{16,0},{20,4},{24,8},{28,12},{1,17},{... | collective-permute-start | bytes 294920 | tf_op jit(solution)/shard_map/ppermute | solution.py:300
  29.4 8.4 %collective-permute-start.7 = (bf16[3,64,256]{2,1,0:T(8,128)(2,1)S(1)}, bf16[3,64,256]{2,1,0:T(8,128)(2,1)S(1)}, u32[]{:S(2)}, u32[]{:S(2)}) collective-permute-start(bf16[3,64,256]{2,1,0:T(8,128)(2,1)S(1)} %get-tuple-element.47), channel_id=1, source_target_pairs={{0,28},{4,24},{8,20},{12,16},{16,12},{20,8},{24,4},{28,0},{1,29},{... | collective-permute-start | bytes 294920 | tf_op jit(solution)/shard_map/ppermute | solution.py:300
  32.0 6.8 %collective-permute-start.8 = (bf16[3,64,256]{2,1,0:T(8,128)(2,1)S(1)}, bf16[3,64,256]{2,1,0:T(8,128)(2,1)S(1)}, u32[]{:S(2)}, u32[]{:S(2)}) collective-permute-start(bf16[3,64,256]{2,1,0:T(8,128)(2,1)S(1)} %get-tuple-element.48), channel_id=1, source_target_pairs={{0,4},{4,0},{8,12},{12,8},{16,20},{20,16},{24,28},{28,24},{1,5},{5... | collective-permute-start | bytes 294920 | tf_op jit(solution)/shard_map/ppermute | solution.py:300
  33.4 7.6 %collective-permute-start.9 = (bf16[3,64,256]{2,1,0:T(8,128)(2,1)S(1)}, bf16[3,64,256]{2,1,0:T(8,128)(2,1)S(1)}, u32[]{:S(2)}, u32[]{:S(2)}) collective-permute-start(bf16[3,64,256]{2,1,0:T(8,128)(2,1)S(1)} %get-tuple-element.49), channel_id=1, source_target_pairs={{0,24},{4,28},{8,16},{12,20},{16,8},{20,12},{24,0},{28,4},{1,25},{... | collective-permute-start | bytes 294920 | tf_op jit(solution)/shard_map/ppermute | solution.py:300
  34.7 8.7 %collective-permute-start.10 = (bf16[3,64,256]{2,1,0:T(8,128)(2,1)S(1)}, bf16[3,64,256]{2,1,0:T(8,128)(2,1)S(1)}, u32[]{:S(2)}, u32[]{:S(2)}) collective-permute-start(bf16[3,64,256]{2,1,0:T(8,128)(2,1)S(1)} %get-tuple-element.50), channel_id=1, source_target_pairs={{0,8},{4,12},{8,0},{12,4},{16,24},{20,28},{24,16},{28,20},{1,9},{5... | collective-permute-start | bytes 294920 | tf_op jit(solution)/shard_map/ppermute | solution.py:300
  34.7 8.7 %collective-permute-start.11 = (bf16[3,64,256]{2,1,0:T(8,128)(2,1)S(1)}, bf16[3,64,256]{2,1,0:T(8,128)(2,1)S(1)}, u32[]{:S(2)}, u32[]{:S(2)}) collective-permute-start(bf16[3,64,256]{2,1,0:T(8,128)(2,1)S(1)} %get-tuple-element.51), channel_id=1, source_target_pairs={{0,20},{4,16},{8,28},{12,24},{16,4},{20,0},{24,12},{28,8},{1,21},{... | collective-permute-start | bytes 294920 | tf_op jit(solution)/shard_map/ppermute | solution.py:300
  37.8 7.7 %collective-permute-start.12 = (bf16[3,64,256]{2,1,0:T(8,128)(2,1)S(1)}, bf16[3,64,256]{2,1,0:T(8,128)(2,1)S(1)}, u32[]{:S(2)}, u32[]{:S(2)}) collective-permute-start(bf16[3,64,256]{2,1,0:T(8,128)(2,1)S(1)} %get-tuple-element.52), channel_id=1, source_target_pairs={{0,12},{4,8},{8,4},{12,0},{16,28},{20,24},{24,20},{28,16},{1,13},{... | collective-permute-start | bytes 294920 | tf_op jit(solution)/shard_map/ppermute | solution.py:300
  38.7 8.7 %collective-permute-start.13 = (bf16[3,64,256]{2,1,0:T(8,128)(2,1)S(1)}, bf16[3,64,256]{2,1,0:T(8,128)(2,1)S(1)}, u32[]{:S(2)}, u32[]{:S(2)}) collective-permute-start(bf16[3,64,256]{2,1,0:T(8,128)(2,1)S(1)} %get-tuple-element.53), channel_id=1, source_target_pairs={{0,16},{4,20},{8,24},{12,28},{16,0},{20,4},{24,8},{28,12},{1,17},{... | collective-permute-start | bytes 294920 | tf_op jit(solution)/shard_map/ppermute | solution.py:300
  48.1 1.6 %collective-permute-start.14 = (bf16[256,512]{1,0:T(8,128)(2,1)S(1)}, bf16[256,512]{1,0:T(8,128)(2,1)S(1)}, u32[]{:S(2)}, u32[]{:S(2)}) collective-permute-start(bf16[256,512]{1,0:T(8,128)(2,1)S(1)} %get-tuple-element.63), channel_id=1, source_target_pairs={{0,1},{1,0},{2,3},{3,2},{4,5},{5,4},{6,7},{7,6},{8,9},{9,8},{10,11... | collective-permute-start | bytes 786440 | tf_op jit(solution)/shard_map/ppermute | solution.py:300
  49.8 8.4 %collective-permute-start.15 = (bf16[256,512]{1,0:T(8,128)(2,1)S(1)}, bf16[256,512]{1,0:T(8,128)(2,1)S(1)}, u32[]{:S(2)}, u32[]{:S(2)}) collective-permute-start(bf16[256,512]{1,0:T(8,128)(2,1)S(1)} %add_convert_fusion.1), channel_id=1, source_target_pairs={{0,2},{1,3},{2,0},{3,1},{4,6},{5,7},{6,4},{7,5},{8,10},{9,11},{10,... | collective-permute-start | bytes 786440 | tf_op jit(solution)/shard_map/ppermute | solution.py:300
  51.3 6.9 %collective-permute-start.16 = (bf16[256,512]{1,0:T(8,128)(2,1)S(1)}, bf16[256,512]{1,0:T(8,128)(2,1)S(1)}, u32[]{:S(2)}, u32[]{:S(2)}) collective-permute-start(bf16[256,512]{1,0:T(8,128)(2,1)S(1)} %get-tuple-element.66), channel_id=1, source_target_pairs={{0,1},{1,0},{2,3},{3,2},{4,5},{5,4},{6,7},{7,6},{8,9},{9,8},{10,11... | collective-permute-start | bytes 786440 | tf_op jit(solution)/shard_map/ppermute | solution.py:300

commit v7 on v6

--- a/solution.py
+++ b/solution.py
@@ -93,10 +93,15 @@
     return [pltpu.with_memory_space_constraint(array, pltpu.HBM) for array in arrays]
 
 
+def distances(blocks):
+    far, near = range(blocks - 1, blocks // 2 - 1, -1), range(1, blocks // 2)
+    return [*near, *far, 0], [*far, *reversed(near), 0]
+
+
 def by_distance(pieces):
-    last = len(pieces) - 1
-    order = [last - i // 2 if i % 2 == 0 else 1 + i // 2 for i in range(last)]
-    return zip([*order, 0], pieces)
+    even, odd = distances(len(pieces))
+    core = lax.axis_index("tp") % 2
+    return [(a + core * (b - a), piece) for a, b, piece in zip(even, odd, pieces)]
 
 
 def fetch(sources, targets, sems):
@@ -301,10 +306,17 @@
 
 
 def swap(pieces):
-    return [
-        exchange(piece, "ctx", distance) if distance else piece
-        for distance, piece in by_distance(pieces)
-    ]
+    blocks, groups = lax.axis_size("ctx"), lax.axis_size("tp")
+    orders = distances(blocks)
+    moved = []
+    for step, piece in enumerate(pieces[:-1]):
+        pairs = [
+            (i * groups + j, (i ^ orders[j % 2][step]) * groups + j)
+            for i in range(blocks)
+            for j in range(groups)
+        ]
+        moved.append(lax.ppermute(piece, ("ctx", "tp"), pairs))
+    return [*moved, pieces[-1]]
 
 
 def per_device(key_act, value_act, query_act, grad_out, long_filter, w_key, w_query, w_value):

time: 59.2 us -> 60 us (1.014)
  waiting for transfers between devices: 20.3 us -> 25.3 us
  starting transfers between devices: 28 us -> 23.8 us
    ppermute x17 -> x3, starting transfers between devices: 28 us -> 1.63 us  [exchange(): return lax.ppermute(block, axis, pairs)]
    ppermute x0 -> x14, starting transfers between devices: none -> 22.2 us  [swap(): moved.append(lax.ppermute(piece, ('ctx', 'tp'), pairs))]
    ppermute x0 -> x14, waiting for transfers between devices: none -> 19.5 us  [swap(): moved.append(lax.ppermute(piece, ('ctx', 'tp'), pairs))]
    ppermute x17 -> x3, waiting for transfers between devices: 20.3 us -> 5.87 us  [exchange(): return lax.ppermute(block, axis, pairs)]
  transfers between devices with their start and end apart: 17 -> 17, of which waited for: 8 -> 11; matrix products, arithmetic and copies ran while one was open for 0% -> 0% of each run, Pallas kernels for 4% -> 4%
where the time goes in v7:
time: 60 us; the launch traced here: 59.9 us
  waiting for transfers between devices  25.3 us (42%)
  starting transfers between devices  23.8 us (40%)
  Pallas kernels  9.14 us (15%)
  other arithmetic  0.87 us (1%)
  between operations  0.7 us (1%)
    ppermute x14, starting transfers between devices, swap(): moved.append(lax.ppermute(piece, ('ctx', 'tp'), pairs))  22.2 us
    ppermute x14, waiting for transfers between devices, swap(): moved.append(lax.ppermute(piece, ('ctx', 'tp'), pairs))  19.5 us
    ppermute x3, waiting for transfers between devices, exchange(): return lax.ppermute(block, axis, pairs)  5.87 us
    pallas_call x1, Pallas kernels, per_device(): pl.pallas_call(conv_kernel, in_specs=[VMEM] * blocks + [HBM] * 9, out_sha...  4.47 us
    ppermute x3, starting transfers between devices, exchange(): return lax.ppermute(block, axis, pairs)  1.63 us
    pallas_call x1, Pallas kernels, per_device(): pl.pallas_call(gate_kernel, in_specs=[HBM] * 5, out_shape=arrays(blocks,...  1.5 us
  transfers between devices with their start and end apart: 17, of which 11 were waited for; matrix products, arithmetic and copies ran while one was open for 0% of the time, Pallas kernels for 4%

profile of v7, /device:TPU:0, one launch (start us, length us, event | category | flops | bytes accessed | tf_op | source)
XLA Modules:
  0.0 59.9 jit_solution(15117537424445604594)
XLA Ops:
  0.6 1.5 %gate.1 = (bf16[3,64,256]{2,1,0:T(8,128)(2,1)S(1)}, bf16[3,64,256]{2,1,0:T(8,128)(2,1)S(1)}, bf16[3,64,256]{2,1,0:T(8,128)(2,1)S(1)}, bf16[3,64,256]{2,1,0:T(8,1...) custom-call(bf16[256,512]{1,0:T(8,128)(2,1)} %refs_0_.1, ...), custom_call_target="tpu_custom_call" | custom-call | tf_op jit(solution)/shard_map/gate/pallas_call | solution.py:337
  2.1 3.0 %collective-permute-start = (bf16[3,64,256]{2,1,0:T(8,128)(2,1)S(1)}, bf16[3,64,256]{2,1,0:T(8,128)(2,1)S(1)}, u32[]{:S(2)}, u32[]{:S(2)}) collective-permute-start(bf16[3,64,256]{2,1,0:T(8,128)(2,1)S(1)} %get-tuple-element.39), channel_id=1, source_target_pairs={{0,4},{1,29},{2,6},{3,31},{4,0},{5,25},{6,2},{7,27},{8,12},{9,21},... | collective-permute-start | bytes 294920 | tf_op jit(solution)/shard_map/ppermute | solution.py:318
  5.2 1.6 %collective-permute-start.1 = (bf16[3,64,256]{2,1,0:T(8,128)(2,1)S(1)}, bf16[3,64,256]{2,1,0:T(8,128)(2,1)S(1)}, u32[]{:S(2)}, u32[]{:S(2)}) collective-permute-start(bf16[3,64,256]{2,1,0:T(8,128)(2,1)S(1)} %get-tuple-element.40), channel_id=1, source_target_pairs={{0,8},{1,25},{2,10},{3,27},{4,12},{5,29},{6,14},{7,31},{8,0},{9,17... | collective-permute-start | bytes 294920 | tf_op jit(solution)/shard_map/ppermute | solution.py:318
  6.8 0.0 collective-permute-start.2
  6.8 4.9 %collective-permute-start.3 = (bf16[3,64,256]{2,1,0:T(8,128)(2,1)S(1)}, bf16[3,64,256]{2,1,0:T(8,128)(2,1)S(1)}, u32[]{:S(2)}, u32[]{:S(2)}) collective-permute-start(bf16[3,64,256]{2,1,0:T(8,128)(2,1)S(1)} %get-tuple-element.42), channel_id=1, source_target_pairs={{0,28},{1,17},{2,30},{3,19},{4,24},{5,21},{6,26},{7,23},{8,20},{9,... | collective-permute-start | bytes 294920 | tf_op jit(solution)/shard_map/ppermute | solution.py:318
  11.7 0.2 collective-permute-start.4
  11.9 0.0 collective-permute-done.refs_0_
  11.9 0.7 %collective-permute-start.5 = (bf16[3,64,256]{2,1,0:T(8,128)(2,1)S(1)}, bf16[3,64,256]{2,1,0:T(8,128)(2,1)S(1)}, u32[]{:S(2)}, u32[]{:S(2)}) collective-permute-start(bf16[3,64,256]{2,1,0:T(8,128)(2,1)S(1)} %get-tuple-element.44), channel_id=1, source_target_pairs={{0,20},{1,9},{2,22},{3,11},{4,16},{5,13},{6,18},{7,15},{8,28},{9,1... | collective-permute-start | bytes 294920 | tf_op jit(solution)/shard_map/ppermute | solution.py:318
  12.7 0.0 collective-permute-done.1.refs_1_
  12.7 2.0 %collective-permute-start.6 = (bf16[3,64,256]{2,1,0:T(8,128)(2,1)S(1)}, bf16[3,64,256]{2,1,0:T(8,128)(2,1)S(1)}, u32[]{:S(2)}, u32[]{:S(2)}) collective-permute-start(bf16[3,64,256]{2,1,0:T(8,128)(2,1)S(1)} %get-tuple-element.45), channel_id=1, source_target_pairs={{0,16},{1,5},{2,18},{3,7},{4,20},{5,1},{6,22},{7,3},{8,24},{9,13},... | collective-permute-start | bytes 294920 | tf_op jit(solution)/shard_map/ppermute | solution.py:318
  14.6 0.0 collective-permute-done.2.refs_2_
  14.6 2.5 %collective-permute-done.3.refs_3_ = bf16[3,64,256]{2,1,0:T(8,128)(2,1)S(1)} collective-permute-done((bf16[3,64,256]{2,1,0:T(8,128)(2,1)S(1)}, bf16[3,64,256]{2,1,0:T(8,128)(2,1)S(1)}, u32[]{:S(2)}, u32[]{:S(2)}) %collective-permute-start.3) | collective-permute-done | bytes 98336 | tf_op jit(solution)/shard_map/ppermute | solution.py:318
  17.1 2.1 %collective-permute-done.4.refs_4_ = bf16[3,64,256]{2,1,0:T(8,128)(2,1)S(1)} collective-permute-done((bf16[3,64,256]{2,1,0:T(8,128)(2,1)S(1)}, bf16[3,64,256]{2,1,0:T(8,128)(2,1)S(1)}, u32[]{:S(2)}, u32[]{:S(2)}) %collective-permute-start.4) | collective-permute-done | bytes 98336 | tf_op jit(solution)/shard_map/ppermute | solution.py:318
  19.2 5.5 %collective-permute-done.5.refs_5_ = bf16[3,64,256]{2,1,0:T(8,128)(2,1)S(1)} collective-permute-done((bf16[3,64,256]{2,1,0:T(8,128)(2,1)S(1)}, bf16[3,64,256]{2,1,0:T(8,128)(2,1)S(1)}, u32[]{:S(2)}, u32[]{:S(2)}) %collective-permute-start.5) | collective-permute-done | bytes 98336 | tf_op jit(solution)/shard_map/ppermute | solution.py:318
  24.8 0.3 collective-permute-done.6.refs_6_
  25.1 4.5 %conv.1 = (bf16[3,64,256]{2,1,0:T(8,128)(2,1)S(1)}, bf16[3,64,256]{2,1,0:T(8,128)(2,1)S(1)}, bf16[3,64,256]{2,1,0:T(8,128)(2,1)S(1)}, bf16[3,64,256]{2,1,0:T(8,1...) custom-call(bf16[3,64,256]{2,1,0:T(8,128)(2,1)S(1)} %collective-perm, ...), custom_call_target="tpu_custom_call" | custom-call | tf_op jit(solution)/shard_map/conv/pallas_call | solution.py:356
  29.6 1.4 %collective-permute-start.7 = (bf16[3,64,256]{2,1,0:T(8,128)(2,1)S(1)}, bf16[3,64,256]{2,1,0:T(8,128)(2,1)S(1)}, u32[]{:S(2)}, u32[]{:S(2)}) collective-permute-start(bf16[3,64,256]{2,1,0:T(8,128)(2,1)S(1)} %get-tuple-element.47), channel_id=1, source_target_pairs={{0,4},{1,29},{2,6},{3,31},{4,0},{5,25},{6,2},{7,27},{8,12},{9,21},... | collective-permute-start | bytes 294920 | tf_op jit(solution)/shard_map/ppermute | solution.py:318
  30.9 0.0 collective-permute-start.8
  30.9 2.2 %collective-permute-start.9 = (bf16[3,64,256]{2,1,0:T(8,128)(2,1)S(1)}, bf16[3,64,256]{2,1,0:T(8,128)(2,1)S(1)}, u32[]{:S(2)}, u32[]{:S(2)}) collective-permute-start(bf16[3,64,256]{2,1,0:T(8,128)(2,1)S(1)} %get-tuple-element.49), channel_id=1, source_target_pairs={{0,12},{1,21},{2,14},{3,23},{4,8},{5,17},{6,10},{7,19},{8,4},{9,29... | collective-permute-start | bytes 294920 | tf_op jit(solution)/shard_map/ppermute | solution.py:318
  33.1 3.4 %collective-permute-start.10 = (bf16[3,64,256]{2,1,0:T(8,128)(2,1)S(1)}, bf16[3,64,256]{2,1,0:T(8,128)(2,1)S(1)}, u32[]{:S(2)}, u32[]{:S(2)}) collective-permute-start(bf16[3,64,256]{2,1,0:T(8,128)(2,1)S(1)} %get-tuple-element.50), channel_id=1, source_target_pairs={{0,28},{1,17},{2,30},{3,19},{4,24},{5,21},{6,26},{7,23},{8,20},{9,... | collective-permute-start | bytes 294920 | tf_op jit(solution)/shard_map/ppermute | solution.py:318
  36.5 1.2 %collective-permute-start.11 = (bf16[3,64,256]{2,1,0:T(8,128)(2,1)S(1)}, bf16[3,64,256]{2,1,0:T(8,128)(2,1)S(1)}, u32[]{:S(2)}, u32[]{:S(2)}) collective-permute-start(bf16[3,64,256]{2,1,0:T(8,128)(2,1)S(1)} %get-tuple-element.51), channel_id=1, source_target_pairs={{0,24},{1,13},{2,26},{3,15},{4,28},{5,9},{6,30},{7,11},{8,16},{9,5... | collective-permute-start | bytes 294920 | tf_op jit(solution)/shard_map/ppermute | solution.py:318
  37.7 0.0 collective-permute-done.7.refs_0_
  37.7 0.2 collective-permute-start.12
  37.8 1.5 %collective-permute-done.8.refs_1_ = bf16[3,64,256]{2,1,0:T(8,128)(2,1)S(1)} collective-permute-done((bf16[3,64,256]{2,1,0:T(8,128)(2,1)S(1)}, bf16[3,64,256]{2,1,0:T(8,128)(2,1)S(1)}, u32[]{:S(2)}, u32[]{:S(2)}) %collective-permute-start.8) | collective-permute-done | bytes 98336 | tf_op jit(solution)/shard_map/ppermute | solution.py:318
  39.3 1.4 %collective-permute-start.13 = (bf16[3,64,256]{2,1,0:T(8,128)(2,1)S(1)}, bf16[3,64,256]{2,1,0:T(8,128)(2,1)S(1)}, u32[]{:S(2)}, u32[]{:S(2)}) collective-permute-start(bf16[3,64,256]{2,1,0:T(8,128)(2,1)S(1)} %get-tuple-element.53), channel_id=1, source_target_pairs={{0,16},{1,5},{2,18},{3,7},{4,20},{5,1},{6,22},{7,3},{8,24},{9,13},... | collective-permute-start | bytes 294920 | tf_op jit(solution)/shard_map/ppermute | solution.py:318
  40.8 0.0 collective-permute-done.9.refs_2_
  40.8 1.6 %collective-permute-done.10.refs_3_ = bf16[3,64,256]{2,1,0:T(8,128)(2,1)S(1)} collective-permute-done((bf16[3,64,256]{2,1,0:T(8,128)(2,1)S(1)}, bf16[3,64,256]{2,1,0:T(8,128)(2,1)S(1)}, u32[]{:S(2)}, u32[]{:S(2)}) %collective-permute-start.10) | collective-permute-done | bytes 98336 | tf_op jit(solution)/shard_map/ppermute | solution.py:318
  42.3 2.0 %collective-permute-done.11.refs_4_ = bf16[3,64,256]{2,1,0:T(8,128)(2,1)S(1)} collective-permute-done((bf16[3,64,256]{2,1,0:T(8,128)(2,1)S(1)}, bf16[3,64,256]{2,1,0:T(8,128)(2,1)S(1)}, u32[]{:S(2)}, u32[]{:S(2)}) %collective-permute-start.11) | collective-permute-done | bytes 98336 | tf_op jit(solution)/shard_map/ppermute | solution.py:318
  44.3 3.8 %collective-permute-done.12.refs_5_ = bf16[3,64,256]{2,1,0:T(8,128)(2,1)S(1)} collective-permute-done((bf16[3,64,256]{2,1,0:T(8,128)(2,1)S(1)}, bf16[3,64,256]{2,1,0:T(8,128)(2,1)S(1)}, u32[]{:S(2)}, u32[]{:S(2)}) %collective-permute-start.12) | collective-permute-done | bytes 98336 | tf_op jit(solution)/shard_map/ppermute | solution.py:318
  48.1 0.2 collective-permute-done.13.refs_6_
  48.3 0.7 %mate.1 = (bf16[3,256,512]{2,1,0:T(8,128)(2,1)S(1)}, bf16[256,512]{1,0:T(8,128)(2,1)S(1)}) custom-call(bf16[3,64,256]{2,1,0:T(8,128)(2,1)S(1)} %collective-permute-done.7.refs_0_, bf16[3,64,256]{2,1,0:T(8,128)(2,1)S(1)} %collective-permute-done.8.refs_1_, bf16[3,64,256]{2,1,0:T(8,128)(2,1)S(1)} %collective-permute-done.9.refs_2_, ...), custom_call_target="tpu_custom_call" | custom-call | flops 805306368 | bytes 4194304 | tf_op jit(solution)/shard_map/mate/pallas_call | solution.py:373
  49.0 0.1 collective-permute-start.14
  49.1 1.0 %far.1 = (f32[256,512]{1,0:T(8,128)S(1)}, bf16[256,512]{1,0:T(8,128)(2,1)S(1)}) custom-call(bf16[3,256,512]{2,1,0:T(8,128)(2,1)S(1)} %get-tuple-element.67.lhs_ref, bf16[2048,512]{1,0:T(8,128)(2,1)S(1)} %get-tuple-element.58.refs_11_.wk_ref, bf16[2048,512]{1,0:T(8,128)(2,1)S(1)} %get-tuple-element.59.refs_12_.wq_ref, ...), custom_call_target="tpu_custom_call" | custom-call | flops 805306368 | bytes 4194304 | tf_op jit(solution)/shard_map/far/pallas_call | solution.py:383
  50.1 0.5 collective-permute-done.14
  50.6 0.1 add_convert_fusion.1
  50.7 1.6 %collective-permute-start.15 = (bf16[256,512]{1,0:T(8,128)(2,1)S(1)}, bf16[256,512]{1,0:T(8,128)(2,1)S(1)}, u32[]{:S(2)}, u32[]{:S(2)}) collective-permute-start(bf16[256,512]{1,0:T(8,128)(2,1)S(1)} %add_convert_fusion.1), channel_id=1, source_target_pairs={{0,2},{1,3},{2,0},{3,1},{4,6},{5,7},{6,4},{7,5},{8,10},{9,11},{10,... | collective-permute-start | bytes 786440 | tf_op jit(solution)/shard_map/ppermute | solution.py:305
  52.2 0.0 collective-permute-start.16
  52.2 0.6 own.1
  52.8 0.9 %turn.1 = bf16[256,512]{1,0:T(8,128)(2,1)} custom-call(bf16[3,64,256]{2,1,0:T(8,128)(2,1)S(1)} %collective-permute-done.7.refs_0_, bf16[3,64,256]{2,1,0:T(8,128)(2,1)S(1)} %collective-permute-done.8.refs_1_, bf16[3,64,256]{2,1,0:T(8,128)(2,1)S(1)} %collective-permute-done.9.refs_2_, bf16[3,64,256]{2,1,0:T(8,128)(2,1)S(1)} %collective-permute-done.10.refs_3_, ...), custom_call_target="tpu_custom_call" | custom-call | flops 805306368 | bytes 4194304 | tf_op jit(solution)/shard_map/turn/pallas_call | solution.py:395
  53.7 5.4 %collective-permute-done.15 = bf16[256,512]{1,0:T(8,128)(2,1)S(1)} collective-permute-done((bf16[256,512]{1,0:T(8,128)(2,1)S(1)}, bf16[256,512]{1,0:T(8,128)(2,1)S(1)}, u32[]{:S(2)}, u32[]{:S(2)}) %collective-permute-start.15) | collective-permute-done | bytes 262176 | tf_op jit(solution)/shard_map/ppermute | solution.py:305
  59.1 0.0 collective-permute-done.16
  59.1 0.8 %add_convert_fusion = bf16[256,512]{1,0:T(8,128)(2,1)} fusion(f32[256,512]{1,0:T(8,128)S(1)} %own.1, bf16[256,512]{1,0:T(8,128)(2,1)S(1)} %collective-permute-done.16, bf16[256,512]{1,0:T(8,128)(2,1)S(1)} %collective-permute-done.15), kind=kLoop, calls=%fused_computation | loop fusion | flops 655360 | bytes 1310720 | tf_op jit(solution)/shard_map/convert_element_type | solution.py:413
Async XLA Ops:
  2.1 9.8 %collective-permute-start = (bf16[3,64,256]{2,1,0:T(8,128)(2,1)S(1)}, bf16[3,64,256]{2,1,0:T(8,128)(2,1)S(1)}, u32[]{:S(2)}, u32[]{:S(2)}) collective-permute-start(bf16[3,64,256]{2,1,0:T(8,128)(2,1)S(1)} %get-tuple-element.39), channel_id=1, source_target_pairs={{0,4},{1,29},{2,6},{3,31},{4,0},{5,25},{6,2},{7,27},{8,12},{9,21},... | collective-permute-start | bytes 294920 | tf_op jit(solution)/shard_map/ppermute | solution.py:318
  5.2 7.5 %collective-permute-start.1 = (bf16[3,64,256]{2,1,0:T(8,128)(2,1)S(1)}, bf16[3,64,256]{2,1,0:T(8,128)(2,1)S(1)}, u32[]{:S(2)}, u32[]{:S(2)}) collective-permute-start(bf16[3,64,256]{2,1,0:T(8,128)(2,1)S(1)} %get-tuple-element.40), channel_id=1, source_target_pairs={{0,8},{1,25},{2,10},{3,27},{4,12},{5,29},{6,14},{7,31},{8,0},{9,17... | collective-permute-start | bytes 294920 | tf_op jit(solution)/shard_map/ppermute | solution.py:318
  6.8 7.9 %collective-permute-start.2 = (bf16[3,64,256]{2,1,0:T(8,128)(2,1)S(1)}, bf16[3,64,256]{2,1,0:T(8,128)(2,1)S(1)}, u32[]{:S(2)}, u32[]{:S(2)}) collective-permute-start(bf16[3,64,256]{2,1,0:T(8,128)(2,1)S(1)} %get-tuple-element.41), channel_id=1, source_target_pairs={{0,12},{1,21},{2,14},{3,23},{4,8},{5,17},{6,10},{7,19},{8,4},{9,29... | collective-permute-start | bytes 294920 | tf_op jit(solution)/shard_map/ppermute | solution.py:318
  6.8 10.4 %collective-permute-start.3 = (bf16[3,64,256]{2,1,0:T(8,128)(2,1)S(1)}, bf16[3,64,256]{2,1,0:T(8,128)(2,1)S(1)}, u32[]{:S(2)}, u32[]{:S(2)}) collective-permute-start(bf16[3,64,256]{2,1,0:T(8,128)(2,1)S(1)} %get-tuple-element.42), channel_id=1, source_target_pairs={{0,28},{1,17},{2,30},{3,19},{4,24},{5,21},{6,26},{7,23},{8,20},{9,... | collective-permute-start | bytes 294920 | tf_op jit(solution)/shard_map/ppermute | solution.py:318
  11.7 7.5 %collective-permute-start.4 = (bf16[3,64,256]{2,1,0:T(8,128)(2,1)S(1)}, bf16[3,64,256]{2,1,0:T(8,128)(2,1)S(1)}, u32[]{:S(2)}, u32[]{:S(2)}) collective-permute-start(bf16[3,64,256]{2,1,0:T(8,128)(2,1)S(1)} %get-tuple-element.43), channel_id=1, source_target_pairs={{0,24},{1,13},{2,26},{3,15},{4,28},{5,9},{6,30},{7,11},{8,16},{9,5... | collective-permute-start | bytes 294920 | tf_op jit(solution)/shard_map/ppermute | solution.py:318
  11.9 12.8 %collective-permute-start.5 = (bf16[3,64,256]{2,1,0:T(8,128)(2,1)S(1)}, bf16[3,64,256]{2,1,0:T(8,128)(2,1)S(1)}, u32[]{:S(2)}, u32[]{:S(2)}) collective-permute-start(bf16[3,64,256]{2,1,0:T(8,128)(2,1)S(1)} %get-tuple-element.44), channel_id=1, source_target_pairs={{0,20},{1,9},{2,22},{3,11},{4,16},{5,13},{6,18},{7,15},{8,28},{9,1... | collective-permute-start | bytes 294920 | tf_op jit(solution)/shard_map/ppermute | solution.py:318
  12.7 12.4 %collective-permute-start.6 = (bf16[3,64,256]{2,1,0:T(8,128)(2,1)S(1)}, bf16[3,64,256]{2,1,0:T(8,128)(2,1)S(1)}, u32[]{:S(2)}, u32[]{:S(2)}) collective-permute-start(bf16[3,64,256]{2,1,0:T(8,128)(2,1)S(1)} %get-tuple-element.45), channel_id=1, source_target_pairs={{0,16},{1,5},{2,18},{3,7},{4,20},{5,1},{6,22},{7,3},{8,24},{9,13},... | collective-permute-start | bytes 294920 | tf_op jit(solution)/shard_map/ppermute | solution.py:318
  29.6 8.1 %collective-permute-start.7 = (bf16[3,64,256]{2,1,0:T(8,128)(2,1)S(1)}, bf16[3,64,256]{2,1,0:T(8,128)(2,1)S(1)}, u32[]{:S(2)}, u32[]{:S(2)}) collective-permute-start(bf16[3,64,256]{2,1,0:T(8,128)(2,1)S(1)} %get-tuple-element.47), channel_id=1, source_target_pairs={{0,4},{1,29},{2,6},{3,31},{4,0},{5,25},{6,2},{7,27},{8,12},{9,21},... | collective-permute-start | bytes 294920 | tf_op jit(solution)/shard_map/ppermute | solution.py:318
  30.9 8.4 %collective-permute-start.8 = (bf16[3,64,256]{2,1,0:T(8,128)(2,1)S(1)}, bf16[3,64,256]{2,1,0:T(8,128)(2,1)S(1)}, u32[]{:S(2)}, u32[]{:S(2)}) collective-permute-start(bf16[3,64,256]{2,1,0:T(8,128)(2,1)S(1)} %get-tuple-element.48), channel_id=1, source_target_pairs={{0,8},{1,25},{2,10},{3,27},{4,12},{5,29},{6,14},{7,31},{8,0},{9,17... | collective-permute-start | bytes 294920 | tf_op jit(solution)/shard_map/ppermute | solution.py:318
  30.9 9.8 %collective-permute-start.9 = (bf16[3,64,256]{2,1,0:T(8,128)(2,1)S(1)}, bf16[3,64,256]{2,1,0:T(8,128)(2,1)S(1)}, u32[]{:S(2)}, u32[]{:S(2)}) collective-permute-start(bf16[3,64,256]{2,1,0:T(8,128)(2,1)S(1)} %get-tuple-element.49), channel_id=1, source_target_pairs={{0,12},{1,21},{2,14},{3,23},{4,8},{5,17},{6,10},{7,19},{8,4},{9,29... | collective-permute-start | bytes 294920 | tf_op jit(solution)/shard_map/ppermute | solution.py:318
  33.1 9.2 %collective-permute-start.10 = (bf16[3,64,256]{2,1,0:T(8,128)(2,1)S(1)}, bf16[3,64,256]{2,1,0:T(8,128)(2,1)S(1)}, u32[]{:S(2)}, u32[]{:S(2)}) collective-permute-start(bf16[3,64,256]{2,1,0:T(8,128)(2,1)S(1)} %get-tuple-element.50), channel_id=1, source_target_pairs={{0,28},{1,17},{2,30},{3,19},{4,24},{5,21},{6,26},{7,23},{8,20},{9,... | collective-permute-start | bytes 294920 | tf_op jit(solution)/shard_map/ppermute | solution.py:318
  36.5 7.8 %collective-permute-start.11 = (bf16[3,64,256]{2,1,0:T(8,128)(2,1)S(1)}, bf16[3,64,256]{2,1,0:T(8,128)(2,1)S(1)}, u32[]{:S(2)}, u32[]{:S(2)}) collective-permute-start(bf16[3,64,256]{2,1,0:T(8,128)(2,1)S(1)} %get-tuple-element.51), channel_id=1, source_target_pairs={{0,24},{1,13},{2,26},{3,15},{4,28},{5,9},{6,30},{7,11},{8,16},{9,5... | collective-permute-start | bytes 294920 | tf_op jit(solution)/shard_map/ppermute | solution.py:318
  37.7 10.5 %collective-permute-start.12 = (bf16[3,64,256]{2,1,0:T(8,128)(2,1)S(1)}, bf16[3,64,256]{2,1,0:T(8,128)(2,1)S(1)}, u32[]{:S(2)}, u32[]{:S(2)}) collective-permute-start(bf16[3,64,256]{2,1,0:T(8,128)(2,1)S(1)} %get-tuple-element.52), channel_id=1, source_target_pairs={{0,20},{1,9},{2,22},{3,11},{4,16},{5,13},{6,18},{7,15},{8,28},{9,1... | collective-permute-start | bytes 294920 | tf_op jit(solution)/shard_map/ppermute | solution.py:318
  39.3 9.0 %collective-permute-start.13 = (bf16[3,64,256]{2,1,0:T(8,128)(2,1)S(1)}, bf16[3,64,256]{2,1,0:T(8,128)(2,1)S(1)}, u32[]{:S(2)}, u32[]{:S(2)}) collective-permute-start(bf16[3,64,256]{2,1,0:T(8,128)(2,1)S(1)} %get-tuple-element.53), channel_id=1, source_target_pairs={{0,16},{1,5},{2,18},{3,7},{4,20},{5,1},{6,22},{7,3},{8,24},{9,13},... | collective-permute-start | bytes 294920 | tf_op jit(solution)/shard_map/ppermute | solution.py:318
  49.0 1.6 %collective-permute-start.14 = (bf16[256,512]{1,0:T(8,128)(2,1)S(1)}, bf16[256,512]{1,0:T(8,128)(2,1)S(1)}, u32[]{:S(2)}, u32[]{:S(2)}) collective-permute-start(bf16[256,512]{1,0:T(8,128)(2,1)S(1)} %get-tuple-element.63), channel_id=1, source_target_pairs={{0,1},{1,0},{2,3},{3,2},{4,5},{5,4},{6,7},{7,6},{8,9},{9,8},{10,11... | collective-permute-start | bytes 786440 | tf_op jit(solution)/shard_map/ppermute | solution.py:305
  50.7 8.4 %collective-permute-start.15 = (bf16[256,512]{1,0:T(8,128)(2,1)S(1)}, bf16[256,512]{1,0:T(8,128)(2,1)S(1)}, u32[]{:S(2)}, u32[]{:S(2)}) collective-permute-start(bf16[256,512]{1,0:T(8,128)(2,1)S(1)} %add_convert_fusion.1), channel_id=1, source_target_pairs={{0,2},{1,3},{2,0},{3,1},{4,6},{5,7},{6,4},{7,5},{8,10},{9,11},{10,... | collective-permute-start | bytes 786440 | tf_op jit(solution)/shard_map/ppermute | solution.py:305
  52.2 6.9 %collective-permute-start.16 = (bf16[256,512]{1,0:T(8,128)(2,1)S(1)}, bf16[256,512]{1,0:T(8,128)(2,1)S(1)}, u32[]{:S(2)}, u32[]{:S(2)}) collective-permute-start(bf16[256,512]{1,0:T(8,128)(2,1)S(1)} %get-tuple-element.66), channel_id=1, source_target_pairs={{0,1},{1,0},{2,3},{3,2},{4,5},{5,4},{6,7},{7,6},{8,9},{9,8},{10,11... | collective-permute-start | bytes 786440 | tf_op jit(solution)/shard_map/ppermute | solution.py:305

commit v8 on v6

--- a/solution.py
+++ b/solution.py
@@ -93,10 +93,18 @@
     return [pltpu.with_memory_space_constraint(array, pltpu.HBM) for array in arrays]
 
 
+def distances(blocks):
+    last = blocks - 1
+    return [last - i // 2 if i % 2 == 0 else 1 + i // 2 for i in range(last)] + [0]
+
+
+def late_steps(blocks):
+    far = [step for step, distance in enumerate(distances(blocks)) if 2 * distance >= blocks]
+    return far[len(far) // 2 :]
+
+
 def by_distance(pieces):
-    last = len(pieces) - 1
-    order = [last - i // 2 if i % 2 == 0 else 1 + i // 2 for i in range(last)]
-    return zip([*order, 0], pieces)
+    return zip(distances(len(pieces)), pieces)
 
 
 def fetch(sources, targets, sems):
@@ -135,8 +143,9 @@
 def conv_kernel(*refs):
     blocks = lax.axis_size("ctx")
     in_refs, sources, refs = refs[:blocks], refs[blocks : blocks + 9], refs[blocks + 9 :]
-    out_refs, held_refs = refs[:blocks], refs[blocks : blocks + 6]
-    in_ref, rows_ref, spec_ref, twid_ref, fwd_ref, inv_ref, sems = refs[blocks + 6 :]
+    late = late_steps(blocks)
+    out_refs, late_refs, held_refs = refs[:blocks], refs[blocks : -13], refs[-13:-7]
+    in_ref, rows_ref, spec_ref, twid_ref, fwd_ref, inv_ref, sems = refs[-7:]
     twid_copy, fwd_copy, inv_copy, *held_copies = fetch(
         sources, (twid_ref, fwd_ref, inv_ref, *held_refs), sems
     )
@@ -238,7 +247,9 @@
             if 0 <= step - depth < groups:
                 stage(step - depth)
     for distance, out_ref in by_distance(out_refs):
-        out_ref[...] = in_ref[me ^ distance]
+        out_ref[...] = in_ref[me ^ distance, : out_ref.shape[0]]
+    for step, late_ref in zip(late, late_refs):
+        late_ref[...] = in_ref[me ^ distances(blocks)[step], 2:]
     for copy in held_copies:
         copy.wait()
 
@@ -261,7 +272,7 @@
     me = lax.axis_index("ctx")
     for distance, ref in by_distance(back_refs):
         for i, slot in enumerate(slots):
-            turn_ref[me ^ distance, i] = ref[slot]
+            turn_ref[me ^ distance, i] = ref[slot % ref.shape[0]]
     return [
         turn_ref[:, i].reshape(blocks * channels, block_len).astype(jnp.float32).T
         for i in range(len(slots))
@@ -292,7 +303,7 @@
 
 def turn_kernel(*refs):
     back_refs, (out_ref, turn_ref) = refs[:-2], refs[-2:]
-    out_ref[...] = natural(back_refs, turn_ref, (2,))[0].astype(jnp.bfloat16)
+    out_ref[...] = natural(back_refs, turn_ref, (-1,))[0].astype(jnp.bfloat16)
 
 
 def exchange(block, axis, distance):
@@ -304,6 +315,13 @@
     return [
         exchange(piece, "ctx", distance) if distance else piece
         for distance, piece in by_distance(pieces)
+    ]
+
+
+def swap_late(pieces, blocks):
+    return [
+        exchange(piece, "ctx", distances(blocks)[step])
+        for step, piece in zip(late_steps(blocks), pieces)
     ]
 
 
@@ -341,10 +359,15 @@
     )
     tables = (twiddle, forward, inverse)
     held = (key_act, value_act, grad_out, w_key, w_query, w_value)
+    late = late_steps(blocks)
     results = pl.pallas_call(
         conv_kernel,
         in_specs=[VMEM] * blocks + [HBM] * 9,
-        out_shape=arrays(blocks, 3, channels, block_len)
+        out_shape=[
+            pltpu.VMEM((2 if step in late else 3, channels, block_len), jnp.bfloat16)
+            for step in range(blocks)
+        ]
+        + arrays(len(late), 1, channels, block_len)
         + [pltpu.VMEM(array.shape, array.dtype) for array in held],
         scratch_shapes=[
             pltpu.VMEM((blocks, 3, channels, block_len), jnp.bfloat16),
@@ -356,7 +379,7 @@
         compiler_params=compiler_params(28),
         name="conv",
     )(*moved, *in_hbm(*tables, *held))
-    back, held = swap(results[:blocks]), results[blocks:]
+    back, late_back, held = swap(results[:blocks]), results[blocks:-6], results[-6:]
     weights = held[3:]
     lhs, to_mate = pl.pallas_call(
         mate_kernel,
@@ -377,9 +400,20 @@
         name="far",
     )(lhs, *weights)
     far = (far + from_mate.astype(jnp.float32)).astype(jnp.bfloat16)
-    far, near, lhs, back = lax.optimization_barrier((far, near, lhs, back))
+    far, near, lhs, back, late_back = lax.optimization_barrier((far, near, lhs, back, late_back))
     from_far = exchange(far, "tp", 2)
     from_near = exchange(near, "tp", 1)
+    own = pl.pallas_call(
+        own_kernel,
+        in_specs=[VMEM] * 4,
+        out_shape=arrays(1, block_len, part, dtype=jnp.float32)[0],
+        compiler_params=compiler_params(16),
+        cost_estimate=block_cost,
+        name="own",
+    )(lhs, *weights)
+    own, late_back = lax.optimization_barrier((own, late_back))
+    for step, piece in zip(late, swap_late(late_back, blocks)):
+        back[step] = piece
     grad_filter = pl.pallas_call(
         turn_kernel,
         in_specs=[VMEM] * blocks,
@@ -389,14 +423,6 @@
         cost_estimate=block_cost,
         name="turn",
     )(*back)
-    own = pl.pallas_call(
-        own_kernel,
-        in_specs=[VMEM] * 4,
-        out_shape=arrays(1, block_len, part, dtype=jnp.float32)[0],
-        compiler_params=compiler_params(16),
-        cost_estimate=block_cost,
-        name="own",
-    )(lhs, *weights)
     total = from_far.astype(jnp.float32) + from_near.astype(jnp.float32) + own
     grad_input = total.astype(jnp.bfloat16)
     return (grad_input, grad_filter)

time: 59.2 us -> 60.5 us (1.022)
  waiting for transfers between devices: 20.3 us -> 21 us
    ppermute x17 -> x19, waiting for transfers between devices: 20.3 us -> 21 us  [exchange(): return lax.ppermute(block, axis, pairs)]
    ppermute x17 -> x19, starting transfers between devices: 28 us -> 28.6 us  [exchange(): return lax.ppermute(block, axis, pairs)]
  transfers between devices with their start and end apart: 17 -> 19, of which waited for: 8 -> 9; matrix products, arithmetic and copies ran while one was open for 0% -> 0% of each run, Pallas kernels for 4% -> 4%
where the time goes in v8:
time: 60.5 us; the launch traced here: 60.4 us
  starting transfers between devices  28.6 us (47%)
  waiting for transfers between devices  21 us (35%)
  Pallas kernels  9.13 us (15%)
  other arithmetic  0.87 us (1%)
  between operations  0.71 us (1%)
    ppermute x19, starting transfers between devices, exchange(): return lax.ppermute(block, axis, pairs)  28.6 us
    ppermute x19, waiting for transfers between devices, exchange(): return lax.ppermute(block, axis, pairs)  21 us
    pallas_call x1, Pallas kernels, per_device(): pl.pallas_call(conv_kernel, in_specs=[VMEM] * blocks + [HBM] * 9, out_sha...  4.48 us
    pallas_call x1, Pallas kernels, per_device(): pl.pallas_call(gate_kernel, in_specs=[HBM] * 5, out_shape=arrays(blocks,...  1.5 us
  transfers between devices with their start and end apart: 19, of which 9 were waited for; matrix products, arithmetic and copies ran while one was open for 0% of the time, Pallas kernels for 4%

profile of v8, /device:TPU:0, one launch (start us, length us, event | category | flops | bytes accessed | tf_op | source)
XLA Modules:
  0.0 60.4 jit_solution(3698028101763407646)
XLA Ops:
  0.6 1.5 %gate.1 = (bf16[3,64,256]{2,1,0:T(8,128)(2,1)S(1)}, bf16[3,64,256]{2,1,0:T(8,128)(2,1)S(1)}, bf16[3,64,256]{2,1,0:T(8,128)(2,1)S(1)}, bf16[3,64,256]{2,1,0:T(8,1...) custom-call(bf16[256,512]{1,0:T(8,128)(2,1)} %refs_0_.1, ...), custom_call_target="tpu_custom_call" | custom-call | tf_op jit(solution)/shard_map/gate/pallas_call | solution.py:343
  2.1 6.1 %collective-permute-start = (bf16[3,64,256]{2,1,0:T(8,128)(2,1)S(1)}, bf16[3,64,256]{2,1,0:T(8,128)(2,1)S(1)}, u32[]{:S(2)}, u32[]{:S(2)}) collective-permute-start(bf16[3,64,256]{2,1,0:T(8,128)(2,1)S(1)} %get-tuple-element.44), channel_id=1, source_target_pairs={{0,28},{4,24},{8,20},{12,16},{16,12},{20,8},{24,4},{28,0},{1,29},{... | collective-permute-start | bytes 294920 | tf_op jit(solution)/shard_map/ppermute | solution.py:311
  8.2 0.5 collective-permute-start.1
  8.7 0.1 collective-permute-start.2
  8.9 0.0 collective-permute-start.3
  8.9 5.2 %collective-permute-start.4 = (bf16[3,64,256]{2,1,0:T(8,128)(2,1)S(1)}, bf16[3,64,256]{2,1,0:T(8,128)(2,1)S(1)}, u32[]{:S(2)}, u32[]{:S(2)}) collective-permute-start(bf16[3,64,256]{2,1,0:T(8,128)(2,1)S(1)} %get-tuple-element.48), channel_id=1, source_target_pairs={{0,20},{4,16},{8,28},{12,24},{16,4},{20,0},{24,12},{28,8},{1,21},{... | collective-permute-start | bytes 294920 | tf_op jit(solution)/shard_map/ppermute | solution.py:311
  14.1 0.0 collective-permute-done.refs_0_
  14.1 1.7 %collective-permute-start.5 = (bf16[3,64,256]{2,1,0:T(8,128)(2,1)S(1)}, bf16[3,64,256]{2,1,0:T(8,128)(2,1)S(1)}, u32[]{:S(2)}, u32[]{:S(2)}) collective-permute-start(bf16[3,64,256]{2,1,0:T(8,128)(2,1)S(1)} %get-tuple-element.49), channel_id=1, source_target_pairs={{0,12},{4,8},{8,4},{12,0},{16,28},{20,24},{24,20},{28,16},{1,13},{... | collective-permute-start | bytes 294920 | tf_op jit(solution)/shard_map/ppermute | solution.py:311
  15.7 0.0 collective-permute-done.1.refs_1_
  15.7 1.5 %collective-permute-start.6 = (bf16[3,64,256]{2,1,0:T(8,128)(2,1)S(1)}, bf16[3,64,256]{2,1,0:T(8,128)(2,1)S(1)}, u32[]{:S(2)}, u32[]{:S(2)}) collective-permute-start(bf16[3,64,256]{2,1,0:T(8,128)(2,1)S(1)} %get-tuple-element.50), channel_id=1, source_target_pairs={{0,16},{4,20},{8,24},{12,28},{16,0},{20,4},{24,8},{28,12},{1,17},{... | collective-permute-start | bytes 294920 | tf_op jit(solution)/shard_map/ppermute | solution.py:311
  17.3 0.0 collective-permute-done.2.refs_2_
  17.3 0.0 collective-permute-done.3.refs_3_
  17.3 5.2 %collective-permute-done.4.refs_4_ = bf16[3,64,256]{2,1,0:T(8,128)(2,1)S(1)} collective-permute-done((bf16[3,64,256]{2,1,0:T(8,128)(2,1)S(1)}, bf16[3,64,256]{2,1,0:T(8,128)(2,1)S(1)}, u32[]{:S(2)}, u32[]{:S(2)}) %collective-permute-start.4) | collective-permute-done | bytes 98336 | tf_op jit(solution)/shard_map/ppermute | solution.py:311
  22.5 0.0 collective-permute-done.5.refs_5_
  22.5 2.4 %collective-permute-done.6.refs_6_ = bf16[3,64,256]{2,1,0:T(8,128)(2,1)S(1)} collective-permute-done((bf16[3,64,256]{2,1,0:T(8,128)(2,1)S(1)}, bf16[3,64,256]{2,1,0:T(8,128)(2,1)S(1)}, u32[]{:S(2)}, u32[]{:S(2)}) %collective-permute-start.6) | collective-permute-done | bytes 98336 | tf_op jit(solution)/shard_map/ppermute | solution.py:311
  24.9 4.5 %conv.1 = (bf16[3,64,256]{2,1,0:T(8,128)(2,1)S(1)}, bf16[3,64,256]{2,1,0:T(8,128)(2,1)S(1)}, bf16[3,64,256]{2,1,0:T(8,128)(2,1)S(1)}, bf16[3,64,256]{2,1,0:T(8,1...) custom-call(bf16[3,64,256]{2,1,0:T(8,128)(2,1)S(1)} %collective-perm, ...), custom_call_target="tpu_custom_call" | custom-call | tf_op jit(solution)/shard_map/conv/pallas_call | solution.py:363
  29.4 0.1 collective-permute-start.11
  29.5 2.9 %collective-permute-start.13 = (bf16[2,64,256]{2,1,0:T(8,128)(2,1)S(1)}, bf16[2,64,256]{2,1,0:T(8,128)(2,1)S(1)}, u32[]{:S(2)}, u32[]{:S(2)}) collective-permute-start(bf16[2,64,256]{2,1,0:T(8,128)(2,1)S(1)} %get-tuple-element.58), channel_id=1, source_target_pairs={{0,16},{4,20},{8,24},{12,28},{16,0},{20,4},{24,8},{28,12},{1,17},{... | collective-permute-start | bytes 196616 | tf_op jit(solution)/shard_map/ppermute | solution.py:311
  32.3 3.5 %collective-permute-start.7 = (bf16[3,64,256]{2,1,0:T(8,128)(2,1)S(1)}, bf16[3,64,256]{2,1,0:T(8,128)(2,1)S(1)}, u32[]{:S(2)}, u32[]{:S(2)}) collective-permute-start(bf16[3,64,256]{2,1,0:T(8,128)(2,1)S(1)} %get-tuple-element.52), channel_id=1, source_target_pairs={{0,28},{4,24},{8,20},{12,16},{16,12},{20,8},{24,4},{28,0},{1,29},{... | collective-permute-start | bytes 294920 | tf_op jit(solution)/shard_map/ppermute | solution.py:311
  35.8 0.5 collective-permute-start.8
  36.3 1.3 %collective-permute-start.9 = (bf16[3,64,256]{2,1,0:T(8,128)(2,1)S(1)}, bf16[3,64,256]{2,1,0:T(8,128)(2,1)S(1)}, u32[]{:S(2)}, u32[]{:S(2)}) collective-permute-start(bf16[3,64,256]{2,1,0:T(8,128)(2,1)S(1)} %get-tuple-element.54), channel_id=1, source_target_pairs={{0,24},{4,28},{8,16},{12,20},{16,8},{20,12},{24,0},{28,4},{1,25},{... | collective-permute-start | bytes 294920 | tf_op jit(solution)/shard_map/ppermute | solution.py:311
  37.6 3.3 %collective-permute-done.11.refs_4_ = bf16[2,64,256]{2,1,0:T(8,128)(2,1)S(1)} collective-permute-done((bf16[2,64,256]{2,1,0:T(8,128)(2,1)S(1)}, bf16[2,64,256]{2,1,0:T(8,128)(2,1)S(1)}, u32[]{:S(2)}, u32[]{:S(2)}) %collective-permute-start.11) | collective-permute-done | bytes 65568 | tf_op jit(solution)/shard_map/ppermute | solution.py:311
  40.9 0.0 collective-permute-start.10
  40.9 0.7 %collective-permute-done.13.refs_6_ = bf16[2,64,256]{2,1,0:T(8,128)(2,1)S(1)} collective-permute-done((bf16[2,64,256]{2,1,0:T(8,128)(2,1)S(1)}, bf16[2,64,256]{2,1,0:T(8,128)(2,1)S(1)}, u32[]{:S(2)}, u32[]{:S(2)}) %collective-permute-start.13) | collective-permute-done | bytes 65568 | tf_op jit(solution)/shard_map/ppermute | solution.py:311
  41.6 0.0 collective-permute-start.12
  41.6 0.0 collective-permute-done.7.refs_0_
  41.6 0.0 collective-permute-done.8.refs_1_
  41.6 1.6 %collective-permute-done.9.refs_2_ = bf16[3,64,256]{2,1,0:T(8,128)(2,1)S(1)} collective-permute-done((bf16[3,64,256]{2,1,0:T(8,128)(2,1)S(1)}, bf16[3,64,256]{2,1,0:T(8,128)(2,1)S(1)}, u32[]{:S(2)}, u32[]{:S(2)}) %collective-permute-start.9) | collective-permute-done | bytes 98336 | tf_op jit(solution)/shard_map/ppermute | solution.py:311
  43.3 2.3 %collective-permute-done.10.refs_3_ = bf16[3,64,256]{2,1,0:T(8,128)(2,1)S(1)} collective-permute-done((bf16[3,64,256]{2,1,0:T(8,128)(2,1)S(1)}, bf16[3,64,256]{2,1,0:T(8,128)(2,1)S(1)}, u32[]{:S(2)}, u32[]{:S(2)}) %collective-permute-start.10) | collective-permute-done | bytes 98336 | tf_op jit(solution)/shard_map/ppermute | solution.py:311
  45.5 1.6 %collective-permute-done.12.refs_5_ = bf16[3,64,256]{2,1,0:T(8,128)(2,1)S(1)} collective-permute-done((bf16[3,64,256]{2,1,0:T(8,128)(2,1)S(1)}, bf16[3,64,256]{2,1,0:T(8,128)(2,1)S(1)}, u32[]{:S(2)}, u32[]{:S(2)}) %collective-permute-start.12) | collective-permute-done | bytes 98336 | tf_op jit(solution)/shard_map/ppermute | solution.py:311
  47.1 0.7 %mate.1 = (bf16[3,256,512]{2,1,0:T(8,128)(2,1)S(1)}, bf16[256,512]{1,0:T(8,128)(2,1)S(1)}) custom-call(bf16[3,64,256]{2,1,0:T(8,128)(2,1)S(1)} %collective-permute-done.7.refs_0_, bf16[3,64,256]{2,1,0:T(8,128)(2,1)S(1)} %collective-permute-done.8.refs_1_, bf16[3,64,256]{2,1,0:T(8,128)(2,1)S(1)} %collective-permute-done.9.refs_2_, ...), custom_call_target="tpu_custom_call" | custom-call | flops 805306368 | bytes 4194304 | tf_op jit(solution)/shard_map/mate/pallas_call | solution.py:384
  47.8 0.1 collective-permute-start.14
  47.9 1.0 %far.1 = (f32[256,512]{1,0:T(8,128)S(1)}, bf16[256,512]{1,0:T(8,128)(2,1)S(1)}) custom-call(bf16[3,256,512]{2,1,0:T(8,128)(2,1)S(1)} %get-tuple-element.74.lhs_ref, bf16[2048,512]{1,0:T(8,128)(2,1)S(1)} %get-tuple-element.63.refs_11_.wk_ref, bf16[2048,512]{1,0:T(8,128)(2,1)S(1)} %get-tuple-element.64.refs_12_.wq_ref, ...), custom_call_target="tpu_custom_call" | custom-call | flops 805306368 | bytes 4194304 | tf_op jit(solution)/shard_map/far/pallas_call | solution.py:394
  48.9 0.5 collective-permute-done.14
  49.4 0.1 add_convert_fusion.1
  49.5 1.6 %collective-permute-start.15 = (bf16[256,512]{1,0:T(8,128)(2,1)S(1)}, bf16[256,512]{1,0:T(8,128)(2,1)S(1)}, u32[]{:S(2)}, u32[]{:S(2)}) collective-permute-start(bf16[256,512]{1,0:T(8,128)(2,1)S(1)} %add_convert_fusion.1), channel_id=1, source_target_pairs={{0,2},{1,3},{2,0},{3,1},{4,6},{5,7},{6,4},{7,5},{8,10},{9,11},{10,... | collective-permute-start | bytes 786440 | tf_op jit(solution)/shard_map/ppermute | solution.py:311
  51.0 0.0 collective-permute-start.16
  51.0 0.6 own.1
  51.6 0.6 collective-permute-start.17
  52.2 3.1 %collective-permute-start.18 = (bf16[1,64,256]{2,1,0:T(8,128)(2,1)S(1)}, bf16[1,64,256]{2,1,0:T(8,128)(2,1)S(1)}, u32[]{:S(2)}, u32[]{:S(2)}) collective-permute-start(bf16[1,64,256]{2,1,0:T(8,128)(2,1)S(1)} %get-tuple-element.84), channel_id=1, source_target_pairs={{0,16},{4,20},{8,24},{12,28},{16,0},{20,4},{24,8},{28,12},{1,17},{... | collective-permute-start | bytes 98312 | tf_op jit(solution)/shard_map/ppermute | solution.py:311
  55.3 3.4 %collective-permute-done.17.refs_4_ = bf16[1,64,256]{2,1,0:T(8,128)(2,1)S(1)} collective-permute-done((bf16[1,64,256]{2,1,0:T(8,128)(2,1)S(1)}, bf16[1,64,256]{2,1,0:T(8,128)(2,1)S(1)}, u32[]{:S(2)}, u32[]{:S(2)}) %collective-permute-start.17) | collective-permute-done | bytes 32800 | tf_op jit(solution)/shard_map/ppermute | solution.py:311
  58.7 0.0 collective-permute-done.18.refs_6_
  58.7 0.9 %turn.1 = bf16[256,512]{1,0:T(8,128)(2,1)} custom-call(bf16[3,64,256]{2,1,0:T(8,128)(2,1)S(1)} %collective-permute-done.7.refs_0_, bf16[3,64,256]{2,1,0:T(8,128)(2,1)S(1)} %collective-permute-done.8.refs_1_, bf16[3,64,256]{2,1,0:T(8,128)(2,1)S(1)} %collective-permute-done.9.refs_2_, bf16[3,64,256]{2,1,0:T(8,128)(2,1)S(1)} %collective-permute-done.10.refs_3_, ...), custom_call_target="tpu_custom_call" | custom-call | flops 805306368 | bytes 4194304 | tf_op jit(solution)/shard_map/turn/pallas_call | solution.py:417
  59.6 0.0 collective-permute-done.15
  59.6 0.0 collective-permute-done.16
  59.6 0.8 %add_convert_fusion = bf16[256,512]{1,0:T(8,128)(2,1)} fusion(f32[256,512]{1,0:T(8,128)S(1)} %own.1, bf16[256,512]{1,0:T(8,128)(2,1)S(1)} %collective-permute-done.16, bf16[256,512]{1,0:T(8,128)(2,1)S(1)} %collective-permute-done.15), kind=kLoop, calls=%fused_computation | loop fusion | flops 655360 | bytes 1310720 | tf_op jit(solution)/shard_map/convert_element_type | solution.py:427
Async XLA Ops:
  2.1 11.9 %collective-permute-start = (bf16[3,64,256]{2,1,0:T(8,128)(2,1)S(1)}, bf16[3,64,256]{2,1,0:T(8,128)(2,1)S(1)}, u32[]{:S(2)}, u32[]{:S(2)}) collective-permute-start(bf16[3,64,256]{2,1,0:T(8,128)(2,1)S(1)} %get-tuple-element.44), channel_id=1, source_target_pairs={{0,28},{4,24},{8,20},{12,16},{16,12},{20,8},{24,4},{28,0},{1,29},{... | collective-permute-start | bytes 294920 | tf_op jit(solution)/shard_map/ppermute | solution.py:311
  8.2 7.5 %collective-permute-start.1 = (bf16[3,64,256]{2,1,0:T(8,128)(2,1)S(1)}, bf16[3,64,256]{2,1,0:T(8,128)(2,1)S(1)}, u32[]{:S(2)}, u32[]{:S(2)}) collective-permute-start(bf16[3,64,256]{2,1,0:T(8,128)(2,1)S(1)} %get-tuple-element.45), channel_id=1, source_target_pairs={{0,4},{4,0},{8,12},{12,8},{16,20},{20,16},{24,28},{28,24},{1,5},{5... | collective-permute-start | bytes 294920 | tf_op jit(solution)/shard_map/ppermute | solution.py:311
  8.7 8.5 %collective-permute-start.2 = (bf16[3,64,256]{2,1,0:T(8,128)(2,1)S(1)}, bf16[3,64,256]{2,1,0:T(8,128)(2,1)S(1)}, u32[]{:S(2)}, u32[]{:S(2)}) collective-permute-start(bf16[3,64,256]{2,1,0:T(8,128)(2,1)S(1)} %get-tuple-element.46), channel_id=1, source_target_pairs={{0,24},{4,28},{8,16},{12,20},{16,8},{20,12},{24,0},{28,4},{1,25},{... | collective-permute-start | bytes 294920 | tf_op jit(solution)/shard_map/ppermute | solution.py:311
  8.9 8.4 %collective-permute-start.3 = (bf16[3,64,256]{2,1,0:T(8,128)(2,1)S(1)}, bf16[3,64,256]{2,1,0:T(8,128)(2,1)S(1)}, u32[]{:S(2)}, u32[]{:S(2)}) collective-permute-start(bf16[3,64,256]{2,1,0:T(8,128)(2,1)S(1)} %get-tuple-element.47), channel_id=1, source_target_pairs={{0,8},{4,12},{8,0},{12,4},{16,24},{20,28},{24,16},{28,20},{1,9},{5... | collective-permute-start | bytes 294920 | tf_op jit(solution)/shard_map/ppermute | solution.py:311
  8.9 13.6 %collective-permute-start.4 = (bf16[3,64,256]{2,1,0:T(8,128)(2,1)S(1)}, bf16[3,64,256]{2,1,0:T(8,128)(2,1)S(1)}, u32[]{:S(2)}, u32[]{:S(2)}) collective-permute-start(bf16[3,64,256]{2,1,0:T(8,128)(2,1)S(1)} %get-tuple-element.48), channel_id=1, source_target_pairs={{0,20},{4,16},{8,28},{12,24},{16,4},{20,0},{24,12},{28,8},{1,21},{... | collective-permute-start | bytes 294920 | tf_op jit(solution)/shard_map/ppermute | solution.py:311
  14.1 8.4 %collective-permute-start.5 = (bf16[3,64,256]{2,1,0:T(8,128)(2,1)S(1)}, bf16[3,64,256]{2,1,0:T(8,128)(2,1)S(1)}, u32[]{:S(2)}, u32[]{:S(2)}) collective-permute-start(bf16[3,64,256]{2,1,0:T(8,128)(2,1)S(1)} %get-tuple-element.49), channel_id=1, source_target_pairs={{0,12},{4,8},{8,4},{12,0},{16,28},{20,24},{24,20},{28,16},{1,13},{... | collective-permute-start | bytes 294920 | tf_op jit(solution)/shard_map/ppermute | solution.py:311
  15.7 9.2 %collective-permute-start.6 = (bf16[3,64,256]{2,1,0:T(8,128)(2,1)S(1)}, bf16[3,64,256]{2,1,0:T(8,128)(2,1)S(1)}, u32[]{:S(2)}, u32[]{:S(2)}) collective-permute-start(bf16[3,64,256]{2,1,0:T(8,128)(2,1)S(1)} %get-tuple-element.50), channel_id=1, source_target_pairs={{0,16},{4,20},{8,24},{12,28},{16,0},{20,4},{24,8},{28,12},{1,17},{... | collective-permute-start | bytes 294920 | tf_op jit(solution)/shard_map/ppermute | solution.py:311
  29.4 11.5 %collective-permute-start.11 = (bf16[2,64,256]{2,1,0:T(8,128)(2,1)S(1)}, bf16[2,64,256]{2,1,0:T(8,128)(2,1)S(1)}, u32[]{:S(2)}, u32[]{:S(2)}) collective-permute-start(bf16[2,64,256]{2,1,0:T(8,128)(2,1)S(1)} %get-tuple-element.56), channel_id=1, source_target_pairs={{0,20},{4,16},{8,28},{12,24},{16,4},{20,0},{24,12},{28,8},{1,21},{... | collective-permute-start | bytes 196616 | tf_op jit(solution)/shard_map/ppermute | solution.py:311
  29.5 12.1 %collective-permute-start.13 = (bf16[2,64,256]{2,1,0:T(8,128)(2,1)S(1)}, bf16[2,64,256]{2,1,0:T(8,128)(2,1)S(1)}, u32[]{:S(2)}, u32[]{:S(2)}) collective-permute-start(bf16[2,64,256]{2,1,0:T(8,128)(2,1)S(1)} %get-tuple-element.58), channel_id=1, source_target_pairs={{0,16},{4,20},{8,24},{12,28},{16,0},{20,4},{24,8},{28,12},{1,17},{... | collective-permute-start | bytes 196616 | tf_op jit(solution)/shard_map/ppermute | solution.py:311
  32.3 9.3 %collective-permute-start.7 = (bf16[3,64,256]{2,1,0:T(8,128)(2,1)S(1)}, bf16[3,64,256]{2,1,0:T(8,128)(2,1)S(1)}, u32[]{:S(2)}, u32[]{:S(2)}) collective-permute-start(bf16[3,64,256]{2,1,0:T(8,128)(2,1)S(1)} %get-tuple-element.52), channel_id=1, source_target_pairs={{0,28},{4,24},{8,20},{12,16},{16,12},{20,8},{24,4},{28,0},{1,29},{... | collective-permute-start | bytes 294920 | tf_op jit(solution)/shard_map/ppermute | solution.py:311
  35.8 5.8 %collective-permute-start.8 = (bf16[3,64,256]{2,1,0:T(8,128)(2,1)S(1)}, bf16[3,64,256]{2,1,0:T(8,128)(2,1)S(1)}, u32[]{:S(2)}, u32[]{:S(2)}) collective-permute-start(bf16[3,64,256]{2,1,0:T(8,128)(2,1)S(1)} %get-tuple-element.53), channel_id=1, source_target_pairs={{0,4},{4,0},{8,12},{12,8},{16,20},{20,16},{24,28},{28,24},{1,5},{5... | collective-permute-start | bytes 294920 | tf_op jit(solution)/shard_map/ppermute | solution.py:311
  36.3 6.9 %collective-permute-start.9 = (bf16[3,64,256]{2,1,0:T(8,128)(2,1)S(1)}, bf16[3,64,256]{2,1,0:T(8,128)(2,1)S(1)}, u32[]{:S(2)}, u32[]{:S(2)}) collective-permute-start(bf16[3,64,256]{2,1,0:T(8,128)(2,1)S(1)} %get-tuple-element.54), channel_id=1, source_target_pairs={{0,24},{4,28},{8,16},{12,20},{16,8},{20,12},{24,0},{28,4},{1,25},{... | collective-permute-start | bytes 294920 | tf_op jit(solution)/shard_map/ppermute | solution.py:311
  40.9 4.6 %collective-permute-start.10 = (bf16[3,64,256]{2,1,0:T(8,128)(2,1)S(1)}, bf16[3,64,256]{2,1,0:T(8,128)(2,1)S(1)}, u32[]{:S(2)}, u32[]{:S(2)}) collective-permute-start(bf16[3,64,256]{2,1,0:T(8,128)(2,1)S(1)} %get-tuple-element.55), channel_id=1, source_target_pairs={{0,8},{4,12},{8,0},{12,4},{16,24},{20,28},{24,16},{28,20},{1,9},{5... | collective-permute-start | bytes 294920 | tf_op jit(solution)/shard_map/ppermute | solution.py:311
  41.6 5.5 %collective-permute-start.12 = (bf16[3,64,256]{2,1,0:T(8,128)(2,1)S(1)}, bf16[3,64,256]{2,1,0:T(8,128)(2,1)S(1)}, u32[]{:S(2)}, u32[]{:S(2)}) collective-permute-start(bf16[3,64,256]{2,1,0:T(8,128)(2,1)S(1)} %get-tuple-element.57), channel_id=1, source_target_pairs={{0,12},{4,8},{8,4},{12,0},{16,28},{20,24},{24,20},{28,16},{1,13},{... | collective-permute-start | bytes 294920 | tf_op jit(solution)/shard_map/ppermute | solution.py:311
  47.8 1.6 %collective-permute-start.14 = (bf16[256,512]{1,0:T(8,128)(2,1)S(1)}, bf16[256,512]{1,0:T(8,128)(2,1)S(1)}, u32[]{:S(2)}, u32[]{:S(2)}) collective-permute-start(bf16[256,512]{1,0:T(8,128)(2,1)S(1)} %get-tuple-element.68), channel_id=1, source_target_pairs={{0,1},{1,0},{2,3},{3,2},{4,5},{5,4},{6,7},{7,6},{8,9},{9,8},{10,11... | collective-permute-start | bytes 786440 | tf_op jit(solution)/shard_map/ppermute | solution.py:311
  49.5 10.1 %collective-permute-start.15 = (bf16[256,512]{1,0:T(8,128)(2,1)S(1)}, bf16[256,512]{1,0:T(8,128)(2,1)S(1)}, u32[]{:S(2)}, u32[]{:S(2)}) collective-permute-start(bf16[256,512]{1,0:T(8,128)(2,1)S(1)} %add_convert_fusion.1), channel_id=1, source_target_pairs={{0,2},{1,3},{2,0},{3,1},{4,6},{5,7},{6,4},{7,5},{8,10},{9,11},{10,... | collective-permute-start | bytes 786440 | tf_op jit(solution)/shard_map/ppermute | solution.py:311
  51.0 8.6 %collective-permute-start.16 = (bf16[256,512]{1,0:T(8,128)(2,1)S(1)}, bf16[256,512]{1,0:T(8,128)(2,1)S(1)}, u32[]{:S(2)}, u32[]{:S(2)}) collective-permute-start(bf16[256,512]{1,0:T(8,128)(2,1)S(1)} %get-tuple-element.73), channel_id=1, source_target_pairs={{0,1},{1,0},{2,3},{3,2},{4,5},{5,4},{6,7},{7,6},{8,9},{9,8},{10,11... | collective-permute-start | bytes 786440 | tf_op jit(solution)/shard_map/ppermute | solution.py:311
  51.6 7.1 %collective-permute-start.17 = (bf16[1,64,256]{2,1,0:T(8,128)(2,1)S(1)}, bf16[1,64,256]{2,1,0:T(8,128)(2,1)S(1)}, u32[]{:S(2)}, u32[]{:S(2)}) collective-permute-start(bf16[1,64,256]{2,1,0:T(8,128)(2,1)S(1)} %get-tuple-element.82), channel_id=1, source_target_pairs={{0,20},{4,16},{8,28},{12,24},{16,4},{20,0},{24,12},{28,8},{1,21},{... | collective-permute-start | bytes 98312 | tf_op jit(solution)/shard_map/ppermute | solution.py:311
  52.2 6.5 %collective-permute-start.18 = (bf16[1,64,256]{2,1,0:T(8,128)(2,1)S(1)}, bf16[1,64,256]{2,1,0:T(8,128)(2,1)S(1)}, u32[]{:S(2)}, u32[]{:S(2)}) collective-permute-start(bf16[1,64,256]{2,1,0:T(8,128)(2,1)S(1)} %get-tuple-element.84), channel_id=1, source_target_pairs={{0,16},{4,20},{8,24},{12,28},{16,0},{20,4},{24,8},{28,12},{1,17},{... | collective-permute-start | bytes 98312 | tf_op jit(solution)/shard_map/ppermute | solution.py:311

commit v9 on v8

--- a/solution.py
+++ b/solution.py
@@ -100,7 +100,7 @@
 
 def late_steps(blocks):
     far = [step for step, distance in enumerate(distances(blocks)) if 2 * distance >= blocks]
-    return far[len(far) // 2 :]
+    return far[: len(far) // 2]
 
 
 def by_distance(pieces):
@@ -302,7 +302,10 @@
 
 
 def turn_kernel(*refs):
-    back_refs, (out_ref, turn_ref) = refs[:-2], refs[-2:]
+    blocks = lax.axis_size("ctx")
+    back_refs, late_refs, (out_ref, turn_ref) = list(refs[:blocks]), refs[blocks:-2], refs[-2:]
+    for step, ref in zip(late_steps(blocks), late_refs):
+        back_refs[step] = ref
     out_ref[...] = natural(back_refs, turn_ref, (-1,))[0].astype(jnp.bfloat16)
 
 
@@ -400,7 +403,7 @@
         name="far",
     )(lhs, *weights)
     far = (far + from_mate.astype(jnp.float32)).astype(jnp.bfloat16)
-    far, near, lhs, back, late_back = lax.optimization_barrier((far, near, lhs, back, late_back))
+    far, near, lhs, late_back = lax.optimization_barrier((far, near, lhs, late_back))
     from_far = exchange(far, "tp", 2)
     from_near = exchange(near, "tp", 1)
     own = pl.pallas_call(
@@ -412,17 +415,15 @@
         name="own",
     )(lhs, *weights)
     own, late_back = lax.optimization_barrier((own, late_back))
-    for step, piece in zip(late, swap_late(late_back, blocks)):
-        back[step] = piece
     grad_filter = pl.pallas_call(
         turn_kernel,
-        in_specs=[VMEM] * blocks,
+        in_specs=[VMEM] * (blocks + len(late)),
         out_shape=jax.ShapeDtypeStruct((block_len, width), jnp.bfloat16),
         scratch_shapes=[pltpu.VMEM((blocks, 1, channels, block_len), jnp.bfloat16)],
         compiler_params=compiler_params(16),
         cost_estimate=block_cost,
         name="turn",
-    )(*back)
+    )(*back, *swap_late(late_back, blocks))
     total = from_far.astype(jnp.float32) + from_near.astype(jnp.float32) + own
     grad_input = total.astype(jnp.bfloat16)
     return (grad_input, grad_filter)

time: 60.5 us -> 60.9 us (level)
  starting transfers between devices: 28.6 us -> 32.9 us
  waiting for transfers between devices: 21 us -> 17.2 us
    ppermute x19, starting transfers between devices: 28.6 us -> 32.9 us  [exchange(): return lax.ppermute(block, axis, pairs)]
    ppermute x19, waiting for transfers between devices: 21 us -> 17.2 us  [exchange(): return lax.ppermute(block, axis, pairs)]
  transfers between devices with their start and end apart: 19 -> 19, of which waited for: 9 -> 8; matrix products, arithmetic and copies ran while one was open for 0% -> 0% of each run, Pallas kernels for 4% -> 4%
where the time goes in v9:
time: 60.9 us; the launch traced here: 60.8 us
  starting transfers between devices  32.9 us (54%)
  waiting for transfers between devices  17.2 us (28%)
  Pallas kernels  9.13 us (15%)
  other arithmetic  0.87 us (1%)
  between operations  0.7 us (1%)
    ppermute x19, starting transfers between devices, exchange(): return lax.ppermute(block, axis, pairs)  32.9 us
    ppermute x19, waiting for transfers between devices, exchange(): return lax.ppermute(block, axis, pairs)  17.2 us
    pallas_call x1, Pallas kernels, per_device(): pl.pallas_call(conv_kernel, in_specs=[VMEM] * blocks + [HBM] * 9, out_sha...  4.48 us
    pallas_call x1, Pallas kernels, per_device(): pl.pallas_call(gate_kernel, in_specs=[HBM] * 5, out_shape=arrays(blocks,...  1.5 us
  transfers between devices with their start and end apart: 19, of which 8 were waited for; matrix products, arithmetic and copies ran while one was open for 0% of the time, Pallas kernels for 4%

profile of v9, /device:TPU:0, one launch (start us, length us, event | category | flops | bytes accessed | tf_op | source)
XLA Modules:
  0.0 60.8 jit_solution(14758774135082415609)
XLA Ops:
  0.6 1.5 %gate.1 = (bf16[3,64,256]{2,1,0:T(8,128)(2,1)S(1)}, bf16[3,64,256]{2,1,0:T(8,128)(2,1)S(1)}, bf16[3,64,256]{2,1,0:T(8,128)(2,1)S(1)}, bf16[3,64,256]{2,1,0:T(8,1...) custom-call(bf16[256,512]{1,0:T(8,128)(2,1)} %refs_0_.1, ...), custom_call_target="tpu_custom_call" | custom-call | tf_op jit(solution)/shard_map/gate/pallas_call | solution.py:346
  2.1 6.1 %collective-permute-start = (bf16[3,64,256]{2,1,0:T(8,128)(2,1)S(1)}, bf16[3,64,256]{2,1,0:T(8,128)(2,1)S(1)}, u32[]{:S(2)}, u32[]{:S(2)}) collective-permute-start(bf16[3,64,256]{2,1,0:T(8,128)(2,1)S(1)} %get-tuple-element.38), channel_id=1, source_target_pairs={{0,28},{4,24},{8,20},{12,16},{16,12},{20,8},{24,4},{28,0},{1,29},{... | collective-permute-start | bytes 294920 | tf_op jit(solution)/shard_map/ppermute | solution.py:314
  8.2 0.5 collective-permute-start.1
  8.7 0.1 collective-permute-start.2
  8.9 0.0 collective-permute-start.3
  8.9 5.2 %collective-permute-start.4 = (bf16[3,64,256]{2,1,0:T(8,128)(2,1)S(1)}, bf16[3,64,256]{2,1,0:T(8,128)(2,1)S(1)}, u32[]{:S(2)}, u32[]{:S(2)}) collective-permute-start(bf16[3,64,256]{2,1,0:T(8,128)(2,1)S(1)} %get-tuple-element.42), channel_id=1, source_target_pairs={{0,20},{4,16},{8,28},{12,24},{16,4},{20,0},{24,12},{28,8},{1,21},{... | collective-permute-start | bytes 294920 | tf_op jit(solution)/shard_map/ppermute | solution.py:314
  14.1 0.0 collective-permute-done.refs_0_
  14.1 1.7 %collective-permute-start.5 = (bf16[3,64,256]{2,1,0:T(8,128)(2,1)S(1)}, bf16[3,64,256]{2,1,0:T(8,128)(2,1)S(1)}, u32[]{:S(2)}, u32[]{:S(2)}) collective-permute-start(bf16[3,64,256]{2,1,0:T(8,128)(2,1)S(1)} %get-tuple-element.43), channel_id=1, source_target_pairs={{0,12},{4,8},{8,4},{12,0},{16,28},{20,24},{24,20},{28,16},{1,13},{... | collective-permute-start | bytes 294920 | tf_op jit(solution)/shard_map/ppermute | solution.py:314
  15.7 0.0 collective-permute-done.1.refs_1_
  15.7 1.5 %collective-permute-start.6 = (bf16[3,64,256]{2,1,0:T(8,128)(2,1)S(1)}, bf16[3,64,256]{2,1,0:T(8,128)(2,1)S(1)}, u32[]{:S(2)}, u32[]{:S(2)}) collective-permute-start(bf16[3,64,256]{2,1,0:T(8,128)(2,1)S(1)} %get-tuple-element.44), channel_id=1, source_target_pairs={{0,16},{4,20},{8,24},{12,28},{16,0},{20,4},{24,8},{28,12},{1,17},{... | collective-permute-start | bytes 294920 | tf_op jit(solution)/shard_map/ppermute | solution.py:314
  17.3 0.0 collective-permute-done.2.refs_2_
  17.3 0.0 collective-permute-done.3.refs_3_
  17.3 5.2 %collective-permute-done.4.refs_4_ = bf16[3,64,256]{2,1,0:T(8,128)(2,1)S(1)} collective-permute-done((bf16[3,64,256]{2,1,0:T(8,128)(2,1)S(1)}, bf16[3,64,256]{2,1,0:T(8,128)(2,1)S(1)}, u32[]{:S(2)}, u32[]{:S(2)}) %collective-permute-start.4) | collective-permute-done | bytes 98336 | tf_op jit(solution)/shard_map/ppermute | solution.py:314
  22.5 0.0 collective-permute-done.5.refs_5_
  22.5 2.4 %collective-permute-done.6.refs_6_ = bf16[3,64,256]{2,1,0:T(8,128)(2,1)S(1)} collective-permute-done((bf16[3,64,256]{2,1,0:T(8,128)(2,1)S(1)}, bf16[3,64,256]{2,1,0:T(8,128)(2,1)S(1)}, u32[]{:S(2)}, u32[]{:S(2)}) %collective-permute-start.6) | collective-permute-done | bytes 98336 | tf_op jit(solution)/shard_map/ppermute | solution.py:314
  24.9 4.5 %conv.1 = (bf16[2,64,256]{2,1,0:T(8,128)(2,1)S(1)}, bf16[3,64,256]{2,1,0:T(8,128)(2,1)S(1)}, bf16[2,64,256]{2,1,0:T(8,128)(2,1)S(1)}, bf16[3,64,256]{2,1,0:T(8,1...) custom-call(bf16[3,64,256]{2,1,0:T(8,128)(2,1)S(1)} %collective-perm, ...), custom_call_target="tpu_custom_call" | custom-call | tf_op jit(solution)/shard_map/conv/pallas_call | solution.py:366
  29.4 2.6 %collective-permute-start.7 = (bf16[2,64,256]{2,1,0:T(8,128)(2,1)S(1)}, bf16[2,64,256]{2,1,0:T(8,128)(2,1)S(1)}, u32[]{:S(2)}, u32[]{:S(2)}) collective-permute-start(bf16[2,64,256]{2,1,0:T(8,128)(2,1)S(1)} %get-tuple-element.46), channel_id=1, source_target_pairs={{0,28},{4,24},{8,20},{12,16},{16,12},{20,8},{24,4},{28,0},{1,29},{... | collective-permute-start | bytes 196616 | tf_op jit(solution)/shard_map/ppermute | solution.py:314
  32.0 1.3 %collective-permute-start.9 = (bf16[2,64,256]{2,1,0:T(8,128)(2,1)S(1)}, bf16[2,64,256]{2,1,0:T(8,128)(2,1)S(1)}, u32[]{:S(2)}, u32[]{:S(2)}) collective-permute-start(bf16[2,64,256]{2,1,0:T(8,128)(2,1)S(1)} %get-tuple-element.48), channel_id=1, source_target_pairs={{0,24},{4,28},{8,16},{12,20},{16,8},{20,12},{24,0},{28,4},{1,25},{... | collective-permute-start | bytes 196616 | tf_op jit(solution)/shard_map/ppermute | solution.py:314
  33.2 1.5 %collective-permute-start.8 = (bf16[3,64,256]{2,1,0:T(8,128)(2,1)S(1)}, bf16[3,64,256]{2,1,0:T(8,128)(2,1)S(1)}, u32[]{:S(2)}, u32[]{:S(2)}) collective-permute-start(bf16[3,64,256]{2,1,0:T(8,128)(2,1)S(1)} %get-tuple-element.47), channel_id=1, source_target_pairs={{0,4},{4,0},{8,12},{12,8},{16,20},{20,16},{24,28},{28,24},{1,5},{5... | collective-permute-start | bytes 294920 | tf_op jit(solution)/shard_map/ppermute | solution.py:314
  34.7 0.0 collective-permute-start.10
  34.7 3.1 %collective-permute-start.11 = (bf16[3,64,256]{2,1,0:T(8,128)(2,1)S(1)}, bf16[3,64,256]{2,1,0:T(8,128)(2,1)S(1)}, u32[]{:S(2)}, u32[]{:S(2)}) collective-permute-start(bf16[3,64,256]{2,1,0:T(8,128)(2,1)S(1)} %get-tuple-element.50), channel_id=1, source_target_pairs={{0,20},{4,16},{8,28},{12,24},{16,4},{20,0},{24,12},{28,8},{1,21},{... | collective-permute-start | bytes 294920 | tf_op jit(solution)/shard_map/ppermute | solution.py:314
  37.8 0.0 collective-permute-done.7.refs_0_
  37.8 0.9 %collective-permute-start.12 = (bf16[3,64,256]{2,1,0:T(8,128)(2,1)S(1)}, bf16[3,64,256]{2,1,0:T(8,128)(2,1)S(1)}, u32[]{:S(2)}, u32[]{:S(2)}) collective-permute-start(bf16[3,64,256]{2,1,0:T(8,128)(2,1)S(1)} %get-tuple-element.51), channel_id=1, source_target_pairs={{0,12},{4,8},{8,4},{12,0},{16,28},{20,24},{24,20},{28,16},{1,13},{... | collective-permute-start | bytes 294920 | tf_op jit(solution)/shard_map/ppermute | solution.py:314
  38.7 0.0 collective-permute-done.9.refs_2_
  38.7 1.9 %collective-permute-start.13 = (bf16[3,64,256]{2,1,0:T(8,128)(2,1)S(1)}, bf16[3,64,256]{2,1,0:T(8,128)(2,1)S(1)}, u32[]{:S(2)}, u32[]{:S(2)}) collective-permute-start(bf16[3,64,256]{2,1,0:T(8,128)(2,1)S(1)} %get-tuple-element.52), channel_id=1, source_target_pairs={{0,16},{4,20},{8,24},{12,28},{16,0},{20,4},{24,8},{28,12},{1,17},{... | collective-permute-start | bytes 294920 | tf_op jit(solution)/shard_map/ppermute | solution.py:314
  40.6 0.0 collective-permute-done.8.refs_1_
  40.6 1.9 %collective-permute-done.10.refs_3_ = bf16[3,64,256]{2,1,0:T(8,128)(2,1)S(1)} collective-permute-done((bf16[3,64,256]{2,1,0:T(8,128)(2,1)S(1)}, bf16[3,64,256]{2,1,0:T(8,128)(2,1)S(1)}, u32[]{:S(2)}, u32[]{:S(2)}) %collective-permute-start.10) | collective-permute-done | bytes 98336 | tf_op jit(solution)/shard_map/ppermute | solution.py:314
  42.5 1.6 %collective-permute-done.11.refs_4_ = bf16[3,64,256]{2,1,0:T(8,128)(2,1)S(1)} collective-permute-done((bf16[3,64,256]{2,1,0:T(8,128)(2,1)S(1)}, bf16[3,64,256]{2,1,0:T(8,128)(2,1)S(1)}, u32[]{:S(2)}, u32[]{:S(2)}) %collective-permute-start.11) | collective-permute-done | bytes 98336 | tf_op jit(solution)/shard_map/ppermute | solution.py:314
  44.1 1.6 %collective-permute-done.12.refs_5_ = bf16[3,64,256]{2,1,0:T(8,128)(2,1)S(1)} collective-permute-done((bf16[3,64,256]{2,1,0:T(8,128)(2,1)S(1)}, bf16[3,64,256]{2,1,0:T(8,128)(2,1)S(1)}, u32[]{:S(2)}, u32[]{:S(2)}) %collective-permute-start.12) | collective-permute-done | bytes 98336 | tf_op jit(solution)/shard_map/ppermute | solution.py:314
  45.7 0.0 collective-permute-done.13.refs_6_
  45.7 0.7 %mate.1 = (bf16[3,256,512]{2,1,0:T(8,128)(2,1)S(1)}, bf16[256,512]{1,0:T(8,128)(2,1)S(1)}) custom-call(bf16[2,64,256]{2,1,0:T(8,128)(2,1)S(1)} %collective-permute-done.7.refs_0_, bf16[3,64,256]{2,1,0:T(8,128)(2,1)S(1)} %collective-permute-done.8.refs_1_, bf16[2,64,256]{2,1,0:T(8,128)(2,1)S(1)} %collective-permute-done.9.refs_2_, ...), custom_call_target="tpu_custom_call" | custom-call | flops 805306368 | bytes 4194304 | tf_op jit(solution)/shard_map/mate/pallas_call | solution.py:387
  46.4 0.1 collective-permute-start.14
  46.5 1.0 %far.1 = (f32[256,512]{1,0:T(8,128)S(1)}, bf16[256,512]{1,0:T(8,128)(2,1)S(1)}) custom-call(bf16[3,256,512]{2,1,0:T(8,128)(2,1)S(1)} %get-tuple-element.68.lhs_ref, bf16[2048,512]{1,0:T(8,128)(2,1)S(1)} %get-tuple-element.57.refs_11_.wk_ref, bf16[2048,512]{1,0:T(8,128)(2,1)S(1)} %get-tuple-element.58.refs_12_.wq_ref, ...), custom_call_target="tpu_custom_call" | custom-call | flops 805306368 | bytes 4194304 | tf_op jit(solution)/shard_map/far/pallas_call | solution.py:397
  47.5 0.5 collective-permute-done.14
  48.0 0.1 add_convert_fusion.1
  48.1 1.6 %collective-permute-start.15 = (bf16[256,512]{1,0:T(8,128)(2,1)S(1)}, bf16[256,512]{1,0:T(8,128)(2,1)S(1)}, u32[]{:S(2)}, u32[]{:S(2)}) collective-permute-start(bf16[256,512]{1,0:T(8,128)(2,1)S(1)} %add_convert_fusion.1), channel_id=1, source_target_pairs={{0,2},{1,3},{2,0},{3,1},{4,6},{5,7},{6,4},{7,5},{8,10},{9,11},{10,... | collective-permute-start | bytes 786440 | tf_op jit(solution)/shard_map/ppermute | solution.py:314
  49.6 0.0 collective-permute-start.16
  49.6 0.6 own.1
  50.2 3.2 %collective-permute-start.17 = (bf16[1,64,256]{2,1,0:T(8,128)(2,1)S(1)}, bf16[1,64,256]{2,1,0:T(8,128)(2,1)S(1)}, u32[]{:S(2)}, u32[]{:S(2)}) collective-permute-start(bf16[1,64,256]{2,1,0:T(8,128)(2,1)S(1)} %get-tuple-element.72), channel_id=1, source_target_pairs={{0,28},{4,24},{8,20},{12,16},{16,12},{20,8},{24,4},{28,0},{1,29},{... | collective-permute-start | bytes 98312 | tf_op jit(solution)/shard_map/ppermute | solution.py:314
  53.4 1.8 %collective-permute-start.18 = (bf16[1,64,256]{2,1,0:T(8,128)(2,1)S(1)}, bf16[1,64,256]{2,1,0:T(8,128)(2,1)S(1)}, u32[]{:S(2)}, u32[]{:S(2)}) collective-permute-start(bf16[1,64,256]{2,1,0:T(8,128)(2,1)S(1)} %get-tuple-element.73), channel_id=1, source_target_pairs={{0,24},{4,28},{8,16},{12,20},{16,8},{20,12},{24,0},{28,4},{1,25},{... | collective-permute-start | bytes 98312 | tf_op jit(solution)/shard_map/ppermute | solution.py:314
  55.2 1.8 %collective-permute-done.17.refs_8_ = bf16[1,64,256]{2,1,0:T(8,128)(2,1)S(1)} collective-permute-done((bf16[1,64,256]{2,1,0:T(8,128)(2,1)S(1)}, bf16[1,64,256]{2,1,0:T(8,128)(2,1)S(1)}, u32[]{:S(2)}, u32[]{:S(2)}) %collective-permute-start.17) | collective-permute-done | bytes 32800 | tf_op jit(solution)/shard_map/ppermute | solution.py:314
  56.9 2.2 %collective-permute-done.18.refs_9_ = bf16[1,64,256]{2,1,0:T(8,128)(2,1)S(1)} collective-permute-done((bf16[1,64,256]{2,1,0:T(8,128)(2,1)S(1)}, bf16[1,64,256]{2,1,0:T(8,128)(2,1)S(1)}, u32[]{:S(2)}, u32[]{:S(2)}) %collective-permute-start.18) | collective-permute-done | bytes 32800 | tf_op jit(solution)/shard_map/ppermute | solution.py:314
  59.1 0.9 %turn.1 = bf16[256,512]{1,0:T(8,128)(2,1)} custom-call(bf16[2,64,256]{2,1,0:T(8,128)(2,1)S(1)} %collective-permute-done.7.refs_0_, bf16[3,64,256]{2,1,0:T(8,128)(2,1)S(1)} %collective-permute-done.8.refs_1_, bf16[2,64,256]{2,1,0:T(8,128)(2,1)S(1)} %collective-permute-done.9.refs_2_, bf16[3,64,256]{2,1,0:T(8,128)(2,1)S(1)} %collective-permute-done.10.refs_3_, ...), custom_call_target="tpu_custom_call" | custom-call | flops 805306368 | bytes 4194304 | tf_op jit(solution)/shard_map/turn/pallas_call | solution.py:418
  60.0 0.0 collective-permute-done.15
  60.0 0.0 collective-permute-done.16
  60.0 0.8 %add_convert_fusion = bf16[256,512]{1,0:T(8,128)(2,1)} fusion(f32[256,512]{1,0:T(8,128)S(1)} %own.1, bf16[256,512]{1,0:T(8,128)(2,1)S(1)} %collective-permute-done.16, bf16[256,512]{1,0:T(8,128)(2,1)S(1)} %collective-permute-done.15), kind=kLoop, calls=%fused_computation | loop fusion | flops 655360 | bytes 1310720 | tf_op jit(solution)/shard_map/convert_element_type | solution.py:428
Async XLA Ops:
  2.1 11.9 %collective-permute-start = (bf16[3,64,256]{2,1,0:T(8,128)(2,1)S(1)}, bf16[3,64,256]{2,1,0:T(8,128)(2,1)S(1)}, u32[]{:S(2)}, u32[]{:S(2)}) collective-permute-start(bf16[3,64,256]{2,1,0:T(8,128)(2,1)S(1)} %get-tuple-element.38), channel_id=1, source_target_pairs={{0,28},{4,24},{8,20},{12,16},{16,12},{20,8},{24,4},{28,0},{1,29},{... | collective-permute-start | bytes 294920 | tf_op jit(solution)/shard_map/ppermute | solution.py:314
  8.2 7.5 %collective-permute-start.1 = (bf16[3,64,256]{2,1,0:T(8,128)(2,1)S(1)}, bf16[3,64,256]{2,1,0:T(8,128)(2,1)S(1)}, u32[]{:S(2)}, u32[]{:S(2)}) collective-permute-start(bf16[3,64,256]{2,1,0:T(8,128)(2,1)S(1)} %get-tuple-element.39), channel_id=1, source_target_pairs={{0,4},{4,0},{8,12},{12,8},{16,20},{20,16},{24,28},{28,24},{1,5},{5... | collective-permute-start | bytes 294920 | tf_op jit(solution)/shard_map/ppermute | solution.py:314
  8.7 8.5 %collective-permute-start.2 = (bf16[3,64,256]{2,1,0:T(8,128)(2,1)S(1)}, bf16[3,64,256]{2,1,0:T(8,128)(2,1)S(1)}, u32[]{:S(2)}, u32[]{:S(2)}) collective-permute-start(bf16[3,64,256]{2,1,0:T(8,128)(2,1)S(1)} %get-tuple-element.40), channel_id=1, source_target_pairs={{0,24},{4,28},{8,16},{12,20},{16,8},{20,12},{24,0},{28,4},{1,25},{... | collective-permute-start | bytes 294920 | tf_op jit(solution)/shard_map/ppermute | solution.py:314
  8.9 8.4 %collective-permute-start.3 = (bf16[3,64,256]{2,1,0:T(8,128)(2,1)S(1)}, bf16[3,64,256]{2,1,0:T(8,128)(2,1)S(1)}, u32[]{:S(2)}, u32[]{:S(2)}) collective-permute-start(bf16[3,64,256]{2,1,0:T(8,128)(2,1)S(1)} %get-tuple-element.41), channel_id=1, source_target_pairs={{0,8},{4,12},{8,0},{12,4},{16,24},{20,28},{24,16},{28,20},{1,9},{5... | collective-permute-start | bytes 294920 | tf_op jit(solution)/shard_map/ppermute | solution.py:314
  8.9 13.6 %collective-permute-start.4 = (bf16[3,64,256]{2,1,0:T(8,128)(2,1)S(1)}, bf16[3,64,256]{2,1,0:T(8,128)(2,1)S(1)}, u32[]{:S(2)}, u32[]{:S(2)}) collective-permute-start(bf16[3,64,256]{2,1,0:T(8,128)(2,1)S(1)} %get-tuple-element.42), channel_id=1, source_target_pairs={{0,20},{4,16},{8,28},{12,24},{16,4},{20,0},{24,12},{28,8},{1,21},{... | collective-permute-start | bytes 294920 | tf_op jit(solution)/shard_map/ppermute | solution.py:314
  14.1 8.4 %collective-permute-start.5 = (bf16[3,64,256]{2,1,0:T(8,128)(2,1)S(1)}, bf16[3,64,256]{2,1,0:T(8,128)(2,1)S(1)}, u32[]{:S(2)}, u32[]{:S(2)}) collective-permute-start(bf16[3,64,256]{2,1,0:T(8,128)(2,1)S(1)} %get-tuple-element.43), channel_id=1, source_target_pairs={{0,12},{4,8},{8,4},{12,0},{16,28},{20,24},{24,20},{28,16},{1,13},{... | collective-permute-start | bytes 294920 | tf_op jit(solution)/shard_map/ppermute | solution.py:314
  15.7 9.2 %collective-permute-start.6 = (bf16[3,64,256]{2,1,0:T(8,128)(2,1)S(1)}, bf16[3,64,256]{2,1,0:T(8,128)(2,1)S(1)}, u32[]{:S(2)}, u32[]{:S(2)}) collective-permute-start(bf16[3,64,256]{2,1,0:T(8,128)(2,1)S(1)} %get-tuple-element.44), channel_id=1, source_target_pairs={{0,16},{4,20},{8,24},{12,28},{16,0},{20,4},{24,8},{28,12},{1,17},{... | collective-permute-start | bytes 294920 | tf_op jit(solution)/shard_map/ppermute | solution.py:314
  29.4 8.4 %collective-permute-start.7 = (bf16[2,64,256]{2,1,0:T(8,128)(2,1)S(1)}, bf16[2,64,256]{2,1,0:T(8,128)(2,1)S(1)}, u32[]{:S(2)}, u32[]{:S(2)}) collective-permute-start(bf16[2,64,256]{2,1,0:T(8,128)(2,1)S(1)} %get-tuple-element.46), channel_id=1, source_target_pairs={{0,28},{4,24},{8,20},{12,16},{16,12},{20,8},{24,4},{28,0},{1,29},{... | collective-permute-start | bytes 196616 | tf_op jit(solution)/shard_map/ppermute | solution.py:314
  32.0 6.8 %collective-permute-start.9 = (bf16[2,64,256]{2,1,0:T(8,128)(2,1)S(1)}, bf16[2,64,256]{2,1,0:T(8,128)(2,1)S(1)}, u32[]{:S(2)}, u32[]{:S(2)}) collective-permute-start(bf16[2,64,256]{2,1,0:T(8,128)(2,1)S(1)} %get-tuple-element.48), channel_id=1, source_target_pairs={{0,24},{4,28},{8,16},{12,20},{16,8},{20,12},{24,0},{28,4},{1,25},{... | collective-permute-start | bytes 196616 | tf_op jit(solution)/shard_map/ppermute | solution.py:314
  33.2 7.4 %collective-permute-start.8 = (bf16[3,64,256]{2,1,0:T(8,128)(2,1)S(1)}, bf16[3,64,256]{2,1,0:T(8,128)(2,1)S(1)}, u32[]{:S(2)}, u32[]{:S(2)}) collective-permute-start(bf16[3,64,256]{2,1,0:T(8,128)(2,1)S(1)} %get-tuple-element.47), channel_id=1, source_target_pairs={{0,4},{4,0},{8,12},{12,8},{16,20},{20,16},{24,28},{28,24},{1,5},{5... | collective-permute-start | bytes 294920 | tf_op jit(solution)/shard_map/ppermute | solution.py:314
  34.7 7.7 %collective-permute-start.10 = (bf16[3,64,256]{2,1,0:T(8,128)(2,1)S(1)}, bf16[3,64,256]{2,1,0:T(8,128)(2,1)S(1)}, u32[]{:S(2)}, u32[]{:S(2)}) collective-permute-start(bf16[3,64,256]{2,1,0:T(8,128)(2,1)S(1)} %get-tuple-element.49), channel_id=1, source_target_pairs={{0,8},{4,12},{8,0},{12,4},{16,24},{20,28},{24,16},{28,20},{1,9},{5... | collective-permute-start | bytes 294920 | tf_op jit(solution)/shard_map/ppermute | solution.py:314
  34.7 9.3 %collective-permute-start.11 = (bf16[3,64,256]{2,1,0:T(8,128)(2,1)S(1)}, bf16[3,64,256]{2,1,0:T(8,128)(2,1)S(1)}, u32[]{:S(2)}, u32[]{:S(2)}) collective-permute-start(bf16[3,64,256]{2,1,0:T(8,128)(2,1)S(1)} %get-tuple-element.50), channel_id=1, source_target_pairs={{0,20},{4,16},{8,28},{12,24},{16,4},{20,0},{24,12},{28,8},{1,21},{... | collective-permute-start | bytes 294920 | tf_op jit(solution)/shard_map/ppermute | solution.py:314
  37.8 7.9 %collective-permute-start.12 = (bf16[3,64,256]{2,1,0:T(8,128)(2,1)S(1)}, bf16[3,64,256]{2,1,0:T(8,128)(2,1)S(1)}, u32[]{:S(2)}, u32[]{:S(2)}) collective-permute-start(bf16[3,64,256]{2,1,0:T(8,128)(2,1)S(1)} %get-tuple-element.51), channel_id=1, source_target_pairs={{0,12},{4,8},{8,4},{12,0},{16,28},{20,24},{24,20},{28,16},{1,13},{... | collective-permute-start | bytes 294920 | tf_op jit(solution)/shard_map/ppermute | solution.py:314
  38.7 7.0 %collective-permute-start.13 = (bf16[3,64,256]{2,1,0:T(8,128)(2,1)S(1)}, bf16[3,64,256]{2,1,0:T(8,128)(2,1)S(1)}, u32[]{:S(2)}, u32[]{:S(2)}) collective-permute-start(bf16[3,64,256]{2,1,0:T(8,128)(2,1)S(1)} %get-tuple-element.52), channel_id=1, source_target_pairs={{0,16},{4,20},{8,24},{12,28},{16,0},{20,4},{24,8},{28,12},{1,17},{... | collective-permute-start | bytes 294920 | tf_op jit(solution)/shard_map/ppermute | solution.py:314
  46.4 1.6 %collective-permute-start.14 = (bf16[256,512]{1,0:T(8,128)(2,1)S(1)}, bf16[256,512]{1,0:T(8,128)(2,1)S(1)}, u32[]{:S(2)}, u32[]{:S(2)}) collective-permute-start(bf16[256,512]{1,0:T(8,128)(2,1)S(1)} %get-tuple-element.62), channel_id=1, source_target_pairs={{0,1},{1,0},{2,3},{3,2},{4,5},{5,4},{6,7},{7,6},{8,9},{9,8},{10,11... | collective-permute-start | bytes 786440 | tf_op jit(solution)/shard_map/ppermute | solution.py:314
  48.1 11.9 %collective-permute-start.15 = (bf16[256,512]{1,0:T(8,128)(2,1)S(1)}, bf16[256,512]{1,0:T(8,128)(2,1)S(1)}, u32[]{:S(2)}, u32[]{:S(2)}) collective-permute-start(bf16[256,512]{1,0:T(8,128)(2,1)S(1)} %add_convert_fusion.1), channel_id=1, source_target_pairs={{0,2},{1,3},{2,0},{3,1},{4,6},{5,7},{6,4},{7,5},{8,10},{9,11},{10,... | collective-permute-start | bytes 786440 | tf_op jit(solution)/shard_map/ppermute | solution.py:314
  49.6 10.3 %collective-permute-start.16 = (bf16[256,512]{1,0:T(8,128)(2,1)S(1)}, bf16[256,512]{1,0:T(8,128)(2,1)S(1)}, u32[]{:S(2)}, u32[]{:S(2)}) collective-permute-start(bf16[256,512]{1,0:T(8,128)(2,1)S(1)} %get-tuple-element.67), channel_id=1, source_target_pairs={{0,1},{1,0},{2,3},{3,2},{4,5},{5,4},{6,7},{7,6},{8,9},{9,8},{10,11... | collective-permute-start | bytes 786440 | tf_op jit(solution)/shard_map/ppermute | solution.py:314
  50.2 6.7 %collective-permute-start.17 = (bf16[1,64,256]{2,1,0:T(8,128)(2,1)S(1)}, bf16[1,64,256]{2,1,0:T(8,128)(2,1)S(1)}, u32[]{:S(2)}, u32[]{:S(2)}) collective-permute-start(bf16[1,64,256]{2,1,0:T(8,128)(2,1)S(1)} %get-tuple-element.72), channel_id=1, source_target_pairs={{0,28},{4,24},{8,20},{12,16},{16,12},{20,8},{24,4},{28,0},{1,29},{... | collective-permute-start | bytes 98312 | tf_op jit(solution)/shard_map/ppermute | solution.py:314
  53.4 5.7 %collective-permute-start.18 = (bf16[1,64,256]{2,1,0:T(8,128)(2,1)S(1)}, bf16[1,64,256]{2,1,0:T(8,128)(2,1)S(1)}, u32[]{:S(2)}, u32[]{:S(2)}) collective-permute-start(bf16[1,64,256]{2,1,0:T(8,128)(2,1)S(1)} %get-tuple-element.73), channel_id=1, source_target_pairs={{0,24},{4,28},{8,16},{12,20},{16,8},{20,12},{24,0},{28,4},{1,25},{... | collective-permute-start | bytes 98312 | tf_op jit(solution)/shard_map/ppermute | solution.py:314

commit v10 on v6

--- a/solution.py
+++ b/solution.py
@@ -93,10 +93,23 @@
     return [pltpu.with_memory_space_constraint(array, pltpu.HBM) for array in arrays]
 
 
-def by_distance(pieces):
-    last = len(pieces) - 1
-    order = [last - i // 2 if i % 2 == 0 else 1 + i // 2 for i in range(last)]
-    return zip([*order, 0], pieces)
+def out_distances(blocks):
+    far, near = range(blocks - 1, blocks // 2 - 1, -1), range(1, blocks // 2)
+    return [*near, *far, 0], [*far, *reversed(near), 0]
+
+
+def back_distances(blocks):
+    last = blocks - 1
+    order = [last - i // 2 if i % 2 == 0 else 1 + i // 2 for i in range(last)] + [0]
+    return order, order
+
+
+def by_distance(pieces, orders):
+    even, odd = orders(len(pieces))
+    core = lax.axis_index("tp") % 2
+    return [
+        (a if a == b else a + core * (b - a), piece) for a, b, piece in zip(even, odd, pieces)
+    ]
 
 
 def fetch(sources, targets, sems):
@@ -128,13 +141,13 @@
         copy.wait()
     put(2, held_ref[3].astype(jnp.float32) * held_ref[4].astype(jnp.float32))
     me = lax.axis_index("ctx")
-    for distance, out_ref in by_distance(out_refs):
+    for distance, out_ref in by_distance(out_refs, out_distances):
         out_ref[...] = turn_ref[me ^ distance]
 
 
 def conv_kernel(*refs):
     blocks = lax.axis_size("ctx")
-    in_refs, sources, refs = refs[:blocks], refs[blocks : blocks + 9], refs[blocks + 9 :]
+    in_refs, sources, refs = refs[:blocks], refs[blocks + 1 : blocks + 10], refs[blocks + 10 :]
     out_refs, held_refs = refs[:blocks], refs[blocks : blocks + 6]
     in_ref, rows_ref, spec_ref, twid_ref, fwd_ref, inv_ref, sems = refs[blocks + 6 :]
     twid_copy, fwd_copy, inv_copy, *held_copies = fetch(
@@ -143,7 +156,7 @@
     groups, bins_count, signals, chunk, _ = rows_ref.shape
     block_len = in_ref.shape[-1]
     me = lax.axis_index("ctx")
-    for distance, ref in by_distance(in_refs):
+    for distance, ref in by_distance(in_refs, out_distances):
         in_ref[me ^ distance] = ref[...]
     twid_copy.wait()
 
@@ -237,7 +250,7 @@
         for depth, stage in reversed(list(enumerate(stages))):
             if 0 <= step - depth < groups:
                 stage(step - depth)
-    for distance, out_ref in by_distance(out_refs):
+    for distance, out_ref in by_distance(out_refs, back_distances):
         out_ref[...] = in_ref[me ^ distance]
     for copy in held_copies:
         copy.wait()
@@ -259,7 +272,7 @@
 def natural(back_refs, turn_ref, slots):
     blocks, _, channels, block_len = turn_ref.shape
     me = lax.axis_index("ctx")
-    for distance, ref in by_distance(back_refs):
+    for distance, ref in by_distance(back_refs, back_distances):
         for i, slot in enumerate(slots):
             turn_ref[me ^ distance, i] = ref[slot]
     return [
@@ -300,11 +313,31 @@
     return lax.ppermute(block, axis, pairs)
 
 
-def swap(pieces):
-    return [
-        exchange(piece, "ctx", distance) if distance else piece
-        for distance, piece in by_distance(pieces)
+def send(piece, step, orders):
+    blocks, groups = lax.axis_size("ctx"), lax.axis_size("tp")
+    chosen = orders(blocks)
+    pairs = [
+        (i * groups + j, (i ^ chosen[j % 2][step]) * groups + j)
+        for i in range(blocks)
+        for j in range(groups)
     ]
+    return lax.ppermute(piece, ("ctx", "tp"), pairs)
+
+
+def swap_out(pieces):
+    near = len(pieces) // 2 - 1
+    moved = [send(piece, step, out_distances) for step, piece in enumerate(pieces[:near])]
+    pairs = [(j, j - 1) for j in range(1, lax.axis_size("tp"), 2)]
+    token = lax.ppermute((moved or pieces)[0][:1, :16, :128], "tp", pairs)
+    *pieces, token = lax.optimization_barrier((*pieces, token))
+    for step, piece in enumerate(pieces[near:-1], near):
+        moved.append(send(piece, step, out_distances))
+    return [*moved, pieces[-1]], token
+
+
+def swap_back(pieces):
+    moved = [send(piece, step, back_distances) for step, piece in enumerate(pieces[:-1])]
+    return [*moved, pieces[-1]]
 
 
 def per_device(key_act, value_act, query_act, grad_out, long_filter, w_key, w_query, w_value):
@@ -334,7 +367,7 @@
         compiler_params=compiler_params(12),
         name="gate",
     )(*in_hbm(long_filter, key_act, value_act, query_act, grad_out))
-    moved = swap(sent)
+    moved, token = swap_out(sent)
 
     forward, inverse, twiddle = dft_tables(
         blocks, block_len, 1.0 / (math.sqrt(seq_len) * 2 * seq_len)
@@ -343,7 +376,7 @@
     held = (key_act, value_act, grad_out, w_key, w_query, w_value)
     results = pl.pallas_call(
         conv_kernel,
-        in_specs=[VMEM] * blocks + [HBM] * 9,
+        in_specs=[VMEM] * (blocks + 1) + [HBM] * 9,
         out_shape=arrays(blocks, 3, channels, block_len)
         + [pltpu.VMEM(array.shape, array.dtype) for array in held],
         scratch_shapes=[
@@ -355,8 +388,8 @@
         ],
         compiler_params=compiler_params(28),
         name="conv",
-    )(*moved, *in_hbm(*tables, *held))
-    back, held = swap(results[:blocks]), results[blocks:]
+    )(*moved, token, *in_hbm(*tables, *held))
+    back, held = swap_back(results[:blocks]), results[blocks:]
     weights = held[3:]
     lhs, to_mate = pl.pallas_call(
         mate_kernel,

time: 59.2 us -> 63.1 us (1.066)
  starting transfers between devices: 28 us -> 30.8 us
  waiting for transfers between devices: 20.3 us -> 21.4 us
    ppermute x0 -> x15, starting transfers between devices: none -> 29.2 us  [the longest x14 27.9 us: send(): return lax.ppermute(piece, ('ctx', 'tp'), pairs)]
    ppermute x17 -> x3, starting transfers between devices: 28 us -> 1.63 us  [exchange(): return lax.ppermute(block, axis, pairs)]
    ppermute x0 -> x15, waiting for transfers between devices: none -> 15.5 us  [the longest x14 15.5 us: send(): return lax.ppermute(piece, ('ctx', 'tp'), pairs)]
    ppermute x17 -> x3, waiting for transfers between devices: 20.3 us -> 5.87 us  [exchange(): return lax.ppermute(block, axis, pairs)]
  transfers between devices with their start and end apart: 17 -> 18, of which waited for: 8 -> 10; matrix products, arithmetic and copies ran while one was open for 0% -> 0% of each run, Pallas kernels for 4% -> 4%
where the time goes in v10:
time: 63.1 us; the launch traced here: 63 us
  starting transfers between devices  30.8 us (49%)
  waiting for transfers between devices  21.4 us (34%)
  Pallas kernels  9.17 us (15%)
  other arithmetic  0.87 us (1%)
  between operations  0.71 us (1%)
    ppermute x14, starting transfers between devices, send(): return lax.ppermute(piece, ('ctx', 'tp'), pairs)  27.9 us
    ppermute x14, waiting for transfers between devices, send(): return lax.ppermute(piece, ('ctx', 'tp'), pairs)  15.5 us
    ppermute x3, waiting for transfers between devices, exchange(): return lax.ppermute(block, axis, pairs)  5.87 us
    pallas_call x1, Pallas kernels, per_device(): pl.pallas_call(conv_kernel, in_specs=[VMEM] * (blocks + 1) + [HBM] * 9, o...  4.48 us
    ppermute x3, starting transfers between devices, exchange(): return lax.ppermute(block, axis, pairs)  1.63 us
    pallas_call x1, Pallas kernels, per_device(): pl.pallas_call(gate_kernel, in_specs=[HBM] * 5, out_shape=arrays(blocks,...  1.5 us
    ppermute x1, starting transfers between devices, swap_out(): token = lax.ppermute((moved or pieces)[0][:1, :16, :128], 'tp', pairs)  1.28 us
  transfers between devices with their start and end apart: 18, of which 10 were waited for; matrix products, arithmetic and copies ran while one was open for 0% of the time, Pallas kernels for 4%

profile of v10, /device:TPU:0, one launch (start us, length us, event | category | flops | bytes accessed | tf_op | source)
XLA Modules:
  0.0 63.0 jit_solution(4437768647030009613)
XLA Ops:
  0.6 1.5 %gate.1 = (bf16[3,64,256]{2,1,0:T(8,128)(2,1)S(1)}, bf16[3,64,256]{2,1,0:T(8,128)(2,1)S(1)}, bf16[3,64,256]{2,1,0:T(8,128)(2,1)S(1)}, bf16[3,64,256]{2,1,0:T(8,1...) custom-call(bf16[256,512]{1,0:T(8,128)(2,1)} %refs_0_.1, ...), custom_call_target="tpu_custom_call" | custom-call | tf_op jit(solution)/shard_map/gate/pallas_call | solution.py:358
  2.1 3.0 %collective-permute-start = (bf16[3,64,256]{2,1,0:T(8,128)(2,1)S(1)}, bf16[3,64,256]{2,1,0:T(8,128)(2,1)S(1)}, u32[]{:S(2)}, u32[]{:S(2)}) collective-permute-start(bf16[3,64,256]{2,1,0:T(8,128)(2,1)S(1)} %get-tuple-element.45), channel_id=1, source_target_pairs={{0,4},{1,29},{2,6},{3,31},{4,0},{5,25},{6,2},{7,27},{8,12},{9,21},... | collective-permute-start | bytes 294920 | tf_op jit(solution)/shard_map/ppermute | solution.py:324
  5.2 1.6 %collective-permute-start.1 = (bf16[3,64,256]{2,1,0:T(8,128)(2,1)S(1)}, bf16[3,64,256]{2,1,0:T(8,128)(2,1)S(1)}, u32[]{:S(2)}, u32[]{:S(2)}) collective-permute-start(bf16[3,64,256]{2,1,0:T(8,128)(2,1)S(1)} %get-tuple-element.46), channel_id=1, source_target_pairs={{0,8},{1,25},{2,10},{3,27},{4,12},{5,29},{6,14},{7,31},{8,0},{9,17... | collective-permute-start | bytes 294920 | tf_op jit(solution)/shard_map/ppermute | solution.py:324
  6.8 1.0 %collective-permute-done.refs_0_ = bf16[3,64,256]{2,1,0:T(8,128)(2,1)S(1)} collective-permute-done((bf16[3,64,256]{2,1,0:T(8,128)(2,1)S(1)}, bf16[3,64,256]{2,1,0:T(8,128)(2,1)S(1)}, u32[]{:S(2)}, u32[]{:S(2)}) %collective-permute-start) | collective-permute-done | bytes 98336 | tf_op jit(solution)/shard_map/ppermute | solution.py:324
  7.8 1.3 %collective-permute-start.3 = (bf16[1,16,128]{2,1,0:T(8,128)(2,1)S(1)}, bf16[1,16,128]{2,1,0:T(8,128)(2,1)S(1)}, u32[]{:S(2)}, u32[]{:S(2)}) collective-permute-start(bf16[1,16,128]{2,1,0:T(8,128)(2,1)S(1)} %slice.4), channel_id=1, source_target_pairs={{1,0},{3,2},{5,4},{7,6},{9,8},{11,10},{13,12},{15,14},{17,16},{19,... | collective-permute-start | bytes 12296 | tf_op jit(solution)/shard_map/ppermute | solution.py:331
  9.1 3.7 %collective-permute-start.2 = (bf16[3,64,256]{2,1,0:T(8,128)(2,1)S(1)}, bf16[3,64,256]{2,1,0:T(8,128)(2,1)S(1)}, u32[]{:S(2)}, u32[]{:S(2)}) collective-permute-start(bf16[3,64,256]{2,1,0:T(8,128)(2,1)S(1)} %get-tuple-element.47), channel_id=1, source_target_pairs={{0,12},{1,21},{2,14},{3,23},{4,8},{5,17},{6,10},{7,19},{8,4},{9,29... | collective-permute-start | bytes 294920 | tf_op jit(solution)/shard_map/ppermute | solution.py:324
  12.8 0.0 collective-permute-done.3.refs_8_
  12.8 4.1 %collective-permute-start.4 = (bf16[3,64,256]{2,1,0:T(8,128)(2,1)S(1)}, bf16[3,64,256]{2,1,0:T(8,128)(2,1)S(1)}, u32[]{:S(2)}, u32[]{:S(2)}) collective-permute-start(bf16[3,64,256]{2,1,0:T(8,128)(2,1)S(1)} %get-tuple-element.53), channel_id=1, source_target_pairs={{0,28},{1,17},{2,30},{3,19},{4,24},{5,21},{6,26},{7,23},{8,20},{9,... | collective-permute-start | bytes 294920 | tf_op jit(solution)/shard_map/ppermute | solution.py:324
  16.9 0.0 collective-permute-start.5
  16.9 0.8 %collective-permute-start.6 = (bf16[3,64,256]{2,1,0:T(8,128)(2,1)S(1)}, bf16[3,64,256]{2,1,0:T(8,128)(2,1)S(1)}, u32[]{:S(2)}, u32[]{:S(2)}) collective-permute-start(bf16[3,64,256]{2,1,0:T(8,128)(2,1)S(1)} %get-tuple-element.55), channel_id=1, source_target_pairs={{0,20},{1,9},{2,22},{3,11},{4,16},{5,13},{6,18},{7,15},{8,28},{9,1... | collective-permute-start | bytes 294920 | tf_op jit(solution)/shard_map/ppermute | solution.py:324
  17.7 0.0 collective-permute-done.1.refs_1_
  17.7 2.8 %collective-permute-start.7 = (bf16[3,64,256]{2,1,0:T(8,128)(2,1)S(1)}, bf16[3,64,256]{2,1,0:T(8,128)(2,1)S(1)}, u32[]{:S(2)}, u32[]{:S(2)}) collective-permute-start(bf16[3,64,256]{2,1,0:T(8,128)(2,1)S(1)} %get-tuple-element.56), channel_id=1, source_target_pairs={{0,16},{1,5},{2,18},{3,7},{4,20},{5,1},{6,22},{7,3},{8,24},{9,13},... | collective-permute-start | bytes 294920 | tf_op jit(solution)/shard_map/ppermute | solution.py:324
  20.5 0.0 collective-permute-done.2.refs_2_
  20.5 0.4 collective-permute-done.4.refs_3_
  20.9 3.6 %collective-permute-done.5.refs_4_ = bf16[3,64,256]{2,1,0:T(8,128)(2,1)S(1)} collective-permute-done((bf16[3,64,256]{2,1,0:T(8,128)(2,1)S(1)}, bf16[3,64,256]{2,1,0:T(8,128)(2,1)S(1)}, u32[]{:S(2)}, u32[]{:S(2)}) %collective-permute-start.5) | collective-permute-done | bytes 98336 | tf_op jit(solution)/shard_map/ppermute | solution.py:324
  24.4 3.5 %collective-permute-done.6.refs_5_ = bf16[3,64,256]{2,1,0:T(8,128)(2,1)S(1)} collective-permute-done((bf16[3,64,256]{2,1,0:T(8,128)(2,1)S(1)}, bf16[3,64,256]{2,1,0:T(8,128)(2,1)S(1)}, u32[]{:S(2)}, u32[]{:S(2)}) %collective-permute-start.6) | collective-permute-done | bytes 98336 | tf_op jit(solution)/shard_map/ppermute | solution.py:324
  27.9 0.8 %collective-permute-done.7.refs_6_ = bf16[3,64,256]{2,1,0:T(8,128)(2,1)S(1)} collective-permute-done((bf16[3,64,256]{2,1,0:T(8,128)(2,1)S(1)}, bf16[3,64,256]{2,1,0:T(8,128)(2,1)S(1)}, u32[]{:S(2)}, u32[]{:S(2)}) %collective-permute-start.7) | collective-permute-done | bytes 98336 | tf_op jit(solution)/shard_map/ppermute | solution.py:324
  28.7 4.5 %conv.1 = (bf16[3,64,256]{2,1,0:T(8,128)(2,1)S(1)}, bf16[3,64,256]{2,1,0:T(8,128)(2,1)S(1)}, bf16[3,64,256]{2,1,0:T(8,128)(2,1)S(1)}, bf16[3,64,256]{2,1,0:T(8,1...) custom-call(bf16[3,64,256]{2,1,0:T(8,128)(2,1)S(1)} %collective-perm, ...), custom_call_target="tpu_custom_call" | custom-call | tf_op jit(solution)/shard_map/conv/pallas_call | solution.py:377
  33.2 3.4 %collective-permute-start.8 = (bf16[3,64,256]{2,1,0:T(8,128)(2,1)S(1)}, bf16[3,64,256]{2,1,0:T(8,128)(2,1)S(1)}, u32[]{:S(2)}, u32[]{:S(2)}) collective-permute-start(bf16[3,64,256]{2,1,0:T(8,128)(2,1)S(1)} %get-tuple-element.59), channel_id=1, source_target_pairs={{0,28},{1,29},{2,30},{3,31},{4,24},{5,25},{6,26},{7,27},{8,20},{9,... | collective-permute-start | bytes 294920 | tf_op jit(solution)/shard_map/ppermute | solution.py:324
  36.6 1.5 %collective-permute-start.9 = (bf16[3,64,256]{2,1,0:T(8,128)(2,1)S(1)}, bf16[3,64,256]{2,1,0:T(8,128)(2,1)S(1)}, u32[]{:S(2)}, u32[]{:S(2)}) collective-permute-start(bf16[3,64,256]{2,1,0:T(8,128)(2,1)S(1)} %get-tuple-element.60), channel_id=1, source_target_pairs={{0,4},{1,5},{2,6},{3,7},{4,0},{5,1},{6,2},{7,3},{8,12},{9,13},{10,... | collective-permute-start | bytes 294920 | tf_op jit(solution)/shard_map/ppermute | solution.py:324
  38.2 0.4 collective-permute-start.10
  38.5 0.0 collective-permute-start.11
  38.5 3.9 %collective-permute-start.12 = (bf16[3,64,256]{2,1,0:T(8,128)(2,1)S(1)}, bf16[3,64,256]{2,1,0:T(8,128)(2,1)S(1)}, u32[]{:S(2)}, u32[]{:S(2)}) collective-permute-start(bf16[3,64,256]{2,1,0:T(8,128)(2,1)S(1)} %get-tuple-element.63), channel_id=1, source_target_pairs={{0,20},{1,21},{2,22},{3,23},{4,16},{5,17},{6,18},{7,19},{8,28},{9,... | collective-permute-start | bytes 294920 | tf_op jit(solution)/shard_map/ppermute | solution.py:324
  42.5 0.0 collective-permute-done.8.refs_0_
  42.5 1.0 %collective-permute-start.13 = (bf16[3,64,256]{2,1,0:T(8,128)(2,1)S(1)}, bf16[3,64,256]{2,1,0:T(8,128)(2,1)S(1)}, u32[]{:S(2)}, u32[]{:S(2)}) collective-permute-start(bf16[3,64,256]{2,1,0:T(8,128)(2,1)S(1)} %get-tuple-element.64), channel_id=1, source_target_pairs={{0,12},{1,13},{2,14},{3,15},{4,8},{5,9},{6,10},{7,11},{8,4},{9,5},... | collective-permute-start | bytes 294920 | tf_op jit(solution)/shard_map/ppermute | solution.py:324
  43.5 0.0 collective-permute-done.9.refs_1_
  43.5 1.6 %collective-permute-start.14 = (bf16[3,64,256]{2,1,0:T(8,128)(2,1)S(1)}, bf16[3,64,256]{2,1,0:T(8,128)(2,1)S(1)}, u32[]{:S(2)}, u32[]{:S(2)}) collective-permute-start(bf16[3,64,256]{2,1,0:T(8,128)(2,1)S(1)} %get-tuple-element.65), channel_id=1, source_target_pairs={{0,16},{1,17},{2,18},{3,19},{4,20},{5,21},{6,22},{7,23},{8,24},{9,... | collective-permute-start | bytes 294920 | tf_op jit(solution)/shard_map/ppermute | solution.py:324
  45.1 0.6 collective-permute-done.10.refs_2_
  45.7 0.0 collective-permute-done.11.refs_3_
  45.7 3.6 %collective-permute-done.12.refs_4_ = bf16[3,64,256]{2,1,0:T(8,128)(2,1)S(1)} collective-permute-done((bf16[3,64,256]{2,1,0:T(8,128)(2,1)S(1)}, bf16[3,64,256]{2,1,0:T(8,128)(2,1)S(1)}, u32[]{:S(2)}, u32[]{:S(2)}) %collective-permute-start.12) | collective-permute-done | bytes 98336 | tf_op jit(solution)/shard_map/ppermute | solution.py:324
  49.3 0.0 collective-permute-done.13.refs_5_
  49.3 2.1 %collective-permute-done.14.refs_6_ = bf16[3,64,256]{2,1,0:T(8,128)(2,1)S(1)} collective-permute-done((bf16[3,64,256]{2,1,0:T(8,128)(2,1)S(1)}, bf16[3,64,256]{2,1,0:T(8,128)(2,1)S(1)}, u32[]{:S(2)}, u32[]{:S(2)}) %collective-permute-start.14) | collective-permute-done | bytes 98336 | tf_op jit(solution)/shard_map/ppermute | solution.py:324
  51.4 0.7 %mate.1 = (bf16[3,256,512]{2,1,0:T(8,128)(2,1)S(1)}, bf16[256,512]{1,0:T(8,128)(2,1)S(1)}) custom-call(bf16[3,64,256]{2,1,0:T(8,128)(2,1)S(1)} %collective-permute-done.8.refs_0_, bf16[3,64,256]{2,1,0:T(8,128)(2,1)S(1)} %collective-permute-done.9.refs_1_, bf16[3,64,256]{2,1,0:T(8,128)(2,1)S(1)} %collective-permute-done.10.refs_2_, ...), custom_call_target="tpu_custom_call" | custom-call | flops 805306368 | bytes 4194304 | tf_op jit(solution)/shard_map/mate/pallas_call | solution.py:394
  52.1 0.1 collective-permute-start.15
  52.1 1.0 %far.1 = (f32[256,512]{1,0:T(8,128)S(1)}, bf16[256,512]{1,0:T(8,128)(2,1)S(1)}) custom-call(bf16[3,256,512]{2,1,0:T(8,128)(2,1)S(1)} %get-tuple-element.79.lhs_ref, bf16[2048,512]{1,0:T(8,128)(2,1)S(1)} %get-tuple-element.70.refs_11_.wk_ref, bf16[2048,512]{1,0:T(8,128)(2,1)S(1)} %get-tuple-element.71.refs_12_.wq_ref, ...), custom_call_target="tpu_custom_call" | custom-call | flops 805306368 | bytes 4194304 | tf_op jit(solution)/shard_map/far/pallas_call | solution.py:404
  53.2 0.5 collective-permute-done.15
  53.7 0.1 add_convert_fusion.1
  53.7 1.6 %collective-permute-start.16 = (bf16[256,512]{1,0:T(8,128)(2,1)S(1)}, bf16[256,512]{1,0:T(8,128)(2,1)S(1)}, u32[]{:S(2)}, u32[]{:S(2)}) collective-permute-start(bf16[256,512]{1,0:T(8,128)(2,1)S(1)} %add_convert_fusion.1), channel_id=1, source_target_pairs={{0,2},{1,3},{2,0},{3,1},{4,6},{5,7},{6,4},{7,5},{8,10},{9,11},{10,... | collective-permute-start | bytes 786440 | tf_op jit(solution)/shard_map/ppermute | solution.py:313
  55.3 0.0 collective-permute-start.17
  55.3 0.6 own.1
  55.9 0.9 %turn.1 = bf16[256,512]{1,0:T(8,128)(2,1)} custom-call(bf16[3,64,256]{2,1,0:T(8,128)(2,1)S(1)} %collective-permute-done.8.refs_0_, bf16[3,64,256]{2,1,0:T(8,128)(2,1)S(1)} %collective-permute-done.9.refs_1_, bf16[3,64,256]{2,1,0:T(8,128)(2,1)S(1)} %collective-permute-done.10.refs_2_, bf16[3,64,256]{2,1,0:T(8,128)(2,1)S(1)} %collective-permute-done.11.refs_3_, ...), custom_call_target="tpu_custom_call" | custom-call | flops 805306368 | bytes 4194304 | tf_op jit(solution)/shard_map/turn/pallas_call | solution.py:416
  56.8 5.4 %collective-permute-done.16 = bf16[256,512]{1,0:T(8,128)(2,1)S(1)} collective-permute-done((bf16[256,512]{1,0:T(8,128)(2,1)S(1)}, bf16[256,512]{1,0:T(8,128)(2,1)S(1)}, u32[]{:S(2)}, u32[]{:S(2)}) %collective-permute-start.16) | collective-permute-done | bytes 262176 | tf_op jit(solution)/shard_map/ppermute | solution.py:313
  62.2 0.0 collective-permute-done.17
  62.2 0.8 %add_convert_fusion = bf16[256,512]{1,0:T(8,128)(2,1)} fusion(f32[256,512]{1,0:T(8,128)S(1)} %own.1, bf16[256,512]{1,0:T(8,128)(2,1)S(1)} %collective-permute-done.17, bf16[256,512]{1,0:T(8,128)(2,1)S(1)} %collective-permute-done.16), kind=kLoop, calls=%fused_computation | loop fusion | flops 655360 | bytes 1310720 | tf_op jit(solution)/shard_map/convert_element_type | solution.py:434
  (1 shorter events, 0.0 us)
Async XLA Ops:
  2.1 5.6 %collective-permute-start = (bf16[3,64,256]{2,1,0:T(8,128)(2,1)S(1)}, bf16[3,64,256]{2,1,0:T(8,128)(2,1)S(1)}, u32[]{:S(2)}, u32[]{:S(2)}) collective-permute-start(bf16[3,64,256]{2,1,0:T(8,128)(2,1)S(1)} %get-tuple-element.45), channel_id=1, source_target_pairs={{0,4},{1,29},{2,6},{3,31},{4,0},{5,25},{6,2},{7,27},{8,12},{9,21},... | collective-permute-start | bytes 294920 | tf_op jit(solution)/shard_map/ppermute | solution.py:324
  5.2 12.5 %collective-permute-start.1 = (bf16[3,64,256]{2,1,0:T(8,128)(2,1)S(1)}, bf16[3,64,256]{2,1,0:T(8,128)(2,1)S(1)}, u32[]{:S(2)}, u32[]{:S(2)}) collective-permute-start(bf16[3,64,256]{2,1,0:T(8,128)(2,1)S(1)} %get-tuple-element.46), channel_id=1, source_target_pairs={{0,8},{1,25},{2,10},{3,27},{4,12},{5,29},{6,14},{7,31},{8,0},{9,17... | collective-permute-start | bytes 294920 | tf_op jit(solution)/shard_map/ppermute | solution.py:324
  7.8 5.0 %collective-permute-start.3 = (bf16[1,16,128]{2,1,0:T(8,128)(2,1)S(1)}, bf16[1,16,128]{2,1,0:T(8,128)(2,1)S(1)}, u32[]{:S(2)}, u32[]{:S(2)}) collective-permute-start(bf16[1,16,128]{2,1,0:T(8,128)(2,1)S(1)} %slice.4), channel_id=1, source_target_pairs={{1,0},{3,2},{5,4},{7,6},{9,8},{11,10},{13,12},{15,14},{17,16},{19,... | collective-permute-start | bytes 12296 | tf_op jit(solution)/shard_map/ppermute | solution.py:331
  9.1 11.4 %collective-permute-start.2 = (bf16[3,64,256]{2,1,0:T(8,128)(2,1)S(1)}, bf16[3,64,256]{2,1,0:T(8,128)(2,1)S(1)}, u32[]{:S(2)}, u32[]{:S(2)}) collective-permute-start(bf16[3,64,256]{2,1,0:T(8,128)(2,1)S(1)} %get-tuple-element.47), channel_id=1, source_target_pairs={{0,12},{1,21},{2,14},{3,23},{4,8},{5,17},{6,10},{7,19},{8,4},{9,29... | collective-permute-start | bytes 294920 | tf_op jit(solution)/shard_map/ppermute | solution.py:324
  12.8 8.0 %collective-permute-start.4 = (bf16[3,64,256]{2,1,0:T(8,128)(2,1)S(1)}, bf16[3,64,256]{2,1,0:T(8,128)(2,1)S(1)}, u32[]{:S(2)}, u32[]{:S(2)}) collective-permute-start(bf16[3,64,256]{2,1,0:T(8,128)(2,1)S(1)} %get-tuple-element.53), channel_id=1, source_target_pairs={{0,28},{1,17},{2,30},{3,19},{4,24},{5,21},{6,26},{7,23},{8,20},{9,... | collective-permute-start | bytes 294920 | tf_op jit(solution)/shard_map/ppermute | solution.py:324
  16.9 7.5 %collective-permute-start.5 = (bf16[3,64,256]{2,1,0:T(8,128)(2,1)S(1)}, bf16[3,64,256]{2,1,0:T(8,128)(2,1)S(1)}, u32[]{:S(2)}, u32[]{:S(2)}) collective-permute-start(bf16[3,64,256]{2,1,0:T(8,128)(2,1)S(1)} %get-tuple-element.54), channel_id=1, source_target_pairs={{0,24},{1,13},{2,26},{3,15},{4,28},{5,9},{6,30},{7,11},{8,16},{9,5... | collective-permute-start | bytes 294920 | tf_op jit(solution)/shard_map/ppermute | solution.py:324
  16.9 11.0 %collective-permute-start.6 = (bf16[3,64,256]{2,1,0:T(8,128)(2,1)S(1)}, bf16[3,64,256]{2,1,0:T(8,128)(2,1)S(1)}, u32[]{:S(2)}, u32[]{:S(2)}) collective-permute-start(bf16[3,64,256]{2,1,0:T(8,128)(2,1)S(1)} %get-tuple-element.55), channel_id=1, source_target_pairs={{0,20},{1,9},{2,22},{3,11},{4,16},{5,13},{6,18},{7,15},{8,28},{9,1... | collective-permute-start | bytes 294920 | tf_op jit(solution)/shard_map/ppermute | solution.py:324
  17.7 11.0 %collective-permute-start.7 = (bf16[3,64,256]{2,1,0:T(8,128)(2,1)S(1)}, bf16[3,64,256]{2,1,0:T(8,128)(2,1)S(1)}, u32[]{:S(2)}, u32[]{:S(2)}) collective-permute-start(bf16[3,64,256]{2,1,0:T(8,128)(2,1)S(1)} %get-tuple-element.56), channel_id=1, source_target_pairs={{0,16},{1,5},{2,18},{3,7},{4,20},{5,1},{6,22},{7,3},{8,24},{9,13},... | collective-permute-start | bytes 294920 | tf_op jit(solution)/shard_map/ppermute | solution.py:324
  33.2 9.3 %collective-permute-start.8 = (bf16[3,64,256]{2,1,0:T(8,128)(2,1)S(1)}, bf16[3,64,256]{2,1,0:T(8,128)(2,1)S(1)}, u32[]{:S(2)}, u32[]{:S(2)}) collective-permute-start(bf16[3,64,256]{2,1,0:T(8,128)(2,1)S(1)} %get-tuple-element.59), channel_id=1, source_target_pairs={{0,28},{1,29},{2,30},{3,31},{4,24},{5,25},{6,26},{7,27},{8,20},{9,... | collective-permute-start | bytes 294920 | tf_op jit(solution)/shard_map/ppermute | solution.py:324
  36.6 6.8 %collective-permute-start.9 = (bf16[3,64,256]{2,1,0:T(8,128)(2,1)S(1)}, bf16[3,64,256]{2,1,0:T(8,128)(2,1)S(1)}, u32[]{:S(2)}, u32[]{:S(2)}) collective-permute-start(bf16[3,64,256]{2,1,0:T(8,128)(2,1)S(1)} %get-tuple-element.60), channel_id=1, source_target_pairs={{0,4},{1,5},{2,6},{3,7},{4,0},{5,1},{6,2},{7,3},{8,12},{9,13},{10,... | collective-permute-start | bytes 294920 | tf_op jit(solution)/shard_map/ppermute | solution.py:324
  38.2 7.5 %collective-permute-start.10 = (bf16[3,64,256]{2,1,0:T(8,128)(2,1)S(1)}, bf16[3,64,256]{2,1,0:T(8,128)(2,1)S(1)}, u32[]{:S(2)}, u32[]{:S(2)}) collective-permute-start(bf16[3,64,256]{2,1,0:T(8,128)(2,1)S(1)} %get-tuple-element.61), channel_id=1, source_target_pairs={{0,24},{1,25},{2,26},{3,27},{4,28},{5,29},{6,30},{7,31},{8,16},{9,... | collective-permute-start | bytes 294920 | tf_op jit(solution)/shard_map/ppermute | solution.py:324
  38.5 7.2 %collective-permute-start.11 = (bf16[3,64,256]{2,1,0:T(8,128)(2,1)S(1)}, bf16[3,64,256]{2,1,0:T(8,128)(2,1)S(1)}, u32[]{:S(2)}, u32[]{:S(2)}) collective-permute-start(bf16[3,64,256]{2,1,0:T(8,128)(2,1)S(1)} %get-tuple-element.62), channel_id=1, source_target_pairs={{0,8},{1,9},{2,10},{3,11},{4,12},{5,13},{6,14},{7,15},{8,0},{9,1},... | collective-permute-start | bytes 294920 | tf_op jit(solution)/shard_map/ppermute | solution.py:324
  38.5 10.7 %collective-permute-start.12 = (bf16[3,64,256]{2,1,0:T(8,128)(2,1)S(1)}, bf16[3,64,256]{2,1,0:T(8,128)(2,1)S(1)}, u32[]{:S(2)}, u32[]{:S(2)}) collective-permute-start(bf16[3,64,256]{2,1,0:T(8,128)(2,1)S(1)} %get-tuple-element.63), channel_id=1, source_target_pairs={{0,20},{1,21},{2,22},{3,23},{4,16},{5,17},{6,18},{7,19},{8,28},{9,... | collective-permute-start | bytes 294920 | tf_op jit(solution)/shard_map/ppermute | solution.py:324
  42.5 6.8 %collective-permute-start.13 = (bf16[3,64,256]{2,1,0:T(8,128)(2,1)S(1)}, bf16[3,64,256]{2,1,0:T(8,128)(2,1)S(1)}, u32[]{:S(2)}, u32[]{:S(2)}) collective-permute-start(bf16[3,64,256]{2,1,0:T(8,128)(2,1)S(1)} %get-tuple-element.64), channel_id=1, source_target_pairs={{0,12},{1,13},{2,14},{3,15},{4,8},{5,9},{6,10},{7,11},{8,4},{9,5},... | collective-permute-start | bytes 294920 | tf_op jit(solution)/shard_map/ppermute | solution.py:324
  43.5 7.9 %collective-permute-start.14 = (bf16[3,64,256]{2,1,0:T(8,128)(2,1)S(1)}, bf16[3,64,256]{2,1,0:T(8,128)(2,1)S(1)}, u32[]{:S(2)}, u32[]{:S(2)}) collective-permute-start(bf16[3,64,256]{2,1,0:T(8,128)(2,1)S(1)} %get-tuple-element.65), channel_id=1, source_target_pairs={{0,16},{1,17},{2,18},{3,19},{4,20},{5,21},{6,22},{7,23},{8,24},{9,... | collective-permute-start | bytes 294920 | tf_op jit(solution)/shard_map/ppermute | solution.py:324
  52.1 1.6 %collective-permute-start.15 = (bf16[256,512]{1,0:T(8,128)(2,1)S(1)}, bf16[256,512]{1,0:T(8,128)(2,1)S(1)}, u32[]{:S(2)}, u32[]{:S(2)}) collective-permute-start(bf16[256,512]{1,0:T(8,128)(2,1)S(1)} %get-tuple-element.75), channel_id=1, source_target_pairs={{0,1},{1,0},{2,3},{3,2},{4,5},{5,4},{6,7},{7,6},{8,9},{9,8},{10,11... | collective-permute-start | bytes 786440 | tf_op jit(solution)/shard_map/ppermute | solution.py:313
  53.7 8.4 %collective-permute-start.16 = (bf16[256,512]{1,0:T(8,128)(2,1)S(1)}, bf16[256,512]{1,0:T(8,128)(2,1)S(1)}, u32[]{:S(2)}, u32[]{:S(2)}) collective-permute-start(bf16[256,512]{1,0:T(8,128)(2,1)S(1)} %add_convert_fusion.1), channel_id=1, source_target_pairs={{0,2},{1,3},{2,0},{3,1},{4,6},{5,7},{6,4},{7,5},{8,10},{9,11},{10,... | collective-permute-start | bytes 786440 | tf_op jit(solution)/shard_map/ppermute | solution.py:313
  55.3 6.9 %collective-permute-start.17 = (bf16[256,512]{1,0:T(8,128)(2,1)S(1)}, bf16[256,512]{1,0:T(8,128)(2,1)S(1)}, u32[]{:S(2)}, u32[]{:S(2)}) collective-permute-start(bf16[256,512]{1,0:T(8,128)(2,1)S(1)} %get-tuple-element.78), channel_id=1, source_target_pairs={{0,1},{1,0},{2,3},{3,2},{4,5},{5,4},{6,7},{7,6},{8,9},{9,8},{10,11... | collective-permute-start | bytes 786440 | tf_op jit(solution)/shard_map/ppermute | solution.py:313

commit v11 on v6

--- a/solution.py
+++ b/solution.py
@@ -93,10 +93,25 @@
     return [pltpu.with_memory_space_constraint(array, pltpu.HBM) for array in arrays]
 
 
-def by_distance(pieces):
-    last = len(pieces) - 1
-    order = [last - i // 2 if i % 2 == 0 else 1 + i // 2 for i in range(last)]
-    return zip([*order, 0], pieces)
+def offsets(blocks):
+    half = blocks // 2
+    shifts = sorted(range(1, half), key=lambda shift: (abs(2 * shift - half), shift))
+    return [(shift, flip) for flip in (1, 0) for shift in shifts] + [(0, 1), (0, 0)]
+
+
+def target(index, offset, blocks, sign=1):
+    high = (index // 2 + sign * offset[0] + blocks // 2) % (blocks // 2)
+    return 2 * high + (index % 2 ^ offset[1])
+
+
+def to_send(refs):
+    me, blocks = lax.axis_index("ctx"), len(refs)
+    return [(target(me, offset, blocks), ref) for offset, ref in zip(offsets(blocks), refs)]
+
+
+def received(refs):
+    me, blocks = lax.axis_index("ctx"), len(refs)
+    return [(target(me, offset, blocks, -1), ref) for offset, ref in zip(offsets(blocks), refs)]
 
 
 def fetch(sources, targets, sems):
@@ -127,9 +142,8 @@
     for copy in copies[2:]:
         copy.wait()
     put(2, held_ref[3].astype(jnp.float32) * held_ref[4].astype(jnp.float32))
-    me = lax.axis_index("ctx")
-    for distance, out_ref in by_distance(out_refs):
-        out_ref[...] = turn_ref[me ^ distance]
+    for block, out_ref in to_send(out_refs):
+        out_ref[...] = turn_ref[block]
 
 
 def conv_kernel(*refs):
@@ -142,9 +156,8 @@
     )
     groups, bins_count, signals, chunk, _ = rows_ref.shape
     block_len = in_ref.shape[-1]
-    me = lax.axis_index("ctx")
-    for distance, ref in by_distance(in_refs):
-        in_ref[me ^ distance] = ref[...]
+    for block, ref in received(in_refs):
+        in_ref[block] = ref[...]
     twid_copy.wait()
 
     def each(count, body):
@@ -237,8 +250,8 @@
         for depth, stage in reversed(list(enumerate(stages))):
             if 0 <= step - depth < groups:
                 stage(step - depth)
-    for distance, out_ref in by_distance(out_refs):
-        out_ref[...] = in_ref[me ^ distance]
+    for block, out_ref in to_send(out_refs):
+        out_ref[...] = in_ref[block]
     for copy in held_copies:
         copy.wait()
 
@@ -258,10 +271,9 @@
 
 def natural(back_refs, turn_ref, slots):
     blocks, _, channels, block_len = turn_ref.shape
-    me = lax.axis_index("ctx")
-    for distance, ref in by_distance(back_refs):
+    for block, ref in received(back_refs):
         for i, slot in enumerate(slots):
-            turn_ref[me ^ distance, i] = ref[slot]
+            turn_ref[block, i] = ref[slot]
     return [
         turn_ref[:, i].reshape(blocks * channels, block_len).astype(jnp.float32).T
         for i in range(len(slots))
@@ -295,16 +307,18 @@
     out_ref[...] = natural(back_refs, turn_ref, (2,))[0].astype(jnp.bfloat16)
 
 
-def exchange(block, axis, distance):
-    pairs = [(i, i ^ distance) for i in range(lax.axis_size(axis))]
-    return lax.ppermute(block, axis, pairs)
+def exchange(block, distance):
+    pairs = [(i, i ^ distance) for i in range(lax.axis_size("tp"))]
+    return lax.ppermute(block, "tp", pairs)
 
 
 def swap(pieces):
-    return [
-        exchange(piece, "ctx", distance) if distance else piece
-        for distance, piece in by_distance(pieces)
+    blocks = len(pieces)
+    moved = [
+        lax.ppermute(piece, "ctx", [(i, target(i, offset, blocks)) for i in range(blocks)])
+        for offset, piece in zip(offsets(blocks)[:-1], pieces)
     ]
+    return [*moved, pieces[-1]]
 
 
 def per_device(key_act, value_act, query_act, grad_out, long_filter, w_key, w_query, w_value):
@@ -367,7 +381,7 @@
         cost_estimate=block_cost,
         name="mate",
     )(*back, *held)
-    from_mate = exchange(to_mate, "tp", 1)
+    from_mate = exchange(to_mate, 1)
     far, near = pl.pallas_call(
         far_kernel,
         in_specs=[VMEM] * 4,
@@ -378,8 +392,8 @@
     )(lhs, *weights)
     far = (far + from_mate.astype(jnp.float32)).astype(jnp.bfloat16)
     far, near, lhs, back = lax.optimization_barrier((far, near, lhs, back))
-    from_far = exchange(far, "tp", 2)
-    from_near = exchange(near, "tp", 1)
+    from_far = exchange(far, 2)
+    from_near = exchange(near, 1)
     grad_filter = pl.pallas_call(
         turn_kernel,
         in_specs=[VMEM] * blocks,

time: 59.2 us -> 59.6 us (level)
  waiting for transfers between devices: 20.3 us -> 22 us
  starting transfers between devices: 28 us -> 26.7 us
    ppermute x17, waiting for transfers between devices: 20.3 us -> 22 us  [the longest x14 16.1 us: swap(): lax.ppermute(piece, 'ctx', [(i, target(i, offset, blocks)) for i in range...]
    ppermute x17, starting transfers between devices: 28 us -> 26.7 us  [the longest x14 25 us: swap(): lax.ppermute(piece, 'ctx', [(i, target(i, offset, blocks)) for i in range...]
  transfers between devices with their start and end apart: 17 -> 17, of which waited for: 8 -> 6; matrix products, arithmetic and copies ran while one was open for 0% -> 0% of each run, Pallas kernels for 4% -> 4%
where the time goes in v11:
time: 59.6 us; the launch traced here: 59.4 us
  starting transfers between devices  26.7 us (45%)
  waiting for transfers between devices  22 us (37%)
  Pallas kernels  9.22 us (15%)
  other arithmetic  0.87 us (1%)
  between operations  0.71 us (1%)
    ppermute x14, starting transfers between devices, swap(): lax.ppermute(piece, 'ctx', [(i, target(i, offset, blocks)) for i in range...  25 us
    ppermute x14, waiting for transfers between devices, swap(): lax.ppermute(piece, 'ctx', [(i, target(i, offset, blocks)) for i in range...  16.1 us
    ppermute x3, waiting for transfers between devices, exchange(): return lax.ppermute(block, 'tp', pairs)  5.86 us
    pallas_call x1, Pallas kernels, per_device(): pl.pallas_call(conv_kernel, in_specs=[VMEM] * blocks + [HBM] * 9, out_sha...  4.52 us
    ppermute x3, starting transfers between devices, exchange(): return lax.ppermute(block, 'tp', pairs)  1.63 us
    pallas_call x1, Pallas kernels, per_device(): pl.pallas_call(gate_kernel, in_specs=[HBM] * 5, out_shape=arrays(blocks,...  1.5 us
  transfers between devices with their start and end apart: 17, of which 6 were waited for; matrix products, arithmetic and copies ran while one was open for 0% of the time, Pallas kernels for 4%

profile of v11, /device:TPU:0, one launch (start us, length us, event | category | flops | bytes accessed | tf_op | source)
XLA Modules:
  0.0 59.4 jit_solution(3318682589867436270)
XLA Ops:
  0.6 1.5 %gate.1 = (bf16[3,64,256]{2,1,0:T(8,128)(2,1)S(1)}, bf16[3,64,256]{2,1,0:T(8,128)(2,1)S(1)}, bf16[3,64,256]{2,1,0:T(8,128)(2,1)S(1)}, bf16[3,64,256]{2,1,0:T(8,1...) custom-call(bf16[256,512]{1,0:T(8,128)(2,1)} %refs_0_.1, ...), custom_call_target="tpu_custom_call" | custom-call | tf_op jit(solution)/shard_map/gate/pallas_call | solution.py:339
  2.1 5.1 %collective-permute-start = (bf16[3,64,256]{2,1,0:T(8,128)(2,1)S(1)}, bf16[3,64,256]{2,1,0:T(8,128)(2,1)S(1)}, u32[]{:S(2)}, u32[]{:S(2)}) collective-permute-start(bf16[3,64,256]{2,1,0:T(8,128)(2,1)S(1)} %get-tuple-element.39), channel_id=1, source_target_pairs={{0,20},{4,16},{8,28},{12,24},{16,4},{20,0},{24,12},{28,8},{1,21},{... | collective-permute-start | bytes 294920 | tf_op jit(solution)/shard_map/ppermute | solution.py:318
  7.2 1.5 %collective-permute-start.1 = (bf16[3,64,256]{2,1,0:T(8,128)(2,1)S(1)}, bf16[3,64,256]{2,1,0:T(8,128)(2,1)S(1)}, u32[]{:S(2)}, u32[]{:S(2)}) collective-permute-start(bf16[3,64,256]{2,1,0:T(8,128)(2,1)S(1)} %get-tuple-element.40), channel_id=1, source_target_pairs={{0,12},{4,8},{8,20},{12,16},{16,28},{20,24},{24,4},{28,0},{1,13},{... | collective-permute-start | bytes 294920 | tf_op jit(solution)/shard_map/ppermute | solution.py:318
  8.7 3.2 %collective-permute-start.2 = (bf16[3,64,256]{2,1,0:T(8,128)(2,1)S(1)}, bf16[3,64,256]{2,1,0:T(8,128)(2,1)S(1)}, u32[]{:S(2)}, u32[]{:S(2)}) collective-permute-start(bf16[3,64,256]{2,1,0:T(8,128)(2,1)S(1)} %get-tuple-element.41), channel_id=1, source_target_pairs={{0,28},{4,24},{8,4},{12,0},{16,12},{20,8},{24,20},{28,16},{1,29},{... | collective-permute-start | bytes 294920 | tf_op jit(solution)/shard_map/ppermute | solution.py:318
  11.9 0.0 collective-permute-start.3
  11.9 0.1 collective-permute-start.4
  12.0 2.4 %collective-permute-done.refs_0_ = bf16[3,64,256]{2,1,0:T(8,128)(2,1)S(1)} collective-permute-done((bf16[3,64,256]{2,1,0:T(8,128)(2,1)S(1)}, bf16[3,64,256]{2,1,0:T(8,128)(2,1)S(1)}, u32[]{:S(2)}, u32[]{:S(2)}) %collective-permute-start) | collective-permute-done | bytes 98336 | tf_op jit(solution)/shard_map/ppermute | solution.py:318
  14.4 1.5 %collective-permute-start.5 = (bf16[3,64,256]{2,1,0:T(8,128)(2,1)S(1)}, bf16[3,64,256]{2,1,0:T(8,128)(2,1)S(1)}, u32[]{:S(2)}, u32[]{:S(2)}) collective-permute-start(bf16[3,64,256]{2,1,0:T(8,128)(2,1)S(1)} %get-tuple-element.44), channel_id=1, source_target_pairs={{0,24},{4,28},{8,0},{12,4},{16,8},{20,12},{24,16},{28,20},{1,25},{... | collective-permute-start | bytes 294920 | tf_op jit(solution)/shard_map/ppermute | solution.py:318
  16.0 0.0 collective-permute-done.1.refs_1_
  16.0 2.1 %collective-permute-start.6 = (bf16[3,64,256]{2,1,0:T(8,128)(2,1)S(1)}, bf16[3,64,256]{2,1,0:T(8,128)(2,1)S(1)}, u32[]{:S(2)}, u32[]{:S(2)}) collective-permute-start(bf16[3,64,256]{2,1,0:T(8,128)(2,1)S(1)} %get-tuple-element.45), channel_id=1, source_target_pairs={{0,4},{4,0},{8,12},{12,8},{16,20},{20,16},{24,28},{28,24},{1,5},{5... | collective-permute-start | bytes 294920 | tf_op jit(solution)/shard_map/ppermute | solution.py:318
  18.0 0.0 collective-permute-done.2.refs_2_
  18.0 5.6 %collective-permute-done.3.refs_3_ = bf16[3,64,256]{2,1,0:T(8,128)(2,1)S(1)} collective-permute-done((bf16[3,64,256]{2,1,0:T(8,128)(2,1)S(1)}, bf16[3,64,256]{2,1,0:T(8,128)(2,1)S(1)}, u32[]{:S(2)}, u32[]{:S(2)}) %collective-permute-start.3) | collective-permute-done | bytes 98336 | tf_op jit(solution)/shard_map/ppermute | solution.py:318
  23.7 0.0 collective-permute-done.4.refs_4_
  23.7 0.0 collective-permute-done.5.refs_5_
  23.7 0.0 collective-permute-done.6.refs_6_
  23.7 4.5 %conv.1 = (bf16[3,64,256]{2,1,0:T(8,128)(2,1)S(1)}, bf16[3,64,256]{2,1,0:T(8,128)(2,1)S(1)}, bf16[3,64,256]{2,1,0:T(8,128)(2,1)S(1)}, bf16[3,64,256]{2,1,0:T(8,1...) custom-call(bf16[3,64,256]{2,1,0:T(8,128)(2,1)S(1)} %collective-perm, ...), custom_call_target="tpu_custom_call" | custom-call | tf_op jit(solution)/shard_map/conv/pallas_call | solution.py:358
  28.2 4.1 %collective-permute-start.7 = (bf16[3,64,256]{2,1,0:T(8,128)(2,1)S(1)}, bf16[3,64,256]{2,1,0:T(8,128)(2,1)S(1)}, u32[]{:S(2)}, u32[]{:S(2)}) collective-permute-start(bf16[3,64,256]{2,1,0:T(8,128)(2,1)S(1)} %get-tuple-element.47), channel_id=1, source_target_pairs={{0,20},{4,16},{8,28},{12,24},{16,4},{20,0},{24,12},{28,8},{1,21},{... | collective-permute-start | bytes 294920 | tf_op jit(solution)/shard_map/ppermute | solution.py:318
  32.3 0.0 collective-permute-start.8
  32.3 4.7 %collective-permute-start.9 = (bf16[3,64,256]{2,1,0:T(8,128)(2,1)S(1)}, bf16[3,64,256]{2,1,0:T(8,128)(2,1)S(1)}, u32[]{:S(2)}, u32[]{:S(2)}) collective-permute-start(bf16[3,64,256]{2,1,0:T(8,128)(2,1)S(1)} %get-tuple-element.49), channel_id=1, source_target_pairs={{0,28},{4,24},{8,4},{12,0},{16,12},{20,8},{24,20},{28,16},{1,29},{... | collective-permute-start | bytes 294920 | tf_op jit(solution)/shard_map/ppermute | solution.py:318
  37.0 0.0 collective-permute-start.10
  37.0 0.2 collective-permute-start.11
  37.2 2.2 %collective-permute-done.7.refs_0_ = bf16[3,64,256]{2,1,0:T(8,128)(2,1)S(1)} collective-permute-done((bf16[3,64,256]{2,1,0:T(8,128)(2,1)S(1)}, bf16[3,64,256]{2,1,0:T(8,128)(2,1)S(1)}, u32[]{:S(2)}, u32[]{:S(2)}) %collective-permute-start.7) | collective-permute-done | bytes 98336 | tf_op jit(solution)/shard_map/ppermute | solution.py:318
  39.4 1.4 %collective-permute-start.12 = (bf16[3,64,256]{2,1,0:T(8,128)(2,1)S(1)}, bf16[3,64,256]{2,1,0:T(8,128)(2,1)S(1)}, u32[]{:S(2)}, u32[]{:S(2)}) collective-permute-start(bf16[3,64,256]{2,1,0:T(8,128)(2,1)S(1)} %get-tuple-element.52), channel_id=1, source_target_pairs={{0,24},{4,28},{8,0},{12,4},{16,8},{20,12},{24,16},{28,20},{1,25},{... | collective-permute-start | bytes 294920 | tf_op jit(solution)/shard_map/ppermute | solution.py:318
  40.8 0.0 collective-permute-done.8.refs_1_
  40.8 1.1 %collective-permute-start.13 = (bf16[3,64,256]{2,1,0:T(8,128)(2,1)S(1)}, bf16[3,64,256]{2,1,0:T(8,128)(2,1)S(1)}, u32[]{:S(2)}, u32[]{:S(2)}) collective-permute-start(bf16[3,64,256]{2,1,0:T(8,128)(2,1)S(1)} %get-tuple-element.53), channel_id=1, source_target_pairs={{0,4},{4,0},{8,12},{12,8},{16,20},{20,16},{24,28},{28,24},{1,5},{5... | collective-permute-start | bytes 294920 | tf_op jit(solution)/shard_map/ppermute | solution.py:318
  42.0 0.0 collective-permute-done.9.refs_2_
  42.0 5.9 %collective-permute-done.10.refs_3_ = bf16[3,64,256]{2,1,0:T(8,128)(2,1)S(1)} collective-permute-done((bf16[3,64,256]{2,1,0:T(8,128)(2,1)S(1)}, bf16[3,64,256]{2,1,0:T(8,128)(2,1)S(1)}, u32[]{:S(2)}, u32[]{:S(2)}) %collective-permute-start.10) | collective-permute-done | bytes 98336 | tf_op jit(solution)/shard_map/ppermute | solution.py:318
  47.8 0.0 collective-permute-done.11.refs_4_
  47.8 0.0 collective-permute-done.12.refs_5_
  47.8 0.0 collective-permute-done.13.refs_6_
  47.8 0.7 %mate.1 = (bf16[3,256,512]{2,1,0:T(8,128)(2,1)S(1)}, bf16[256,512]{1,0:T(8,128)(2,1)S(1)}) custom-call(bf16[3,64,256]{2,1,0:T(8,128)(2,1)S(1)} %collective-permute-done.7.refs_0_, bf16[3,64,256]{2,1,0:T(8,128)(2,1)S(1)} %collective-permute-done.8.refs_1_, bf16[3,64,256]{2,1,0:T(8,128)(2,1)S(1)} %collective-permute-done.9.refs_2_, ...), custom_call_target="tpu_custom_call" | custom-call | flops 805306368 | bytes 4194304 | tf_op jit(solution)/shard_map/mate/pallas_call | solution.py:375
  48.5 0.1 collective-permute-start.14
  48.6 1.0 %far.1 = (f32[256,512]{1,0:T(8,128)S(1)}, bf16[256,512]{1,0:T(8,128)(2,1)S(1)}) custom-call(bf16[3,256,512]{2,1,0:T(8,128)(2,1)S(1)} %get-tuple-element.67.lhs_ref, bf16[2048,512]{1,0:T(8,128)(2,1)S(1)} %get-tuple-element.58.refs_11_.wk_ref, bf16[2048,512]{1,0:T(8,128)(2,1)S(1)} %get-tuple-element.59.refs_12_.wq_ref, ...), custom_call_target="tpu_custom_call" | custom-call | flops 805306368 | bytes 4194304 | tf_op jit(solution)/shard_map/far/pallas_call | solution.py:385
  49.6 0.5 collective-permute-done.14
  50.1 0.1 add_convert_fusion.1
  50.2 1.6 %collective-permute-start.15 = (bf16[256,512]{1,0:T(8,128)(2,1)S(1)}, bf16[256,512]{1,0:T(8,128)(2,1)S(1)}, u32[]{:S(2)}, u32[]{:S(2)}) collective-permute-start(bf16[256,512]{1,0:T(8,128)(2,1)S(1)} %add_convert_fusion.1), channel_id=1, source_target_pairs={{0,2},{1,3},{2,0},{3,1},{4,6},{5,7},{6,4},{7,5},{8,10},{9,11},{10,... | collective-permute-start | bytes 786440 | tf_op jit(solution)/shard_map/ppermute | solution.py:312
  51.8 0.0 collective-permute-start.16
  51.8 0.6 %own.1 = f32[256,512]{1,0:T(8,128)S(1)} custom-call(bf16[3,256,512]{2,1,0:T(8,128)(2,1)S(1)} %get-tuple-element.67.lhs_ref, bf16[2048,512]{1,0:T(8,128)(2,1)S(1)} %get-tuple-element.58.refs_11_.wk_ref, bf16[2048,512]{1,0:T(8,128)(2,1)S(1)} %get-tuple-element.59.refs_12_.wq_ref, bf16[2048,512]{1,0:T(8,128)(2,1)S(1)} %get-tuple-element.60.refs_13_.wv_ref), custom_call_target="tpu_custom_call" | custom-call | flops 805306368 | bytes 4194304 | tf_op jit(solution)/shard_map/own/pallas_call | solution.py:406
  52.4 0.9 %turn.1 = bf16[256,512]{1,0:T(8,128)(2,1)} custom-call(bf16[3,64,256]{2,1,0:T(8,128)(2,1)S(1)} %collective-permute-done.7.refs_0_, bf16[3,64,256]{2,1,0:T(8,128)(2,1)S(1)} %collective-permute-done.8.refs_1_, bf16[3,64,256]{2,1,0:T(8,128)(2,1)S(1)} %collective-permute-done.9.refs_2_, bf16[3,64,256]{2,1,0:T(8,128)(2,1)S(1)} %collective-permute-done.10.refs_3_, ...), custom_call_target="tpu_custom_call" | custom-call | flops 805306368 | bytes 4194304 | tf_op jit(solution)/shard_map/turn/pallas_call | solution.py:397
  53.3 5.4 %collective-permute-done.15 = bf16[256,512]{1,0:T(8,128)(2,1)S(1)} collective-permute-done((bf16[256,512]{1,0:T(8,128)(2,1)S(1)}, bf16[256,512]{1,0:T(8,128)(2,1)S(1)}, u32[]{:S(2)}, u32[]{:S(2)}) %collective-permute-start.15) | collective-permute-done | bytes 262176 | tf_op jit(solution)/shard_map/ppermute | solution.py:312
  58.6 0.0 collective-permute-done.16
  58.6 0.8 %add_convert_fusion = bf16[256,512]{1,0:T(8,128)(2,1)} fusion(f32[256,512]{1,0:T(8,128)S(1)} %own.1, bf16[256,512]{1,0:T(8,128)(2,1)S(1)} %collective-permute-done.16, bf16[256,512]{1,0:T(8,128)(2,1)S(1)} %collective-permute-done.15), kind=kLoop, calls=%fused_computation | loop fusion | flops 655360 | bytes 1310720 | tf_op jit(solution)/shard_map/convert_element_type | solution.py:415
Async XLA Ops:
  2.1 12.3 %collective-permute-start = (bf16[3,64,256]{2,1,0:T(8,128)(2,1)S(1)}, bf16[3,64,256]{2,1,0:T(8,128)(2,1)S(1)}, u32[]{:S(2)}, u32[]{:S(2)}) collective-permute-start(bf16[3,64,256]{2,1,0:T(8,128)(2,1)S(1)} %get-tuple-element.39), channel_id=1, source_target_pairs={{0,20},{4,16},{8,28},{12,24},{16,4},{20,0},{24,12},{28,8},{1,21},{... | collective-permute-start | bytes 294920 | tf_op jit(solution)/shard_map/ppermute | solution.py:318
  7.2 8.8 %collective-permute-start.1 = (bf16[3,64,256]{2,1,0:T(8,128)(2,1)S(1)}, bf16[3,64,256]{2,1,0:T(8,128)(2,1)S(1)}, u32[]{:S(2)}, u32[]{:S(2)}) collective-permute-start(bf16[3,64,256]{2,1,0:T(8,128)(2,1)S(1)} %get-tuple-element.40), channel_id=1, source_target_pairs={{0,12},{4,8},{8,20},{12,16},{16,28},{20,24},{24,4},{28,0},{1,13},{... | collective-permute-start | bytes 294920 | tf_op jit(solution)/shard_map/ppermute | solution.py:318
  8.7 9.3 %collective-permute-start.2 = (bf16[3,64,256]{2,1,0:T(8,128)(2,1)S(1)}, bf16[3,64,256]{2,1,0:T(8,128)(2,1)S(1)}, u32[]{:S(2)}, u32[]{:S(2)}) collective-permute-start(bf16[3,64,256]{2,1,0:T(8,128)(2,1)S(1)} %get-tuple-element.41), channel_id=1, source_target_pairs={{0,28},{4,24},{8,4},{12,0},{16,12},{20,8},{24,20},{28,16},{1,29},{... | collective-permute-start | bytes 294920 | tf_op jit(solution)/shard_map/ppermute | solution.py:318
  11.9 11.8 %collective-permute-start.3 = (bf16[3,64,256]{2,1,0:T(8,128)(2,1)S(1)}, bf16[3,64,256]{2,1,0:T(8,128)(2,1)S(1)}, u32[]{:S(2)}, u32[]{:S(2)}) collective-permute-start(bf16[3,64,256]{2,1,0:T(8,128)(2,1)S(1)} %get-tuple-element.42), channel_id=1, source_target_pairs={{0,16},{4,20},{8,24},{12,28},{16,0},{20,4},{24,8},{28,12},{1,17},{... | collective-permute-start | bytes 294920 | tf_op jit(solution)/shard_map/ppermute | solution.py:318
  11.9 11.8 %collective-permute-start.4 = (bf16[3,64,256]{2,1,0:T(8,128)(2,1)S(1)}, bf16[3,64,256]{2,1,0:T(8,128)(2,1)S(1)}, u32[]{:S(2)}, u32[]{:S(2)}) collective-permute-start(bf16[3,64,256]{2,1,0:T(8,128)(2,1)S(1)} %get-tuple-element.43), channel_id=1, source_target_pairs={{0,8},{4,12},{8,16},{12,20},{16,24},{20,28},{24,0},{28,4},{1,9},{5... | collective-permute-start | bytes 294920 | tf_op jit(solution)/shard_map/ppermute | solution.py:318
  14.4 9.2 %collective-permute-start.5 = (bf16[3,64,256]{2,1,0:T(8,128)(2,1)S(1)}, bf16[3,64,256]{2,1,0:T(8,128)(2,1)S(1)}, u32[]{:S(2)}, u32[]{:S(2)}) collective-permute-start(bf16[3,64,256]{2,1,0:T(8,128)(2,1)S(1)} %get-tuple-element.44), channel_id=1, source_target_pairs={{0,24},{4,28},{8,0},{12,4},{16,8},{20,12},{24,16},{28,20},{1,25},{... | collective-permute-start | bytes 294920 | tf_op jit(solution)/shard_map/ppermute | solution.py:318
  16.0 7.7 %collective-permute-start.6 = (bf16[3,64,256]{2,1,0:T(8,128)(2,1)S(1)}, bf16[3,64,256]{2,1,0:T(8,128)(2,1)S(1)}, u32[]{:S(2)}, u32[]{:S(2)}) collective-permute-start(bf16[3,64,256]{2,1,0:T(8,128)(2,1)S(1)} %get-tuple-element.45), channel_id=1, source_target_pairs={{0,4},{4,0},{8,12},{12,8},{16,20},{20,16},{24,28},{28,24},{1,5},{5... | collective-permute-start | bytes 294920 | tf_op jit(solution)/shard_map/ppermute | solution.py:318
  28.2 11.2 %collective-permute-start.7 = (bf16[3,64,256]{2,1,0:T(8,128)(2,1)S(1)}, bf16[3,64,256]{2,1,0:T(8,128)(2,1)S(1)}, u32[]{:S(2)}, u32[]{:S(2)}) collective-permute-start(bf16[3,64,256]{2,1,0:T(8,128)(2,1)S(1)} %get-tuple-element.47), channel_id=1, source_target_pairs={{0,20},{4,16},{8,28},{12,24},{16,4},{20,0},{24,12},{28,8},{1,21},{... | collective-permute-start | bytes 294920 | tf_op jit(solution)/shard_map/ppermute | solution.py:318
  32.3 8.6 %collective-permute-start.8 = (bf16[3,64,256]{2,1,0:T(8,128)(2,1)S(1)}, bf16[3,64,256]{2,1,0:T(8,128)(2,1)S(1)}, u32[]{:S(2)}, u32[]{:S(2)}) collective-permute-start(bf16[3,64,256]{2,1,0:T(8,128)(2,1)S(1)} %get-tuple-element.48), channel_id=1, source_target_pairs={{0,12},{4,8},{8,20},{12,16},{16,28},{20,24},{24,4},{28,0},{1,13},{... | collective-permute-start | bytes 294920 | tf_op jit(solution)/shard_map/ppermute | solution.py:318
  32.3 9.6 %collective-permute-start.9 = (bf16[3,64,256]{2,1,0:T(8,128)(2,1)S(1)}, bf16[3,64,256]{2,1,0:T(8,128)(2,1)S(1)}, u32[]{:S(2)}, u32[]{:S(2)}) collective-permute-start(bf16[3,64,256]{2,1,0:T(8,128)(2,1)S(1)} %get-tuple-element.49), channel_id=1, source_target_pairs={{0,28},{4,24},{8,4},{12,0},{16,12},{20,8},{24,20},{28,16},{1,29},{... | collective-permute-start | bytes 294920 | tf_op jit(solution)/shard_map/ppermute | solution.py:318
  37.0 10.8 %collective-permute-start.10 = (bf16[3,64,256]{2,1,0:T(8,128)(2,1)S(1)}, bf16[3,64,256]{2,1,0:T(8,128)(2,1)S(1)}, u32[]{:S(2)}, u32[]{:S(2)}) collective-permute-start(bf16[3,64,256]{2,1,0:T(8,128)(2,1)S(1)} %get-tuple-element.50), channel_id=1, source_target_pairs={{0,16},{4,20},{8,24},{12,28},{16,0},{20,4},{24,8},{28,12},{1,17},{... | collective-permute-start | bytes 294920 | tf_op jit(solution)/shard_map/ppermute | solution.py:318
  37.0 10.8 %collective-permute-start.11 = (bf16[3,64,256]{2,1,0:T(8,128)(2,1)S(1)}, bf16[3,64,256]{2,1,0:T(8,128)(2,1)S(1)}, u32[]{:S(2)}, u32[]{:S(2)}) collective-permute-start(bf16[3,64,256]{2,1,0:T(8,128)(2,1)S(1)} %get-tuple-element.51), channel_id=1, source_target_pairs={{0,8},{4,12},{8,16},{12,20},{16,24},{20,28},{24,0},{28,4},{1,9},{5... | collective-permute-start | bytes 294920 | tf_op jit(solution)/shard_map/ppermute | solution.py:318
  39.4 8.4 %collective-permute-start.12 = (bf16[3,64,256]{2,1,0:T(8,128)(2,1)S(1)}, bf16[3,64,256]{2,1,0:T(8,128)(2,1)S(1)}, u32[]{:S(2)}, u32[]{:S(2)}) collective-permute-start(bf16[3,64,256]{2,1,0:T(8,128)(2,1)S(1)} %get-tuple-element.52), channel_id=1, source_target_pairs={{0,24},{4,28},{8,0},{12,4},{16,8},{20,12},{24,16},{28,20},{1,25},{... | collective-permute-start | bytes 294920 | tf_op jit(solution)/shard_map/ppermute | solution.py:318
  40.8 7.0 %collective-permute-start.13 = (bf16[3,64,256]{2,1,0:T(8,128)(2,1)S(1)}, bf16[3,64,256]{2,1,0:T(8,128)(2,1)S(1)}, u32[]{:S(2)}, u32[]{:S(2)}) collective-permute-start(bf16[3,64,256]{2,1,0:T(8,128)(2,1)S(1)} %get-tuple-element.53), channel_id=1, source_target_pairs={{0,4},{4,0},{8,12},{12,8},{16,20},{20,16},{24,28},{28,24},{1,5},{5... | collective-permute-start | bytes 294920 | tf_op jit(solution)/shard_map/ppermute | solution.py:318
  48.5 1.6 %collective-permute-start.14 = (bf16[256,512]{1,0:T(8,128)(2,1)S(1)}, bf16[256,512]{1,0:T(8,128)(2,1)S(1)}, u32[]{:S(2)}, u32[]{:S(2)}) collective-permute-start(bf16[256,512]{1,0:T(8,128)(2,1)S(1)} %get-tuple-element.63), channel_id=1, source_target_pairs={{0,1},{1,0},{2,3},{3,2},{4,5},{5,4},{6,7},{7,6},{8,9},{9,8},{10,11... | collective-permute-start | bytes 786440 | tf_op jit(solution)/shard_map/ppermute | solution.py:312
  50.2 8.4 %collective-permute-start.15 = (bf16[256,512]{1,0:T(8,128)(2,1)S(1)}, bf16[256,512]{1,0:T(8,128)(2,1)S(1)}, u32[]{:S(2)}, u32[]{:S(2)}) collective-permute-start(bf16[256,512]{1,0:T(8,128)(2,1)S(1)} %add_convert_fusion.1), channel_id=1, source_target_pairs={{0,2},{1,3},{2,0},{3,1},{4,6},{5,7},{6,4},{7,5},{8,10},{9,11},{10,... | collective-permute-start | bytes 786440 | tf_op jit(solution)/shard_map/ppermute | solution.py:312
  51.8 6.9 %collective-permute-start.16 = (bf16[256,512]{1,0:T(8,128)(2,1)S(1)}, bf16[256,512]{1,0:T(8,128)(2,1)S(1)}, u32[]{:S(2)}, u32[]{:S(2)}) collective-permute-start(bf16[256,512]{1,0:T(8,128)(2,1)S(1)} %get-tuple-element.66), channel_id=1, source_target_pairs={{0,1},{1,0},{2,3},{3,2},{4,5},{5,4},{6,7},{7,6},{8,9},{9,8},{10,11... | collective-permute-start | bytes 786440 | tf_op jit(solution)/shard_map/ppermute | solution.py:312

commit v12 on v9

--- a/solution.py
+++ b/solution.py
@@ -100,7 +100,7 @@
 
 def late_steps(blocks):
     far = [step for step, distance in enumerate(distances(blocks)) if 2 * distance >= blocks]
-    return far[: len(far) // 2]
+    return far[len(far) // 2 : len(far) // 2 + 1]
 
 
 def by_distance(pieces):

time: 60.9 us -> 61.1 us (level)
  waiting for transfers between devices: 17.2 us -> 21.6 us
  starting transfers between devices: 32.9 us -> 28.7 us
    ppermute x19 -> x18, waiting for transfers between devices: 17.2 us -> 21.6 us  [exchange(): return lax.ppermute(block, axis, pairs)]
    ppermute x19 -> x18, starting transfers between devices: 32.9 us -> 28.7 us  [exchange(): return lax.ppermute(block, axis, pairs)]
  transfers between devices with their start and end apart: 19 -> 18, of which waited for: 8 -> 7; matrix products, arithmetic and copies ran while one was open for 0% -> 0% of each run, Pallas kernels for 4% -> 4%
where the time goes in v12:
time: 61.1 us; the launch traced here: 61 us
  starting transfers between devices  28.7 us (47%)
  waiting for transfers between devices  21.6 us (35%)
  Pallas kernels  9.13 us (15%)
  other arithmetic  0.87 us (1%)
  between operations  0.7 us (1%)
    ppermute x18, starting transfers between devices, exchange(): return lax.ppermute(block, axis, pairs)  28.7 us
    ppermute x18, waiting for transfers between devices, exchange(): return lax.ppermute(block, axis, pairs)  21.6 us
    pallas_call x1, Pallas kernels, per_device(): pl.pallas_call(conv_kernel, in_specs=[VMEM] * blocks + [HBM] * 9, out_sha...  4.48 us
    pallas_call x1, Pallas kernels, per_device(): pl.pallas_call(gate_kernel, in_specs=[HBM] * 5, out_shape=arrays(blocks,...  1.5 us
  transfers between devices with their start and end apart: 18, of which 7 were waited for; matrix products, arithmetic and copies ran while one was open for 0% of the time, Pallas kernels for 4%

profile of v12, /device:TPU:0, one launch (start us, length us, event | category | flops | bytes accessed | tf_op | source)
XLA Modules:
  0.0 61.0 jit_solution(10991096149739121543)
XLA Ops:
  0.6 1.5 %gate.1 = (bf16[3,64,256]{2,1,0:T(8,128)(2,1)S(1)}, bf16[3,64,256]{2,1,0:T(8,128)(2,1)S(1)}, bf16[3,64,256]{2,1,0:T(8,128)(2,1)S(1)}, bf16[3,64,256]{2,1,0:T(8,1...) custom-call(bf16[256,512]{1,0:T(8,128)(2,1)} %refs_0_.1, ...), custom_call_target="tpu_custom_call" | custom-call | tf_op jit(solution)/shard_map/gate/pallas_call | solution.py:346
  2.1 6.1 %collective-permute-start = (bf16[3,64,256]{2,1,0:T(8,128)(2,1)S(1)}, bf16[3,64,256]{2,1,0:T(8,128)(2,1)S(1)}, u32[]{:S(2)}, u32[]{:S(2)}) collective-permute-start(bf16[3,64,256]{2,1,0:T(8,128)(2,1)S(1)} %get-tuple-element.35), channel_id=1, source_target_pairs={{0,28},{4,24},{8,20},{12,16},{16,12},{20,8},{24,4},{28,0},{1,29},{... | collective-permute-start | bytes 294920 | tf_op jit(solution)/shard_map/ppermute | solution.py:314
  8.2 0.5 collective-permute-start.1
  8.7 0.1 collective-permute-start.2
  8.9 0.0 collective-permute-start.3
  8.9 5.2 %collective-permute-start.4 = (bf16[3,64,256]{2,1,0:T(8,128)(2,1)S(1)}, bf16[3,64,256]{2,1,0:T(8,128)(2,1)S(1)}, u32[]{:S(2)}, u32[]{:S(2)}) collective-permute-start(bf16[3,64,256]{2,1,0:T(8,128)(2,1)S(1)} %get-tuple-element.39), channel_id=1, source_target_pairs={{0,20},{4,16},{8,28},{12,24},{16,4},{20,0},{24,12},{28,8},{1,21},{... | collective-permute-start | bytes 294920 | tf_op jit(solution)/shard_map/ppermute | solution.py:314
  14.1 0.0 collective-permute-done.refs_0_
  14.1 1.7 %collective-permute-start.5 = (bf16[3,64,256]{2,1,0:T(8,128)(2,1)S(1)}, bf16[3,64,256]{2,1,0:T(8,128)(2,1)S(1)}, u32[]{:S(2)}, u32[]{:S(2)}) collective-permute-start(bf16[3,64,256]{2,1,0:T(8,128)(2,1)S(1)} %get-tuple-element.40), channel_id=1, source_target_pairs={{0,12},{4,8},{8,4},{12,0},{16,28},{20,24},{24,20},{28,16},{1,13},{... | collective-permute-start | bytes 294920 | tf_op jit(solution)/shard_map/ppermute | solution.py:314
  15.7 0.0 collective-permute-done.1.refs_1_
  15.7 1.5 %collective-permute-start.6 = (bf16[3,64,256]{2,1,0:T(8,128)(2,1)S(1)}, bf16[3,64,256]{2,1,0:T(8,128)(2,1)S(1)}, u32[]{:S(2)}, u32[]{:S(2)}) collective-permute-start(bf16[3,64,256]{2,1,0:T(8,128)(2,1)S(1)} %get-tuple-element.41), channel_id=1, source_target_pairs={{0,16},{4,20},{8,24},{12,28},{16,0},{20,4},{24,8},{28,12},{1,17},{... | collective-permute-start | bytes 294920 | tf_op jit(solution)/shard_map/ppermute | solution.py:314
  17.3 0.0 collective-permute-done.2.refs_2_
  17.3 0.0 collective-permute-done.3.refs_3_
  17.3 5.2 %collective-permute-done.4.refs_4_ = bf16[3,64,256]{2,1,0:T(8,128)(2,1)S(1)} collective-permute-done((bf16[3,64,256]{2,1,0:T(8,128)(2,1)S(1)}, bf16[3,64,256]{2,1,0:T(8,128)(2,1)S(1)}, u32[]{:S(2)}, u32[]{:S(2)}) %collective-permute-start.4) | collective-permute-done | bytes 98336 | tf_op jit(solution)/shard_map/ppermute | solution.py:314
  22.5 0.0 collective-permute-done.5.refs_5_
  22.5 2.4 %collective-permute-done.6.refs_6_ = bf16[3,64,256]{2,1,0:T(8,128)(2,1)S(1)} collective-permute-done((bf16[3,64,256]{2,1,0:T(8,128)(2,1)S(1)}, bf16[3,64,256]{2,1,0:T(8,128)(2,1)S(1)}, u32[]{:S(2)}, u32[]{:S(2)}) %collective-permute-start.6) | collective-permute-done | bytes 98336 | tf_op jit(solution)/shard_map/ppermute | solution.py:314
  24.9 4.5 %conv.1 = (bf16[3,64,256]{2,1,0:T(8,128)(2,1)S(1)}, bf16[3,64,256]{2,1,0:T(8,128)(2,1)S(1)}, bf16[3,64,256]{2,1,0:T(8,128)(2,1)S(1)}, bf16[3,64,256]{2,1,0:T(8,1...) custom-call(bf16[3,64,256]{2,1,0:T(8,128)(2,1)S(1)} %collective-perm, ...), custom_call_target="tpu_custom_call" | custom-call | tf_op jit(solution)/shard_map/conv/pallas_call | solution.py:366
  29.4 2.6 %collective-permute-start.7 = (bf16[3,64,256]{2,1,0:T(8,128)(2,1)S(1)}, bf16[3,64,256]{2,1,0:T(8,128)(2,1)S(1)}, u32[]{:S(2)}, u32[]{:S(2)}) collective-permute-start(bf16[3,64,256]{2,1,0:T(8,128)(2,1)S(1)} %get-tuple-element.43), channel_id=1, source_target_pairs={{0,28},{4,24},{8,20},{12,16},{16,12},{20,8},{24,4},{28,0},{1,29},{... | collective-permute-start | bytes 294920 | tf_op jit(solution)/shard_map/ppermute | solution.py:314
  32.0 0.0 collective-permute-start.11
  32.0 1.5 %collective-permute-start.8 = (bf16[3,64,256]{2,1,0:T(8,128)(2,1)S(1)}, bf16[3,64,256]{2,1,0:T(8,128)(2,1)S(1)}, u32[]{:S(2)}, u32[]{:S(2)}) collective-permute-start(bf16[3,64,256]{2,1,0:T(8,128)(2,1)S(1)} %get-tuple-element.44), channel_id=1, source_target_pairs={{0,4},{4,0},{8,12},{12,8},{16,20},{20,16},{24,28},{28,24},{1,5},{5... | collective-permute-start | bytes 294920 | tf_op jit(solution)/shard_map/ppermute | solution.py:314
  33.4 1.3 %collective-permute-start.9 = (bf16[3,64,256]{2,1,0:T(8,128)(2,1)S(1)}, bf16[3,64,256]{2,1,0:T(8,128)(2,1)S(1)}, u32[]{:S(2)}, u32[]{:S(2)}) collective-permute-start(bf16[3,64,256]{2,1,0:T(8,128)(2,1)S(1)} %get-tuple-element.45), channel_id=1, source_target_pairs={{0,24},{4,28},{8,16},{12,20},{16,8},{20,12},{24,0},{28,4},{1,25},{... | collective-permute-start | bytes 294920 | tf_op jit(solution)/shard_map/ppermute | solution.py:314
  34.8 2.2 %collective-permute-start.10 = (bf16[3,64,256]{2,1,0:T(8,128)(2,1)S(1)}, bf16[3,64,256]{2,1,0:T(8,128)(2,1)S(1)}, u32[]{:S(2)}, u32[]{:S(2)}) collective-permute-start(bf16[3,64,256]{2,1,0:T(8,128)(2,1)S(1)} %get-tuple-element.46), channel_id=1, source_target_pairs={{0,8},{4,12},{8,0},{12,4},{16,24},{20,28},{24,16},{28,20},{1,9},{5... | collective-permute-start | bytes 294920 | tf_op jit(solution)/shard_map/ppermute | solution.py:314
  36.9 4.3 %collective-permute-done.11.refs_4_ = bf16[2,64,256]{2,1,0:T(8,128)(2,1)S(1)} collective-permute-done((bf16[2,64,256]{2,1,0:T(8,128)(2,1)S(1)}, bf16[2,64,256]{2,1,0:T(8,128)(2,1)S(1)}, u32[]{:S(2)}, u32[]{:S(2)}) %collective-permute-start.11) | collective-permute-done | bytes 65568 | tf_op jit(solution)/shard_map/ppermute | solution.py:314
  41.2 0.0 collective-permute-start.12
  41.2 0.0 collective-permute-done.7.refs_0_
  41.2 3.1 %collective-permute-start.13 = (bf16[3,64,256]{2,1,0:T(8,128)(2,1)S(1)}, bf16[3,64,256]{2,1,0:T(8,128)(2,1)S(1)}, u32[]{:S(2)}, u32[]{:S(2)}) collective-permute-start(bf16[3,64,256]{2,1,0:T(8,128)(2,1)S(1)} %get-tuple-element.49), channel_id=1, source_target_pairs={{0,16},{4,20},{8,24},{12,28},{16,0},{20,4},{24,8},{28,12},{1,17},{... | collective-permute-start | bytes 294920 | tf_op jit(solution)/shard_map/ppermute | solution.py:314
  44.3 0.0 collective-permute-done.8.refs_1_
  44.3 0.0 collective-permute-done.9.refs_2_
  44.3 0.0 collective-permute-done.10.refs_3_
  44.3 4.3 %collective-permute-done.12.refs_5_ = bf16[3,64,256]{2,1,0:T(8,128)(2,1)S(1)} collective-permute-done((bf16[3,64,256]{2,1,0:T(8,128)(2,1)S(1)}, bf16[3,64,256]{2,1,0:T(8,128)(2,1)S(1)}, u32[]{:S(2)}, u32[]{:S(2)}) %collective-permute-start.12) | collective-permute-done | bytes 98336 | tf_op jit(solution)/shard_map/ppermute | solution.py:314
  48.6 0.5 collective-permute-done.13.refs_6_
  49.0 0.7 %mate.1 = (bf16[3,256,512]{2,1,0:T(8,128)(2,1)S(1)}, bf16[256,512]{1,0:T(8,128)(2,1)S(1)}) custom-call(bf16[3,64,256]{2,1,0:T(8,128)(2,1)S(1)} %collective-permute-done.7.refs_0_, bf16[3,64,256]{2,1,0:T(8,128)(2,1)S(1)} %collective-permute-done.8.refs_1_, bf16[3,64,256]{2,1,0:T(8,128)(2,1)S(1)} %collective-permute-done.9.refs_2_, ...), custom_call_target="tpu_custom_call" | custom-call | flops 805306368 | bytes 4194304 | tf_op jit(solution)/shard_map/mate/pallas_call | solution.py:387
  49.7 0.1 collective-permute-start.14
  49.8 1.0 %far.1 = (f32[256,512]{1,0:T(8,128)S(1)}, bf16[256,512]{1,0:T(8,128)(2,1)S(1)}) custom-call(bf16[3,256,512]{2,1,0:T(8,128)(2,1)S(1)} %get-tuple-element.64.lhs_ref, bf16[2048,512]{1,0:T(8,128)(2,1)S(1)} %get-tuple-element.54.refs_11_.wk_ref, bf16[2048,512]{1,0:T(8,128)(2,1)S(1)} %get-tuple-element.55.refs_12_.wq_ref, ...), custom_call_target="tpu_custom_call" | custom-call | flops 805306368 | bytes 4194304 | tf_op jit(solution)/shard_map/far/pallas_call | solution.py:397
  50.8 0.5 collective-permute-done.14
  51.3 0.1 add_convert_fusion.1
  51.4 1.6 %collective-permute-start.15 = (bf16[256,512]{1,0:T(8,128)(2,1)S(1)}, bf16[256,512]{1,0:T(8,128)(2,1)S(1)}, u32[]{:S(2)}, u32[]{:S(2)}) collective-permute-start(bf16[256,512]{1,0:T(8,128)(2,1)S(1)} %add_convert_fusion.1), channel_id=1, source_target_pairs={{0,2},{1,3},{2,0},{3,1},{4,6},{5,7},{6,4},{7,5},{8,10},{9,11},{10,... | collective-permute-start | bytes 786440 | tf_op jit(solution)/shard_map/ppermute | solution.py:314
  52.9 0.0 collective-permute-start.16
  52.9 0.6 own.1
  53.5 1.4 %collective-permute-start.17 = (bf16[1,64,256]{2,1,0:T(8,128)(2,1)S(1)}, bf16[1,64,256]{2,1,0:T(8,128)(2,1)S(1)}, u32[]{:S(2)}, u32[]{:S(2)}) collective-permute-start(bf16[1,64,256]{2,1,0:T(8,128)(2,1)S(1)} %get-tuple-element.67), channel_id=1, source_target_pairs={{0,20},{4,16},{8,28},{12,24},{16,4},{20,0},{24,12},{28,8},{1,21},{... | collective-permute-start | bytes 98312 | tf_op jit(solution)/shard_map/ppermute | solution.py:314
  54.9 4.4 %collective-permute-done.17.refs_8_ = bf16[1,64,256]{2,1,0:T(8,128)(2,1)S(1)} collective-permute-done((bf16[1,64,256]{2,1,0:T(8,128)(2,1)S(1)}, bf16[1,64,256]{2,1,0:T(8,128)(2,1)S(1)}, u32[]{:S(2)}, u32[]{:S(2)}) %collective-permute-start.17) | collective-permute-done | bytes 32800 | tf_op jit(solution)/shard_map/ppermute | solution.py:314
  59.3 0.9 %turn.1 = bf16[256,512]{1,0:T(8,128)(2,1)} custom-call(bf16[3,64,256]{2,1,0:T(8,128)(2,1)S(1)} %collective-permute-done.7.refs_0_, bf16[3,64,256]{2,1,0:T(8,128)(2,1)S(1)} %collective-permute-done.8.refs_1_, bf16[3,64,256]{2,1,0:T(8,128)(2,1)S(1)} %collective-permute-done.9.refs_2_, bf16[3,64,256]{2,1,0:T(8,128)(2,1)S(1)} %collective-permute-done.10.refs_3_, ...), custom_call_target="tpu_custom_call" | custom-call | flops 805306368 | bytes 4194304 | tf_op jit(solution)/shard_map/turn/pallas_call | solution.py:418
  60.2 0.0 collective-permute-done.15
  60.2 0.0 collective-permute-done.16
  60.2 0.8 %add_convert_fusion = bf16[256,512]{1,0:T(8,128)(2,1)} fusion(f32[256,512]{1,0:T(8,128)S(1)} %own.1, bf16[256,512]{1,0:T(8,128)(2,1)S(1)} %collective-permute-done.16, bf16[256,512]{1,0:T(8,128)(2,1)S(1)} %collective-permute-done.15), kind=kLoop, calls=%fused_computation | loop fusion | flops 655360 | bytes 1310720 | tf_op jit(solution)/shard_map/convert_element_type | solution.py:428
Async XLA Ops:
  2.1 11.9 %collective-permute-start = (bf16[3,64,256]{2,1,0:T(8,128)(2,1)S(1)}, bf16[3,64,256]{2,1,0:T(8,128)(2,1)S(1)}, u32[]{:S(2)}, u32[]{:S(2)}) collective-permute-start(bf16[3,64,256]{2,1,0:T(8,128)(2,1)S(1)} %get-tuple-element.35), channel_id=1, source_target_pairs={{0,28},{4,24},{8,20},{12,16},{16,12},{20,8},{24,4},{28,0},{1,29},{... | collective-permute-start | bytes 294920 | tf_op jit(solution)/shard_map/ppermute | solution.py:314
  8.2 7.5 %collective-permute-start.1 = (bf16[3,64,256]{2,1,0:T(8,128)(2,1)S(1)}, bf16[3,64,256]{2,1,0:T(8,128)(2,1)S(1)}, u32[]{:S(2)}, u32[]{:S(2)}) collective-permute-start(bf16[3,64,256]{2,1,0:T(8,128)(2,1)S(1)} %get-tuple-element.36), channel_id=1, source_target_pairs={{0,4},{4,0},{8,12},{12,8},{16,20},{20,16},{24,28},{28,24},{1,5},{5... | collective-permute-start | bytes 294920 | tf_op jit(solution)/shard_map/ppermute | solution.py:314
  8.7 8.5 %collective-permute-start.2 = (bf16[3,64,256]{2,1,0:T(8,128)(2,1)S(1)}, bf16[3,64,256]{2,1,0:T(8,128)(2,1)S(1)}, u32[]{:S(2)}, u32[]{:S(2)}) collective-permute-start(bf16[3,64,256]{2,1,0:T(8,128)(2,1)S(1)} %get-tuple-element.37), channel_id=1, source_target_pairs={{0,24},{4,28},{8,16},{12,20},{16,8},{20,12},{24,0},{28,4},{1,25},{... | collective-permute-start | bytes 294920 | tf_op jit(solution)/shard_map/ppermute | solution.py:314
  8.9 8.4 %collective-permute-start.3 = (bf16[3,64,256]{2,1,0:T(8,128)(2,1)S(1)}, bf16[3,64,256]{2,1,0:T(8,128)(2,1)S(1)}, u32[]{:S(2)}, u32[]{:S(2)}) collective-permute-start(bf16[3,64,256]{2,1,0:T(8,128)(2,1)S(1)} %get-tuple-element.38), channel_id=1, source_target_pairs={{0,8},{4,12},{8,0},{12,4},{16,24},{20,28},{24,16},{28,20},{1,9},{5... | collective-permute-start | bytes 294920 | tf_op jit(solution)/shard_map/ppermute | solution.py:314
  8.9 13.6 %collective-permute-start.4 = (bf16[3,64,256]{2,1,0:T(8,128)(2,1)S(1)}, bf16[3,64,256]{2,1,0:T(8,128)(2,1)S(1)}, u32[]{:S(2)}, u32[]{:S(2)}) collective-permute-start(bf16[3,64,256]{2,1,0:T(8,128)(2,1)S(1)} %get-tuple-element.39), channel_id=1, source_target_pairs={{0,20},{4,16},{8,28},{12,24},{16,4},{20,0},{24,12},{28,8},{1,21},{... | collective-permute-start | bytes 294920 | tf_op jit(solution)/shard_map/ppermute | solution.py:314
  14.1 8.4 %collective-permute-start.5 = (bf16[3,64,256]{2,1,0:T(8,128)(2,1)S(1)}, bf16[3,64,256]{2,1,0:T(8,128)(2,1)S(1)}, u32[]{:S(2)}, u32[]{:S(2)}) collective-permute-start(bf16[3,64,256]{2,1,0:T(8,128)(2,1)S(1)} %get-tuple-element.40), channel_id=1, source_target_pairs={{0,12},{4,8},{8,4},{12,0},{16,28},{20,24},{24,20},{28,16},{1,13},{... | collective-permute-start | bytes 294920 | tf_op jit(solution)/shard_map/ppermute | solution.py:314
  15.7 9.2 %collective-permute-start.6 = (bf16[3,64,256]{2,1,0:T(8,128)(2,1)S(1)}, bf16[3,64,256]{2,1,0:T(8,128)(2,1)S(1)}, u32[]{:S(2)}, u32[]{:S(2)}) collective-permute-start(bf16[3,64,256]{2,1,0:T(8,128)(2,1)S(1)} %get-tuple-element.41), channel_id=1, source_target_pairs={{0,16},{4,20},{8,24},{12,28},{16,0},{20,4},{24,8},{28,12},{1,17},{... | collective-permute-start | bytes 294920 | tf_op jit(solution)/shard_map/ppermute | solution.py:314
  29.4 11.8 %collective-permute-start.7 = (bf16[3,64,256]{2,1,0:T(8,128)(2,1)S(1)}, bf16[3,64,256]{2,1,0:T(8,128)(2,1)S(1)}, u32[]{:S(2)}, u32[]{:S(2)}) collective-permute-start(bf16[3,64,256]{2,1,0:T(8,128)(2,1)S(1)} %get-tuple-element.43), channel_id=1, source_target_pairs={{0,28},{4,24},{8,20},{12,16},{16,12},{20,8},{24,4},{28,0},{1,29},{... | collective-permute-start | bytes 294920 | tf_op jit(solution)/shard_map/ppermute | solution.py:314
  32.0 9.2 %collective-permute-start.11 = (bf16[2,64,256]{2,1,0:T(8,128)(2,1)S(1)}, bf16[2,64,256]{2,1,0:T(8,128)(2,1)S(1)}, u32[]{:S(2)}, u32[]{:S(2)}) collective-permute-start(bf16[2,64,256]{2,1,0:T(8,128)(2,1)S(1)} %get-tuple-element.47), channel_id=1, source_target_pairs={{0,20},{4,16},{8,28},{12,24},{16,4},{20,0},{24,12},{28,8},{1,21},{... | collective-permute-start | bytes 196616 | tf_op jit(solution)/shard_map/ppermute | solution.py:314
  32.0 12.3 %collective-permute-start.8 = (bf16[3,64,256]{2,1,0:T(8,128)(2,1)S(1)}, bf16[3,64,256]{2,1,0:T(8,128)(2,1)S(1)}, u32[]{:S(2)}, u32[]{:S(2)}) collective-permute-start(bf16[3,64,256]{2,1,0:T(8,128)(2,1)S(1)} %get-tuple-element.44), channel_id=1, source_target_pairs={{0,4},{4,0},{8,12},{12,8},{16,20},{20,16},{24,28},{28,24},{1,5},{5... | collective-permute-start | bytes 294920 | tf_op jit(solution)/shard_map/ppermute | solution.py:314
  33.4 10.8 %collective-permute-start.9 = (bf16[3,64,256]{2,1,0:T(8,128)(2,1)S(1)}, bf16[3,64,256]{2,1,0:T(8,128)(2,1)S(1)}, u32[]{:S(2)}, u32[]{:S(2)}) collective-permute-start(bf16[3,64,256]{2,1,0:T(8,128)(2,1)S(1)} %get-tuple-element.45), channel_id=1, source_target_pairs={{0,24},{4,28},{8,16},{12,20},{16,8},{20,12},{24,0},{28,4},{1,25},{... | collective-permute-start | bytes 294920 | tf_op jit(solution)/shard_map/ppermute | solution.py:314
  34.8 9.5 %collective-permute-start.10 = (bf16[3,64,256]{2,1,0:T(8,128)(2,1)S(1)}, bf16[3,64,256]{2,1,0:T(8,128)(2,1)S(1)}, u32[]{:S(2)}, u32[]{:S(2)}) collective-permute-start(bf16[3,64,256]{2,1,0:T(8,128)(2,1)S(1)} %get-tuple-element.46), channel_id=1, source_target_pairs={{0,8},{4,12},{8,0},{12,4},{16,24},{20,28},{24,16},{28,20},{1,9},{5... | collective-permute-start | bytes 294920 | tf_op jit(solution)/shard_map/ppermute | solution.py:314
  41.2 7.4 %collective-permute-start.12 = (bf16[3,64,256]{2,1,0:T(8,128)(2,1)S(1)}, bf16[3,64,256]{2,1,0:T(8,128)(2,1)S(1)}, u32[]{:S(2)}, u32[]{:S(2)}) collective-permute-start(bf16[3,64,256]{2,1,0:T(8,128)(2,1)S(1)} %get-tuple-element.48), channel_id=1, source_target_pairs={{0,12},{4,8},{8,4},{12,0},{16,28},{20,24},{24,20},{28,16},{1,13},{... | collective-permute-start | bytes 294920 | tf_op jit(solution)/shard_map/ppermute | solution.py:314
  41.2 7.8 %collective-permute-start.13 = (bf16[3,64,256]{2,1,0:T(8,128)(2,1)S(1)}, bf16[3,64,256]{2,1,0:T(8,128)(2,1)S(1)}, u32[]{:S(2)}, u32[]{:S(2)}) collective-permute-start(bf16[3,64,256]{2,1,0:T(8,128)(2,1)S(1)} %get-tuple-element.49), channel_id=1, source_target_pairs={{0,16},{4,20},{8,24},{12,28},{16,0},{20,4},{24,8},{28,12},{1,17},{... | collective-permute-start | bytes 294920 | tf_op jit(solution)/shard_map/ppermute | solution.py:314
  49.7 1.6 %collective-permute-start.14 = (bf16[256,512]{1,0:T(8,128)(2,1)S(1)}, bf16[256,512]{1,0:T(8,128)(2,1)S(1)}, u32[]{:S(2)}, u32[]{:S(2)}) collective-permute-start(bf16[256,512]{1,0:T(8,128)(2,1)S(1)} %get-tuple-element.59), channel_id=1, source_target_pairs={{0,1},{1,0},{2,3},{3,2},{4,5},{5,4},{6,7},{7,6},{8,9},{9,8},{10,11... | collective-permute-start | bytes 786440 | tf_op jit(solution)/shard_map/ppermute | solution.py:314
  51.4 8.8 %collective-permute-start.15 = (bf16[256,512]{1,0:T(8,128)(2,1)S(1)}, bf16[256,512]{1,0:T(8,128)(2,1)S(1)}, u32[]{:S(2)}, u32[]{:S(2)}) collective-permute-start(bf16[256,512]{1,0:T(8,128)(2,1)S(1)} %add_convert_fusion.1), channel_id=1, source_target_pairs={{0,2},{1,3},{2,0},{3,1},{4,6},{5,7},{6,4},{7,5},{8,10},{9,11},{10,... | collective-permute-start | bytes 786440 | tf_op jit(solution)/shard_map/ppermute | solution.py:314
  52.9 7.3 %collective-permute-start.16 = (bf16[256,512]{1,0:T(8,128)(2,1)S(1)}, bf16[256,512]{1,0:T(8,128)(2,1)S(1)}, u32[]{:S(2)}, u32[]{:S(2)}) collective-permute-start(bf16[256,512]{1,0:T(8,128)(2,1)S(1)} %get-tuple-element.63), channel_id=1, source_target_pairs={{0,1},{1,0},{2,3},{3,2},{4,5},{5,4},{6,7},{7,6},{8,9},{9,8},{10,11... | collective-permute-start | bytes 786440 | tf_op jit(solution)/shard_map/ppermute | solution.py:314
  53.5 5.8 %collective-permute-start.17 = (bf16[1,64,256]{2,1,0:T(8,128)(2,1)S(1)}, bf16[1,64,256]{2,1,0:T(8,128)(2,1)S(1)}, u32[]{:S(2)}, u32[]{:S(2)}) collective-permute-start(bf16[1,64,256]{2,1,0:T(8,128)(2,1)S(1)} %get-tuple-element.67), channel_id=1, source_target_pairs={{0,20},{4,16},{8,28},{12,24},{16,4},{20,0},{24,12},{28,8},{1,21},{... | collective-permute-start | bytes 98312 | tf_op jit(solution)/shard_map/ppermute | solution.py:314

commit v13 on v6

--- a/solution.py
+++ b/solution.py
@@ -13,7 +13,7 @@
     return pltpu.CompilerParams(vmem_limit_bytes=int(mib * 1024 * 1024))
 
 
-def dft_tables(blocks, block_len, scale):
+def dft_tables(blocks, block_len, scale, rows_count):
     index = np.arange(block_len)
     angle = 2.0 * np.pi * (np.outer(index, index) % block_len) / block_len
     cos, sin = np.cos(angle), np.sin(angle)
@@ -22,13 +22,13 @@
     rows = np.arange(blocks + 1)
     phase = 2.0 * np.pi * np.outer(rows, index) / (2 * blocks * block_len)
     weight = np.where((rows == 0) | (rows == blocks), 1.0, 2.0)[:, None] * scale
-    twiddle = np.stack(
-        [np.cos(phase), np.sin(phase), weight * np.cos(phase), weight * np.sin(phase)]
-    )
+    twiddle = np.stack([np.cos(phase), np.sin(phase)])
+    untwiddle = np.repeat((weight * twiddle)[:, :, None, :], rows_count, axis=2)
     return (
         jnp.asarray(forward, jnp.bfloat16),
         jnp.asarray(inverse, jnp.bfloat16),
         jnp.asarray(twiddle, jnp.float32),
+        jnp.asarray(untwiddle, jnp.bfloat16),
     )
 
 
@@ -134,11 +134,11 @@
 
 def conv_kernel(*refs):
     blocks = lax.axis_size("ctx")
-    in_refs, sources, refs = refs[:blocks], refs[blocks : blocks + 9], refs[blocks + 9 :]
+    in_refs, sources, refs = refs[:blocks], refs[blocks : blocks + 10], refs[blocks + 10 :]
     out_refs, held_refs = refs[:blocks], refs[blocks : blocks + 6]
-    in_ref, rows_ref, spec_ref, twid_ref, fwd_ref, inv_ref, sems = refs[blocks + 6 :]
-    twid_copy, fwd_copy, inv_copy, *held_copies = fetch(
-        sources, (twid_ref, fwd_ref, inv_ref, *held_refs), sems
+    in_ref, rows_ref, spec_ref, twid_ref, back_ref, fwd_ref, inv_ref, sems = refs[blocks + 6 :]
+    twid_copy, back_copy, fwd_copy, inv_copy, *held_copies = fetch(
+        sources, (twid_ref, back_ref, fwd_ref, inv_ref, *held_refs), sems
     )
     groups, bins_count, signals, chunk, _ = rows_ref.shape
     block_len = in_ref.shape[-1]
@@ -159,7 +159,8 @@
         rows_ref[group, k, slot, :, block_len:] = im.astype(jnp.bfloat16)
 
     def get(group, k, slot):
-        return spec_ref[group, k, slot, :, :block_len], spec_ref[group, k, slot, :, block_len:]
+        re, im = spec_ref[group, k, slot, :, :block_len], spec_ref[group, k, slot, :, block_len:]
+        return re.astype(jnp.bfloat16), im.astype(jnp.bfloat16)
 
     def analyse(group):
         rows = pl.ds(group * chunk, chunk)
@@ -211,6 +212,7 @@
     def inverse(group):
         if group == 0:
             inv_copy.wait()
+            back_copy.wait()
         transform(group, inv_ref)
 
     def synthesise(group):
@@ -220,7 +222,7 @@
             bins = []
             for k in range(bins_count):
                 re, im = get(group, k, signal)
-                cos, sin = twid_ref[2, k : k + 1, :], twid_ref[3, k : k + 1, :]
+                cos, sin = back_ref[0, k], back_ref[1, k]
                 if k == 0:
                     bins.append((re * cos, None))
                 elif k == blocks:
@@ -228,7 +230,7 @@
                 else:
                     bins.append((re * cos - im * sin, im * cos + re * sin))
             for p, value in enumerate(half_spectrum_adjoint(bins)):
-                in_ref[p, signal, rows, :] = value.astype(jnp.bfloat16)
+                in_ref[p, signal, rows, :] = value
 
         each(signals, one)
 
@@ -336,14 +338,14 @@
     )(*in_hbm(long_filter, key_act, value_act, query_act, grad_out))
     moved = swap(sent)
 
-    forward, inverse, twiddle = dft_tables(
-        blocks, block_len, 1.0 / (math.sqrt(seq_len) * 2 * seq_len)
+    forward, inverse, twiddle, untwiddle = dft_tables(
+        blocks, block_len, 1.0 / (math.sqrt(seq_len) * 2 * seq_len), chunk
     )
-    tables = (twiddle, forward, inverse)
+    tables = (twiddle, untwiddle, forward, inverse)
     held = (key_act, value_act, grad_out, w_key, w_query, w_value)
     results = pl.pallas_call(
         conv_kernel,
-        in_specs=[VMEM] * blocks + [HBM] * 9,
+        in_specs=[VMEM] * blocks + [HBM] * 10,
         out_shape=arrays(blocks, 3, channels, block_len)
         + [pltpu.VMEM(array.shape, array.dtype) for array in held],
         scratch_shapes=[
@@ -351,7 +353,7 @@
             pltpu.VMEM((channels // chunk, blocks + 1, 3, chunk, 2 * block_len), jnp.bfloat16),
             pltpu.VMEM((channels // chunk, blocks + 1, 3, chunk, 2 * block_len), jnp.float32),
             *[pltpu.VMEM(array.shape, array.dtype) for array in tables],
-            pltpu.SemaphoreType.DMA((9,)),
+            pltpu.SemaphoreType.DMA((10,)),
         ],
         compiler_params=compiler_params(28),
         name="conv",

time: 59.2 us -> 58.8 us (level)
  no operation moved by 1% of the time
where the time goes in v13:
time: 58.8 us; the launch traced here: 58.6 us
  starting transfers between devices  28 us (48%)
  waiting for transfers between devices  20.3 us (35%)
  Pallas kernels  8.74 us (15%)
  other arithmetic  0.87 us (1%)
  between operations  0.7 us (1%)
    ppermute x17, starting transfers between devices, exchange(): return lax.ppermute(block, axis, pairs)  28 us
    ppermute x17, waiting for transfers between devices, exchange(): return lax.ppermute(block, axis, pairs)  20.3 us
    pallas_call x1, Pallas kernels, per_device(): pl.pallas_call(conv_kernel, in_specs=[VMEM] * blocks + [HBM] * 10, out_sh...  4.09 us
    pallas_call x1, Pallas kernels, per_device(): pl.pallas_call(gate_kernel, in_specs=[HBM] * 5, out_shape=arrays(blocks,...  1.5 us
  transfers between devices with their start and end apart: 17, of which 8 were waited for; matrix products, arithmetic and copies ran while one was open for 0% of the time, Pallas kernels for 4%

profile of v13, /device:TPU:0, one launch (start us, length us, event | category | flops | bytes accessed | tf_op | source)
XLA Modules:
  0.0 58.6 jit_solution(2009106903363633824)
XLA Ops:
  0.6 1.5 %gate.1 = (bf16[3,64,256]{2,1,0:T(8,128)(2,1)S(1)}, bf16[3,64,256]{2,1,0:T(8,128)(2,1)S(1)}, bf16[3,64,256]{2,1,0:T(8,128)(2,1)S(1)}, bf16[3,64,256]{2,1,0:T(8,1...) custom-call(bf16[256,512]{1,0:T(8,128)(2,1)} %refs_0_.1, ...), custom_call_target="tpu_custom_call" | custom-call | tf_op jit(solution)/shard_map/gate/pallas_call | solution.py:327
  2.1 6.1 %collective-permute-start = (bf16[3,64,256]{2,1,0:T(8,128)(2,1)S(1)}, bf16[3,64,256]{2,1,0:T(8,128)(2,1)S(1)}, u32[]{:S(2)}, u32[]{:S(2)}) collective-permute-start(bf16[3,64,256]{2,1,0:T(8,128)(2,1)S(1)} %get-tuple-element.39), channel_id=1, source_target_pairs={{0,28},{4,24},{8,20},{12,16},{16,12},{20,8},{24,4},{28,0},{1,29},{... | collective-permute-start | bytes 294920 | tf_op jit(solution)/shard_map/ppermute | solution.py:302
  8.2 0.5 collective-permute-start.1
  8.7 0.1 collective-permute-start.2
  8.9 0.0 collective-permute-start.3
  8.9 5.2 %collective-permute-start.4 = (bf16[3,64,256]{2,1,0:T(8,128)(2,1)S(1)}, bf16[3,64,256]{2,1,0:T(8,128)(2,1)S(1)}, u32[]{:S(2)}, u32[]{:S(2)}) collective-permute-start(bf16[3,64,256]{2,1,0:T(8,128)(2,1)S(1)} %get-tuple-element.43), channel_id=1, source_target_pairs={{0,20},{4,16},{8,28},{12,24},{16,4},{20,0},{24,12},{28,8},{1,21},{... | collective-permute-start | bytes 294920 | tf_op jit(solution)/shard_map/ppermute | solution.py:302
  14.1 0.0 collective-permute-done.refs_0_
  14.1 1.7 %collective-permute-start.5 = (bf16[3,64,256]{2,1,0:T(8,128)(2,1)S(1)}, bf16[3,64,256]{2,1,0:T(8,128)(2,1)S(1)}, u32[]{:S(2)}, u32[]{:S(2)}) collective-permute-start(bf16[3,64,256]{2,1,0:T(8,128)(2,1)S(1)} %get-tuple-element.44), channel_id=1, source_target_pairs={{0,12},{4,8},{8,4},{12,0},{16,28},{20,24},{24,20},{28,16},{1,13},{... | collective-permute-start | bytes 294920 | tf_op jit(solution)/shard_map/ppermute | solution.py:302
  15.7 0.0 collective-permute-done.1.refs_1_
  15.7 1.5 %collective-permute-start.6 = (bf16[3,64,256]{2,1,0:T(8,128)(2,1)S(1)}, bf16[3,64,256]{2,1,0:T(8,128)(2,1)S(1)}, u32[]{:S(2)}, u32[]{:S(2)}) collective-permute-start(bf16[3,64,256]{2,1,0:T(8,128)(2,1)S(1)} %get-tuple-element.45), channel_id=1, source_target_pairs={{0,16},{4,20},{8,24},{12,28},{16,0},{20,4},{24,8},{28,12},{1,17},{... | collective-permute-start | bytes 294920 | tf_op jit(solution)/shard_map/ppermute | solution.py:302
  17.3 0.0 collective-permute-done.2.refs_2_
  17.3 0.0 collective-permute-done.3.refs_3_
  17.3 5.2 %collective-permute-done.4.refs_4_ = bf16[3,64,256]{2,1,0:T(8,128)(2,1)S(1)} collective-permute-done((bf16[3,64,256]{2,1,0:T(8,128)(2,1)S(1)}, bf16[3,64,256]{2,1,0:T(8,128)(2,1)S(1)}, u32[]{:S(2)}, u32[]{:S(2)}) %collective-permute-start.4) | collective-permute-done | bytes 98336 | tf_op jit(solution)/shard_map/ppermute | solution.py:302
  22.5 0.0 collective-permute-done.5.refs_5_
  22.5 2.4 %collective-permute-done.6.refs_6_ = bf16[3,64,256]{2,1,0:T(8,128)(2,1)S(1)} collective-permute-done((bf16[3,64,256]{2,1,0:T(8,128)(2,1)S(1)}, bf16[3,64,256]{2,1,0:T(8,128)(2,1)S(1)}, u32[]{:S(2)}, u32[]{:S(2)}) %collective-permute-start.6) | collective-permute-done | bytes 98336 | tf_op jit(solution)/shard_map/ppermute | solution.py:302
  24.9 4.1 %conv.1 = (bf16[3,64,256]{2,1,0:T(8,128)(2,1)S(1)}, bf16[3,64,256]{2,1,0:T(8,128)(2,1)S(1)}, bf16[3,64,256]{2,1,0:T(8,128)(2,1)S(1)}, bf16[3,64,256]{2,1,0:T(8,1...) custom-call(bf16[3,64,256]{2,1,0:T(8,128)(2,1)S(1)} %collective-perm, ...), custom_call_target="tpu_custom_call" | custom-call | tf_op jit(solution)/shard_map/conv/pallas_call | solution.py:346
  29.0 2.6 %collective-permute-start.7 = (bf16[3,64,256]{2,1,0:T(8,128)(2,1)S(1)}, bf16[3,64,256]{2,1,0:T(8,128)(2,1)S(1)}, u32[]{:S(2)}, u32[]{:S(2)}) collective-permute-start(bf16[3,64,256]{2,1,0:T(8,128)(2,1)S(1)} %get-tuple-element.47), channel_id=1, source_target_pairs={{0,28},{4,24},{8,20},{12,16},{16,12},{20,8},{24,4},{28,0},{1,29},{... | collective-permute-start | bytes 294920 | tf_op jit(solution)/shard_map/ppermute | solution.py:302
  31.6 1.5 %collective-permute-start.8 = (bf16[3,64,256]{2,1,0:T(8,128)(2,1)S(1)}, bf16[3,64,256]{2,1,0:T(8,128)(2,1)S(1)}, u32[]{:S(2)}, u32[]{:S(2)}) collective-permute-start(bf16[3,64,256]{2,1,0:T(8,128)(2,1)S(1)} %get-tuple-element.48), channel_id=1, source_target_pairs={{0,4},{4,0},{8,12},{12,8},{16,20},{20,16},{24,28},{28,24},{1,5},{5... | collective-permute-start | bytes 294920 | tf_op jit(solution)/shard_map/ppermute | solution.py:302
  33.0 1.3 %collective-permute-start.9 = (bf16[3,64,256]{2,1,0:T(8,128)(2,1)S(1)}, bf16[3,64,256]{2,1,0:T(8,128)(2,1)S(1)}, u32[]{:S(2)}, u32[]{:S(2)}) collective-permute-start(bf16[3,64,256]{2,1,0:T(8,128)(2,1)S(1)} %get-tuple-element.49), channel_id=1, source_target_pairs={{0,24},{4,28},{8,16},{12,20},{16,8},{20,12},{24,0},{28,4},{1,25},{... | collective-permute-start | bytes 294920 | tf_op jit(solution)/shard_map/ppermute | solution.py:302
  34.4 0.0 collective-permute-start.10
  34.4 3.1 %collective-permute-start.11 = (bf16[3,64,256]{2,1,0:T(8,128)(2,1)S(1)}, bf16[3,64,256]{2,1,0:T(8,128)(2,1)S(1)}, u32[]{:S(2)}, u32[]{:S(2)}) collective-permute-start(bf16[3,64,256]{2,1,0:T(8,128)(2,1)S(1)} %get-tuple-element.51), channel_id=1, source_target_pairs={{0,20},{4,16},{8,28},{12,24},{16,4},{20,0},{24,12},{28,8},{1,21},{... | collective-permute-start | bytes 294920 | tf_op jit(solution)/shard_map/ppermute | solution.py:302
  37.4 0.0 collective-permute-done.7.refs_0_
  37.4 0.9 %collective-permute-start.12 = (bf16[3,64,256]{2,1,0:T(8,128)(2,1)S(1)}, bf16[3,64,256]{2,1,0:T(8,128)(2,1)S(1)}, u32[]{:S(2)}, u32[]{:S(2)}) collective-permute-start(bf16[3,64,256]{2,1,0:T(8,128)(2,1)S(1)} %get-tuple-element.52), channel_id=1, source_target_pairs={{0,12},{4,8},{8,4},{12,0},{16,28},{20,24},{24,20},{28,16},{1,13},{... | collective-permute-start | bytes 294920 | tf_op jit(solution)/shard_map/ppermute | solution.py:302
  38.3 0.0 collective-permute-done.8.refs_1_
  38.3 2.0 %collective-permute-start.13 = (bf16[3,64,256]{2,1,0:T(8,128)(2,1)S(1)}, bf16[3,64,256]{2,1,0:T(8,128)(2,1)S(1)}, u32[]{:S(2)}, u32[]{:S(2)}) collective-permute-start(bf16[3,64,256]{2,1,0:T(8,128)(2,1)S(1)} %get-tuple-element.53), channel_id=1, source_target_pairs={{0,16},{4,20},{8,24},{12,28},{16,0},{20,4},{24,8},{28,12},{1,17},{... | collective-permute-start | bytes 294920 | tf_op jit(solution)/shard_map/ppermute | solution.py:302
  40.3 0.3 collective-permute-done.9.refs_2_
  40.6 2.5 %collective-permute-done.10.refs_3_ = bf16[3,64,256]{2,1,0:T(8,128)(2,1)S(1)} collective-permute-done((bf16[3,64,256]{2,1,0:T(8,128)(2,1)S(1)}, bf16[3,64,256]{2,1,0:T(8,128)(2,1)S(1)}, u32[]{:S(2)}, u32[]{:S(2)}) %collective-permute-start.10) | collective-permute-done | bytes 98336 | tf_op jit(solution)/shard_map/ppermute | solution.py:302
  43.1 0.0 collective-permute-done.11.refs_4_
  43.1 2.0 %collective-permute-done.12.refs_5_ = bf16[3,64,256]{2,1,0:T(8,128)(2,1)S(1)} collective-permute-done((bf16[3,64,256]{2,1,0:T(8,128)(2,1)S(1)}, bf16[3,64,256]{2,1,0:T(8,128)(2,1)S(1)}, u32[]{:S(2)}, u32[]{:S(2)}) %collective-permute-start.12) | collective-permute-done | bytes 98336 | tf_op jit(solution)/shard_map/ppermute | solution.py:302
  45.1 2.0 %collective-permute-done.13.refs_6_ = bf16[3,64,256]{2,1,0:T(8,128)(2,1)S(1)} collective-permute-done((bf16[3,64,256]{2,1,0:T(8,128)(2,1)S(1)}, bf16[3,64,256]{2,1,0:T(8,128)(2,1)S(1)}, u32[]{:S(2)}, u32[]{:S(2)}) %collective-permute-start.13) | collective-permute-done | bytes 98336 | tf_op jit(solution)/shard_map/ppermute | solution.py:302
  47.1 0.7 %mate.1 = (bf16[3,256,512]{2,1,0:T(8,128)(2,1)S(1)}, bf16[256,512]{1,0:T(8,128)(2,1)S(1)}) custom-call(bf16[3,64,256]{2,1,0:T(8,128)(2,1)S(1)} %collective-permute-done.7.refs_0_, bf16[3,64,256]{2,1,0:T(8,128)(2,1)S(1)} %collective-permute-done.8.refs_1_, bf16[3,64,256]{2,1,0:T(8,128)(2,1)S(1)} %collective-permute-done.9.refs_2_, ...), custom_call_target="tpu_custom_call" | custom-call | flops 805306368 | bytes 4194304 | tf_op jit(solution)/shard_map/mate/pallas_call | solution.py:363
  47.7 0.1 collective-permute-start.14
  47.8 1.0 %far.1 = (f32[256,512]{1,0:T(8,128)S(1)}, bf16[256,512]{1,0:T(8,128)(2,1)S(1)}) custom-call(bf16[3,256,512]{2,1,0:T(8,128)(2,1)S(1)} %get-tuple-element.67.lhs_ref, bf16[2048,512]{1,0:T(8,128)(2,1)S(1)} %get-tuple-element.58.refs_11_.wk_ref, bf16[2048,512]{1,0:T(8,128)(2,1)S(1)} %get-tuple-element.59.refs_12_.wq_ref, ...), custom_call_target="tpu_custom_call" | custom-call | flops 805306368 | bytes 4194304 | tf_op jit(solution)/shard_map/far/pallas_call | solution.py:373
  48.8 0.5 collective-permute-done.14
  49.3 0.1 add_convert_fusion.1
  49.4 1.6 %collective-permute-start.15 = (bf16[256,512]{1,0:T(8,128)(2,1)S(1)}, bf16[256,512]{1,0:T(8,128)(2,1)S(1)}, u32[]{:S(2)}, u32[]{:S(2)}) collective-permute-start(bf16[256,512]{1,0:T(8,128)(2,1)S(1)} %add_convert_fusion.1), channel_id=1, source_target_pairs={{0,2},{1,3},{2,0},{3,1},{4,6},{5,7},{6,4},{7,5},{8,10},{9,11},{10,... | collective-permute-start | bytes 786440 | tf_op jit(solution)/shard_map/ppermute | solution.py:302
  51.0 0.0 collective-permute-start.16
  51.0 0.6 %own.1 = f32[256,512]{1,0:T(8,128)S(1)} custom-call(bf16[3,256,512]{2,1,0:T(8,128)(2,1)S(1)} %get-tuple-element.67.lhs_ref, bf16[2048,512]{1,0:T(8,128)(2,1)S(1)} %get-tuple-element.58.refs_11_.wk_ref, bf16[2048,512]{1,0:T(8,128)(2,1)S(1)} %get-tuple-element.59.refs_12_.wq_ref, bf16[2048,512]{1,0:T(8,128)(2,1)S(1)} %get-tuple-element.60.refs_13_.wv_ref), custom_call_target="tpu_custom_call" | custom-call | flops 805306368 | bytes 4194304 | tf_op jit(solution)/shard_map/own/pallas_call | solution.py:394
  51.6 0.9 %turn.1 = bf16[256,512]{1,0:T(8,128)(2,1)} custom-call(bf16[3,64,256]{2,1,0:T(8,128)(2,1)S(1)} %collective-permute-done.7.refs_0_, bf16[3,64,256]{2,1,0:T(8,128)(2,1)S(1)} %collective-permute-done.8.refs_1_, bf16[3,64,256]{2,1,0:T(8,128)(2,1)S(1)} %collective-permute-done.9.refs_2_, bf16[3,64,256]{2,1,0:T(8,128)(2,1)S(1)} %collective-permute-done.10.refs_3_, ...), custom_call_target="tpu_custom_call" | custom-call | flops 805306368 | bytes 4194304 | tf_op jit(solution)/shard_map/turn/pallas_call | solution.py:385
  52.4 5.4 %collective-permute-done.15 = bf16[256,512]{1,0:T(8,128)(2,1)S(1)} collective-permute-done((bf16[256,512]{1,0:T(8,128)(2,1)S(1)}, bf16[256,512]{1,0:T(8,128)(2,1)S(1)}, u32[]{:S(2)}, u32[]{:S(2)}) %collective-permute-start.15) | collective-permute-done | bytes 262176 | tf_op jit(solution)/shard_map/ppermute | solution.py:302
  57.8 0.0 collective-permute-done.16
  57.8 0.8 %add_convert_fusion = bf16[256,512]{1,0:T(8,128)(2,1)} fusion(f32[256,512]{1,0:T(8,128)S(1)} %own.1, bf16[256,512]{1,0:T(8,128)(2,1)S(1)} %collective-permute-done.16, bf16[256,512]{1,0:T(8,128)(2,1)S(1)} %collective-permute-done.15), kind=kLoop, calls=%fused_computation | loop fusion | flops 655360 | bytes 1310720 | tf_op jit(solution)/shard_map/convert_element_type | solution.py:403
Async XLA Ops:
  2.1 11.9 %collective-permute-start = (bf16[3,64,256]{2,1,0:T(8,128)(2,1)S(1)}, bf16[3,64,256]{2,1,0:T(8,128)(2,1)S(1)}, u32[]{:S(2)}, u32[]{:S(2)}) collective-permute-start(bf16[3,64,256]{2,1,0:T(8,128)(2,1)S(1)} %get-tuple-element.39), channel_id=1, source_target_pairs={{0,28},{4,24},{8,20},{12,16},{16,12},{20,8},{24,4},{28,0},{1,29},{... | collective-permute-start | bytes 294920 | tf_op jit(solution)/shard_map/ppermute | solution.py:302
  8.2 7.5 %collective-permute-start.1 = (bf16[3,64,256]{2,1,0:T(8,128)(2,1)S(1)}, bf16[3,64,256]{2,1,0:T(8,128)(2,1)S(1)}, u32[]{:S(2)}, u32[]{:S(2)}) collective-permute-start(bf16[3,64,256]{2,1,0:T(8,128)(2,1)S(1)} %get-tuple-element.40), channel_id=1, source_target_pairs={{0,4},{4,0},{8,12},{12,8},{16,20},{20,16},{24,28},{28,24},{1,5},{5... | collective-permute-start | bytes 294920 | tf_op jit(solution)/shard_map/ppermute | solution.py:302
  8.7 8.5 %collective-permute-start.2 = (bf16[3,64,256]{2,1,0:T(8,128)(2,1)S(1)}, bf16[3,64,256]{2,1,0:T(8,128)(2,1)S(1)}, u32[]{:S(2)}, u32[]{:S(2)}) collective-permute-start(bf16[3,64,256]{2,1,0:T(8,128)(2,1)S(1)} %get-tuple-element.41), channel_id=1, source_target_pairs={{0,24},{4,28},{8,16},{12,20},{16,8},{20,12},{24,0},{28,4},{1,25},{... | collective-permute-start | bytes 294920 | tf_op jit(solution)/shard_map/ppermute | solution.py:302
  8.9 8.4 %collective-permute-start.3 = (bf16[3,64,256]{2,1,0:T(8,128)(2,1)S(1)}, bf16[3,64,256]{2,1,0:T(8,128)(2,1)S(1)}, u32[]{:S(2)}, u32[]{:S(2)}) collective-permute-start(bf16[3,64,256]{2,1,0:T(8,128)(2,1)S(1)} %get-tuple-element.42), channel_id=1, source_target_pairs={{0,8},{4,12},{8,0},{12,4},{16,24},{20,28},{24,16},{28,20},{1,9},{5... | collective-permute-start | bytes 294920 | tf_op jit(solution)/shard_map/ppermute | solution.py:302
  8.9 13.6 %collective-permute-start.4 = (bf16[3,64,256]{2,1,0:T(8,128)(2,1)S(1)}, bf16[3,64,256]{2,1,0:T(8,128)(2,1)S(1)}, u32[]{:S(2)}, u32[]{:S(2)}) collective-permute-start(bf16[3,64,256]{2,1,0:T(8,128)(2,1)S(1)} %get-tuple-element.43), channel_id=1, source_target_pairs={{0,20},{4,16},{8,28},{12,24},{16,4},{20,0},{24,12},{28,8},{1,21},{... | collective-permute-start | bytes 294920 | tf_op jit(solution)/shard_map/ppermute | solution.py:302
  14.1 8.4 %collective-permute-start.5 = (bf16[3,64,256]{2,1,0:T(8,128)(2,1)S(1)}, bf16[3,64,256]{2,1,0:T(8,128)(2,1)S(1)}, u32[]{:S(2)}, u32[]{:S(2)}) collective-permute-start(bf16[3,64,256]{2,1,0:T(8,128)(2,1)S(1)} %get-tuple-element.44), channel_id=1, source_target_pairs={{0,12},{4,8},{8,4},{12,0},{16,28},{20,24},{24,20},{28,16},{1,13},{... | collective-permute-start | bytes 294920 | tf_op jit(solution)/shard_map/ppermute | solution.py:302
  15.7 9.2 %collective-permute-start.6 = (bf16[3,64,256]{2,1,0:T(8,128)(2,1)S(1)}, bf16[3,64,256]{2,1,0:T(8,128)(2,1)S(1)}, u32[]{:S(2)}, u32[]{:S(2)}) collective-permute-start(bf16[3,64,256]{2,1,0:T(8,128)(2,1)S(1)} %get-tuple-element.45), channel_id=1, source_target_pairs={{0,16},{4,20},{8,24},{12,28},{16,0},{20,4},{24,8},{28,12},{1,17},{... | collective-permute-start | bytes 294920 | tf_op jit(solution)/shard_map/ppermute | solution.py:302
  29.0 8.4 %collective-permute-start.7 = (bf16[3,64,256]{2,1,0:T(8,128)(2,1)S(1)}, bf16[3,64,256]{2,1,0:T(8,128)(2,1)S(1)}, u32[]{:S(2)}, u32[]{:S(2)}) collective-permute-start(bf16[3,64,256]{2,1,0:T(8,128)(2,1)S(1)} %get-tuple-element.47), channel_id=1, source_target_pairs={{0,28},{4,24},{8,20},{12,16},{16,12},{20,8},{24,4},{28,0},{1,29},{... | collective-permute-start | bytes 294920 | tf_op jit(solution)/shard_map/ppermute | solution.py:302
  31.6 6.8 %collective-permute-start.8 = (bf16[3,64,256]{2,1,0:T(8,128)(2,1)S(1)}, bf16[3,64,256]{2,1,0:T(8,128)(2,1)S(1)}, u32[]{:S(2)}, u32[]{:S(2)}) collective-permute-start(bf16[3,64,256]{2,1,0:T(8,128)(2,1)S(1)} %get-tuple-element.48), channel_id=1, source_target_pairs={{0,4},{4,0},{8,12},{12,8},{16,20},{20,16},{24,28},{28,24},{1,5},{5... | collective-permute-start | bytes 294920 | tf_op jit(solution)/shard_map/ppermute | solution.py:302
  33.0 7.6 %collective-permute-start.9 = (bf16[3,64,256]{2,1,0:T(8,128)(2,1)S(1)}, bf16[3,64,256]{2,1,0:T(8,128)(2,1)S(1)}, u32[]{:S(2)}, u32[]{:S(2)}) collective-permute-start(bf16[3,64,256]{2,1,0:T(8,128)(2,1)S(1)} %get-tuple-element.49), channel_id=1, source_target_pairs={{0,24},{4,28},{8,16},{12,20},{16,8},{20,12},{24,0},{28,4},{1,25},{... | collective-permute-start | bytes 294920 | tf_op jit(solution)/shard_map/ppermute | solution.py:302
  34.4 8.7 %collective-permute-start.10 = (bf16[3,64,256]{2,1,0:T(8,128)(2,1)S(1)}, bf16[3,64,256]{2,1,0:T(8,128)(2,1)S(1)}, u32[]{:S(2)}, u32[]{:S(2)}) collective-permute-start(bf16[3,64,256]{2,1,0:T(8,128)(2,1)S(1)} %get-tuple-element.50), channel_id=1, source_target_pairs={{0,8},{4,12},{8,0},{12,4},{16,24},{20,28},{24,16},{28,20},{1,9},{5... | collective-permute-start | bytes 294920 | tf_op jit(solution)/shard_map/ppermute | solution.py:302
  34.4 8.7 %collective-permute-start.11 = (bf16[3,64,256]{2,1,0:T(8,128)(2,1)S(1)}, bf16[3,64,256]{2,1,0:T(8,128)(2,1)S(1)}, u32[]{:S(2)}, u32[]{:S(2)}) collective-permute-start(bf16[3,64,256]{2,1,0:T(8,128)(2,1)S(1)} %get-tuple-element.51), channel_id=1, source_target_pairs={{0,20},{4,16},{8,28},{12,24},{16,4},{20,0},{24,12},{28,8},{1,21},{... | collective-permute-start | bytes 294920 | tf_op jit(solution)/shard_map/ppermute | solution.py:302
  37.4 7.7 %collective-permute-start.12 = (bf16[3,64,256]{2,1,0:T(8,128)(2,1)S(1)}, bf16[3,64,256]{2,1,0:T(8,128)(2,1)S(1)}, u32[]{:S(2)}, u32[]{:S(2)}) collective-permute-start(bf16[3,64,256]{2,1,0:T(8,128)(2,1)S(1)} %get-tuple-element.52), channel_id=1, source_target_pairs={{0,12},{4,8},{8,4},{12,0},{16,28},{20,24},{24,20},{28,16},{1,13},{... | collective-permute-start | bytes 294920 | tf_op jit(solution)/shard_map/ppermute | solution.py:302
  38.3 8.7 %collective-permute-start.13 = (bf16[3,64,256]{2,1,0:T(8,128)(2,1)S(1)}, bf16[3,64,256]{2,1,0:T(8,128)(2,1)S(1)}, u32[]{:S(2)}, u32[]{:S(2)}) collective-permute-start(bf16[3,64,256]{2,1,0:T(8,128)(2,1)S(1)} %get-tuple-element.53), channel_id=1, source_target_pairs={{0,16},{4,20},{8,24},{12,28},{16,0},{20,4},{24,8},{28,12},{1,17},{... | collective-permute-start | bytes 294920 | tf_op jit(solution)/shard_map/ppermute | solution.py:302
  47.7 1.6 %collective-permute-start.14 = (bf16[256,512]{1,0:T(8,128)(2,1)S(1)}, bf16[256,512]{1,0:T(8,128)(2,1)S(1)}, u32[]{:S(2)}, u32[]{:S(2)}) collective-permute-start(bf16[256,512]{1,0:T(8,128)(2,1)S(1)} %get-tuple-element.63), channel_id=1, source_target_pairs={{0,1},{1,0},{2,3},{3,2},{4,5},{5,4},{6,7},{7,6},{8,9},{9,8},{10,11... | collective-permute-start | bytes 786440 | tf_op jit(solution)/shard_map/ppermute | solution.py:302
  49.4 8.4 %collective-permute-start.15 = (bf16[256,512]{1,0:T(8,128)(2,1)S(1)}, bf16[256,512]{1,0:T(8,128)(2,1)S(1)}, u32[]{:S(2)}, u32[]{:S(2)}) collective-permute-start(bf16[256,512]{1,0:T(8,128)(2,1)S(1)} %add_convert_fusion.1), channel_id=1, source_target_pairs={{0,2},{1,3},{2,0},{3,1},{4,6},{5,7},{6,4},{7,5},{8,10},{9,11},{10,... | collective-permute-start | bytes 786440 | tf_op jit(solution)/shard_map/ppermute | solution.py:302
  51.0 6.9 %collective-permute-start.16 = (bf16[256,512]{1,0:T(8,128)(2,1)S(1)}, bf16[256,512]{1,0:T(8,128)(2,1)S(1)}, u32[]{:S(2)}, u32[]{:S(2)}) collective-permute-start(bf16[256,512]{1,0:T(8,128)(2,1)S(1)} %get-tuple-element.66), channel_id=1, source_target_pairs={{0,1},{1,0},{2,3},{3,2},{4,5},{5,4},{6,7},{7,6},{8,9},{9,8},{10,11... | collective-permute-start | bytes 786440 | tf_op jit(solution)/shard_map/ppermute | solution.py:302

commit v14 on v13

--- a/solution.py
+++ b/solution.py
@@ -14,11 +14,12 @@
 
 
 def dft_tables(blocks, block_len, scale, rows_count):
-    index = np.arange(block_len)
-    angle = 2.0 * np.pi * (np.outer(index, index) % block_len) / block_len
+    index, half = np.arange(block_len), np.arange(block_len // 2)
+    bins = 2 * half[None, :] + np.arange(2)[:, None]
+    angle = 2.0 * np.pi * (half[None, :, None] * bins[:, None, :] % block_len) / block_len
     cos, sin = np.cos(angle), np.sin(angle)
     forward = np.block([[cos, -sin], [sin, cos]])
-    inverse = forward.T
+    inverse = forward.transpose(0, 2, 1)
     rows = np.arange(blocks + 1)
     phase = 2.0 * np.pi * np.outer(rows, index) / (2 * blocks * block_len)
     weight = np.where((rows == 0) | (rows == blocks), 1.0, 2.0)[:, None] * scale
@@ -154,12 +155,30 @@
         else:
             pl.loop(0, count)(body)
 
-    def put(group, k, slot, re, im):
-        rows_ref[group, k, slot, :, :block_len] = re.astype(jnp.bfloat16)
-        rows_ref[group, k, slot, :, block_len:] = im.astype(jnp.bfloat16)
-
-    def get(group, k, slot):
-        re, im = spec_ref[group, k, slot, :, :block_len], spec_ref[group, k, slot, :, block_len:]
+    half = block_len // 2
+
+    def put(group, k, slot, part, re, im):
+        rows_ref[group, k, slot, :, part * block_len : part * block_len + half] = re.astype(
+            jnp.bfloat16
+        )
+        rows_ref[group, k, slot, :, part * block_len + half : (part + 1) * block_len] = im.astype(
+            jnp.bfloat16
+        )
+
+    def get(group, k, slot, part):
+        re = spec_ref[group, k, slot, :, part * block_len : part * block_len + half]
+        im = spec_ref[group, k, slot, :, part * block_len + half : (part + 1) * block_len]
+        return re, im
+
+    def put_halves(group, k, slot, re, im):
+        put(group, k, slot, 0, re[:, :half] + re[:, half:], im[:, :half] + im[:, half:])
+        put(group, k, slot, 1, re[:, :half] - re[:, half:], im[:, :half] - im[:, half:])
+
+    def get_halves(group, k, slot):
+        even_re, even_im = get(group, k, slot, 0)
+        odd_re, odd_im = get(group, k, slot, 1)
+        re = jnp.concatenate([even_re + odd_re, even_re - odd_re], axis=1)
+        im = jnp.concatenate([even_im + odd_im, even_im - odd_im], axis=1)
         return re.astype(jnp.bfloat16), im.astype(jnp.bfloat16)
 
     def analyse(group):
@@ -172,20 +191,22 @@
             for k, (re, im) in enumerate(bins):
                 cos, sin = twid_ref[0, k : k + 1, :], twid_ref[1, k : k + 1, :]
                 if k == 0:
-                    put(group, k, signal, re, jnp.zeros_like(re))
+                    put_halves(group, k, signal, re, jnp.zeros_like(re))
                 elif im is None:
-                    put(group, k, signal, re * cos, -(re * sin))
+                    put_halves(group, k, signal, re * cos, -(re * sin))
                 else:
-                    put(group, k, signal, re * cos + im * sin, im * cos - re * sin)
+                    put_halves(group, k, signal, re * cos + im * sin, im * cos - re * sin)
 
         each(signals, one)
 
     def transform(group, table_ref):
-        spec_ref[group] = jnp.dot(
-            rows_ref[group].reshape(bins_count * signals * chunk, 2 * block_len),
-            table_ref[...],
-            preferred_element_type=jnp.float32,
-        ).reshape(spec_ref.shape[1:])
+        for part in range(2):
+            lanes = slice(part * block_len, (part + 1) * block_len)
+            spec_ref[group, :, :, :, lanes] = jnp.dot(
+                rows_ref[group, :, :, :, lanes].reshape(bins_count * signals * chunk, block_len),
+                table_ref[part],
+                preferred_element_type=jnp.float32,
+            ).reshape(bins_count, signals, chunk, block_len)
 
     def forward(group):
         if group == 0:
@@ -193,19 +214,24 @@
         transform(group, fwd_ref)
 
     def combine(group):
-        def one(k):
-            prod_re, prod_im = get(group, k, 0)
-            kern_re, kern_im = get(group, k, 1)
-            grad_re, grad_im = get(group, k, 2)
+        def product(k, part):
+            (prod_re, prod_im), (kern_re, kern_im), (grad_re, grad_im) = [
+                [value.astype(jnp.bfloat16) for value in get(group, k, slot, part)]
+                for slot in range(3)
+            ]
             conv_re = prod_re * kern_re - prod_im * kern_im
             conv_im = prod_re * kern_im + prod_im * kern_re
             back_re = grad_re * kern_re + grad_im * kern_im
             back_im = grad_im * kern_re - grad_re * kern_im
             filt_re = grad_re * prod_re + grad_im * prod_im
             filt_im = grad_im * prod_re - grad_re * prod_im
-            put(group, k, 0, conv_re, conv_im)
-            put(group, k, 1, back_re, back_im)
-            put(group, k, 2, filt_re, filt_im)
+            put(group, k, 0, part, conv_re, conv_im)
+            put(group, k, 1, part, back_re, back_im)
+            put(group, k, 2, part, filt_re, filt_im)
+
+        def one(k):
+            product(k, 0)
+            product(k, 1)
 
         each(bins_count, one)
 
@@ -221,7 +247,7 @@
         def one(signal):
             bins = []
             for k in range(bins_count):
-                re, im = get(group, k, signal)
+                re, im = get_halves(group, k, signal)
                 cos, sin = back_ref[0, k], back_ref[1, k]
                 if k == 0:
                     bins.append((re * cos, None))

time: 58.8 us -> 58.3 us (level)
  no operation moved by 1% of the time
where the time goes in v14:
time: 58.3 us; the launch traced here: 58.1 us
  starting transfers between devices  28 us (48%)
  waiting for transfers between devices  20.3 us (35%)
  Pallas kernels  8.26 us (14%)
  other arithmetic  0.87 us (1%)
  between operations  0.7 us (1%)
    ppermute x17, starting transfers between devices, exchange(): return lax.ppermute(block, axis, pairs)  28 us
    ppermute x17, waiting for transfers between devices, exchange(): return lax.ppermute(block, axis, pairs)  20.3 us
    pallas_call x1, Pallas kernels, per_device(): pl.pallas_call(conv_kernel, in_specs=[VMEM] * blocks + [HBM] * 10, out_sh...  3.61 us
    pallas_call x1, Pallas kernels, per_device(): pl.pallas_call(gate_kernel, in_specs=[HBM] * 5, out_shape=arrays(blocks,...  1.5 us
  transfers between devices with their start and end apart: 17, of which 8 were waited for; matrix products, arithmetic and copies ran while one was open for 0% of the time, Pallas kernels for 4%

profile of v14, /device:TPU:0, one launch (start us, length us, event | category | flops | bytes accessed | tf_op | source)
XLA Modules:
  0.0 58.1 jit_solution(9113295216786637683)
XLA Ops:
  0.6 1.5 %gate.1 = (bf16[3,64,256]{2,1,0:T(8,128)(2,1)S(1)}, bf16[3,64,256]{2,1,0:T(8,128)(2,1)S(1)}, bf16[3,64,256]{2,1,0:T(8,128)(2,1)S(1)}, bf16[3,64,256]{2,1,0:T(8,1...) custom-call(bf16[256,512]{1,0:T(8,128)(2,1)} %refs_0_.1, ...), custom_call_target="tpu_custom_call" | custom-call | tf_op jit(solution)/shard_map/gate/pallas_call | solution.py:353
  2.1 6.1 %collective-permute-start = (bf16[3,64,256]{2,1,0:T(8,128)(2,1)S(1)}, bf16[3,64,256]{2,1,0:T(8,128)(2,1)S(1)}, u32[]{:S(2)}, u32[]{:S(2)}) collective-permute-start(bf16[3,64,256]{2,1,0:T(8,128)(2,1)S(1)} %get-tuple-element.39), channel_id=1, source_target_pairs={{0,28},{4,24},{8,20},{12,16},{16,12},{20,8},{24,4},{28,0},{1,29},{... | collective-permute-start | bytes 294920 | tf_op jit(solution)/shard_map/ppermute | solution.py:328
  8.2 0.5 collective-permute-start.1
  8.7 0.1 collective-permute-start.2
  8.9 0.0 collective-permute-start.3
  8.9 5.2 %collective-permute-start.4 = (bf16[3,64,256]{2,1,0:T(8,128)(2,1)S(1)}, bf16[3,64,256]{2,1,0:T(8,128)(2,1)S(1)}, u32[]{:S(2)}, u32[]{:S(2)}) collective-permute-start(bf16[3,64,256]{2,1,0:T(8,128)(2,1)S(1)} %get-tuple-element.43), channel_id=1, source_target_pairs={{0,20},{4,16},{8,28},{12,24},{16,4},{20,0},{24,12},{28,8},{1,21},{... | collective-permute-start | bytes 294920 | tf_op jit(solution)/shard_map/ppermute | solution.py:328
  14.1 0.0 collective-permute-done.refs_0_
  14.1 1.7 %collective-permute-start.5 = (bf16[3,64,256]{2,1,0:T(8,128)(2,1)S(1)}, bf16[3,64,256]{2,1,0:T(8,128)(2,1)S(1)}, u32[]{:S(2)}, u32[]{:S(2)}) collective-permute-start(bf16[3,64,256]{2,1,0:T(8,128)(2,1)S(1)} %get-tuple-element.44), channel_id=1, source_target_pairs={{0,12},{4,8},{8,4},{12,0},{16,28},{20,24},{24,20},{28,16},{1,13},{... | collective-permute-start | bytes 294920 | tf_op jit(solution)/shard_map/ppermute | solution.py:328
  15.7 0.0 collective-permute-done.1.refs_1_
  15.7 1.5 %collective-permute-start.6 = (bf16[3,64,256]{2,1,0:T(8,128)(2,1)S(1)}, bf16[3,64,256]{2,1,0:T(8,128)(2,1)S(1)}, u32[]{:S(2)}, u32[]{:S(2)}) collective-permute-start(bf16[3,64,256]{2,1,0:T(8,128)(2,1)S(1)} %get-tuple-element.45), channel_id=1, source_target_pairs={{0,16},{4,20},{8,24},{12,28},{16,0},{20,4},{24,8},{28,12},{1,17},{... | collective-permute-start | bytes 294920 | tf_op jit(solution)/shard_map/ppermute | solution.py:328
  17.3 0.0 collective-permute-done.2.refs_2_
  17.3 0.0 collective-permute-done.3.refs_3_
  17.3 5.2 %collective-permute-done.4.refs_4_ = bf16[3,64,256]{2,1,0:T(8,128)(2,1)S(1)} collective-permute-done((bf16[3,64,256]{2,1,0:T(8,128)(2,1)S(1)}, bf16[3,64,256]{2,1,0:T(8,128)(2,1)S(1)}, u32[]{:S(2)}, u32[]{:S(2)}) %collective-permute-start.4) | collective-permute-done | bytes 98336 | tf_op jit(solution)/shard_map/ppermute | solution.py:328
  22.5 0.0 collective-permute-done.5.refs_5_
  22.5 2.4 %collective-permute-done.6.refs_6_ = bf16[3,64,256]{2,1,0:T(8,128)(2,1)S(1)} collective-permute-done((bf16[3,64,256]{2,1,0:T(8,128)(2,1)S(1)}, bf16[3,64,256]{2,1,0:T(8,128)(2,1)S(1)}, u32[]{:S(2)}, u32[]{:S(2)}) %collective-permute-start.6) | collective-permute-done | bytes 98336 | tf_op jit(solution)/shard_map/ppermute | solution.py:328
  24.9 3.6 %conv.1 = (bf16[3,64,256]{2,1,0:T(8,128)(2,1)S(1)}, bf16[3,64,256]{2,1,0:T(8,128)(2,1)S(1)}, bf16[3,64,256]{2,1,0:T(8,128)(2,1)S(1)}, bf16[3,64,256]{2,1,0:T(8,1...) custom-call(bf16[3,64,256]{2,1,0:T(8,128)(2,1)S(1)} %collective-perm, ...), custom_call_target="tpu_custom_call" | custom-call | tf_op jit(solution)/shard_map/conv/pallas_call | solution.py:372
  28.5 2.6 %collective-permute-start.7 = (bf16[3,64,256]{2,1,0:T(8,128)(2,1)S(1)}, bf16[3,64,256]{2,1,0:T(8,128)(2,1)S(1)}, u32[]{:S(2)}, u32[]{:S(2)}) collective-permute-start(bf16[3,64,256]{2,1,0:T(8,128)(2,1)S(1)} %get-tuple-element.47), channel_id=1, source_target_pairs={{0,28},{4,24},{8,20},{12,16},{16,12},{20,8},{24,4},{28,0},{1,29},{... | collective-permute-start | bytes 294920 | tf_op jit(solution)/shard_map/ppermute | solution.py:328
  31.1 1.5 %collective-permute-start.8 = (bf16[3,64,256]{2,1,0:T(8,128)(2,1)S(1)}, bf16[3,64,256]{2,1,0:T(8,128)(2,1)S(1)}, u32[]{:S(2)}, u32[]{:S(2)}) collective-permute-start(bf16[3,64,256]{2,1,0:T(8,128)(2,1)S(1)} %get-tuple-element.48), channel_id=1, source_target_pairs={{0,4},{4,0},{8,12},{12,8},{16,20},{20,16},{24,28},{28,24},{1,5},{5... | collective-permute-start | bytes 294920 | tf_op jit(solution)/shard_map/ppermute | solution.py:328
  32.6 1.3 %collective-permute-start.9 = (bf16[3,64,256]{2,1,0:T(8,128)(2,1)S(1)}, bf16[3,64,256]{2,1,0:T(8,128)(2,1)S(1)}, u32[]{:S(2)}, u32[]{:S(2)}) collective-permute-start(bf16[3,64,256]{2,1,0:T(8,128)(2,1)S(1)} %get-tuple-element.49), channel_id=1, source_target_pairs={{0,24},{4,28},{8,16},{12,20},{16,8},{20,12},{24,0},{28,4},{1,25},{... | collective-permute-start | bytes 294920 | tf_op jit(solution)/shard_map/ppermute | solution.py:328
  33.9 0.0 collective-permute-start.10
  33.9 3.1 %collective-permute-start.11 = (bf16[3,64,256]{2,1,0:T(8,128)(2,1)S(1)}, bf16[3,64,256]{2,1,0:T(8,128)(2,1)S(1)}, u32[]{:S(2)}, u32[]{:S(2)}) collective-permute-start(bf16[3,64,256]{2,1,0:T(8,128)(2,1)S(1)} %get-tuple-element.51), channel_id=1, source_target_pairs={{0,20},{4,16},{8,28},{12,24},{16,4},{20,0},{24,12},{28,8},{1,21},{... | collective-permute-start | bytes 294920 | tf_op jit(solution)/shard_map/ppermute | solution.py:328
  36.9 0.0 collective-permute-done.7.refs_0_
  36.9 0.9 %collective-permute-start.12 = (bf16[3,64,256]{2,1,0:T(8,128)(2,1)S(1)}, bf16[3,64,256]{2,1,0:T(8,128)(2,1)S(1)}, u32[]{:S(2)}, u32[]{:S(2)}) collective-permute-start(bf16[3,64,256]{2,1,0:T(8,128)(2,1)S(1)} %get-tuple-element.52), channel_id=1, source_target_pairs={{0,12},{4,8},{8,4},{12,0},{16,28},{20,24},{24,20},{28,16},{1,13},{... | collective-permute-start | bytes 294920 | tf_op jit(solution)/shard_map/ppermute | solution.py:328
  37.9 0.0 collective-permute-done.8.refs_1_
  37.9 2.0 %collective-permute-start.13 = (bf16[3,64,256]{2,1,0:T(8,128)(2,1)S(1)}, bf16[3,64,256]{2,1,0:T(8,128)(2,1)S(1)}, u32[]{:S(2)}, u32[]{:S(2)}) collective-permute-start(bf16[3,64,256]{2,1,0:T(8,128)(2,1)S(1)} %get-tuple-element.53), channel_id=1, source_target_pairs={{0,16},{4,20},{8,24},{12,28},{16,0},{20,4},{24,8},{28,12},{1,17},{... | collective-permute-start | bytes 294920 | tf_op jit(solution)/shard_map/ppermute | solution.py:328
  39.8 0.3 collective-permute-done.9.refs_2_
  40.1 2.5 %collective-permute-done.10.refs_3_ = bf16[3,64,256]{2,1,0:T(8,128)(2,1)S(1)} collective-permute-done((bf16[3,64,256]{2,1,0:T(8,128)(2,1)S(1)}, bf16[3,64,256]{2,1,0:T(8,128)(2,1)S(1)}, u32[]{:S(2)}, u32[]{:S(2)}) %collective-permute-start.10) | collective-permute-done | bytes 98336 | tf_op jit(solution)/shard_map/ppermute | solution.py:328
  42.6 0.0 collective-permute-done.11.refs_4_
  42.6 2.0 %collective-permute-done.12.refs_5_ = bf16[3,64,256]{2,1,0:T(8,128)(2,1)S(1)} collective-permute-done((bf16[3,64,256]{2,1,0:T(8,128)(2,1)S(1)}, bf16[3,64,256]{2,1,0:T(8,128)(2,1)S(1)}, u32[]{:S(2)}, u32[]{:S(2)}) %collective-permute-start.12) | collective-permute-done | bytes 98336 | tf_op jit(solution)/shard_map/ppermute | solution.py:328
  44.6 2.0 %collective-permute-done.13.refs_6_ = bf16[3,64,256]{2,1,0:T(8,128)(2,1)S(1)} collective-permute-done((bf16[3,64,256]{2,1,0:T(8,128)(2,1)S(1)}, bf16[3,64,256]{2,1,0:T(8,128)(2,1)S(1)}, u32[]{:S(2)}, u32[]{:S(2)}) %collective-permute-start.13) | collective-permute-done | bytes 98336 | tf_op jit(solution)/shard_map/ppermute | solution.py:328
  46.6 0.7 %mate.1 = (bf16[3,256,512]{2,1,0:T(8,128)(2,1)S(1)}, bf16[256,512]{1,0:T(8,128)(2,1)S(1)}) custom-call(bf16[3,64,256]{2,1,0:T(8,128)(2,1)S(1)} %collective-permute-done.7.refs_0_, bf16[3,64,256]{2,1,0:T(8,128)(2,1)S(1)} %collective-permute-done.8.refs_1_, bf16[3,64,256]{2,1,0:T(8,128)(2,1)S(1)} %collective-permute-done.9.refs_2_, ...), custom_call_target="tpu_custom_call" | custom-call | flops 805306368 | bytes 4194304 | tf_op jit(solution)/shard_map/mate/pallas_call | solution.py:389
  47.2 0.1 collective-permute-start.14
  47.3 1.0 %far.1 = (f32[256,512]{1,0:T(8,128)S(1)}, bf16[256,512]{1,0:T(8,128)(2,1)S(1)}) custom-call(bf16[3,256,512]{2,1,0:T(8,128)(2,1)S(1)} %get-tuple-element.67.lhs_ref, bf16[2048,512]{1,0:T(8,128)(2,1)S(1)} %get-tuple-element.58.refs_11_.wk_ref, bf16[2048,512]{1,0:T(8,128)(2,1)S(1)} %get-tuple-element.59.refs_12_.wq_ref, ...), custom_call_target="tpu_custom_call" | custom-call | flops 805306368 | bytes 4194304 | tf_op jit(solution)/shard_map/far/pallas_call | solution.py:399
  48.3 0.5 collective-permute-done.14
  48.8 0.1 add_convert_fusion.1
  48.9 1.5 %collective-permute-start.15 = (bf16[256,512]{1,0:T(8,128)(2,1)S(1)}, bf16[256,512]{1,0:T(8,128)(2,1)S(1)}, u32[]{:S(2)}, u32[]{:S(2)}) collective-permute-start(bf16[256,512]{1,0:T(8,128)(2,1)S(1)} %add_convert_fusion.1), channel_id=1, source_target_pairs={{0,2},{1,3},{2,0},{3,1},{4,6},{5,7},{6,4},{7,5},{8,10},{9,11},{10,... | collective-permute-start | bytes 786440 | tf_op jit(solution)/shard_map/ppermute | solution.py:328
  50.5 0.0 collective-permute-start.16
  50.5 0.6 %own.1 = f32[256,512]{1,0:T(8,128)S(1)} custom-call(bf16[3,256,512]{2,1,0:T(8,128)(2,1)S(1)} %get-tuple-element.67.lhs_ref, bf16[2048,512]{1,0:T(8,128)(2,1)S(1)} %get-tuple-element.58.refs_11_.wk_ref, bf16[2048,512]{1,0:T(8,128)(2,1)S(1)} %get-tuple-element.59.refs_12_.wq_ref, bf16[2048,512]{1,0:T(8,128)(2,1)S(1)} %get-tuple-element.60.refs_13_.wv_ref), custom_call_target="tpu_custom_call" | custom-call | flops 805306368 | bytes 4194304 | tf_op jit(solution)/shard_map/own/pallas_call | solution.py:420
  51.1 0.9 %turn.1 = bf16[256,512]{1,0:T(8,128)(2,1)} custom-call(bf16[3,64,256]{2,1,0:T(8,128)(2,1)S(1)} %collective-permute-done.7.refs_0_, bf16[3,64,256]{2,1,0:T(8,128)(2,1)S(1)} %collective-permute-done.8.refs_1_, bf16[3,64,256]{2,1,0:T(8,128)(2,1)S(1)} %collective-permute-done.9.refs_2_, bf16[3,64,256]{2,1,0:T(8,128)(2,1)S(1)} %collective-permute-done.10.refs_3_, ...), custom_call_target="tpu_custom_call" | custom-call | flops 805306368 | bytes 4194304 | tf_op jit(solution)/shard_map/turn/pallas_call | solution.py:411
  52.0 5.4 %collective-permute-done.15 = bf16[256,512]{1,0:T(8,128)(2,1)S(1)} collective-permute-done((bf16[256,512]{1,0:T(8,128)(2,1)S(1)}, bf16[256,512]{1,0:T(8,128)(2,1)S(1)}, u32[]{:S(2)}, u32[]{:S(2)}) %collective-permute-start.15) | collective-permute-done | bytes 262176 | tf_op jit(solution)/shard_map/ppermute | solution.py:328
  57.3 0.0 collective-permute-done.16
  57.3 0.8 %add_convert_fusion = bf16[256,512]{1,0:T(8,128)(2,1)} fusion(f32[256,512]{1,0:T(8,128)S(1)} %own.1, bf16[256,512]{1,0:T(8,128)(2,1)S(1)} %collective-permute-done.16, bf16[256,512]{1,0:T(8,128)(2,1)S(1)} %collective-permute-done.15), kind=kLoop, calls=%fused_computation | loop fusion | flops 655360 | bytes 1310720 | tf_op jit(solution)/shard_map/convert_element_type | solution.py:429
Async XLA Ops:
  2.1 11.9 %collective-permute-start = (bf16[3,64,256]{2,1,0:T(8,128)(2,1)S(1)}, bf16[3,64,256]{2,1,0:T(8,128)(2,1)S(1)}, u32[]{:S(2)}, u32[]{:S(2)}) collective-permute-start(bf16[3,64,256]{2,1,0:T(8,128)(2,1)S(1)} %get-tuple-element.39), channel_id=1, source_target_pairs={{0,28},{4,24},{8,20},{12,16},{16,12},{20,8},{24,4},{28,0},{1,29},{... | collective-permute-start | bytes 294920 | tf_op jit(solution)/shard_map/ppermute | solution.py:328
  8.2 7.5 %collective-permute-start.1 = (bf16[3,64,256]{2,1,0:T(8,128)(2,1)S(1)}, bf16[3,64,256]{2,1,0:T(8,128)(2,1)S(1)}, u32[]{:S(2)}, u32[]{:S(2)}) collective-permute-start(bf16[3,64,256]{2,1,0:T(8,128)(2,1)S(1)} %get-tuple-element.40), channel_id=1, source_target_pairs={{0,4},{4,0},{8,12},{12,8},{16,20},{20,16},{24,28},{28,24},{1,5},{5... | collective-permute-start | bytes 294920 | tf_op jit(solution)/shard_map/ppermute | solution.py:328
  8.7 8.5 %collective-permute-start.2 = (bf16[3,64,256]{2,1,0:T(8,128)(2,1)S(1)}, bf16[3,64,256]{2,1,0:T(8,128)(2,1)S(1)}, u32[]{:S(2)}, u32[]{:S(2)}) collective-permute-start(bf16[3,64,256]{2,1,0:T(8,128)(2,1)S(1)} %get-tuple-element.41), channel_id=1, source_target_pairs={{0,24},{4,28},{8,16},{12,20},{16,8},{20,12},{24,0},{28,4},{1,25},{... | collective-permute-start | bytes 294920 | tf_op jit(solution)/shard_map/ppermute | solution.py:328
  8.9 8.4 %collective-permute-start.3 = (bf16[3,64,256]{2,1,0:T(8,128)(2,1)S(1)}, bf16[3,64,256]{2,1,0:T(8,128)(2,1)S(1)}, u32[]{:S(2)}, u32[]{:S(2)}) collective-permute-start(bf16[3,64,256]{2,1,0:T(8,128)(2,1)S(1)} %get-tuple-element.42), channel_id=1, source_target_pairs={{0,8},{4,12},{8,0},{12,4},{16,24},{20,28},{24,16},{28,20},{1,9},{5... | collective-permute-start | bytes 294920 | tf_op jit(solution)/shard_map/ppermute | solution.py:328
  8.9 13.6 %collective-permute-start.4 = (bf16[3,64,256]{2,1,0:T(8,128)(2,1)S(1)}, bf16[3,64,256]{2,1,0:T(8,128)(2,1)S(1)}, u32[]{:S(2)}, u32[]{:S(2)}) collective-permute-start(bf16[3,64,256]{2,1,0:T(8,128)(2,1)S(1)} %get-tuple-element.43), channel_id=1, source_target_pairs={{0,20},{4,16},{8,28},{12,24},{16,4},{20,0},{24,12},{28,8},{1,21},{... | collective-permute-start | bytes 294920 | tf_op jit(solution)/shard_map/ppermute | solution.py:328
  14.1 8.4 %collective-permute-start.5 = (bf16[3,64,256]{2,1,0:T(8,128)(2,1)S(1)}, bf16[3,64,256]{2,1,0:T(8,128)(2,1)S(1)}, u32[]{:S(2)}, u32[]{:S(2)}) collective-permute-start(bf16[3,64,256]{2,1,0:T(8,128)(2,1)S(1)} %get-tuple-element.44), channel_id=1, source_target_pairs={{0,12},{4,8},{8,4},{12,0},{16,28},{20,24},{24,20},{28,16},{1,13},{... | collective-permute-start | bytes 294920 | tf_op jit(solution)/shard_map/ppermute | solution.py:328
  15.7 9.2 %collective-permute-start.6 = (bf16[3,64,256]{2,1,0:T(8,128)(2,1)S(1)}, bf16[3,64,256]{2,1,0:T(8,128)(2,1)S(1)}, u32[]{:S(2)}, u32[]{:S(2)}) collective-permute-start(bf16[3,64,256]{2,1,0:T(8,128)(2,1)S(1)} %get-tuple-element.45), channel_id=1, source_target_pairs={{0,16},{4,20},{8,24},{12,28},{16,0},{20,4},{24,8},{28,12},{1,17},{... | collective-permute-start | bytes 294920 | tf_op jit(solution)/shard_map/ppermute | solution.py:328
  28.5 8.4 %collective-permute-start.7 = (bf16[3,64,256]{2,1,0:T(8,128)(2,1)S(1)}, bf16[3,64,256]{2,1,0:T(8,128)(2,1)S(1)}, u32[]{:S(2)}, u32[]{:S(2)}) collective-permute-start(bf16[3,64,256]{2,1,0:T(8,128)(2,1)S(1)} %get-tuple-element.47), channel_id=1, source_target_pairs={{0,28},{4,24},{8,20},{12,16},{16,12},{20,8},{24,4},{28,0},{1,29},{... | collective-permute-start | bytes 294920 | tf_op jit(solution)/shard_map/ppermute | solution.py:328
  31.1 6.8 %collective-permute-start.8 = (bf16[3,64,256]{2,1,0:T(8,128)(2,1)S(1)}, bf16[3,64,256]{2,1,0:T(8,128)(2,1)S(1)}, u32[]{:S(2)}, u32[]{:S(2)}) collective-permute-start(bf16[3,64,256]{2,1,0:T(8,128)(2,1)S(1)} %get-tuple-element.48), channel_id=1, source_target_pairs={{0,4},{4,0},{8,12},{12,8},{16,20},{20,16},{24,28},{28,24},{1,5},{5... | collective-permute-start | bytes 294920 | tf_op jit(solution)/shard_map/ppermute | solution.py:328
  32.6 7.6 %collective-permute-start.9 = (bf16[3,64,256]{2,1,0:T(8,128)(2,1)S(1)}, bf16[3,64,256]{2,1,0:T(8,128)(2,1)S(1)}, u32[]{:S(2)}, u32[]{:S(2)}) collective-permute-start(bf16[3,64,256]{2,1,0:T(8,128)(2,1)S(1)} %get-tuple-element.49), channel_id=1, source_target_pairs={{0,24},{4,28},{8,16},{12,20},{16,8},{20,12},{24,0},{28,4},{1,25},{... | collective-permute-start | bytes 294920 | tf_op jit(solution)/shard_map/ppermute | solution.py:328
  33.9 8.7 %collective-permute-start.10 = (bf16[3,64,256]{2,1,0:T(8,128)(2,1)S(1)}, bf16[3,64,256]{2,1,0:T(8,128)(2,1)S(1)}, u32[]{:S(2)}, u32[]{:S(2)}) collective-permute-start(bf16[3,64,256]{2,1,0:T(8,128)(2,1)S(1)} %get-tuple-element.50), channel_id=1, source_target_pairs={{0,8},{4,12},{8,0},{12,4},{16,24},{20,28},{24,16},{28,20},{1,9},{5... | collective-permute-start | bytes 294920 | tf_op jit(solution)/shard_map/ppermute | solution.py:328
  33.9 8.7 %collective-permute-start.11 = (bf16[3,64,256]{2,1,0:T(8,128)(2,1)S(1)}, bf16[3,64,256]{2,1,0:T(8,128)(2,1)S(1)}, u32[]{:S(2)}, u32[]{:S(2)}) collective-permute-start(bf16[3,64,256]{2,1,0:T(8,128)(2,1)S(1)} %get-tuple-element.51), channel_id=1, source_target_pairs={{0,20},{4,16},{8,28},{12,24},{16,4},{20,0},{24,12},{28,8},{1,21},{... | collective-permute-start | bytes 294920 | tf_op jit(solution)/shard_map/ppermute | solution.py:328
  36.9 7.7 %collective-permute-start.12 = (bf16[3,64,256]{2,1,0:T(8,128)(2,1)S(1)}, bf16[3,64,256]{2,1,0:T(8,128)(2,1)S(1)}, u32[]{:S(2)}, u32[]{:S(2)}) collective-permute-start(bf16[3,64,256]{2,1,0:T(8,128)(2,1)S(1)} %get-tuple-element.52), channel_id=1, source_target_pairs={{0,12},{4,8},{8,4},{12,0},{16,28},{20,24},{24,20},{28,16},{1,13},{... | collective-permute-start | bytes 294920 | tf_op jit(solution)/shard_map/ppermute | solution.py:328
  37.9 8.7 %collective-permute-start.13 = (bf16[3,64,256]{2,1,0:T(8,128)(2,1)S(1)}, bf16[3,64,256]{2,1,0:T(8,128)(2,1)S(1)}, u32[]{:S(2)}, u32[]{:S(2)}) collective-permute-start(bf16[3,64,256]{2,1,0:T(8,128)(2,1)S(1)} %get-tuple-element.53), channel_id=1, source_target_pairs={{0,16},{4,20},{8,24},{12,28},{16,0},{20,4},{24,8},{28,12},{1,17},{... | collective-permute-start | bytes 294920 | tf_op jit(solution)/shard_map/ppermute | solution.py:328
  47.2 1.6 %collective-permute-start.14 = (bf16[256,512]{1,0:T(8,128)(2,1)S(1)}, bf16[256,512]{1,0:T(8,128)(2,1)S(1)}, u32[]{:S(2)}, u32[]{:S(2)}) collective-permute-start(bf16[256,512]{1,0:T(8,128)(2,1)S(1)} %get-tuple-element.63), channel_id=1, source_target_pairs={{0,1},{1,0},{2,3},{3,2},{4,5},{5,4},{6,7},{7,6},{8,9},{9,8},{10,11... | collective-permute-start | bytes 786440 | tf_op jit(solution)/shard_map/ppermute | solution.py:328
  48.9 8.4 %collective-permute-start.15 = (bf16[256,512]{1,0:T(8,128)(2,1)S(1)}, bf16[256,512]{1,0:T(8,128)(2,1)S(1)}, u32[]{:S(2)}, u32[]{:S(2)}) collective-permute-start(bf16[256,512]{1,0:T(8,128)(2,1)S(1)} %add_convert_fusion.1), channel_id=1, source_target_pairs={{0,2},{1,3},{2,0},{3,1},{4,6},{5,7},{6,4},{7,5},{8,10},{9,11},{10,... | collective-permute-start | bytes 786440 | tf_op jit(solution)/shard_map/ppermute | solution.py:328
  50.5 6.9 %collective-permute-start.16 = (bf16[256,512]{1,0:T(8,128)(2,1)S(1)}, bf16[256,512]{1,0:T(8,128)(2,1)S(1)}, u32[]{:S(2)}, u32[]{:S(2)}) collective-permute-start(bf16[256,512]{1,0:T(8,128)(2,1)S(1)} %get-tuple-element.66), channel_id=1, source_target_pairs={{0,1},{1,0},{2,3},{3,2},{4,5},{5,4},{6,7},{7,6},{8,9},{9,8},{10,11... | collective-permute-start | bytes 786440 | tf_op jit(solution)/shard_map/ppermute | solution.py:328

commit v15 on v14

--- a/solution.py
+++ b/solution.py
@@ -96,7 +96,7 @@
 
 def by_distance(pieces):
     last = len(pieces) - 1
-    order = [last - i // 2 if i % 2 == 0 else 1 + i // 2 for i in range(last)]
+    order = [1 + i // 2 if i % 2 == 0 else last - i // 2 for i in range(last)]
     return zip([*order, 0], pieces)
 
 

time: 58.3 us -> 61.2 us (1.050)
  waiting for transfers between devices: 20.3 us -> 26.2 us
  starting transfers between devices: 28 us -> 25.1 us
    ppermute x17, waiting for transfers between devices: 20.3 us -> 26.2 us  [exchange(): return lax.ppermute(block, axis, pairs)]
    ppermute x17, starting transfers between devices: 28 us -> 25.1 us  [exchange(): return lax.ppermute(block, axis, pairs)]
  transfers between devices with their start and end apart: 17 -> 17, of which waited for: 8 -> 12; matrix products, arithmetic and copies ran while one was open for 0% -> 0% of each run, Pallas kernels for 4% -> 4%
where the time goes in v15:
time: 61.2 us; the launch traced here: 61.1 us
  waiting for transfers between devices  26.2 us (43%)
  starting transfers between devices  25.1 us (41%)
  Pallas kernels  8.26 us (13%)
  other arithmetic  0.87 us (1%)
  between operations  0.7 us (1%)
    ppermute x17, waiting for transfers between devices, exchange(): return lax.ppermute(block, axis, pairs)  26.2 us
    ppermute x17, starting transfers between devices, exchange(): return lax.ppermute(block, axis, pairs)  25.1 us
    pallas_call x1, Pallas kernels, per_device(): pl.pallas_call(conv_kernel, in_specs=[VMEM] * blocks + [HBM] * 10, out_sh...  3.61 us
    pallas_call x1, Pallas kernels, per_device(): pl.pallas_call(gate_kernel, in_specs=[HBM] * 5, out_shape=arrays(blocks,...  1.5 us
  transfers between devices with their start and end apart: 17, of which 12 were waited for; matrix products, arithmetic and copies ran while one was open for 0% of the time, Pallas kernels for 4%

profile of v15, /device:TPU:0, one launch (start us, length us, event | category | flops | bytes accessed | tf_op | source)
XLA Modules:
  0.0 61.1 jit_solution(457643823130536905)
XLA Ops:
  0.6 1.5 %gate.1 = (bf16[3,64,256]{2,1,0:T(8,128)(2,1)S(1)}, bf16[3,64,256]{2,1,0:T(8,128)(2,1)S(1)}, bf16[3,64,256]{2,1,0:T(8,128)(2,1)S(1)}, bf16[3,64,256]{2,1,0:T(8,1...) custom-call(bf16[256,512]{1,0:T(8,128)(2,1)} %refs_0_.1, ...), custom_call_target="tpu_custom_call" | custom-call | tf_op jit(solution)/shard_map/gate/pallas_call | solution.py:353
  2.1 3.0 %collective-permute-start = (bf16[3,64,256]{2,1,0:T(8,128)(2,1)S(1)}, bf16[3,64,256]{2,1,0:T(8,128)(2,1)S(1)}, u32[]{:S(2)}, u32[]{:S(2)}) collective-permute-start(bf16[3,64,256]{2,1,0:T(8,128)(2,1)S(1)} %get-tuple-element.39), channel_id=1, source_target_pairs={{0,4},{4,0},{8,12},{12,8},{16,20},{20,16},{24,28},{28,24},{1,5},{5... | collective-permute-start | bytes 294920 | tf_op jit(solution)/shard_map/ppermute | solution.py:328
  5.2 3.5 %collective-permute-start.1 = (bf16[3,64,256]{2,1,0:T(8,128)(2,1)S(1)}, bf16[3,64,256]{2,1,0:T(8,128)(2,1)S(1)}, u32[]{:S(2)}, u32[]{:S(2)}) collective-permute-start(bf16[3,64,256]{2,1,0:T(8,128)(2,1)S(1)} %get-tuple-element.40), channel_id=1, source_target_pairs={{0,28},{4,24},{8,20},{12,16},{16,12},{20,8},{24,4},{28,0},{1,29},{... | collective-permute-start | bytes 294920 | tf_op jit(solution)/shard_map/ppermute | solution.py:328
  8.7 0.0 collective-permute-start.2
  8.7 0.9 %collective-permute-start.3 = (bf16[3,64,256]{2,1,0:T(8,128)(2,1)S(1)}, bf16[3,64,256]{2,1,0:T(8,128)(2,1)S(1)}, u32[]{:S(2)}, u32[]{:S(2)}) collective-permute-start(bf16[3,64,256]{2,1,0:T(8,128)(2,1)S(1)} %get-tuple-element.42), channel_id=1, source_target_pairs={{0,24},{4,28},{8,16},{12,20},{16,8},{20,12},{24,0},{28,4},{1,25},{... | collective-permute-start | bytes 294920 | tf_op jit(solution)/shard_map/ppermute | solution.py:328
  9.6 2.1 %collective-permute-start.4 = (bf16[3,64,256]{2,1,0:T(8,128)(2,1)S(1)}, bf16[3,64,256]{2,1,0:T(8,128)(2,1)S(1)}, u32[]{:S(2)}, u32[]{:S(2)}) collective-permute-start(bf16[3,64,256]{2,1,0:T(8,128)(2,1)S(1)} %get-tuple-element.43), channel_id=1, source_target_pairs={{0,12},{4,8},{8,4},{12,0},{16,28},{20,24},{24,20},{28,16},{1,13},{... | collective-permute-start | bytes 294920 | tf_op jit(solution)/shard_map/ppermute | solution.py:328
  11.7 0.0 collective-permute-done.refs_0_
  11.7 2.3 %collective-permute-start.5 = (bf16[3,64,256]{2,1,0:T(8,128)(2,1)S(1)}, bf16[3,64,256]{2,1,0:T(8,128)(2,1)S(1)}, u32[]{:S(2)}, u32[]{:S(2)}) collective-permute-start(bf16[3,64,256]{2,1,0:T(8,128)(2,1)S(1)} %get-tuple-element.44), channel_id=1, source_target_pairs={{0,20},{4,16},{8,28},{12,24},{16,4},{20,0},{24,12},{28,8},{1,21},{... | collective-permute-start | bytes 294920 | tf_op jit(solution)/shard_map/ppermute | solution.py:328
  14.0 0.0 collective-permute-done.1.refs_1_
  14.0 1.4 %collective-permute-start.6 = (bf16[3,64,256]{2,1,0:T(8,128)(2,1)S(1)}, bf16[3,64,256]{2,1,0:T(8,128)(2,1)S(1)}, u32[]{:S(2)}, u32[]{:S(2)}) collective-permute-start(bf16[3,64,256]{2,1,0:T(8,128)(2,1)S(1)} %get-tuple-element.45), channel_id=1, source_target_pairs={{0,16},{4,20},{8,24},{12,28},{16,0},{20,4},{24,8},{28,12},{1,17},{... | collective-permute-start | bytes 294920 | tf_op jit(solution)/shard_map/ppermute | solution.py:328
  15.4 1.6 %collective-permute-done.2.refs_2_ = bf16[3,64,256]{2,1,0:T(8,128)(2,1)S(1)} collective-permute-done((bf16[3,64,256]{2,1,0:T(8,128)(2,1)S(1)}, bf16[3,64,256]{2,1,0:T(8,128)(2,1)S(1)}, u32[]{:S(2)}, u32[]{:S(2)}) %collective-permute-start.2) | collective-permute-done | bytes 98336 | tf_op jit(solution)/shard_map/ppermute | solution.py:328
  17.1 0.0 collective-permute-done.3.refs_3_
  17.1 2.7 %collective-permute-done.4.refs_4_ = bf16[3,64,256]{2,1,0:T(8,128)(2,1)S(1)} collective-permute-done((bf16[3,64,256]{2,1,0:T(8,128)(2,1)S(1)}, bf16[3,64,256]{2,1,0:T(8,128)(2,1)S(1)}, u32[]{:S(2)}, u32[]{:S(2)}) %collective-permute-start.4) | collective-permute-done | bytes 98336 | tf_op jit(solution)/shard_map/ppermute | solution.py:328
  19.7 4.9 %collective-permute-done.5.refs_5_ = bf16[3,64,256]{2,1,0:T(8,128)(2,1)S(1)} collective-permute-done((bf16[3,64,256]{2,1,0:T(8,128)(2,1)S(1)}, bf16[3,64,256]{2,1,0:T(8,128)(2,1)S(1)}, u32[]{:S(2)}, u32[]{:S(2)}) %collective-permute-start.5) | collective-permute-done | bytes 98336 | tf_op jit(solution)/shard_map/ppermute | solution.py:328
  24.6 0.5 collective-permute-done.6.refs_6_
  25.1 3.6 %conv.1 = (bf16[3,64,256]{2,1,0:T(8,128)(2,1)S(1)}, bf16[3,64,256]{2,1,0:T(8,128)(2,1)S(1)}, bf16[3,64,256]{2,1,0:T(8,128)(2,1)S(1)}, bf16[3,64,256]{2,1,0:T(8,1...) custom-call(bf16[3,64,256]{2,1,0:T(8,128)(2,1)S(1)} %collective-perm, ...), custom_call_target="tpu_custom_call" | custom-call | tf_op jit(solution)/shard_map/conv/pallas_call | solution.py:372
  28.7 1.6 %collective-permute-start.7 = (bf16[3,64,256]{2,1,0:T(8,128)(2,1)S(1)}, bf16[3,64,256]{2,1,0:T(8,128)(2,1)S(1)}, u32[]{:S(2)}, u32[]{:S(2)}) collective-permute-start(bf16[3,64,256]{2,1,0:T(8,128)(2,1)S(1)} %get-tuple-element.47), channel_id=1, source_target_pairs={{0,4},{4,0},{8,12},{12,8},{16,20},{20,16},{24,28},{28,24},{1,5},{5... | collective-permute-start | bytes 294920 | tf_op jit(solution)/shard_map/ppermute | solution.py:328
  30.3 2.8 %collective-permute-start.8 = (bf16[3,64,256]{2,1,0:T(8,128)(2,1)S(1)}, bf16[3,64,256]{2,1,0:T(8,128)(2,1)S(1)}, u32[]{:S(2)}, u32[]{:S(2)}) collective-permute-start(bf16[3,64,256]{2,1,0:T(8,128)(2,1)S(1)} %get-tuple-element.48), channel_id=1, source_target_pairs={{0,28},{4,24},{8,20},{12,16},{16,12},{20,8},{24,4},{28,0},{1,29},{... | collective-permute-start | bytes 294920 | tf_op jit(solution)/shard_map/ppermute | solution.py:328
  33.1 0.0 collective-permute-start.9
  33.1 1.0 %collective-permute-start.10 = (bf16[3,64,256]{2,1,0:T(8,128)(2,1)S(1)}, bf16[3,64,256]{2,1,0:T(8,128)(2,1)S(1)}, u32[]{:S(2)}, u32[]{:S(2)}) collective-permute-start(bf16[3,64,256]{2,1,0:T(8,128)(2,1)S(1)} %get-tuple-element.50), channel_id=1, source_target_pairs={{0,24},{4,28},{8,16},{12,20},{16,8},{20,12},{24,0},{28,4},{1,25},{... | collective-permute-start | bytes 294920 | tf_op jit(solution)/shard_map/ppermute | solution.py:328
  34.1 2.1 %collective-permute-start.11 = (bf16[3,64,256]{2,1,0:T(8,128)(2,1)S(1)}, bf16[3,64,256]{2,1,0:T(8,128)(2,1)S(1)}, u32[]{:S(2)}, u32[]{:S(2)}) collective-permute-start(bf16[3,64,256]{2,1,0:T(8,128)(2,1)S(1)} %get-tuple-element.51), channel_id=1, source_target_pairs={{0,12},{4,8},{8,4},{12,0},{16,28},{20,24},{24,20},{28,16},{1,13},{... | collective-permute-start | bytes 294920 | tf_op jit(solution)/shard_map/ppermute | solution.py:328
  36.2 0.0 collective-permute-done.7.refs_0_
  36.2 2.2 %collective-permute-start.12 = (bf16[3,64,256]{2,1,0:T(8,128)(2,1)S(1)}, bf16[3,64,256]{2,1,0:T(8,128)(2,1)S(1)}, u32[]{:S(2)}, u32[]{:S(2)}) collective-permute-start(bf16[3,64,256]{2,1,0:T(8,128)(2,1)S(1)} %get-tuple-element.52), channel_id=1, source_target_pairs={{0,20},{4,16},{8,28},{12,24},{16,4},{20,0},{24,12},{28,8},{1,21},{... | collective-permute-start | bytes 294920 | tf_op jit(solution)/shard_map/ppermute | solution.py:328
  38.4 0.1 collective-permute-done.8.refs_1_
  38.6 0.5 collective-permute-start.13
  39.1 2.5 %collective-permute-done.9.refs_2_ = bf16[3,64,256]{2,1,0:T(8,128)(2,1)S(1)} collective-permute-done((bf16[3,64,256]{2,1,0:T(8,128)(2,1)S(1)}, bf16[3,64,256]{2,1,0:T(8,128)(2,1)S(1)}, u32[]{:S(2)}, u32[]{:S(2)}) %collective-permute-start.9) | collective-permute-done | bytes 98336 | tf_op jit(solution)/shard_map/ppermute | solution.py:328
  41.6 0.3 collective-permute-done.10.refs_3_
  41.9 2.4 %collective-permute-done.11.refs_4_ = bf16[3,64,256]{2,1,0:T(8,128)(2,1)S(1)} collective-permute-done((bf16[3,64,256]{2,1,0:T(8,128)(2,1)S(1)}, bf16[3,64,256]{2,1,0:T(8,128)(2,1)S(1)}, u32[]{:S(2)}, u32[]{:S(2)}) %collective-permute-start.11) | collective-permute-done | bytes 98336 | tf_op jit(solution)/shard_map/ppermute | solution.py:328
  44.3 4.6 %collective-permute-done.12.refs_5_ = bf16[3,64,256]{2,1,0:T(8,128)(2,1)S(1)} collective-permute-done((bf16[3,64,256]{2,1,0:T(8,128)(2,1)S(1)}, bf16[3,64,256]{2,1,0:T(8,128)(2,1)S(1)}, u32[]{:S(2)}, u32[]{:S(2)}) %collective-permute-start.12) | collective-permute-done | bytes 98336 | tf_op jit(solution)/shard_map/ppermute | solution.py:328
  48.9 0.6 collective-permute-done.13.refs_6_
  49.5 0.7 %mate.1 = (bf16[3,256,512]{2,1,0:T(8,128)(2,1)S(1)}, bf16[256,512]{1,0:T(8,128)(2,1)S(1)}) custom-call(bf16[3,64,256]{2,1,0:T(8,128)(2,1)S(1)} %collective-permute-done.7.refs_0_, bf16[3,64,256]{2,1,0:T(8,128)(2,1)S(1)} %collective-permute-done.8.refs_1_, bf16[3,64,256]{2,1,0:T(8,128)(2,1)S(1)} %collective-permute-done.9.refs_2_, ...), custom_call_target="tpu_custom_call" | custom-call | flops 805306368 | bytes 4194304 | tf_op jit(solution)/shard_map/mate/pallas_call | solution.py:389
  50.2 0.1 collective-permute-start.14
  50.3 1.0 %far.1 = (f32[256,512]{1,0:T(8,128)S(1)}, bf16[256,512]{1,0:T(8,128)(2,1)S(1)}) custom-call(bf16[3,256,512]{2,1,0:T(8,128)(2,1)S(1)} %get-tuple-element.67.lhs_ref, bf16[2048,512]{1,0:T(8,128)(2,1)S(1)} %get-tuple-element.58.refs_11_.wk_ref, bf16[2048,512]{1,0:T(8,128)(2,1)S(1)} %get-tuple-element.59.refs_12_.wq_ref, ...), custom_call_target="tpu_custom_call" | custom-call | flops 805306368 | bytes 4194304 | tf_op jit(solution)/shard_map/far/pallas_call | solution.py:399
  51.3 0.5 collective-permute-done.14
  51.8 0.1 add_convert_fusion.1
  51.9 1.6 %collective-permute-start.15 = (bf16[256,512]{1,0:T(8,128)(2,1)S(1)}, bf16[256,512]{1,0:T(8,128)(2,1)S(1)}, u32[]{:S(2)}, u32[]{:S(2)}) collective-permute-start(bf16[256,512]{1,0:T(8,128)(2,1)S(1)} %add_convert_fusion.1), channel_id=1, source_target_pairs={{0,2},{1,3},{2,0},{3,1},{4,6},{5,7},{6,4},{7,5},{8,10},{9,11},{10,... | collective-permute-start | bytes 786440 | tf_op jit(solution)/shard_map/ppermute | solution.py:328
  53.4 0.0 collective-permute-start.16
  53.4 0.6 own.1
  54.0 0.9 %turn.1 = bf16[256,512]{1,0:T(8,128)(2,1)} custom-call(bf16[3,64,256]{2,1,0:T(8,128)(2,1)S(1)} %collective-permute-done.7.refs_0_, bf16[3,64,256]{2,1,0:T(8,128)(2,1)S(1)} %collective-permute-done.8.refs_1_, bf16[3,64,256]{2,1,0:T(8,128)(2,1)S(1)} %collective-permute-done.9.refs_2_, bf16[3,64,256]{2,1,0:T(8,128)(2,1)S(1)} %collective-permute-done.10.refs_3_, ...), custom_call_target="tpu_custom_call" | custom-call | flops 805306368 | bytes 4194304 | tf_op jit(solution)/shard_map/turn/pallas_call | solution.py:411
  54.9 5.4 %collective-permute-done.15 = bf16[256,512]{1,0:T(8,128)(2,1)S(1)} collective-permute-done((bf16[256,512]{1,0:T(8,128)(2,1)S(1)}, bf16[256,512]{1,0:T(8,128)(2,1)S(1)}, u32[]{:S(2)}, u32[]{:S(2)}) %collective-permute-start.15) | collective-permute-done | bytes 262176 | tf_op jit(solution)/shard_map/ppermute | solution.py:328
  60.3 0.0 collective-permute-done.16
  60.3 0.8 %add_convert_fusion = bf16[256,512]{1,0:T(8,128)(2,1)} fusion(f32[256,512]{1,0:T(8,128)S(1)} %own.1, bf16[256,512]{1,0:T(8,128)(2,1)S(1)} %collective-permute-done.16, bf16[256,512]{1,0:T(8,128)(2,1)S(1)} %collective-permute-done.15), kind=kLoop, calls=%fused_computation | loop fusion | flops 655360 | bytes 1310720 | tf_op jit(solution)/shard_map/convert_element_type | solution.py:429
Async XLA Ops:
  2.1 9.6 %collective-permute-start = (bf16[3,64,256]{2,1,0:T(8,128)(2,1)S(1)}, bf16[3,64,256]{2,1,0:T(8,128)(2,1)S(1)}, u32[]{:S(2)}, u32[]{:S(2)}) collective-permute-start(bf16[3,64,256]{2,1,0:T(8,128)(2,1)S(1)} %get-tuple-element.39), channel_id=1, source_target_pairs={{0,4},{4,0},{8,12},{12,8},{16,20},{20,16},{24,28},{28,24},{1,5},{5... | collective-permute-start | bytes 294920 | tf_op jit(solution)/shard_map/ppermute | solution.py:328
  5.2 8.8 %collective-permute-start.1 = (bf16[3,64,256]{2,1,0:T(8,128)(2,1)S(1)}, bf16[3,64,256]{2,1,0:T(8,128)(2,1)S(1)}, u32[]{:S(2)}, u32[]{:S(2)}) collective-permute-start(bf16[3,64,256]{2,1,0:T(8,128)(2,1)S(1)} %get-tuple-element.40), channel_id=1, source_target_pairs={{0,28},{4,24},{8,20},{12,16},{16,12},{20,8},{24,4},{28,0},{1,29},{... | collective-permute-start | bytes 294920 | tf_op jit(solution)/shard_map/ppermute | solution.py:328
  8.7 8.3 %collective-permute-start.2 = (bf16[3,64,256]{2,1,0:T(8,128)(2,1)S(1)}, bf16[3,64,256]{2,1,0:T(8,128)(2,1)S(1)}, u32[]{:S(2)}, u32[]{:S(2)}) collective-permute-start(bf16[3,64,256]{2,1,0:T(8,128)(2,1)S(1)} %get-tuple-element.41), channel_id=1, source_target_pairs={{0,8},{4,12},{8,0},{12,4},{16,24},{20,28},{24,16},{28,20},{1,9},{5... | collective-permute-start | bytes 294920 | tf_op jit(solution)/shard_map/ppermute | solution.py:328
  8.7 8.3 %collective-permute-start.3 = (bf16[3,64,256]{2,1,0:T(8,128)(2,1)S(1)}, bf16[3,64,256]{2,1,0:T(8,128)(2,1)S(1)}, u32[]{:S(2)}, u32[]{:S(2)}) collective-permute-start(bf16[3,64,256]{2,1,0:T(8,128)(2,1)S(1)} %get-tuple-element.42), channel_id=1, source_target_pairs={{0,24},{4,28},{8,16},{12,20},{16,8},{20,12},{24,0},{28,4},{1,25},{... | collective-permute-start | bytes 294920 | tf_op jit(solution)/shard_map/ppermute | solution.py:328
  9.6 10.1 %collective-permute-start.4 = (bf16[3,64,256]{2,1,0:T(8,128)(2,1)S(1)}, bf16[3,64,256]{2,1,0:T(8,128)(2,1)S(1)}, u32[]{:S(2)}, u32[]{:S(2)}) collective-permute-start(bf16[3,64,256]{2,1,0:T(8,128)(2,1)S(1)} %get-tuple-element.43), channel_id=1, source_target_pairs={{0,12},{4,8},{8,4},{12,0},{16,28},{20,24},{24,20},{28,16},{1,13},{... | collective-permute-start | bytes 294920 | tf_op jit(solution)/shard_map/ppermute | solution.py:328
  11.7 12.9 %collective-permute-start.5 = (bf16[3,64,256]{2,1,0:T(8,128)(2,1)S(1)}, bf16[3,64,256]{2,1,0:T(8,128)(2,1)S(1)}, u32[]{:S(2)}, u32[]{:S(2)}) collective-permute-start(bf16[3,64,256]{2,1,0:T(8,128)(2,1)S(1)} %get-tuple-element.44), channel_id=1, source_target_pairs={{0,20},{4,16},{8,28},{12,24},{16,4},{20,0},{24,12},{28,8},{1,21},{... | collective-permute-start | bytes 294920 | tf_op jit(solution)/shard_map/ppermute | solution.py:328
  14.0 11.1 %collective-permute-start.6 = (bf16[3,64,256]{2,1,0:T(8,128)(2,1)S(1)}, bf16[3,64,256]{2,1,0:T(8,128)(2,1)S(1)}, u32[]{:S(2)}, u32[]{:S(2)}) collective-permute-start(bf16[3,64,256]{2,1,0:T(8,128)(2,1)S(1)} %get-tuple-element.45), channel_id=1, source_target_pairs={{0,16},{4,20},{8,24},{12,28},{16,0},{20,4},{24,8},{28,12},{1,17},{... | collective-permute-start | bytes 294920 | tf_op jit(solution)/shard_map/ppermute | solution.py:328
  28.7 7.4 %collective-permute-start.7 = (bf16[3,64,256]{2,1,0:T(8,128)(2,1)S(1)}, bf16[3,64,256]{2,1,0:T(8,128)(2,1)S(1)}, u32[]{:S(2)}, u32[]{:S(2)}) collective-permute-start(bf16[3,64,256]{2,1,0:T(8,128)(2,1)S(1)} %get-tuple-element.47), channel_id=1, source_target_pairs={{0,4},{4,0},{8,12},{12,8},{16,20},{20,16},{24,28},{28,24},{1,5},{5... | collective-permute-start | bytes 294920 | tf_op jit(solution)/shard_map/ppermute | solution.py:328
  30.3 8.2 %collective-permute-start.8 = (bf16[3,64,256]{2,1,0:T(8,128)(2,1)S(1)}, bf16[3,64,256]{2,1,0:T(8,128)(2,1)S(1)}, u32[]{:S(2)}, u32[]{:S(2)}) collective-permute-start(bf16[3,64,256]{2,1,0:T(8,128)(2,1)S(1)} %get-tuple-element.48), channel_id=1, source_target_pairs={{0,28},{4,24},{8,20},{12,16},{16,12},{20,8},{24,4},{28,0},{1,29},{... | collective-permute-start | bytes 294920 | tf_op jit(solution)/shard_map/ppermute | solution.py:328
  33.1 8.5 %collective-permute-start.9 = (bf16[3,64,256]{2,1,0:T(8,128)(2,1)S(1)}, bf16[3,64,256]{2,1,0:T(8,128)(2,1)S(1)}, u32[]{:S(2)}, u32[]{:S(2)}) collective-permute-start(bf16[3,64,256]{2,1,0:T(8,128)(2,1)S(1)} %get-tuple-element.49), channel_id=1, source_target_pairs={{0,8},{4,12},{8,0},{12,4},{16,24},{20,28},{24,16},{28,20},{1,9},{5... | collective-permute-start | bytes 294920 | tf_op jit(solution)/shard_map/ppermute | solution.py:328
  33.1 8.8 %collective-permute-start.10 = (bf16[3,64,256]{2,1,0:T(8,128)(2,1)S(1)}, bf16[3,64,256]{2,1,0:T(8,128)(2,1)S(1)}, u32[]{:S(2)}, u32[]{:S(2)}) collective-permute-start(bf16[3,64,256]{2,1,0:T(8,128)(2,1)S(1)} %get-tuple-element.50), channel_id=1, source_target_pairs={{0,24},{4,28},{8,16},{12,20},{16,8},{20,12},{24,0},{28,4},{1,25},{... | collective-permute-start | bytes 294920 | tf_op jit(solution)/shard_map/ppermute | solution.py:328
  34.1 10.2 %collective-permute-start.11 = (bf16[3,64,256]{2,1,0:T(8,128)(2,1)S(1)}, bf16[3,64,256]{2,1,0:T(8,128)(2,1)S(1)}, u32[]{:S(2)}, u32[]{:S(2)}) collective-permute-start(bf16[3,64,256]{2,1,0:T(8,128)(2,1)S(1)} %get-tuple-element.51), channel_id=1, source_target_pairs={{0,12},{4,8},{8,4},{12,0},{16,28},{20,24},{24,20},{28,16},{1,13},{... | collective-permute-start | bytes 294920 | tf_op jit(solution)/shard_map/ppermute | solution.py:328
  36.2 12.7 %collective-permute-start.12 = (bf16[3,64,256]{2,1,0:T(8,128)(2,1)S(1)}, bf16[3,64,256]{2,1,0:T(8,128)(2,1)S(1)}, u32[]{:S(2)}, u32[]{:S(2)}) collective-permute-start(bf16[3,64,256]{2,1,0:T(8,128)(2,1)S(1)} %get-tuple-element.52), channel_id=1, source_target_pairs={{0,20},{4,16},{8,28},{12,24},{16,4},{20,0},{24,12},{28,8},{1,21},{... | collective-permute-start | bytes 294920 | tf_op jit(solution)/shard_map/ppermute | solution.py:328
  38.6 11.0 %collective-permute-start.13 = (bf16[3,64,256]{2,1,0:T(8,128)(2,1)S(1)}, bf16[3,64,256]{2,1,0:T(8,128)(2,1)S(1)}, u32[]{:S(2)}, u32[]{:S(2)}) collective-permute-start(bf16[3,64,256]{2,1,0:T(8,128)(2,1)S(1)} %get-tuple-element.53), channel_id=1, source_target_pairs={{0,16},{4,20},{8,24},{12,28},{16,0},{20,4},{24,8},{28,12},{1,17},{... | collective-permute-start | bytes 294920 | tf_op jit(solution)/shard_map/ppermute | solution.py:328
  50.2 1.6 %collective-permute-start.14 = (bf16[256,512]{1,0:T(8,128)(2,1)S(1)}, bf16[256,512]{1,0:T(8,128)(2,1)S(1)}, u32[]{:S(2)}, u32[]{:S(2)}) collective-permute-start(bf16[256,512]{1,0:T(8,128)(2,1)S(1)} %get-tuple-element.63), channel_id=1, source_target_pairs={{0,1},{1,0},{2,3},{3,2},{4,5},{5,4},{6,7},{7,6},{8,9},{9,8},{10,11... | collective-permute-start | bytes 786440 | tf_op jit(solution)/shard_map/ppermute | solution.py:328
  51.9 8.4 %collective-permute-start.15 = (bf16[256,512]{1,0:T(8,128)(2,1)S(1)}, bf16[256,512]{1,0:T(8,128)(2,1)S(1)}, u32[]{:S(2)}, u32[]{:S(2)}) collective-permute-start(bf16[256,512]{1,0:T(8,128)(2,1)S(1)} %add_convert_fusion.1), channel_id=1, source_target_pairs={{0,2},{1,3},{2,0},{3,1},{4,6},{5,7},{6,4},{7,5},{8,10},{9,11},{10,... | collective-permute-start | bytes 786440 | tf_op jit(solution)/shard_map/ppermute | solution.py:328
  53.4 6.9 %collective-permute-start.16 = (bf16[256,512]{1,0:T(8,128)(2,1)S(1)}, bf16[256,512]{1,0:T(8,128)(2,1)S(1)}, u32[]{:S(2)}, u32[]{:S(2)}) collective-permute-start(bf16[256,512]{1,0:T(8,128)(2,1)S(1)} %get-tuple-element.66), channel_id=1, source_target_pairs={{0,1},{1,0},{2,3},{3,2},{4,5},{5,4},{6,7},{7,6},{8,9},{9,8},{10,11... | collective-permute-start | bytes 786440 | tf_op jit(solution)/shard_map/ppermute | solution.py:328

commit v16 on v15

--- a/solution.py
+++ b/solution.py
@@ -95,8 +95,10 @@
 
 
 def by_distance(pieces):
-    last = len(pieces) - 1
-    order = [1 + i // 2 if i % 2 == 0 else last - i // 2 for i in range(last)]
+    blocks, last = len(pieces), len(pieces) - 1
+    far, near = list(range(last, blocks // 2 - 1, -1)), list(range(1, blocks // 2))
+    far.insert(0, far.pop(len(far) // 2))
+    order = [far[i // 2] if i % 2 == 0 else near[i // 2] for i in range(last)]
     return zip([*order, 0], pieces)
 
 

time: 61.2 us -> 60.4 us (0.987)
  waiting for transfers between devices: 26.2 us -> 20.3 us
  starting transfers between devices: 25.1 us -> 30.1 us
    ppermute x17, waiting for transfers between devices: 26.2 us -> 20.3 us  [exchange(): return lax.ppermute(block, axis, pairs)]
    ppermute x17, starting transfers between devices: 25.1 us -> 30.1 us  [exchange(): return lax.ppermute(block, axis, pairs)]
  transfers between devices with their start and end apart: 17 -> 17, of which waited for: 12 -> 9; matrix products, arithmetic and copies ran while one was open for 0% -> 0% of each run, Pallas kernels for 4% -> 4%
where the time goes in v16:
time: 60.4 us; the launch traced here: 60.2 us
  starting transfers between devices  30.1 us (50%)
  waiting for transfers between devices  20.3 us (34%)
  Pallas kernels  8.26 us (14%)
  other arithmetic  0.87 us (1%)
  between operations  0.7 us (1%)
    ppermute x17, starting transfers between devices, exchange(): return lax.ppermute(block, axis, pairs)  30.1 us
    ppermute x17, waiting for transfers between devices, exchange(): return lax.ppermute(block, axis, pairs)  20.3 us
    pallas_call x1, Pallas kernels, per_device(): pl.pallas_call(conv_kernel, in_specs=[VMEM] * blocks + [HBM] * 10, out_sh...  3.6 us
    pallas_call x1, Pallas kernels, per_device(): pl.pallas_call(gate_kernel, in_specs=[HBM] * 5, out_shape=arrays(blocks,...  1.5 us
  transfers between devices with their start and end apart: 17, of which 9 were waited for; matrix products, arithmetic and copies ran while one was open for 0% of the time, Pallas kernels for 4%

profile of v16, /device:TPU:0, one launch (start us, length us, event | category | flops | bytes accessed | tf_op | source)
XLA Modules:
  0.0 60.2 jit_solution(2574918803556910282)
XLA Ops:
  0.6 1.5 %gate.1 = (bf16[3,64,256]{2,1,0:T(8,128)(2,1)S(1)}, bf16[3,64,256]{2,1,0:T(8,128)(2,1)S(1)}, bf16[3,64,256]{2,1,0:T(8,128)(2,1)S(1)}, bf16[3,64,256]{2,1,0:T(8,1...) custom-call(bf16[256,512]{1,0:T(8,128)(2,1)} %refs_0_.1, ...), custom_call_target="tpu_custom_call" | custom-call | tf_op jit(solution)/shard_map/gate/pallas_call | solution.py:355
  2.1 5.1 %collective-permute-start = (bf16[3,64,256]{2,1,0:T(8,128)(2,1)S(1)}, bf16[3,64,256]{2,1,0:T(8,128)(2,1)S(1)}, u32[]{:S(2)}, u32[]{:S(2)}) collective-permute-start(bf16[3,64,256]{2,1,0:T(8,128)(2,1)S(1)} %get-tuple-element.39), channel_id=1, source_target_pairs={{0,20},{4,16},{8,28},{12,24},{16,4},{20,0},{24,12},{28,8},{1,21},{... | collective-permute-start | bytes 294920 | tf_op jit(solution)/shard_map/ppermute | solution.py:330
  7.2 0.5 collective-permute-start.1
  7.7 2.3 %collective-permute-start.2 = (bf16[3,64,256]{2,1,0:T(8,128)(2,1)S(1)}, bf16[3,64,256]{2,1,0:T(8,128)(2,1)S(1)}, u32[]{:S(2)}, u32[]{:S(2)}) collective-permute-start(bf16[3,64,256]{2,1,0:T(8,128)(2,1)S(1)} %get-tuple-element.41), channel_id=1, source_target_pairs={{0,28},{4,24},{8,20},{12,16},{16,12},{20,8},{24,4},{28,0},{1,29},{... | collective-permute-start | bytes 294920 | tf_op jit(solution)/shard_map/ppermute | solution.py:330
  10.0 0.0 collective-permute-start.3
  10.0 3.1 %collective-permute-start.4 = (bf16[3,64,256]{2,1,0:T(8,128)(2,1)S(1)}, bf16[3,64,256]{2,1,0:T(8,128)(2,1)S(1)}, u32[]{:S(2)}, u32[]{:S(2)}) collective-permute-start(bf16[3,64,256]{2,1,0:T(8,128)(2,1)S(1)} %get-tuple-element.43), channel_id=1, source_target_pairs={{0,24},{4,28},{8,16},{12,20},{16,8},{20,12},{24,0},{28,4},{1,25},{... | collective-permute-start | bytes 294920 | tf_op jit(solution)/shard_map/ppermute | solution.py:330
  13.2 0.5 collective-permute-done.refs_0_
  13.7 2.3 %collective-permute-start.5 = (bf16[3,64,256]{2,1,0:T(8,128)(2,1)S(1)}, bf16[3,64,256]{2,1,0:T(8,128)(2,1)S(1)}, u32[]{:S(2)}, u32[]{:S(2)}) collective-permute-start(bf16[3,64,256]{2,1,0:T(8,128)(2,1)S(1)} %get-tuple-element.44), channel_id=1, source_target_pairs={{0,12},{4,8},{8,4},{12,0},{16,28},{20,24},{24,20},{28,16},{1,13},{... | collective-permute-start | bytes 294920 | tf_op jit(solution)/shard_map/ppermute | solution.py:330
  16.0 0.0 collective-permute-done.1.refs_1_
  16.0 4.4 %collective-permute-start.6 = (bf16[3,64,256]{2,1,0:T(8,128)(2,1)S(1)}, bf16[3,64,256]{2,1,0:T(8,128)(2,1)S(1)}, u32[]{:S(2)}, u32[]{:S(2)}) collective-permute-start(bf16[3,64,256]{2,1,0:T(8,128)(2,1)S(1)} %get-tuple-element.45), channel_id=1, source_target_pairs={{0,16},{4,20},{8,24},{12,28},{16,0},{20,4},{24,8},{28,12},{1,17},{... | collective-permute-start | bytes 294920 | tf_op jit(solution)/shard_map/ppermute | solution.py:330
  20.4 0.0 collective-permute-done.2.refs_2_
  20.4 0.0 collective-permute-done.3.refs_3_
  20.4 0.0 collective-permute-done.4.refs_4_
  20.4 0.1 collective-permute-done.5.refs_5_
  20.6 4.5 %collective-permute-done.6.refs_6_ = bf16[3,64,256]{2,1,0:T(8,128)(2,1)S(1)} collective-permute-done((bf16[3,64,256]{2,1,0:T(8,128)(2,1)S(1)}, bf16[3,64,256]{2,1,0:T(8,128)(2,1)S(1)}, u32[]{:S(2)}, u32[]{:S(2)}) %collective-permute-start.6) | collective-permute-done | bytes 98336 | tf_op jit(solution)/shard_map/ppermute | solution.py:330
  25.1 3.6 %conv.1 = (bf16[3,64,256]{2,1,0:T(8,128)(2,1)S(1)}, bf16[3,64,256]{2,1,0:T(8,128)(2,1)S(1)}, bf16[3,64,256]{2,1,0:T(8,128)(2,1)S(1)}, bf16[3,64,256]{2,1,0:T(8,1...) custom-call(bf16[3,64,256]{2,1,0:T(8,128)(2,1)S(1)} %collective-perm, ...), custom_call_target="tpu_custom_call" | custom-call | tf_op jit(solution)/shard_map/conv/pallas_call | solution.py:374
  28.7 0.8 %collective-permute-start.7 = (bf16[3,64,256]{2,1,0:T(8,128)(2,1)S(1)}, bf16[3,64,256]{2,1,0:T(8,128)(2,1)S(1)}, u32[]{:S(2)}, u32[]{:S(2)}) collective-permute-start(bf16[3,64,256]{2,1,0:T(8,128)(2,1)S(1)} %get-tuple-element.47), channel_id=1, source_target_pairs={{0,20},{4,16},{8,28},{12,24},{16,4},{20,0},{24,12},{28,8},{1,21},{... | collective-permute-start | bytes 294920 | tf_op jit(solution)/shard_map/ppermute | solution.py:330
  29.5 1.5 %collective-permute-start.8 = (bf16[3,64,256]{2,1,0:T(8,128)(2,1)S(1)}, bf16[3,64,256]{2,1,0:T(8,128)(2,1)S(1)}, u32[]{:S(2)}, u32[]{:S(2)}) collective-permute-start(bf16[3,64,256]{2,1,0:T(8,128)(2,1)S(1)} %get-tuple-element.48), channel_id=1, source_target_pairs={{0,4},{4,0},{8,12},{12,8},{16,20},{20,16},{24,28},{28,24},{1,5},{5... | collective-permute-start | bytes 294920 | tf_op jit(solution)/shard_map/ppermute | solution.py:330
  31.1 2.5 %collective-permute-start.9 = (bf16[3,64,256]{2,1,0:T(8,128)(2,1)S(1)}, bf16[3,64,256]{2,1,0:T(8,128)(2,1)S(1)}, u32[]{:S(2)}, u32[]{:S(2)}) collective-permute-start(bf16[3,64,256]{2,1,0:T(8,128)(2,1)S(1)} %get-tuple-element.49), channel_id=1, source_target_pairs={{0,28},{4,24},{8,20},{12,16},{16,12},{20,8},{24,4},{28,0},{1,29},{... | collective-permute-start | bytes 294920 | tf_op jit(solution)/shard_map/ppermute | solution.py:330
  33.5 0.5 collective-permute-start.10
  34.0 2.9 %collective-permute-start.11 = (bf16[3,64,256]{2,1,0:T(8,128)(2,1)S(1)}, bf16[3,64,256]{2,1,0:T(8,128)(2,1)S(1)}, u32[]{:S(2)}, u32[]{:S(2)}) collective-permute-start(bf16[3,64,256]{2,1,0:T(8,128)(2,1)S(1)} %get-tuple-element.51), channel_id=1, source_target_pairs={{0,24},{4,28},{8,16},{12,20},{16,8},{20,12},{24,0},{28,4},{1,25},{... | collective-permute-start | bytes 294920 | tf_op jit(solution)/shard_map/ppermute | solution.py:330
  36.9 2.2 %collective-permute-done.7.refs_0_ = bf16[3,64,256]{2,1,0:T(8,128)(2,1)S(1)} collective-permute-done((bf16[3,64,256]{2,1,0:T(8,128)(2,1)S(1)}, bf16[3,64,256]{2,1,0:T(8,128)(2,1)S(1)}, u32[]{:S(2)}, u32[]{:S(2)}) %collective-permute-start.7) | collective-permute-done | bytes 98336 | tf_op jit(solution)/shard_map/ppermute | solution.py:330
  39.1 0.0 collective-permute-start.12
  39.1 0.0 collective-permute-done.8.refs_1_
  39.1 2.6 %collective-permute-start.13 = (bf16[3,64,256]{2,1,0:T(8,128)(2,1)S(1)}, bf16[3,64,256]{2,1,0:T(8,128)(2,1)S(1)}, u32[]{:S(2)}, u32[]{:S(2)}) collective-permute-start(bf16[3,64,256]{2,1,0:T(8,128)(2,1)S(1)} %get-tuple-element.53), channel_id=1, source_target_pairs={{0,16},{4,20},{8,24},{12,28},{16,0},{20,4},{24,8},{28,12},{1,17},{... | collective-permute-start | bytes 294920 | tf_op jit(solution)/shard_map/ppermute | solution.py:330
  41.7 0.0 collective-permute-done.9.refs_2_
  41.7 1.0 %collective-permute-done.10.refs_3_ = bf16[3,64,256]{2,1,0:T(8,128)(2,1)S(1)} collective-permute-done((bf16[3,64,256]{2,1,0:T(8,128)(2,1)S(1)}, bf16[3,64,256]{2,1,0:T(8,128)(2,1)S(1)}, u32[]{:S(2)}, u32[]{:S(2)}) %collective-permute-start.10) | collective-permute-done | bytes 98336 | tf_op jit(solution)/shard_map/ppermute | solution.py:330
  42.7 0.0 collective-permute-done.11.refs_4_
  42.7 2.2 %collective-permute-done.12.refs_5_ = bf16[3,64,256]{2,1,0:T(8,128)(2,1)S(1)} collective-permute-done((bf16[3,64,256]{2,1,0:T(8,128)(2,1)S(1)}, bf16[3,64,256]{2,1,0:T(8,128)(2,1)S(1)}, u32[]{:S(2)}, u32[]{:S(2)}) %collective-permute-start.12) | collective-permute-done | bytes 98336 | tf_op jit(solution)/shard_map/ppermute | solution.py:330
  44.9 3.8 %collective-permute-done.13.refs_6_ = bf16[3,64,256]{2,1,0:T(8,128)(2,1)S(1)} collective-permute-done((bf16[3,64,256]{2,1,0:T(8,128)(2,1)S(1)}, bf16[3,64,256]{2,1,0:T(8,128)(2,1)S(1)}, u32[]{:S(2)}, u32[]{:S(2)}) %collective-permute-start.13) | collective-permute-done | bytes 98336 | tf_op jit(solution)/shard_map/ppermute | solution.py:330
  48.7 0.7 %mate.1 = (bf16[3,256,512]{2,1,0:T(8,128)(2,1)S(1)}, bf16[256,512]{1,0:T(8,128)(2,1)S(1)}) custom-call(bf16[3,64,256]{2,1,0:T(8,128)(2,1)S(1)} %collective-permute-done.7.refs_0_, bf16[3,64,256]{2,1,0:T(8,128)(2,1)S(1)} %collective-permute-done.8.refs_1_, bf16[3,64,256]{2,1,0:T(8,128)(2,1)S(1)} %collective-permute-done.9.refs_2_, ...), custom_call_target="tpu_custom_call" | custom-call | flops 805306368 | bytes 4194304 | tf_op jit(solution)/shard_map/mate/pallas_call | solution.py:391
  49.3 0.1 collective-permute-start.14
  49.4 1.0 %far.1 = (f32[256,512]{1,0:T(8,128)S(1)}, bf16[256,512]{1,0:T(8,128)(2,1)S(1)}) custom-call(bf16[3,256,512]{2,1,0:T(8,128)(2,1)S(1)} %get-tuple-element.67.lhs_ref, bf16[2048,512]{1,0:T(8,128)(2,1)S(1)} %get-tuple-element.58.refs_11_.wk_ref, bf16[2048,512]{1,0:T(8,128)(2,1)S(1)} %get-tuple-element.59.refs_12_.wq_ref, ...), custom_call_target="tpu_custom_call" | custom-call | flops 805306368 | bytes 4194304 | tf_op jit(solution)/shard_map/far/pallas_call | solution.py:401
  50.4 0.5 collective-permute-done.14
  50.9 0.1 add_convert_fusion.1
  51.0 1.6 %collective-permute-start.15 = (bf16[256,512]{1,0:T(8,128)(2,1)S(1)}, bf16[256,512]{1,0:T(8,128)(2,1)S(1)}, u32[]{:S(2)}, u32[]{:S(2)}) collective-permute-start(bf16[256,512]{1,0:T(8,128)(2,1)S(1)} %add_convert_fusion.1), channel_id=1, source_target_pairs={{0,2},{1,3},{2,0},{3,1},{4,6},{5,7},{6,4},{7,5},{8,10},{9,11},{10,... | collective-permute-start | bytes 786440 | tf_op jit(solution)/shard_map/ppermute | solution.py:330
  52.6 0.0 collective-permute-start.16
  52.6 0.6 own.1
  53.2 0.9 %turn.1 = bf16[256,512]{1,0:T(8,128)(2,1)} custom-call(bf16[3,64,256]{2,1,0:T(8,128)(2,1)S(1)} %collective-permute-done.7.refs_0_, bf16[3,64,256]{2,1,0:T(8,128)(2,1)S(1)} %collective-permute-done.8.refs_1_, bf16[3,64,256]{2,1,0:T(8,128)(2,1)S(1)} %collective-permute-done.9.refs_2_, bf16[3,64,256]{2,1,0:T(8,128)(2,1)S(1)} %collective-permute-done.10.refs_3_, ...), custom_call_target="tpu_custom_call" | custom-call | flops 805306368 | bytes 4194304 | tf_op jit(solution)/shard_map/turn/pallas_call | solution.py:413
  54.1 5.4 %collective-permute-done.15 = bf16[256,512]{1,0:T(8,128)(2,1)S(1)} collective-permute-done((bf16[256,512]{1,0:T(8,128)(2,1)S(1)}, bf16[256,512]{1,0:T(8,128)(2,1)S(1)}, u32[]{:S(2)}, u32[]{:S(2)}) %collective-permute-start.15) | collective-permute-done | bytes 262176 | tf_op jit(solution)/shard_map/ppermute | solution.py:330
  59.4 0.0 collective-permute-done.16
  59.4 0.8 %add_convert_fusion = bf16[256,512]{1,0:T(8,128)(2,1)} fusion(f32[256,512]{1,0:T(8,128)S(1)} %own.1, bf16[256,512]{1,0:T(8,128)(2,1)S(1)} %collective-permute-done.16, bf16[256,512]{1,0:T(8,128)(2,1)S(1)} %collective-permute-done.15), kind=kLoop, calls=%fused_computation | loop fusion | flops 655360 | bytes 1310720 | tf_op jit(solution)/shard_map/convert_element_type | solution.py:431
Async XLA Ops:
  2.1 11.6 %collective-permute-start = (bf16[3,64,256]{2,1,0:T(8,128)(2,1)S(1)}, bf16[3,64,256]{2,1,0:T(8,128)(2,1)S(1)}, u32[]{:S(2)}, u32[]{:S(2)}) collective-permute-start(bf16[3,64,256]{2,1,0:T(8,128)(2,1)S(1)} %get-tuple-element.39), channel_id=1, source_target_pairs={{0,20},{4,16},{8,28},{12,24},{16,4},{20,0},{24,12},{28,8},{1,21},{... | collective-permute-start | bytes 294920 | tf_op jit(solution)/shard_map/ppermute | solution.py:330
  7.2 8.8 %collective-permute-start.1 = (bf16[3,64,256]{2,1,0:T(8,128)(2,1)S(1)}, bf16[3,64,256]{2,1,0:T(8,128)(2,1)S(1)}, u32[]{:S(2)}, u32[]{:S(2)}) collective-permute-start(bf16[3,64,256]{2,1,0:T(8,128)(2,1)S(1)} %get-tuple-element.40), channel_id=1, source_target_pairs={{0,4},{4,0},{8,12},{12,8},{16,20},{20,16},{24,28},{28,24},{1,5},{5... | collective-permute-start | bytes 294920 | tf_op jit(solution)/shard_map/ppermute | solution.py:330
  7.7 12.7 %collective-permute-start.2 = (bf16[3,64,256]{2,1,0:T(8,128)(2,1)S(1)}, bf16[3,64,256]{2,1,0:T(8,128)(2,1)S(1)}, u32[]{:S(2)}, u32[]{:S(2)}) collective-permute-start(bf16[3,64,256]{2,1,0:T(8,128)(2,1)S(1)} %get-tuple-element.41), channel_id=1, source_target_pairs={{0,28},{4,24},{8,20},{12,16},{16,12},{20,8},{24,4},{28,0},{1,29},{... | collective-permute-start | bytes 294920 | tf_op jit(solution)/shard_map/ppermute | solution.py:330
  10.0 10.4 %collective-permute-start.3 = (bf16[3,64,256]{2,1,0:T(8,128)(2,1)S(1)}, bf16[3,64,256]{2,1,0:T(8,128)(2,1)S(1)}, u32[]{:S(2)}, u32[]{:S(2)}) collective-permute-start(bf16[3,64,256]{2,1,0:T(8,128)(2,1)S(1)} %get-tuple-element.42), channel_id=1, source_target_pairs={{0,8},{4,12},{8,0},{12,4},{16,24},{20,28},{24,16},{28,20},{1,9},{5... | collective-permute-start | bytes 294920 | tf_op jit(solution)/shard_map/ppermute | solution.py:330
  10.0 10.4 %collective-permute-start.4 = (bf16[3,64,256]{2,1,0:T(8,128)(2,1)S(1)}, bf16[3,64,256]{2,1,0:T(8,128)(2,1)S(1)}, u32[]{:S(2)}, u32[]{:S(2)}) collective-permute-start(bf16[3,64,256]{2,1,0:T(8,128)(2,1)S(1)} %get-tuple-element.43), channel_id=1, source_target_pairs={{0,24},{4,28},{8,16},{12,20},{16,8},{20,12},{24,0},{28,4},{1,25},{... | collective-permute-start | bytes 294920 | tf_op jit(solution)/shard_map/ppermute | solution.py:330
  13.7 6.9 %collective-permute-start.5 = (bf16[3,64,256]{2,1,0:T(8,128)(2,1)S(1)}, bf16[3,64,256]{2,1,0:T(8,128)(2,1)S(1)}, u32[]{:S(2)}, u32[]{:S(2)}) collective-permute-start(bf16[3,64,256]{2,1,0:T(8,128)(2,1)S(1)} %get-tuple-element.44), channel_id=1, source_target_pairs={{0,12},{4,8},{8,4},{12,0},{16,28},{20,24},{24,20},{28,16},{1,13},{... | collective-permute-start | bytes 294920 | tf_op jit(solution)/shard_map/ppermute | solution.py:330
  16.0 9.1 %collective-permute-start.6 = (bf16[3,64,256]{2,1,0:T(8,128)(2,1)S(1)}, bf16[3,64,256]{2,1,0:T(8,128)(2,1)S(1)}, u32[]{:S(2)}, u32[]{:S(2)}) collective-permute-start(bf16[3,64,256]{2,1,0:T(8,128)(2,1)S(1)} %get-tuple-element.45), channel_id=1, source_target_pairs={{0,16},{4,20},{8,24},{12,28},{16,0},{20,4},{24,8},{28,12},{1,17},{... | collective-permute-start | bytes 294920 | tf_op jit(solution)/shard_map/ppermute | solution.py:330
  28.7 10.4 %collective-permute-start.7 = (bf16[3,64,256]{2,1,0:T(8,128)(2,1)S(1)}, bf16[3,64,256]{2,1,0:T(8,128)(2,1)S(1)}, u32[]{:S(2)}, u32[]{:S(2)}) collective-permute-start(bf16[3,64,256]{2,1,0:T(8,128)(2,1)S(1)} %get-tuple-element.47), channel_id=1, source_target_pairs={{0,20},{4,16},{8,28},{12,24},{16,4},{20,0},{24,12},{28,8},{1,21},{... | collective-permute-start | bytes 294920 | tf_op jit(solution)/shard_map/ppermute | solution.py:330
  29.5 9.5 %collective-permute-start.8 = (bf16[3,64,256]{2,1,0:T(8,128)(2,1)S(1)}, bf16[3,64,256]{2,1,0:T(8,128)(2,1)S(1)}, u32[]{:S(2)}, u32[]{:S(2)}) collective-permute-start(bf16[3,64,256]{2,1,0:T(8,128)(2,1)S(1)} %get-tuple-element.48), channel_id=1, source_target_pairs={{0,4},{4,0},{8,12},{12,8},{16,20},{20,16},{24,28},{28,24},{1,5},{5... | collective-permute-start | bytes 294920 | tf_op jit(solution)/shard_map/ppermute | solution.py:330
  31.1 10.6 %collective-permute-start.9 = (bf16[3,64,256]{2,1,0:T(8,128)(2,1)S(1)}, bf16[3,64,256]{2,1,0:T(8,128)(2,1)S(1)}, u32[]{:S(2)}, u32[]{:S(2)}) collective-permute-start(bf16[3,64,256]{2,1,0:T(8,128)(2,1)S(1)} %get-tuple-element.49), channel_id=1, source_target_pairs={{0,28},{4,24},{8,20},{12,16},{16,12},{20,8},{24,4},{28,0},{1,29},{... | collective-permute-start | bytes 294920 | tf_op jit(solution)/shard_map/ppermute | solution.py:330
  33.5 9.2 %collective-permute-start.10 = (bf16[3,64,256]{2,1,0:T(8,128)(2,1)S(1)}, bf16[3,64,256]{2,1,0:T(8,128)(2,1)S(1)}, u32[]{:S(2)}, u32[]{:S(2)}) collective-permute-start(bf16[3,64,256]{2,1,0:T(8,128)(2,1)S(1)} %get-tuple-element.50), channel_id=1, source_target_pairs={{0,8},{4,12},{8,0},{12,4},{16,24},{20,28},{24,16},{28,20},{1,9},{5... | collective-permute-start | bytes 294920 | tf_op jit(solution)/shard_map/ppermute | solution.py:330
  34.0 8.7 %collective-permute-start.11 = (bf16[3,64,256]{2,1,0:T(8,128)(2,1)S(1)}, bf16[3,64,256]{2,1,0:T(8,128)(2,1)S(1)}, u32[]{:S(2)}, u32[]{:S(2)}) collective-permute-start(bf16[3,64,256]{2,1,0:T(8,128)(2,1)S(1)} %get-tuple-element.51), channel_id=1, source_target_pairs={{0,24},{4,28},{8,16},{12,20},{16,8},{20,12},{24,0},{28,4},{1,25},{... | collective-permute-start | bytes 294920 | tf_op jit(solution)/shard_map/ppermute | solution.py:330
  39.1 5.8 %collective-permute-start.12 = (bf16[3,64,256]{2,1,0:T(8,128)(2,1)S(1)}, bf16[3,64,256]{2,1,0:T(8,128)(2,1)S(1)}, u32[]{:S(2)}, u32[]{:S(2)}) collective-permute-start(bf16[3,64,256]{2,1,0:T(8,128)(2,1)S(1)} %get-tuple-element.52), channel_id=1, source_target_pairs={{0,12},{4,8},{8,4},{12,0},{16,28},{20,24},{24,20},{28,16},{1,13},{... | collective-permute-start | bytes 294920 | tf_op jit(solution)/shard_map/ppermute | solution.py:330
  39.1 9.6 %collective-permute-start.13 = (bf16[3,64,256]{2,1,0:T(8,128)(2,1)S(1)}, bf16[3,64,256]{2,1,0:T(8,128)(2,1)S(1)}, u32[]{:S(2)}, u32[]{:S(2)}) collective-permute-start(bf16[3,64,256]{2,1,0:T(8,128)(2,1)S(1)} %get-tuple-element.53), channel_id=1, source_target_pairs={{0,16},{4,20},{8,24},{12,28},{16,0},{20,4},{24,8},{28,12},{1,17},{... | collective-permute-start | bytes 294920 | tf_op jit(solution)/shard_map/ppermute | solution.py:330
  49.3 1.6 %collective-permute-start.14 = (bf16[256,512]{1,0:T(8,128)(2,1)S(1)}, bf16[256,512]{1,0:T(8,128)(2,1)S(1)}, u32[]{:S(2)}, u32[]{:S(2)}) collective-permute-start(bf16[256,512]{1,0:T(8,128)(2,1)S(1)} %get-tuple-element.63), channel_id=1, source_target_pairs={{0,1},{1,0},{2,3},{3,2},{4,5},{5,4},{6,7},{7,6},{8,9},{9,8},{10,11... | collective-permute-start | bytes 786440 | tf_op jit(solution)/shard_map/ppermute | solution.py:330
  51.0 8.4 %collective-permute-start.15 = (bf16[256,512]{1,0:T(8,128)(2,1)S(1)}, bf16[256,512]{1,0:T(8,128)(2,1)S(1)}, u32[]{:S(2)}, u32[]{:S(2)}) collective-permute-start(bf16[256,512]{1,0:T(8,128)(2,1)S(1)} %add_convert_fusion.1), channel_id=1, source_target_pairs={{0,2},{1,3},{2,0},{3,1},{4,6},{5,7},{6,4},{7,5},{8,10},{9,11},{10,... | collective-permute-start | bytes 786440 | tf_op jit(solution)/shard_map/ppermute | solution.py:330
  52.6 6.9 %collective-permute-start.16 = (bf16[256,512]{1,0:T(8,128)(2,1)S(1)}, bf16[256,512]{1,0:T(8,128)(2,1)S(1)}, u32[]{:S(2)}, u32[]{:S(2)}) collective-permute-start(bf16[256,512]{1,0:T(8,128)(2,1)S(1)} %get-tuple-element.66), channel_id=1, source_target_pairs={{0,1},{1,0},{2,3},{3,2},{4,5},{5,4},{6,7},{7,6},{8,9},{9,8},{10,11... | collective-permute-start | bytes 786440 | tf_op jit(solution)/shard_map/ppermute | solution.py:330

commit v17 on v16

--- a/solution.py
+++ b/solution.py
@@ -96,9 +96,8 @@
 
 def by_distance(pieces):
     blocks, last = len(pieces), len(pieces) - 1
-    far, near = list(range(last, blocks // 2 - 1, -1)), list(range(1, blocks // 2))
-    far.insert(0, far.pop(len(far) // 2))
-    order = [far[i // 2] if i % 2 == 0 else near[i // 2] for i in range(last)]
+    middle = [*range(last, 3 * blocks // 4 - 1, -1), *range(blocks // 2, 3 * blocks // 4)]
+    order = [middle[i // 2] if i % 2 == 0 else 1 + i // 2 for i in range(last)]
     return zip([*order, 0], pieces)
 
 

time: 60.4 us -> 59 us (0.977)
  waiting for transfers between devices: 20.3 us -> 19 us
    ppermute x17, waiting for transfers between devices: 20.3 us -> 19 us  [exchange(): return lax.ppermute(block, axis, pairs)]
  transfers between devices with their start and end apart: 17 -> 17, of which waited for: 9 -> 8; matrix products, arithmetic and copies ran while one was open for 0% -> 0% of each run, Pallas kernels for 4% -> 4%
where the time goes in v17:
time: 59 us; the launch traced here: 58.8 us
  starting transfers between devices  30 us (51%)
  waiting for transfers between devices  19 us (32%)
  Pallas kernels  8.26 us (14%)
  other arithmetic  0.87 us (1%)
  between operations  0.7 us (1%)
    ppermute x17, starting transfers between devices, exchange(): return lax.ppermute(block, axis, pairs)  30 us
    ppermute x17, waiting for transfers between devices, exchange(): return lax.ppermute(block, axis, pairs)  19 us
    pallas_call x1, Pallas kernels, per_device(): pl.pallas_call(conv_kernel, in_specs=[VMEM] * blocks + [HBM] * 10, out_sh...  3.61 us
    pallas_call x1, Pallas kernels, per_device(): pl.pallas_call(gate_kernel, in_specs=[HBM] * 5, out_shape=arrays(blocks,...  1.5 us
  transfers between devices with their start and end apart: 17, of which 8 were waited for; matrix products, arithmetic and copies ran while one was open for 0% of the time, Pallas kernels for 4%

profile of v17, /device:TPU:0, one launch (start us, length us, event | category | flops | bytes accessed | tf_op | source)
XLA Modules:
  0.0 58.8 jit_solution(889773683269590882)
XLA Ops:
  0.6 1.5 %gate.1 = (bf16[3,64,256]{2,1,0:T(8,128)(2,1)S(1)}, bf16[3,64,256]{2,1,0:T(8,128)(2,1)S(1)}, bf16[3,64,256]{2,1,0:T(8,128)(2,1)S(1)}, bf16[3,64,256]{2,1,0:T(8,1...) custom-call(bf16[256,512]{1,0:T(8,128)(2,1)} %refs_0_.1, ...), custom_call_target="tpu_custom_call" | custom-call | tf_op jit(solution)/shard_map/gate/pallas_call | solution.py:354
  2.1 6.1 %collective-permute-start = (bf16[3,64,256]{2,1,0:T(8,128)(2,1)S(1)}, bf16[3,64,256]{2,1,0:T(8,128)(2,1)S(1)}, u32[]{:S(2)}, u32[]{:S(2)}) collective-permute-start(bf16[3,64,256]{2,1,0:T(8,128)(2,1)S(1)} %get-tuple-element.39), channel_id=1, source_target_pairs={{0,28},{4,24},{8,20},{12,16},{16,12},{20,8},{24,4},{28,0},{1,29},{... | collective-permute-start | bytes 294920 | tf_op jit(solution)/shard_map/ppermute | solution.py:329
  8.2 0.5 collective-permute-start.1
  8.7 0.1 collective-permute-start.2
  8.9 0.0 collective-permute-start.3
  8.9 4.2 %collective-permute-start.4 = (bf16[3,64,256]{2,1,0:T(8,128)(2,1)S(1)}, bf16[3,64,256]{2,1,0:T(8,128)(2,1)S(1)}, u32[]{:S(2)}, u32[]{:S(2)}) collective-permute-start(bf16[3,64,256]{2,1,0:T(8,128)(2,1)S(1)} %get-tuple-element.43), channel_id=1, source_target_pairs={{0,16},{4,20},{8,24},{12,28},{16,0},{20,4},{24,8},{28,12},{1,17},{... | collective-permute-start | bytes 294920 | tf_op jit(solution)/shard_map/ppermute | solution.py:329
  13.1 0.0 collective-permute-done.refs_0_
  13.1 2.6 %collective-permute-start.5 = (bf16[3,64,256]{2,1,0:T(8,128)(2,1)S(1)}, bf16[3,64,256]{2,1,0:T(8,128)(2,1)S(1)}, u32[]{:S(2)}, u32[]{:S(2)}) collective-permute-start(bf16[3,64,256]{2,1,0:T(8,128)(2,1)S(1)} %get-tuple-element.44), channel_id=1, source_target_pairs={{0,12},{4,8},{8,4},{12,0},{16,28},{20,24},{24,20},{28,16},{1,13},{... | collective-permute-start | bytes 294920 | tf_op jit(solution)/shard_map/ppermute | solution.py:329
  15.7 0.0 collective-permute-done.1.refs_1_
  15.7 2.6 %collective-permute-start.6 = (bf16[3,64,256]{2,1,0:T(8,128)(2,1)S(1)}, bf16[3,64,256]{2,1,0:T(8,128)(2,1)S(1)}, u32[]{:S(2)}, u32[]{:S(2)}) collective-permute-start(bf16[3,64,256]{2,1,0:T(8,128)(2,1)S(1)} %get-tuple-element.45), channel_id=1, source_target_pairs={{0,20},{4,16},{8,28},{12,24},{16,4},{20,0},{24,12},{28,8},{1,21},{... | collective-permute-start | bytes 294920 | tf_op jit(solution)/shard_map/ppermute | solution.py:329
  18.3 0.0 collective-permute-done.2.refs_2_
  18.3 0.0 collective-permute-done.3.refs_3_
  18.3 5.4 %collective-permute-done.4.refs_4_ = bf16[3,64,256]{2,1,0:T(8,128)(2,1)S(1)} collective-permute-done((bf16[3,64,256]{2,1,0:T(8,128)(2,1)S(1)}, bf16[3,64,256]{2,1,0:T(8,128)(2,1)S(1)}, u32[]{:S(2)}, u32[]{:S(2)}) %collective-permute-start.4) | collective-permute-done | bytes 98336 | tf_op jit(solution)/shard_map/ppermute | solution.py:329
  23.7 0.0 collective-permute-done.5.refs_5_
  23.7 1.1 %collective-permute-done.6.refs_6_ = bf16[3,64,256]{2,1,0:T(8,128)(2,1)S(1)} collective-permute-done((bf16[3,64,256]{2,1,0:T(8,128)(2,1)S(1)}, bf16[3,64,256]{2,1,0:T(8,128)(2,1)S(1)}, u32[]{:S(2)}, u32[]{:S(2)}) %collective-permute-start.6) | collective-permute-done | bytes 98336 | tf_op jit(solution)/shard_map/ppermute | solution.py:329
  24.8 3.6 %conv.1 = (bf16[3,64,256]{2,1,0:T(8,128)(2,1)S(1)}, bf16[3,64,256]{2,1,0:T(8,128)(2,1)S(1)}, bf16[3,64,256]{2,1,0:T(8,128)(2,1)S(1)}, bf16[3,64,256]{2,1,0:T(8,1...) custom-call(bf16[3,64,256]{2,1,0:T(8,128)(2,1)S(1)} %collective-perm, ...), custom_call_target="tpu_custom_call" | custom-call | tf_op jit(solution)/shard_map/conv/pallas_call | solution.py:373
  28.5 3.5 %collective-permute-start.7 = (bf16[3,64,256]{2,1,0:T(8,128)(2,1)S(1)}, bf16[3,64,256]{2,1,0:T(8,128)(2,1)S(1)}, u32[]{:S(2)}, u32[]{:S(2)}) collective-permute-start(bf16[3,64,256]{2,1,0:T(8,128)(2,1)S(1)} %get-tuple-element.47), channel_id=1, source_target_pairs={{0,28},{4,24},{8,20},{12,16},{16,12},{20,8},{24,4},{28,0},{1,29},{... | collective-permute-start | bytes 294920 | tf_op jit(solution)/shard_map/ppermute | solution.py:329
  32.0 0.5 collective-permute-start.8
  32.5 1.3 %collective-permute-start.9 = (bf16[3,64,256]{2,1,0:T(8,128)(2,1)S(1)}, bf16[3,64,256]{2,1,0:T(8,128)(2,1)S(1)}, u32[]{:S(2)}, u32[]{:S(2)}) collective-permute-start(bf16[3,64,256]{2,1,0:T(8,128)(2,1)S(1)} %get-tuple-element.49), channel_id=1, source_target_pairs={{0,24},{4,28},{8,16},{12,20},{16,8},{20,12},{24,0},{28,4},{1,25},{... | collective-permute-start | bytes 294920 | tf_op jit(solution)/shard_map/ppermute | solution.py:329
  33.8 0.0 collective-permute-start.10
  33.8 3.1 %collective-permute-start.11 = (bf16[3,64,256]{2,1,0:T(8,128)(2,1)S(1)}, bf16[3,64,256]{2,1,0:T(8,128)(2,1)S(1)}, u32[]{:S(2)}, u32[]{:S(2)}) collective-permute-start(bf16[3,64,256]{2,1,0:T(8,128)(2,1)S(1)} %get-tuple-element.51), channel_id=1, source_target_pairs={{0,16},{4,20},{8,24},{12,28},{16,0},{20,4},{24,8},{28,12},{1,17},{... | collective-permute-start | bytes 294920 | tf_op jit(solution)/shard_map/ppermute | solution.py:329
  36.9 0.0 collective-permute-done.7.refs_0_
  36.9 0.9 %collective-permute-start.12 = (bf16[3,64,256]{2,1,0:T(8,128)(2,1)S(1)}, bf16[3,64,256]{2,1,0:T(8,128)(2,1)S(1)}, u32[]{:S(2)}, u32[]{:S(2)}) collective-permute-start(bf16[3,64,256]{2,1,0:T(8,128)(2,1)S(1)} %get-tuple-element.52), channel_id=1, source_target_pairs={{0,12},{4,8},{8,4},{12,0},{16,28},{20,24},{24,20},{28,16},{1,13},{... | collective-permute-start | bytes 294920 | tf_op jit(solution)/shard_map/ppermute | solution.py:329
  37.9 0.0 collective-permute-done.8.refs_1_
  37.9 2.9 %collective-permute-start.13 = (bf16[3,64,256]{2,1,0:T(8,128)(2,1)S(1)}, bf16[3,64,256]{2,1,0:T(8,128)(2,1)S(1)}, u32[]{:S(2)}, u32[]{:S(2)}) collective-permute-start(bf16[3,64,256]{2,1,0:T(8,128)(2,1)S(1)} %get-tuple-element.53), channel_id=1, source_target_pairs={{0,20},{4,16},{8,28},{12,24},{16,4},{20,0},{24,12},{28,8},{1,21},{... | collective-permute-start | bytes 294920 | tf_op jit(solution)/shard_map/ppermute | solution.py:329
  40.7 0.0 collective-permute-done.9.refs_2_
  40.7 2.7 %collective-permute-done.10.refs_3_ = bf16[3,64,256]{2,1,0:T(8,128)(2,1)S(1)} collective-permute-done((bf16[3,64,256]{2,1,0:T(8,128)(2,1)S(1)}, bf16[3,64,256]{2,1,0:T(8,128)(2,1)S(1)}, u32[]{:S(2)}, u32[]{:S(2)}) %collective-permute-start.10) | collective-permute-done | bytes 98336 | tf_op jit(solution)/shard_map/ppermute | solution.py:329
  43.5 1.1 %collective-permute-done.11.refs_4_ = bf16[3,64,256]{2,1,0:T(8,128)(2,1)S(1)} collective-permute-done((bf16[3,64,256]{2,1,0:T(8,128)(2,1)S(1)}, bf16[3,64,256]{2,1,0:T(8,128)(2,1)S(1)}, u32[]{:S(2)}, u32[]{:S(2)}) %collective-permute-start.11) | collective-permute-done | bytes 98336 | tf_op jit(solution)/shard_map/ppermute | solution.py:329
  44.5 1.4 %collective-permute-done.12.refs_5_ = bf16[3,64,256]{2,1,0:T(8,128)(2,1)S(1)} collective-permute-done((bf16[3,64,256]{2,1,0:T(8,128)(2,1)S(1)}, bf16[3,64,256]{2,1,0:T(8,128)(2,1)S(1)}, u32[]{:S(2)}, u32[]{:S(2)}) %collective-permute-start.12) | collective-permute-done | bytes 98336 | tf_op jit(solution)/shard_map/ppermute | solution.py:329
  45.9 1.3 %collective-permute-done.13.refs_6_ = bf16[3,64,256]{2,1,0:T(8,128)(2,1)S(1)} collective-permute-done((bf16[3,64,256]{2,1,0:T(8,128)(2,1)S(1)}, bf16[3,64,256]{2,1,0:T(8,128)(2,1)S(1)}, u32[]{:S(2)}, u32[]{:S(2)}) %collective-permute-start.13) | collective-permute-done | bytes 98336 | tf_op jit(solution)/shard_map/ppermute | solution.py:329
  47.3 0.7 %mate.1 = (bf16[3,256,512]{2,1,0:T(8,128)(2,1)S(1)}, bf16[256,512]{1,0:T(8,128)(2,1)S(1)}) custom-call(bf16[3,64,256]{2,1,0:T(8,128)(2,1)S(1)} %collective-permute-done.7.refs_0_, bf16[3,64,256]{2,1,0:T(8,128)(2,1)S(1)} %collective-permute-done.8.refs_1_, bf16[3,64,256]{2,1,0:T(8,128)(2,1)S(1)} %collective-permute-done.9.refs_2_, ...), custom_call_target="tpu_custom_call" | custom-call | flops 805306368 | bytes 4194304 | tf_op jit(solution)/shard_map/mate/pallas_call | solution.py:390
  48.0 0.1 collective-permute-start.14
  48.0 1.0 %far.1 = (f32[256,512]{1,0:T(8,128)S(1)}, bf16[256,512]{1,0:T(8,128)(2,1)S(1)}) custom-call(bf16[3,256,512]{2,1,0:T(8,128)(2,1)S(1)} %get-tuple-element.67.lhs_ref, bf16[2048,512]{1,0:T(8,128)(2,1)S(1)} %get-tuple-element.58.refs_11_.wk_ref, bf16[2048,512]{1,0:T(8,128)(2,1)S(1)} %get-tuple-element.59.refs_12_.wq_ref, ...), custom_call_target="tpu_custom_call" | custom-call | flops 805306368 | bytes 4194304 | tf_op jit(solution)/shard_map/far/pallas_call | solution.py:400
  49.1 0.5 collective-permute-done.14
  49.6 0.1 add_convert_fusion.1
  49.6 1.6 %collective-permute-start.15 = (bf16[256,512]{1,0:T(8,128)(2,1)S(1)}, bf16[256,512]{1,0:T(8,128)(2,1)S(1)}, u32[]{:S(2)}, u32[]{:S(2)}) collective-permute-start(bf16[256,512]{1,0:T(8,128)(2,1)S(1)} %add_convert_fusion.1), channel_id=1, source_target_pairs={{0,2},{1,3},{2,0},{3,1},{4,6},{5,7},{6,4},{7,5},{8,10},{9,11},{10,... | collective-permute-start | bytes 786440 | tf_op jit(solution)/shard_map/ppermute | solution.py:329
  51.2 0.0 collective-permute-start.16
  51.2 0.6 %own.1 = f32[256,512]{1,0:T(8,128)S(1)} custom-call(bf16[3,256,512]{2,1,0:T(8,128)(2,1)S(1)} %get-tuple-element.67.lhs_ref, bf16[2048,512]{1,0:T(8,128)(2,1)S(1)} %get-tuple-element.58.refs_11_.wk_ref, bf16[2048,512]{1,0:T(8,128)(2,1)S(1)} %get-tuple-element.59.refs_12_.wq_ref, bf16[2048,512]{1,0:T(8,128)(2,1)S(1)} %get-tuple-element.60.refs_13_.wv_ref), custom_call_target="tpu_custom_call" | custom-call | flops 805306368 | bytes 4194304 | tf_op jit(solution)/shard_map/own/pallas_call | solution.py:421
  51.8 0.9 %turn.1 = bf16[256,512]{1,0:T(8,128)(2,1)} custom-call(bf16[3,64,256]{2,1,0:T(8,128)(2,1)S(1)} %collective-permute-done.7.refs_0_, bf16[3,64,256]{2,1,0:T(8,128)(2,1)S(1)} %collective-permute-done.8.refs_1_, bf16[3,64,256]{2,1,0:T(8,128)(2,1)S(1)} %collective-permute-done.9.refs_2_, bf16[3,64,256]{2,1,0:T(8,128)(2,1)S(1)} %collective-permute-done.10.refs_3_, ...), custom_call_target="tpu_custom_call" | custom-call | flops 805306368 | bytes 4194304 | tf_op jit(solution)/shard_map/turn/pallas_call | solution.py:412
  52.7 5.4 %collective-permute-done.15 = bf16[256,512]{1,0:T(8,128)(2,1)S(1)} collective-permute-done((bf16[256,512]{1,0:T(8,128)(2,1)S(1)}, bf16[256,512]{1,0:T(8,128)(2,1)S(1)}, u32[]{:S(2)}, u32[]{:S(2)}) %collective-permute-start.15) | collective-permute-done | bytes 262176 | tf_op jit(solution)/shard_map/ppermute | solution.py:329
  58.0 0.0 collective-permute-done.16
  58.0 0.8 %add_convert_fusion = bf16[256,512]{1,0:T(8,128)(2,1)} fusion(f32[256,512]{1,0:T(8,128)S(1)} %own.1, bf16[256,512]{1,0:T(8,128)(2,1)S(1)} %collective-permute-done.16, bf16[256,512]{1,0:T(8,128)(2,1)S(1)} %collective-permute-done.15), kind=kLoop, calls=%fused_computation | loop fusion | flops 655360 | bytes 1310720 | tf_op jit(solution)/shard_map/convert_element_type | solution.py:430
Async XLA Ops:
  2.1 11.0 %collective-permute-start = (bf16[3,64,256]{2,1,0:T(8,128)(2,1)S(1)}, bf16[3,64,256]{2,1,0:T(8,128)(2,1)S(1)}, u32[]{:S(2)}, u32[]{:S(2)}) collective-permute-start(bf16[3,64,256]{2,1,0:T(8,128)(2,1)S(1)} %get-tuple-element.39), channel_id=1, source_target_pairs={{0,28},{4,24},{8,20},{12,16},{16,12},{20,8},{24,4},{28,0},{1,29},{... | collective-permute-start | bytes 294920 | tf_op jit(solution)/shard_map/ppermute | solution.py:329
  8.2 7.5 %collective-permute-start.1 = (bf16[3,64,256]{2,1,0:T(8,128)(2,1)S(1)}, bf16[3,64,256]{2,1,0:T(8,128)(2,1)S(1)}, u32[]{:S(2)}, u32[]{:S(2)}) collective-permute-start(bf16[3,64,256]{2,1,0:T(8,128)(2,1)S(1)} %get-tuple-element.40), channel_id=1, source_target_pairs={{0,4},{4,0},{8,12},{12,8},{16,20},{20,16},{24,28},{28,24},{1,5},{5... | collective-permute-start | bytes 294920 | tf_op jit(solution)/shard_map/ppermute | solution.py:329
  8.7 9.6 %collective-permute-start.2 = (bf16[3,64,256]{2,1,0:T(8,128)(2,1)S(1)}, bf16[3,64,256]{2,1,0:T(8,128)(2,1)S(1)}, u32[]{:S(2)}, u32[]{:S(2)}) collective-permute-start(bf16[3,64,256]{2,1,0:T(8,128)(2,1)S(1)} %get-tuple-element.41), channel_id=1, source_target_pairs={{0,24},{4,28},{8,16},{12,20},{16,8},{20,12},{24,0},{28,4},{1,25},{... | collective-permute-start | bytes 294920 | tf_op jit(solution)/shard_map/ppermute | solution.py:329
  8.9 9.5 %collective-permute-start.3 = (bf16[3,64,256]{2,1,0:T(8,128)(2,1)S(1)}, bf16[3,64,256]{2,1,0:T(8,128)(2,1)S(1)}, u32[]{:S(2)}, u32[]{:S(2)}) collective-permute-start(bf16[3,64,256]{2,1,0:T(8,128)(2,1)S(1)} %get-tuple-element.42), channel_id=1, source_target_pairs={{0,8},{4,12},{8,0},{12,4},{16,24},{20,28},{24,16},{28,20},{1,9},{5... | collective-permute-start | bytes 294920 | tf_op jit(solution)/shard_map/ppermute | solution.py:329
  8.9 14.8 %collective-permute-start.4 = (bf16[3,64,256]{2,1,0:T(8,128)(2,1)S(1)}, bf16[3,64,256]{2,1,0:T(8,128)(2,1)S(1)}, u32[]{:S(2)}, u32[]{:S(2)}) collective-permute-start(bf16[3,64,256]{2,1,0:T(8,128)(2,1)S(1)} %get-tuple-element.43), channel_id=1, source_target_pairs={{0,16},{4,20},{8,24},{12,28},{16,0},{20,4},{24,8},{28,12},{1,17},{... | collective-permute-start | bytes 294920 | tf_op jit(solution)/shard_map/ppermute | solution.py:329
  13.1 10.6 %collective-permute-start.5 = (bf16[3,64,256]{2,1,0:T(8,128)(2,1)S(1)}, bf16[3,64,256]{2,1,0:T(8,128)(2,1)S(1)}, u32[]{:S(2)}, u32[]{:S(2)}) collective-permute-start(bf16[3,64,256]{2,1,0:T(8,128)(2,1)S(1)} %get-tuple-element.44), channel_id=1, source_target_pairs={{0,12},{4,8},{8,4},{12,0},{16,28},{20,24},{24,20},{28,16},{1,13},{... | collective-permute-start | bytes 294920 | tf_op jit(solution)/shard_map/ppermute | solution.py:329
  15.7 9.1 %collective-permute-start.6 = (bf16[3,64,256]{2,1,0:T(8,128)(2,1)S(1)}, bf16[3,64,256]{2,1,0:T(8,128)(2,1)S(1)}, u32[]{:S(2)}, u32[]{:S(2)}) collective-permute-start(bf16[3,64,256]{2,1,0:T(8,128)(2,1)S(1)} %get-tuple-element.45), channel_id=1, source_target_pairs={{0,20},{4,16},{8,28},{12,24},{16,4},{20,0},{24,12},{28,8},{1,21},{... | collective-permute-start | bytes 294920 | tf_op jit(solution)/shard_map/ppermute | solution.py:329
  28.5 8.5 %collective-permute-start.7 = (bf16[3,64,256]{2,1,0:T(8,128)(2,1)S(1)}, bf16[3,64,256]{2,1,0:T(8,128)(2,1)S(1)}, u32[]{:S(2)}, u32[]{:S(2)}) collective-permute-start(bf16[3,64,256]{2,1,0:T(8,128)(2,1)S(1)} %get-tuple-element.47), channel_id=1, source_target_pairs={{0,28},{4,24},{8,20},{12,16},{16,12},{20,8},{24,4},{28,0},{1,29},{... | collective-permute-start | bytes 294920 | tf_op jit(solution)/shard_map/ppermute | solution.py:329
  32.0 5.9 %collective-permute-start.8 = (bf16[3,64,256]{2,1,0:T(8,128)(2,1)S(1)}, bf16[3,64,256]{2,1,0:T(8,128)(2,1)S(1)}, u32[]{:S(2)}, u32[]{:S(2)}) collective-permute-start(bf16[3,64,256]{2,1,0:T(8,128)(2,1)S(1)} %get-tuple-element.48), channel_id=1, source_target_pairs={{0,4},{4,0},{8,12},{12,8},{16,20},{20,16},{24,28},{28,24},{1,5},{5... | collective-permute-start | bytes 294920 | tf_op jit(solution)/shard_map/ppermute | solution.py:329
  32.5 8.2 %collective-permute-start.9 = (bf16[3,64,256]{2,1,0:T(8,128)(2,1)S(1)}, bf16[3,64,256]{2,1,0:T(8,128)(2,1)S(1)}, u32[]{:S(2)}, u32[]{:S(2)}) collective-permute-start(bf16[3,64,256]{2,1,0:T(8,128)(2,1)S(1)} %get-tuple-element.49), channel_id=1, source_target_pairs={{0,24},{4,28},{8,16},{12,20},{16,8},{20,12},{24,0},{28,4},{1,25},{... | collective-permute-start | bytes 294920 | tf_op jit(solution)/shard_map/ppermute | solution.py:329
  33.8 9.7 %collective-permute-start.10 = (bf16[3,64,256]{2,1,0:T(8,128)(2,1)S(1)}, bf16[3,64,256]{2,1,0:T(8,128)(2,1)S(1)}, u32[]{:S(2)}, u32[]{:S(2)}) collective-permute-start(bf16[3,64,256]{2,1,0:T(8,128)(2,1)S(1)} %get-tuple-element.50), channel_id=1, source_target_pairs={{0,8},{4,12},{8,0},{12,4},{16,24},{20,28},{24,16},{28,20},{1,9},{5... | collective-permute-start | bytes 294920 | tf_op jit(solution)/shard_map/ppermute | solution.py:329
  33.8 10.7 %collective-permute-start.11 = (bf16[3,64,256]{2,1,0:T(8,128)(2,1)S(1)}, bf16[3,64,256]{2,1,0:T(8,128)(2,1)S(1)}, u32[]{:S(2)}, u32[]{:S(2)}) collective-permute-start(bf16[3,64,256]{2,1,0:T(8,128)(2,1)S(1)} %get-tuple-element.51), channel_id=1, source_target_pairs={{0,16},{4,20},{8,24},{12,28},{16,0},{20,4},{24,8},{28,12},{1,17},{... | collective-permute-start | bytes 294920 | tf_op jit(solution)/shard_map/ppermute | solution.py:329
  36.9 9.0 %collective-permute-start.12 = (bf16[3,64,256]{2,1,0:T(8,128)(2,1)S(1)}, bf16[3,64,256]{2,1,0:T(8,128)(2,1)S(1)}, u32[]{:S(2)}, u32[]{:S(2)}) collective-permute-start(bf16[3,64,256]{2,1,0:T(8,128)(2,1)S(1)} %get-tuple-element.52), channel_id=1, source_target_pairs={{0,12},{4,8},{8,4},{12,0},{16,28},{20,24},{24,20},{28,16},{1,13},{... | collective-permute-start | bytes 294920 | tf_op jit(solution)/shard_map/ppermute | solution.py:329
  37.9 9.4 %collective-permute-start.13 = (bf16[3,64,256]{2,1,0:T(8,128)(2,1)S(1)}, bf16[3,64,256]{2,1,0:T(8,128)(2,1)S(1)}, u32[]{:S(2)}, u32[]{:S(2)}) collective-permute-start(bf16[3,64,256]{2,1,0:T(8,128)(2,1)S(1)} %get-tuple-element.53), channel_id=1, source_target_pairs={{0,20},{4,16},{8,28},{12,24},{16,4},{20,0},{24,12},{28,8},{1,21},{... | collective-permute-start | bytes 294920 | tf_op jit(solution)/shard_map/ppermute | solution.py:329
  48.0 1.6 %collective-permute-start.14 = (bf16[256,512]{1,0:T(8,128)(2,1)S(1)}, bf16[256,512]{1,0:T(8,128)(2,1)S(1)}, u32[]{:S(2)}, u32[]{:S(2)}) collective-permute-start(bf16[256,512]{1,0:T(8,128)(2,1)S(1)} %get-tuple-element.63), channel_id=1, source_target_pairs={{0,1},{1,0},{2,3},{3,2},{4,5},{5,4},{6,7},{7,6},{8,9},{9,8},{10,11... | collective-permute-start | bytes 786440 | tf_op jit(solution)/shard_map/ppermute | solution.py:329
  49.6 8.4 %collective-permute-start.15 = (bf16[256,512]{1,0:T(8,128)(2,1)S(1)}, bf16[256,512]{1,0:T(8,128)(2,1)S(1)}, u32[]{:S(2)}, u32[]{:S(2)}) collective-permute-start(bf16[256,512]{1,0:T(8,128)(2,1)S(1)} %add_convert_fusion.1), channel_id=1, source_target_pairs={{0,2},{1,3},{2,0},{3,1},{4,6},{5,7},{6,4},{7,5},{8,10},{9,11},{10,... | collective-permute-start | bytes 786440 | tf_op jit(solution)/shard_map/ppermute | solution.py:329
  51.2 6.9 %collective-permute-start.16 = (bf16[256,512]{1,0:T(8,128)(2,1)S(1)}, bf16[256,512]{1,0:T(8,128)(2,1)S(1)}, u32[]{:S(2)}, u32[]{:S(2)}) collective-permute-start(bf16[256,512]{1,0:T(8,128)(2,1)S(1)} %get-tuple-element.66), channel_id=1, source_target_pairs={{0,1},{1,0},{2,3},{3,2},{4,5},{5,4},{6,7},{7,6},{8,9},{9,8},{10,11... | collective-permute-start | bytes 786440 | tf_op jit(solution)/shard_map/ppermute | solution.py:329

commit v18 on v14

--- a/solution.py
+++ b/solution.py
@@ -262,9 +262,9 @@
 
     stages = (analyse, forward, combine, inverse, synthesise)
     for step in range(groups + len(stages) - 1):
-        for depth, stage in reversed(list(enumerate(stages))):
+        for depth in (3, 1, 4, 2, 0):
             if 0 <= step - depth < groups:
-                stage(step - depth)
+                stages[depth](step - depth)
     for distance, out_ref in by_distance(out_refs):
         out_ref[...] = in_ref[me ^ distance]
     for copy in held_copies:

time: 58.3 us -> 58.3 us (level)
  no operation moved by 1% of the time
where the time goes in v18:
time: 58.3 us; the launch traced here: 58.1 us
  starting transfers between devices  28 us (48%)
  waiting for transfers between devices  20.3 us (35%)
  Pallas kernels  8.26 us (14%)
  other arithmetic  0.87 us (1%)
  between operations  0.7 us (1%)
    ppermute x17, starting transfers between devices, exchange(): return lax.ppermute(block, axis, pairs)  28 us
    ppermute x17, waiting for transfers between devices, exchange(): return lax.ppermute(block, axis, pairs)  20.3 us
    pallas_call x1, Pallas kernels, per_device(): pl.pallas_call(conv_kernel, in_specs=[VMEM] * blocks + [HBM] * 10, out_sh...  3.61 us
    pallas_call x1, Pallas kernels, per_device(): pl.pallas_call(gate_kernel, in_specs=[HBM] * 5, out_shape=arrays(blocks,...  1.5 us
  transfers between devices with their start and end apart: 17, of which 8 were waited for; matrix products, arithmetic and copies ran while one was open for 0% of the time, Pallas kernels for 4%

profile of v18, /device:TPU:0, one launch (start us, length us, event | category | flops | bytes accessed | tf_op | source)
XLA Modules:
  0.0 58.1 jit_solution(9113295216786637683)
XLA Ops:
  0.6 1.5 %gate.1 = (bf16[3,64,256]{2,1,0:T(8,128)(2,1)S(1)}, bf16[3,64,256]{2,1,0:T(8,128)(2,1)S(1)}, bf16[3,64,256]{2,1,0:T(8,128)(2,1)S(1)}, bf16[3,64,256]{2,1,0:T(8,1...) custom-call(bf16[256,512]{1,0:T(8,128)(2,1)} %refs_0_.1, ...), custom_call_target="tpu_custom_call" | custom-call | tf_op jit(solution)/shard_map/gate/pallas_call | solution.py:353
  2.1 6.1 %collective-permute-start = (bf16[3,64,256]{2,1,0:T(8,128)(2,1)S(1)}, bf16[3,64,256]{2,1,0:T(8,128)(2,1)S(1)}, u32[]{:S(2)}, u32[]{:S(2)}) collective-permute-start(bf16[3,64,256]{2,1,0:T(8,128)(2,1)S(1)} %get-tuple-element.39), channel_id=1, source_target_pairs={{0,28},{4,24},{8,20},{12,16},{16,12},{20,8},{24,4},{28,0},{1,29},{... | collective-permute-start | bytes 294920 | tf_op jit(solution)/shard_map/ppermute | solution.py:328
  8.2 0.5 collective-permute-start.1
  8.7 0.1 collective-permute-start.2
  8.9 0.0 collective-permute-start.3
  8.9 5.2 %collective-permute-start.4 = (bf16[3,64,256]{2,1,0:T(8,128)(2,1)S(1)}, bf16[3,64,256]{2,1,0:T(8,128)(2,1)S(1)}, u32[]{:S(2)}, u32[]{:S(2)}) collective-permute-start(bf16[3,64,256]{2,1,0:T(8,128)(2,1)S(1)} %get-tuple-element.43), channel_id=1, source_target_pairs={{0,20},{4,16},{8,28},{12,24},{16,4},{20,0},{24,12},{28,8},{1,21},{... | collective-permute-start | bytes 294920 | tf_op jit(solution)/shard_map/ppermute | solution.py:328
  14.1 0.0 collective-permute-done.refs_0_
  14.1 1.7 %collective-permute-start.5 = (bf16[3,64,256]{2,1,0:T(8,128)(2,1)S(1)}, bf16[3,64,256]{2,1,0:T(8,128)(2,1)S(1)}, u32[]{:S(2)}, u32[]{:S(2)}) collective-permute-start(bf16[3,64,256]{2,1,0:T(8,128)(2,1)S(1)} %get-tuple-element.44), channel_id=1, source_target_pairs={{0,12},{4,8},{8,4},{12,0},{16,28},{20,24},{24,20},{28,16},{1,13},{... | collective-permute-start | bytes 294920 | tf_op jit(solution)/shard_map/ppermute | solution.py:328
  15.7 0.0 collective-permute-done.1.refs_1_
  15.7 1.5 %collective-permute-start.6 = (bf16[3,64,256]{2,1,0:T(8,128)(2,1)S(1)}, bf16[3,64,256]{2,1,0:T(8,128)(2,1)S(1)}, u32[]{:S(2)}, u32[]{:S(2)}) collective-permute-start(bf16[3,64,256]{2,1,0:T(8,128)(2,1)S(1)} %get-tuple-element.45), channel_id=1, source_target_pairs={{0,16},{4,20},{8,24},{12,28},{16,0},{20,4},{24,8},{28,12},{1,17},{... | collective-permute-start | bytes 294920 | tf_op jit(solution)/shard_map/ppermute | solution.py:328
  17.3 0.0 collective-permute-done.2.refs_2_
  17.3 0.0 collective-permute-done.3.refs_3_
  17.3 5.2 %collective-permute-done.4.refs_4_ = bf16[3,64,256]{2,1,0:T(8,128)(2,1)S(1)} collective-permute-done((bf16[3,64,256]{2,1,0:T(8,128)(2,1)S(1)}, bf16[3,64,256]{2,1,0:T(8,128)(2,1)S(1)}, u32[]{:S(2)}, u32[]{:S(2)}) %collective-permute-start.4) | collective-permute-done | bytes 98336 | tf_op jit(solution)/shard_map/ppermute | solution.py:328
  22.5 0.0 collective-permute-done.5.refs_5_
  22.5 2.4 %collective-permute-done.6.refs_6_ = bf16[3,64,256]{2,1,0:T(8,128)(2,1)S(1)} collective-permute-done((bf16[3,64,256]{2,1,0:T(8,128)(2,1)S(1)}, bf16[3,64,256]{2,1,0:T(8,128)(2,1)S(1)}, u32[]{:S(2)}, u32[]{:S(2)}) %collective-permute-start.6) | collective-permute-done | bytes 98336 | tf_op jit(solution)/shard_map/ppermute | solution.py:328
  24.9 3.6 %conv.1 = (bf16[3,64,256]{2,1,0:T(8,128)(2,1)S(1)}, bf16[3,64,256]{2,1,0:T(8,128)(2,1)S(1)}, bf16[3,64,256]{2,1,0:T(8,128)(2,1)S(1)}, bf16[3,64,256]{2,1,0:T(8,1...) custom-call(bf16[3,64,256]{2,1,0:T(8,128)(2,1)S(1)} %collective-perm, ...), custom_call_target="tpu_custom_call" | custom-call | tf_op jit(solution)/shard_map/conv/pallas_call | solution.py:372
  28.5 2.6 %collective-permute-start.7 = (bf16[3,64,256]{2,1,0:T(8,128)(2,1)S(1)}, bf16[3,64,256]{2,1,0:T(8,128)(2,1)S(1)}, u32[]{:S(2)}, u32[]{:S(2)}) collective-permute-start(bf16[3,64,256]{2,1,0:T(8,128)(2,1)S(1)} %get-tuple-element.47), channel_id=1, source_target_pairs={{0,28},{4,24},{8,20},{12,16},{16,12},{20,8},{24,4},{28,0},{1,29},{... | collective-permute-start | bytes 294920 | tf_op jit(solution)/shard_map/ppermute | solution.py:328
  31.1 1.5 %collective-permute-start.8 = (bf16[3,64,256]{2,1,0:T(8,128)(2,1)S(1)}, bf16[3,64,256]{2,1,0:T(8,128)(2,1)S(1)}, u32[]{:S(2)}, u32[]{:S(2)}) collective-permute-start(bf16[3,64,256]{2,1,0:T(8,128)(2,1)S(1)} %get-tuple-element.48), channel_id=1, source_target_pairs={{0,4},{4,0},{8,12},{12,8},{16,20},{20,16},{24,28},{28,24},{1,5},{5... | collective-permute-start | bytes 294920 | tf_op jit(solution)/shard_map/ppermute | solution.py:328
  32.6 1.3 %collective-permute-start.9 = (bf16[3,64,256]{2,1,0:T(8,128)(2,1)S(1)}, bf16[3,64,256]{2,1,0:T(8,128)(2,1)S(1)}, u32[]{:S(2)}, u32[]{:S(2)}) collective-permute-start(bf16[3,64,256]{2,1,0:T(8,128)(2,1)S(1)} %get-tuple-element.49), channel_id=1, source_target_pairs={{0,24},{4,28},{8,16},{12,20},{16,8},{20,12},{24,0},{28,4},{1,25},{... | collective-permute-start | bytes 294920 | tf_op jit(solution)/shard_map/ppermute | solution.py:328
  33.9 0.0 collective-permute-start.10
  33.9 3.1 %collective-permute-start.11 = (bf16[3,64,256]{2,1,0:T(8,128)(2,1)S(1)}, bf16[3,64,256]{2,1,0:T(8,128)(2,1)S(1)}, u32[]{:S(2)}, u32[]{:S(2)}) collective-permute-start(bf16[3,64,256]{2,1,0:T(8,128)(2,1)S(1)} %get-tuple-element.51), channel_id=1, source_target_pairs={{0,20},{4,16},{8,28},{12,24},{16,4},{20,0},{24,12},{28,8},{1,21},{... | collective-permute-start | bytes 294920 | tf_op jit(solution)/shard_map/ppermute | solution.py:328
  36.9 0.0 collective-permute-done.7.refs_0_
  36.9 0.9 %collective-permute-start.12 = (bf16[3,64,256]{2,1,0:T(8,128)(2,1)S(1)}, bf16[3,64,256]{2,1,0:T(8,128)(2,1)S(1)}, u32[]{:S(2)}, u32[]{:S(2)}) collective-permute-start(bf16[3,64,256]{2,1,0:T(8,128)(2,1)S(1)} %get-tuple-element.52), channel_id=1, source_target_pairs={{0,12},{4,8},{8,4},{12,0},{16,28},{20,24},{24,20},{28,16},{1,13},{... | collective-permute-start | bytes 294920 | tf_op jit(solution)/shard_map/ppermute | solution.py:328
  37.9 0.0 collective-permute-done.8.refs_1_
  37.9 2.0 %collective-permute-start.13 = (bf16[3,64,256]{2,1,0:T(8,128)(2,1)S(1)}, bf16[3,64,256]{2,1,0:T(8,128)(2,1)S(1)}, u32[]{:S(2)}, u32[]{:S(2)}) collective-permute-start(bf16[3,64,256]{2,1,0:T(8,128)(2,1)S(1)} %get-tuple-element.53), channel_id=1, source_target_pairs={{0,16},{4,20},{8,24},{12,28},{16,0},{20,4},{24,8},{28,12},{1,17},{... | collective-permute-start | bytes 294920 | tf_op jit(solution)/shard_map/ppermute | solution.py:328
  39.8 0.3 collective-permute-done.9.refs_2_
  40.1 2.5 %collective-permute-done.10.refs_3_ = bf16[3,64,256]{2,1,0:T(8,128)(2,1)S(1)} collective-permute-done((bf16[3,64,256]{2,1,0:T(8,128)(2,1)S(1)}, bf16[3,64,256]{2,1,0:T(8,128)(2,1)S(1)}, u32[]{:S(2)}, u32[]{:S(2)}) %collective-permute-start.10) | collective-permute-done | bytes 98336 | tf_op jit(solution)/shard_map/ppermute | solution.py:328
  42.6 0.0 collective-permute-done.11.refs_4_
  42.6 2.0 %collective-permute-done.12.refs_5_ = bf16[3,64,256]{2,1,0:T(8,128)(2,1)S(1)} collective-permute-done((bf16[3,64,256]{2,1,0:T(8,128)(2,1)S(1)}, bf16[3,64,256]{2,1,0:T(8,128)(2,1)S(1)}, u32[]{:S(2)}, u32[]{:S(2)}) %collective-permute-start.12) | collective-permute-done | bytes 98336 | tf_op jit(solution)/shard_map/ppermute | solution.py:328
  44.6 2.0 %collective-permute-done.13.refs_6_ = bf16[3,64,256]{2,1,0:T(8,128)(2,1)S(1)} collective-permute-done((bf16[3,64,256]{2,1,0:T(8,128)(2,1)S(1)}, bf16[3,64,256]{2,1,0:T(8,128)(2,1)S(1)}, u32[]{:S(2)}, u32[]{:S(2)}) %collective-permute-start.13) | collective-permute-done | bytes 98336 | tf_op jit(solution)/shard_map/ppermute | solution.py:328
  46.6 0.7 %mate.1 = (bf16[3,256,512]{2,1,0:T(8,128)(2,1)S(1)}, bf16[256,512]{1,0:T(8,128)(2,1)S(1)}) custom-call(bf16[3,64,256]{2,1,0:T(8,128)(2,1)S(1)} %collective-permute-done.7.refs_0_, bf16[3,64,256]{2,1,0:T(8,128)(2,1)S(1)} %collective-permute-done.8.refs_1_, bf16[3,64,256]{2,1,0:T(8,128)(2,1)S(1)} %collective-permute-done.9.refs_2_, ...), custom_call_target="tpu_custom_call" | custom-call | flops 805306368 | bytes 4194304 | tf_op jit(solution)/shard_map/mate/pallas_call | solution.py:389
  47.2 0.1 collective-permute-start.14
  47.3 1.0 %far.1 = (f32[256,512]{1,0:T(8,128)S(1)}, bf16[256,512]{1,0:T(8,128)(2,1)S(1)}) custom-call(bf16[3,256,512]{2,1,0:T(8,128)(2,1)S(1)} %get-tuple-element.67.lhs_ref, bf16[2048,512]{1,0:T(8,128)(2,1)S(1)} %get-tuple-element.58.refs_11_.wk_ref, bf16[2048,512]{1,0:T(8,128)(2,1)S(1)} %get-tuple-element.59.refs_12_.wq_ref, ...), custom_call_target="tpu_custom_call" | custom-call | flops 805306368 | bytes 4194304 | tf_op jit(solution)/shard_map/far/pallas_call | solution.py:399
  48.3 0.5 collective-permute-done.14
  48.8 0.1 add_convert_fusion.1
  48.9 1.5 %collective-permute-start.15 = (bf16[256,512]{1,0:T(8,128)(2,1)S(1)}, bf16[256,512]{1,0:T(8,128)(2,1)S(1)}, u32[]{:S(2)}, u32[]{:S(2)}) collective-permute-start(bf16[256,512]{1,0:T(8,128)(2,1)S(1)} %add_convert_fusion.1), channel_id=1, source_target_pairs={{0,2},{1,3},{2,0},{3,1},{4,6},{5,7},{6,4},{7,5},{8,10},{9,11},{10,... | collective-permute-start | bytes 786440 | tf_op jit(solution)/shard_map/ppermute | solution.py:328
  50.5 0.0 collective-permute-start.16
  50.5 0.6 %own.1 = f32[256,512]{1,0:T(8,128)S(1)} custom-call(bf16[3,256,512]{2,1,0:T(8,128)(2,1)S(1)} %get-tuple-element.67.lhs_ref, bf16[2048,512]{1,0:T(8,128)(2,1)S(1)} %get-tuple-element.58.refs_11_.wk_ref, bf16[2048,512]{1,0:T(8,128)(2,1)S(1)} %get-tuple-element.59.refs_12_.wq_ref, bf16[2048,512]{1,0:T(8,128)(2,1)S(1)} %get-tuple-element.60.refs_13_.wv_ref), custom_call_target="tpu_custom_call" | custom-call | flops 805306368 | bytes 4194304 | tf_op jit(solution)/shard_map/own/pallas_call | solution.py:420
  51.1 0.9 %turn.1 = bf16[256,512]{1,0:T(8,128)(2,1)} custom-call(bf16[3,64,256]{2,1,0:T(8,128)(2,1)S(1)} %collective-permute-done.7.refs_0_, bf16[3,64,256]{2,1,0:T(8,128)(2,1)S(1)} %collective-permute-done.8.refs_1_, bf16[3,64,256]{2,1,0:T(8,128)(2,1)S(1)} %collective-permute-done.9.refs_2_, bf16[3,64,256]{2,1,0:T(8,128)(2,1)S(1)} %collective-permute-done.10.refs_3_, ...), custom_call_target="tpu_custom_call" | custom-call | flops 805306368 | bytes 4194304 | tf_op jit(solution)/shard_map/turn/pallas_call | solution.py:411
  52.0 5.4 %collective-permute-done.15 = bf16[256,512]{1,0:T(8,128)(2,1)S(1)} collective-permute-done((bf16[256,512]{1,0:T(8,128)(2,1)S(1)}, bf16[256,512]{1,0:T(8,128)(2,1)S(1)}, u32[]{:S(2)}, u32[]{:S(2)}) %collective-permute-start.15) | collective-permute-done | bytes 262176 | tf_op jit(solution)/shard_map/ppermute | solution.py:328
  57.3 0.0 collective-permute-done.16
  57.3 0.8 %add_convert_fusion = bf16[256,512]{1,0:T(8,128)(2,1)} fusion(f32[256,512]{1,0:T(8,128)S(1)} %own.1, bf16[256,512]{1,0:T(8,128)(2,1)S(1)} %collective-permute-done.16, bf16[256,512]{1,0:T(8,128)(2,1)S(1)} %collective-permute-done.15), kind=kLoop, calls=%fused_computation | loop fusion | flops 655360 | bytes 1310720 | tf_op jit(solution)/shard_map/convert_element_type | solution.py:429
Async XLA Ops:
  2.1 11.9 %collective-permute-start = (bf16[3,64,256]{2,1,0:T(8,128)(2,1)S(1)}, bf16[3,64,256]{2,1,0:T(8,128)(2,1)S(1)}, u32[]{:S(2)}, u32[]{:S(2)}) collective-permute-start(bf16[3,64,256]{2,1,0:T(8,128)(2,1)S(1)} %get-tuple-element.39), channel_id=1, source_target_pairs={{0,28},{4,24},{8,20},{12,16},{16,12},{20,8},{24,4},{28,0},{1,29},{... | collective-permute-start | bytes 294920 | tf_op jit(solution)/shard_map/ppermute | solution.py:328
  8.2 7.5 %collective-permute-start.1 = (bf16[3,64,256]{2,1,0:T(8,128)(2,1)S(1)}, bf16[3,64,256]{2,1,0:T(8,128)(2,1)S(1)}, u32[]{:S(2)}, u32[]{:S(2)}) collective-permute-start(bf16[3,64,256]{2,1,0:T(8,128)(2,1)S(1)} %get-tuple-element.40), channel_id=1, source_target_pairs={{0,4},{4,0},{8,12},{12,8},{16,20},{20,16},{24,28},{28,24},{1,5},{5... | collective-permute-start | bytes 294920 | tf_op jit(solution)/shard_map/ppermute | solution.py:328
  8.7 8.5 %collective-permute-start.2 = (bf16[3,64,256]{2,1,0:T(8,128)(2,1)S(1)}, bf16[3,64,256]{2,1,0:T(8,128)(2,1)S(1)}, u32[]{:S(2)}, u32[]{:S(2)}) collective-permute-start(bf16[3,64,256]{2,1,0:T(8,128)(2,1)S(1)} %get-tuple-element.41), channel_id=1, source_target_pairs={{0,24},{4,28},{8,16},{12,20},{16,8},{20,12},{24,0},{28,4},{1,25},{... | collective-permute-start | bytes 294920 | tf_op jit(solution)/shard_map/ppermute | solution.py:328
  8.9 8.4 %collective-permute-start.3 = (bf16[3,64,256]{2,1,0:T(8,128)(2,1)S(1)}, bf16[3,64,256]{2,1,0:T(8,128)(2,1)S(1)}, u32[]{:S(2)}, u32[]{:S(2)}) collective-permute-start(bf16[3,64,256]{2,1,0:T(8,128)(2,1)S(1)} %get-tuple-element.42), channel_id=1, source_target_pairs={{0,8},{4,12},{8,0},{12,4},{16,24},{20,28},{24,16},{28,20},{1,9},{5... | collective-permute-start | bytes 294920 | tf_op jit(solution)/shard_map/ppermute | solution.py:328
  8.9 13.6 %collective-permute-start.4 = (bf16[3,64,256]{2,1,0:T(8,128)(2,1)S(1)}, bf16[3,64,256]{2,1,0:T(8,128)(2,1)S(1)}, u32[]{:S(2)}, u32[]{:S(2)}) collective-permute-start(bf16[3,64,256]{2,1,0:T(8,128)(2,1)S(1)} %get-tuple-element.43), channel_id=1, source_target_pairs={{0,20},{4,16},{8,28},{12,24},{16,4},{20,0},{24,12},{28,8},{1,21},{... | collective-permute-start | bytes 294920 | tf_op jit(solution)/shard_map/ppermute | solution.py:328
  14.1 8.4 %collective-permute-start.5 = (bf16[3,64,256]{2,1,0:T(8,128)(2,1)S(1)}, bf16[3,64,256]{2,1,0:T(8,128)(2,1)S(1)}, u32[]{:S(2)}, u32[]{:S(2)}) collective-permute-start(bf16[3,64,256]{2,1,0:T(8,128)(2,1)S(1)} %get-tuple-element.44), channel_id=1, source_target_pairs={{0,12},{4,8},{8,4},{12,0},{16,28},{20,24},{24,20},{28,16},{1,13},{... | collective-permute-start | bytes 294920 | tf_op jit(solution)/shard_map/ppermute | solution.py:328
  15.7 9.2 %collective-permute-start.6 = (bf16[3,64,256]{2,1,0:T(8,128)(2,1)S(1)}, bf16[3,64,256]{2,1,0:T(8,128)(2,1)S(1)}, u32[]{:S(2)}, u32[]{:S(2)}) collective-permute-start(bf16[3,64,256]{2,1,0:T(8,128)(2,1)S(1)} %get-tuple-element.45), channel_id=1, source_target_pairs={{0,16},{4,20},{8,24},{12,28},{16,0},{20,4},{24,8},{28,12},{1,17},{... | collective-permute-start | bytes 294920 | tf_op jit(solution)/shard_map/ppermute | solution.py:328
  28.5 8.4 %collective-permute-start.7 = (bf16[3,64,256]{2,1,0:T(8,128)(2,1)S(1)}, bf16[3,64,256]{2,1,0:T(8,128)(2,1)S(1)}, u32[]{:S(2)}, u32[]{:S(2)}) collective-permute-start(bf16[3,64,256]{2,1,0:T(8,128)(2,1)S(1)} %get-tuple-element.47), channel_id=1, source_target_pairs={{0,28},{4,24},{8,20},{12,16},{16,12},{20,8},{24,4},{28,0},{1,29},{... | collective-permute-start | bytes 294920 | tf_op jit(solution)/shard_map/ppermute | solution.py:328
  31.1 6.8 %collective-permute-start.8 = (bf16[3,64,256]{2,1,0:T(8,128)(2,1)S(1)}, bf16[3,64,256]{2,1,0:T(8,128)(2,1)S(1)}, u32[]{:S(2)}, u32[]{:S(2)}) collective-permute-start(bf16[3,64,256]{2,1,0:T(8,128)(2,1)S(1)} %get-tuple-element.48), channel_id=1, source_target_pairs={{0,4},{4,0},{8,12},{12,8},{16,20},{20,16},{24,28},{28,24},{1,5},{5... | collective-permute-start | bytes 294920 | tf_op jit(solution)/shard_map/ppermute | solution.py:328
  32.6 7.6 %collective-permute-start.9 = (bf16[3,64,256]{2,1,0:T(8,128)(2,1)S(1)}, bf16[3,64,256]{2,1,0:T(8,128)(2,1)S(1)}, u32[]{:S(2)}, u32[]{:S(2)}) collective-permute-start(bf16[3,64,256]{2,1,0:T(8,128)(2,1)S(1)} %get-tuple-element.49), channel_id=1, source_target_pairs={{0,24},{4,28},{8,16},{12,20},{16,8},{20,12},{24,0},{28,4},{1,25},{... | collective-permute-start | bytes 294920 | tf_op jit(solution)/shard_map/ppermute | solution.py:328
  33.9 8.7 %collective-permute-start.10 = (bf16[3,64,256]{2,1,0:T(8,128)(2,1)S(1)}, bf16[3,64,256]{2,1,0:T(8,128)(2,1)S(1)}, u32[]{:S(2)}, u32[]{:S(2)}) collective-permute-start(bf16[3,64,256]{2,1,0:T(8,128)(2,1)S(1)} %get-tuple-element.50), channel_id=1, source_target_pairs={{0,8},{4,12},{8,0},{12,4},{16,24},{20,28},{24,16},{28,20},{1,9},{5... | collective-permute-start | bytes 294920 | tf_op jit(solution)/shard_map/ppermute | solution.py:328
  33.9 8.7 %collective-permute-start.11 = (bf16[3,64,256]{2,1,0:T(8,128)(2,1)S(1)}, bf16[3,64,256]{2,1,0:T(8,128)(2,1)S(1)}, u32[]{:S(2)}, u32[]{:S(2)}) collective-permute-start(bf16[3,64,256]{2,1,0:T(8,128)(2,1)S(1)} %get-tuple-element.51), channel_id=1, source_target_pairs={{0,20},{4,16},{8,28},{12,24},{16,4},{20,0},{24,12},{28,8},{1,21},{... | collective-permute-start | bytes 294920 | tf_op jit(solution)/shard_map/ppermute | solution.py:328
  36.9 7.7 %collective-permute-start.12 = (bf16[3,64,256]{2,1,0:T(8,128)(2,1)S(1)}, bf16[3,64,256]{2,1,0:T(8,128)(2,1)S(1)}, u32[]{:S(2)}, u32[]{:S(2)}) collective-permute-start(bf16[3,64,256]{2,1,0:T(8,128)(2,1)S(1)} %get-tuple-element.52), channel_id=1, source_target_pairs={{0,12},{4,8},{8,4},{12,0},{16,28},{20,24},{24,20},{28,16},{1,13},{... | collective-permute-start | bytes 294920 | tf_op jit(solution)/shard_map/ppermute | solution.py:328
  37.9 8.7 %collective-permute-start.13 = (bf16[3,64,256]{2,1,0:T(8,128)(2,1)S(1)}, bf16[3,64,256]{2,1,0:T(8,128)(2,1)S(1)}, u32[]{:S(2)}, u32[]{:S(2)}) collective-permute-start(bf16[3,64,256]{2,1,0:T(8,128)(2,1)S(1)} %get-tuple-element.53), channel_id=1, source_target_pairs={{0,16},{4,20},{8,24},{12,28},{16,0},{20,4},{24,8},{28,12},{1,17},{... | collective-permute-start | bytes 294920 | tf_op jit(solution)/shard_map/ppermute | solution.py:328
  47.2 1.6 %collective-permute-start.14 = (bf16[256,512]{1,0:T(8,128)(2,1)S(1)}, bf16[256,512]{1,0:T(8,128)(2,1)S(1)}, u32[]{:S(2)}, u32[]{:S(2)}) collective-permute-start(bf16[256,512]{1,0:T(8,128)(2,1)S(1)} %get-tuple-element.63), channel_id=1, source_target_pairs={{0,1},{1,0},{2,3},{3,2},{4,5},{5,4},{6,7},{7,6},{8,9},{9,8},{10,11... | collective-permute-start | bytes 786440 | tf_op jit(solution)/shard_map/ppermute | solution.py:328
  48.9 8.4 %collective-permute-start.15 = (bf16[256,512]{1,0:T(8,128)(2,1)S(1)}, bf16[256,512]{1,0:T(8,128)(2,1)S(1)}, u32[]{:S(2)}, u32[]{:S(2)}) collective-permute-start(bf16[256,512]{1,0:T(8,128)(2,1)S(1)} %add_convert_fusion.1), channel_id=1, source_target_pairs={{0,2},{1,3},{2,0},{3,1},{4,6},{5,7},{6,4},{7,5},{8,10},{9,11},{10,... | collective-permute-start | bytes 786440 | tf_op jit(solution)/shard_map/ppermute | solution.py:328
  50.5 6.9 %collective-permute-start.16 = (bf16[256,512]{1,0:T(8,128)(2,1)S(1)}, bf16[256,512]{1,0:T(8,128)(2,1)S(1)}, u32[]{:S(2)}, u32[]{:S(2)}) collective-permute-start(bf16[256,512]{1,0:T(8,128)(2,1)S(1)} %get-tuple-element.66), channel_id=1, source_target_pairs={{0,1},{1,0},{2,3},{3,2},{4,5},{5,4},{6,7},{7,6},{8,9},{9,8},{10,11... | collective-permute-start | bytes 786440 | tf_op jit(solution)/shard_map/ppermute | solution.py:328
